TPU v7x, 32 devices: a whole 2x2x4 slice. The times are simulated.
32 devices in a mesh: req: 8 (over z, x), head: 4 (over y, core).
Axes of the slice: x: 2, y: 2, z: 4, core: 2. Of those that a mesh axis runs over, the one named last changes fastest.
Arguments:
- token_ids: int32 [256, 4], P('req'), may hold values from 0 to 31999
- state_perm: int32 [256], P('req'), may hold values from 0 to 255, as said below
- token_count: int32 [256], P('req'), may hold values from 1 to 4
- tenant_bounds: int32 [5], replicated, may hold values from 0 to 256, as said below
- old_states: bfloat16 [256, 16, 128, 128], P('req', 'head'), may hold values from -6 to 6
- embedding: bfloat16 [32000, 2048], P('req', 'head'), may hold values from -6 to 6
- mixer_gain: float32 [2048], replicated, may hold values from 0.5 to 1.5
- query_weight: bfloat16 [2048, 2048], P(None, 'head'), may hold values from -0.125 to 0.125
- forget_weight: bfloat16 [2048, 2048], P(None, 'head'), may hold values from -0.125 to 0.125
- input_weight: bfloat16 [2048, 2048], P(None, 'head'), may hold values from -0.125 to 0.125
- forget_floor: float32 [2048], P('head'), may hold values from 0 to 0.9
- group_gain: float32 [2048], P('head'), may hold values from 0.5 to 1.5
- output_weight: bfloat16 [2048, 2048], P('head'), may hold values from -0.125 to 0.125
- feed_gain: float32 [2048], replicated, may hold values from 0.5 to 1.5
- gate_weight: bfloat16 [2048, 5632], P('head', 'req'), may hold values from -0.125 to 0.125
- up_weight: bfloat16 [2048, 5632], P('head', 'req'), may hold values from -0.125 to 0.125
- down_weight: bfloat16 [5632, 2048], P('req', 'head'), may hold values from -0.078125 to 0.078125
- final_gain: float32 [2048], P('head'), may hold values from 0.5 to 1.5
- tenant_gain: float32 [4, 2048], P(None, 'head'), may hold values from 0.1 to 1.9
- vocab_weight: bfloat16 [2048, 32000], P(None, ('req', 'head')), may hold values from -0.3984375 to 0.3984375
Outputs:
- hidden: float32 [256, 4, 2048], P('req', None, 'head')
- new_states: bfloat16 [256, 16, 128, 128], P('req', 'head')
- last_norm: float32 [256], P('req')
- greatest: float32 [256], P('req')
Inputs may be any that keep to these rules, and one draw needn't show every extreme that they name: A permutation of the 256 slots: new slot n takes the state of old slot state_perm[n]. The 32 new slots k * 32 to k * 32 + 31 take exactly 4 old slots from each aligned block of 32 old slots. `tenant_bounds`: entry 0 is 0, entry 4 is 256, and the entries rise strictly.
All inputs are finite; a program needn't handle non-finite values.
Results may differ from a plain program's by a relative error of at most 0.018.
Values may be sent and summed in bfloat16 or wider, within the bound.
No kernel may reach another device: no remote copies, remote signals or barrier semaphores. Data moves between devices by JAX's collectives and lax.ppermute only.
A program may use at most 128 MiB of HBM per device.

v0:
```python
import jax
import jax.numpy as jnp
from jax import lax
from jax.sharding import PartitionSpec as P

D = 2048
HEAD_DIM = 128


epsilon = 1e-06


def norm_scale(values):
    return lax.rsqrt(jnp.mean(values * values, axis=-1, keepdims=True) + epsilon)


def rounded(values):
    return lax.optimization_barrier(values.astype(jnp.bfloat16)).astype(jnp.float32)


def on_device(
    token_ids,
    state_perm,
    token_count,
    tenant_bounds,
    old_states,
    embedding,
    mixer_gain,
    query_weight,
    forget_weight,
    input_weight,
    forget_floor,
    group_gain,
    output_weight,
    feed_gain,
    gate_weight,
    up_weight,
    down_weight,
    final_gain,
    tenant_gain,
    vocab_weight,
):
    local_requests = token_ids.shape[0]
    step_count = token_ids.shape[1]
    local_tokens = local_requests * step_count
    req_count = lax.axis_size("req")
    head_count = lax.axis_size("head")
    req_index = lax.axis_index("req")
    head_index = lax.axis_index("head")
    all_ids, all_perm, all_count = (
        lax.all_gather(token_ids, "req", axis=0, tiled=True),
        lax.all_gather(state_perm, "req", axis=0, tiled=True),
        lax.all_gather(token_count, "req", axis=0, tiled=True),
    )
    all_requests = all_perm.shape[0]
    vocab_rows = embedding.shape[0]
    vocab_start = req_index * vocab_rows
    flat_ids = all_ids.reshape(-1)
    local_ids = flat_ids - vocab_start
    inside = (local_ids >= 0) & (local_ids < vocab_rows)
    picked = jnp.take(embedding, jnp.clip(local_ids, 0, vocab_rows - 1), axis=0)
    embed_part = lax.psum_scatter(
        jnp.where(inside[:, None], picked.astype(jnp.float32), 0.0).astype(jnp.bfloat16),
        "req",
        scatter_dimension=0,
        tiled=True,
    )
    embedded = lax.all_gather(embed_part, "head", axis=1, tiled=True)
    stream = embedded.astype(jnp.float32)
    normed = (stream * norm_scale(stream) * mixer_gain).astype(jnp.bfloat16)
    slot_range = jnp.arange(local_requests, dtype=jnp.int32)
    slot_global = req_index * local_requests + slot_range
    every_slot = jnp.arange(all_requests, dtype=jnp.int32)
    new_slot = jnp.sum(
        jnp.where(all_perm[None, :] == slot_global[:, None], every_slot[None, :], 0), axis=1
    )
    dest_device = new_slot // local_requests
    sends = local_requests // req_count
    dest_rank = jnp.sum(
        (
            (dest_device[None, :] == dest_device[:, None]) & (new_slot[None, :] < new_slot[:, None])
        ).astype(jnp.int32),
        axis=1,
    )
    send_place = dest_device * sends + dest_rank
    send_order = jnp.sum(
        jnp.where(send_place[None, :] == slot_range[:, None], slot_range[None, :], 0), axis=1
    )
    outgoing = jnp.take(old_states, send_order, axis=0)
    arrived = lax.all_to_all(outgoing, "req", split_axis=0, concat_axis=0, tiled=True)
    source = state_perm // local_requests
    source_rank = jnp.sum(
        ((source[None, :] == source[:, None]) & (slot_range[None, :] < slot_range[:, None])).astype(
            jnp.int32
        ),
        axis=1,
    )
    state_now = jnp.take(arrived, source * sends + source_rank, axis=0).astype(jnp.float32)
    local_heads = old_states.shape[1]
    key_width = old_states.shape[2]
    query_raw = jnp.dot(normed, query_weight, preferred_element_type=jnp.float32)
    forget_raw = jnp.dot(normed, forget_weight, preferred_element_type=jnp.float32)
    value_part = jnp.dot(normed, input_weight, preferred_element_type=jnp.float32)
    query_act = query_raw * jax.nn.sigmoid(query_raw) * HEAD_DIM ** (-0.5)
    live_mask = (jnp.arange(step_count)[None, :] < token_count[:, None]).reshape(local_tokens, 1)
    forget_gate = jnp.where(
        live_mask, forget_floor + (1.0 - forget_floor) * jax.nn.sigmoid(forget_raw), 1.0
    )
    key_part = 1.0 - forget_gate
    head_shape = (local_requests, step_count, local_heads, key_width)
    query_act = query_act.reshape(head_shape)
    forget_gate = forget_gate.reshape(head_shape)
    key_part = key_part.reshape(head_shape)
    value_part = value_part.reshape(head_shape)
    outputs = []
    for position in range(step_count):
        state_now = (
            forget_gate[:, position, :, :, None] * state_now
            + key_part[:, position, :, :, None] * value_part[:, position, :, None, :]
        )
        outputs.append(
            jnp.einsum(
                "rhk,rhkv->rhv", query_act[:, position], state_now, precision=lax.Precision.HIGHEST
            )
        )
    new_states = state_now.astype(jnp.bfloat16)
    mixed_out = jnp.stack(outputs, axis=1).reshape(local_tokens, local_heads * key_width)
    group_square = lax.psum(jnp.sum(mixed_out * mixed_out, axis=1), "head")
    grouped = (mixed_out * lax.rsqrt(group_square / D + epsilon)[:, None] * group_gain).astype(
        jnp.bfloat16
    )
    mixer_part = jnp.dot(grouped, output_weight, preferred_element_type=jnp.float32)
    width_head = D // head_count
    column_start = head_index * width_head
    after_mixer = stream + lax.psum(mixer_part.astype(jnp.bfloat16), "head").astype(jnp.float32)
    feed_full = (after_mixer * norm_scale(after_mixer) * feed_gain).astype(jnp.bfloat16)
    mixer_mine = lax.dynamic_slice_in_dim(after_mixer, column_start, width_head, 1)
    feed_mine = lax.dynamic_slice_in_dim(feed_full, column_start, width_head, 1)
    units_local = gate_weight.shape[1]
    row_piece = lax.all_gather(feed_mine, "req", axis=0, tiled=True)
    gate_part = jnp.dot(row_piece, gate_weight, preferred_element_type=jnp.float32)
    up_part = jnp.dot(row_piece, up_weight, preferred_element_type=jnp.float32)
    partial_sums = rounded(jnp.concatenate([gate_part, up_part], axis=1))
    summed = lax.psum(partial_sums.astype(jnp.bfloat16), "head").astype(jnp.float32)
    activated = (jax.nn.silu(summed[:, :units_local]) * summed[:, units_local:]).astype(
        jnp.bfloat16
    )
    hidden_mine = mixer_mine + lax.psum_scatter(
        rounded(jnp.dot(activated, down_weight, preferred_element_type=jnp.float32)).astype(
            jnp.bfloat16
        ),
        "req",
        scatter_dimension=0,
        tiled=True,
    ).astype(jnp.float32)
    final_square = lax.psum(jnp.sum(hidden_mine * hidden_mine, axis=1), "head")
    mean_square = final_square / D
    tenant_index = jnp.sum(
        (slot_global[:, None] >= tenant_bounds[None, 1:-1]).astype(jnp.int32), axis=1
    )
    tenant_total = tenant_gain.shape[0]
    tenant_onehot = (tenant_index[:, None] == jnp.arange(tenant_total)[None, :]).astype(jnp.float32)
    request_gain = jnp.dot(tenant_onehot, tenant_gain, precision=lax.Precision.HIGHEST)
    token_gain = jnp.repeat(request_gain, step_count, axis=0)
    final_hidden = (
        hidden_mine * lax.rsqrt(mean_square + epsilon)[:, None] * final_gain * token_gain
    ).astype(jnp.bfloat16)
    last_pick = jnp.arange(step_count)[None, :] == (token_count - 1)[:, None]
    last_norm = jnp.sqrt(
        jnp.sum(jnp.where(last_pick, mean_square.reshape(local_requests, step_count), 0.0), axis=1)
        + epsilon
    )
    full_final = lax.all_gather(final_hidden, "head", axis=1, tiled=True)
    live_all = jnp.arange(step_count)[None, :] < all_count[:, None]
    token_best = jnp.max(
        jnp.dot(
            lax.all_gather(full_final, "req", axis=0, tiled=True),
            vocab_weight,
            preferred_element_type=jnp.float32,
        ),
        axis=1,
    )
    per_request = jnp.max(
        jnp.where(live_all, token_best.reshape(all_requests, step_count), -1e30), axis=1
    )
    best_value = lax.pmax(per_request, ("req", "head"))
    greatest = lax.dynamic_slice_in_dim(best_value, req_index * local_requests, local_requests, 0)
    return (
        hidden_mine.reshape(local_requests, step_count, width_head),
        new_states,
        last_norm,
        greatest,
    )


def solution(mesh):
    placed = (
        P("req", None),
        P("req"),
        P("req"),
        P(),
        P("req", "head", None, None),
        P("req", "head"),
        P(),
        P(None, "head"),
        P(None, "head"),
        P(None, "head"),
        P("head"),
        P("head"),
        P("head", None),
        P(),
        P("head", "req"),
        P("head", "req"),
        P("req", "head"),
        P("head"),
        P(None, "head"),
        P(None, ("req", "head")),
    )
    return jax.shard_map(
        on_device,
        mesh=mesh,
        in_specs=placed,
        out_specs=(P("req", None, "head"), P("req", "head", None, None), P("req"), P("req")),
        check_vma=False,
    )
```

profile of v0, /device:TPU:0, one launch (start us, length us, event | category | flops | bytes accessed | tf_op | source)
XLA Modules:
  0.0 689.9 jit_solution(7857962502097559398)
XLA Ops:
  11.0 13.6 %all-reduce.2 = (s32[256]{0:T(256)S(1)}, s32[256]{0:T(256)}) all-reduce(s32[256]{0:T(256)S(1)} %dynamic-update-slice, s32[256]{0:T(256)S(1)} %dynamic-update-slice.1), channel_id=1, replica_groups=mesh['req'=8,'head'=4] {'req'}, use_global_device_ids=true, to_apply=%add | all-reduce | flops 512 | bytes 4096
  25.2 5.3 gather_fusion.1
  30.4 4.7 broadcast_select_fusion.1
  35.1 4.7 all-to-all-start
  39.9 108.9 %all-gather = s32[8,32,4]{1,2,0:T(4,128)S(1)} all-gather(s32[1,32,4]{1,2,0:T(4,128)S(1)} %bitcast.92), channel_id=1, replica_groups=mesh['req'=8,'head'=4] {'req'}, dimensions={0}, use_global_device_ids=true | all-gather | bytes 4608 | tf_op jit(solution)/shard_map/all_gather | solution.py:51
  149.5 6.7 gather_fusion
  158.4 60.3 %reduce-scatter.3.cloned.1.call-done = bf16[128,512]{1,0:T(8,128)(2,1)} async-done(((bf16[1024,512]{1,0:T(8,128)(2,1)}), bf16[128,512]{1,0:T(8,128)(2,1)}) %reduce-scatter.3.cloned.1.call-update) | async-done | bytes 131088 | tf_op jit(solution)/shard_map/reduce_scatter | solution.py:62
  218.8 7.5 %all_gather.22 = bf16[128,2048]{1,0:T(8,128)(2,1)S(1)} all-gather(bf16[128,512]{1,0:T(8,128)(2,1)} %reduce-scatter.3.cloned.1.call-done), channel_id=1, replica_groups=mesh['req'=8,'head'=4] {'head'}, dimensions={1}, use_global_device_ids=true | all-gather | bytes 655360 | tf_op jit(solution)/shard_map/all_gather | solution.py:68
  226.5 2.1 fusion.38
  228.7 2.1 multiply_multiply_fusion
  230.9 2.8 broadcast_subtract_fusion
  238.1 5.3 gather_fusion.2
  243.4 11.9 %fusion = f32[32,4,1,128]{3,2,1,0:T(1,128)S(1)} fusion(f32[32,4,128,1]{2,3,1,0:T(1,128)S(1)} %bitcast.90, f32[32,4,128]{2,1,0:T(4,128)S(1)} %get-tuple-element.27, f32[32,4,128]{2,1,0:T(4,128)S(1)} %get-tuple-element.38, f32[32,4,128]{2,1,0:T(4,128)S(1)} %get-tuple-element.19, bf16[32,4,128,128]{3,2,1,0:T(8,128)(2,1)} %gather_fusion.2, ...), kind=kOutput, calls=%fused_computation.7 | convolution fusion | flops 35651584 | bytes 4522016 | tf_op jit(solution)/shard_map/rhk,rhkv->rhv/dot_general | solution.py:122
  255.4 17.2 %fusion.1 = f32[32,4,1,128]{3,2,1,0:T(1,128)S(1)} fusion(f32[32,4,128,1]{2,3,1,0:T(1,128)S(1)} %bitcast.89, f32[32,4,128]{2,1,0:T(4,128)S(1)} %get-tuple-element.30, f32[32,4,128]{2,1,0:T(4,128)S(1)} %get-tuple-element.35, f32[32,4,128]{2,1,0:T(4,128)S(1)} %copy-done.12, f32[32,4,128]{2,1,0:T(4,128)S(1)} %get-tuple-element.27, ...), kind=kOutput, calls=%fused_computation.8 | convolution fusion | flops 41943040 | bytes 4718624 | tf_op jit(solution)/shard_map/rhk,rhkv->rhv/dot_general | solution.py:122
  272.6 24.7 %fusion.16 = f32[32,4,1,128]{3,2,1,0:T(1,128)S(1)} fusion(f32[32,4,128,1]{2,3,1,0:T(1,128)S(1)} %bitcast.88, f32[32,4,128]{2,1,0:T(4,128)S(1)} %get-tuple-element.29, f32[32,4,128]{2,1,0:T(4,128)S(1)} %get-tuple-element.36, f32[32,4,128]{2,1,0:T(4,128)S(1)} %copy-done.11, f32[32,4,128]{2,1,0:T(4,128)S(1)} %get-tuple-element.30, ...), kind=kOutput, calls=%fused_computation.25 | convolution fusion | flops 48234496 | bytes 4915232 | tf_op jit(solution)/shard_map/rhk,rhkv->rhv/dot_general | solution.py:122
  297.4 29.1 %fusion.3 = f32[32,4,1,128]{3,2,1,0:T(1,128)S(1)} fusion(f32[32,4,128,1]{2,3,1,0:T(1,128)S(1)} %bitcast.87, f32[32,4,128]{2,1,0:T(4,128)S(1)} %get-tuple-element.28, f32[32,4,128]{2,1,0:T(4,128)S(1)} %get-tuple-element.37, f32[32,4,128]{2,1,0:T(4,128)S(1)} %get-tuple-element.20, f32[32,4,128]{2,1,0:T(4,128)S(1)} %get-tuple-element.29, ...), kind=kOutput, calls=%fused_computation.10 | convolution fusion | flops 54525952 | bytes 5111840 | tf_op jit(solution)/shard_map/rhk,rhkv->rhv/dot_general | solution.py:122
  326.9 6.4 psum.28
  333.3 2.0 convolution_convert_fusion
  336.1 31.3 %all-reduce.6.cloned.1.call-done = bf16[128,2048]{1,0:T(8,128)(2,1)} async-done(((bf16[128,2048]{1,0:T(8,128)(2,1)}), bf16[128,2048]{1,0:T(8,128)(2,1)}) %all-reduce.6.cloned.1.call-update) | async-done | bytes 524304 | tf_op jit(solution)/shard_map/psum | solution.py:135
  370.5 40.3 %all-gather.4.cloned.1.call-done = bf16[1024,512]{1,0:T(8,128)(2,1)} async-done(((bf16[128,512]{1,0:T(8,128)(2,1)}), bf16[1024,512]{1,0:T(8,128)(2,1)}) %all-gather.4.cloned.1.call-update) | async-done | bytes 1048592 | tf_op jit(solution)/shard_map/all_gather | solution.py:140
  410.7 2.5 convolution_convert_fusion.1
  414.2 1.9 pad_maximum_fusion
  416.2 63.0 %all-reduce.8.cloned.1.call-done = bf16[1024,1408]{0,1:T(8,128)(2,1)} async-done(((bf16[1024,1408]{0,1:T(8,128)(2,1)}), bf16[1024,1408]{0,1:T(8,128)(2,1)}) %all-reduce.8.cloned.1.call-update) | async-done | bytes 2883600 | tf_op jit(solution)/shard_map/psum | solution.py:144
  479.2 2.5 convert_element_type.71
  481.8 3.3 convolution_convert_fusion.3
  485.9 62.8 %reduce-scatter.5.cloned.1.call-done = bf16[128,512]{1,0:T(8,128)(2,1)} async-done(((bf16[1024,512]{1,0:T(8,128)(2,1)}), bf16[128,512]{1,0:T(8,128)(2,1)}) %reduce-scatter.5.cloned.1.call-update) | async-done | bytes 131088 | tf_op jit(solution)/shard_map/reduce_scatter | solution.py:148
  549.9 5.7 psum.31
  555.7 7.9 %all_gather.26 = bf16[128,2048]{1,0:T(8,128)(2,1)} all-gather(bf16[128,512]{1,0:T(8,128)(2,1)S(1)} %multiply_convert_fusion), channel_id=1, replica_groups=mesh['req'=8,'head'=4] {'head'}, dimensions={1}, use_global_device_ids=true | all-gather | bytes 655360 | tf_op jit(solution)/shard_map/all_gather | solution.py:173
  563.7 21.9 %fusion.2 = bf16[32,4,128,128]{3,2,1,0:T(8,128)(2,1)} fusion(f32[32,4,128]{2,1,0:T(4,128)S(1)} %get-tuple-element.28, f32[32,4,128]{2,1,0:T(4,128)S(1)} %copy-done.4, f32[32,4,128]{2,1,0:T(4,128)S(1)} %copy-done.10, f32[32,4,128]{2,1,0:T(4,128)S(1)} %get-tuple-element.29, f32[32,4,128]{2,1,0:T(4,128)S(1)} %get-tuple-element.36, ...), kind=kLoop, calls=%fused_computation.9 | loop fusion | flops 31457280 | bytes 9175072 | tf_op jit(solution)/shard_map/convert_element_type | solution.py:126
  587.2 48.4 %all-gather.6.cloned.1.call-done = bf16[1024,2048]{1,0:T(8,128)(2,1)} async-done(((bf16[128,2048]{1,0:T(8,128)(2,1)}), bf16[1024,2048]{1,0:T(8,128)(2,1)}) %all-gather.6.cloned.1.call-update) | async-done | bytes 4194320 | tf_op jit(solution)/shard_map/all_gather | solution.py:177
  635.6 7.9 %convolution_reduce_fusion = f32[1024]{0:T(1024)S(1)} fusion(bf16[1024,2048]{1,0:T(8,128)(2,1)} %all-gather.6.cloned.1.call-done, bf16[2048,1000]{0,1:T(8,128)(2,1)} %param.41), kind=kOutput, calls=%fused_computation.33 | convolution fusion | flops 4195326976 | bytes 8294400 | tf_op jit(solution)/shard_map/dot_general | solution.py:176
  643.8 38.6 %pmax.7 = f32[256]{0:T(256)S(1)} all-reduce(f32[256]{0:T(256)S(1)} %select_reduce_fusion), channel_id=1, replica_groups=mesh['req'=8,'head'=4] {'req','head'}, use_global_device_ids=true, to_apply=%region_18.20 | all-reduce | flops 256 | bytes 2048 | tf_op jit(solution)/shard_map/pmax | solution.py:186
  (144 shorter events, 21.1 us)
Async XLA Ops:
  7.2 326.1 %copy-start = (bf16[512,2048]{1,0:T(8,128)(2,1)S(1)}, bf16[512,2048]{1,0:T(8,128)(2,1)}, u32[]{:S(2)}) copy-start(bf16[512,2048]{1,0:T(8,128)(2,1)} %param.34) | copy-start | bytes 6291460
  7.2 27.9 %copy-start.28 = (s32[32]{0:T(128)}, s32[32]{0:T(128)S(1)}, u32[]{:S(2)}) copy-start(s32[32]{0:T(128)S(1)} %iota_add_fusion) | copy-start | bytes 388
  35.1 203.0 %all-to-all-start = ((bf16[32,4,128,128]{3,2,1,0:T(8,128)(2,1)}), bf16[32,4,128,128]{3,2,1,0:T(8,128)(2,1)}, u32[]{:S(2)}, u32[]{:S(2)}) async-start(bf16[32,4,128,128]{3,2,1,0:T(8,128)(2,1)} %broadcast_select_fusion.1), calls=%async_computation.1 | async-start | bytes 8388608 | tf_op jit(solution)/shard_map/all_to_all | solution.py:90
  39.8 179.0 %reduce-scatter.3.cloned.1.call-start = ((), (), s32[]{:S(2)}) async-start(), calls=%async_computation.3 | async-start | bytes 1179648 | tf_op jit(solution)/shard_map/reduce_scatter | solution.py:62
  149.5 8.7 %copy-start.27 = (s32[32]{0:T(128)S(1)}, s32[32]{0:T(128)}, u32[]{:S(2)}) copy-start(s32[32]{0:T(128)} %param.23) | copy-start | bytes 388
  149.5 8.9 %copy-start.23 = (f32[512]{0:T(512)S(1)}, f32[512]{0:T(512)}, u32[]{:S(2)}) copy-start(f32[512]{0:T(512)} %param.32) | copy-start | bytes 6148
  149.5 77.0 %copy-start.17 = (f32[2048]{0:T(1024)S(1)}, f32[2048]{0:T(1024)}, u32[]{:S(2)}) copy-start(f32[2048]{0:T(1024)} %param.28) | copy-start | bytes 24580
  157.9 209.5 %all-reduce.6.cloned.1.call-start = ((), (), s32[]{:S(2)}) async-start(), calls=%async_computation.4 | async-start | bytes 1048576 | tf_op jit(solution)/shard_map/psum | solution.py:135
  158.4 138.9 %copy-start.20 = (pred[32]{0:T(512)(128)(4,1)}, pred[32]{0:T(512)(128)(4,1)S(1)}, u32[]{:S(2)}) copy-start(pred[32]{0:T(512)(128)(4,1)S(1)} %get-tuple-element.11) | copy-start | bytes 100
  237.0 60.3 %copy-start.7 = (f32[32,4,128]{2,1,0:T(4,128)}, f32[32,4,128]{2,1,0:T(4,128)S(1)}, u32[]{:S(2)}) copy-start(f32[32,4,128]{2,1,0:T(4,128)S(1)} %get-tuple-element.19) | copy-start | bytes 196612
  237.0 60.4 %copy-start.9 = (f32[32,4,128]{2,1,0:T(4,128)}, f32[32,4,128]{2,1,0:T(4,128)S(1)}, u32[]{:S(2)}) copy-start(f32[32,4,128]{2,1,0:T(4,128)S(1)} %get-tuple-element.20) | copy-start | bytes 196612
  238.0 59.3 %copy-start.3 = (f32[32,4,128]{2,1,0:T(4,128)}, f32[32,4,128]{2,1,0:T(4,128)S(1)}, u32[]{:S(2)}) copy-start(f32[32,4,128]{2,1,0:T(4,128)S(1)} %get-tuple-element.37) | copy-start | bytes 196612
  238.0 59.3 %copy-start.5 = (f32[32,4,128]{2,1,0:T(4,128)}, f32[32,4,128]{2,1,0:T(4,128)S(1)}, u32[]{:S(2)}) copy-start(f32[32,4,128]{2,1,0:T(4,128)S(1)} %get-tuple-element.38) | copy-start | bytes 196612
  243.4 11.9 %copy-start.1 = (bf16[32,4,128,128]{3,2,1,0:T(8,128)(2,1)S(1)}, bf16[32,4,128,128]{3,2,1,0:T(8,128)(2,1)}, u32[]{:S(2)}) copy-start(bf16[32,4,128,128]{3,2,1,0:T(8,128)(2,1)} %gather_fusion.2) | copy-start | bytes 12582916
  243.4 11.9 %copy-start.12 = (f32[32,4,128]{2,1,0:T(4,128)S(1)}, f32[32,4,128]{2,1,0:T(4,128)}, u32[]{:S(2)}) copy-start(f32[32,4,128]{2,1,0:T(4,128)} %get-tuple-element.22) | copy-start | bytes 196612
  243.4 11.9 %copy-start.15 = (f32[32,1,4,128]{3,2,1,0:T(4,128)S(1)}, f32[32,1,4,128]{3,2,1,0:T(4,128)}, u32[]{:S(2)}) copy-start(f32[32,1,4,128]{3,2,1,0:T(4,128)} %get-tuple-element.18) | copy-start | bytes 196612
  255.3 17.2 %copy-start.11 = (f32[32,4,128]{2,1,0:T(4,128)S(1)}, f32[32,4,128]{2,1,0:T(4,128)}, u32[]{:S(2)}) copy-start(f32[32,4,128]{2,1,0:T(4,128)} %get-tuple-element.21) | copy-start | bytes 196612
  255.4 17.2 %copy-start.14 = (f32[32,1,4,128]{3,2,1,0:T(4,128)S(1)}, f32[32,1,4,128]{3,2,1,0:T(4,128)}, u32[]{:S(2)}) copy-start(f32[32,1,4,128]{3,2,1,0:T(4,128)} %get-tuple-element.17) | copy-start | bytes 196612
  272.6 24.8 %copy-start.13 = (f32[32,1,4,128]{3,2,1,0:T(4,128)S(1)}, f32[32,1,4,128]{3,2,1,0:T(4,128)}, u32[]{:S(2)}) copy-start(f32[32,1,4,128]{3,2,1,0:T(4,128)} %get-tuple-element.16) | copy-start | bytes 196612
  335.3 75.4 %all-gather.4.cloned.1.call-start = ((), (), s32[]{:S(2)}) async-start(), calls=%async_computation.5 | async-start | bytes 1179648 | tf_op jit(solution)/shard_map/all_gather | solution.py:140
  368.7 44.5 %copy-start.31 = (bf16[512,704]{0,1:T(8,128)(2,1)S(1)}, bf16[512,704]{0,1:T(8,128)(2,1)}, u32[]{:S(2)}) copy-start(bf16[512,704]{0,1:T(8,128)(2,1)} %param.36) | copy-start | bytes 2162692
  370.4 108.8 %all-reduce.8.cloned.1.call-start = ((), (), s32[]{:S(2)}) async-start(), calls=%async_computation.6 | async-start | bytes 5767168 | tf_op jit(solution)/shard_map/psum | solution.py:144
  416.1 132.7 %reduce-scatter.5.cloned.1.call-start = ((), (), s32[]{:S(2)}) async-start(), calls=%async_computation.7 | async-start | bytes 1179648 | tf_op jit(solution)/shard_map/reduce_scatter | solution.py:148
  481.8 73.8 %copy-start.19 = (f32[512]{0:T(512)S(1)}, f32[512]{0:T(512)}, u32[]{:S(2)}) copy-start(f32[512]{0:T(512)} %param.39) | copy-start | bytes 6148
  481.8 81.8 %copy-start.26 = (s32[32]{0:T(128)S(1)}, s32[32]{0:T(128)}, u32[]{:S(2)}) copy-start(s32[32]{0:T(128)} %param.24) | copy-start | bytes 388
  481.8 81.8 %copy-start.4 = (f32[32,4,128]{2,1,0:T(4,128)S(1)}, f32[32,4,128]{2,1,0:T(4,128)}, u32[]{:S(2)}) copy-start(f32[32,4,128]{2,1,0:T(4,128)} %copy-done.3) | copy-start | bytes 196612
  481.8 81.8 %copy-start.6 = (f32[32,4,128]{2,1,0:T(4,128)S(1)}, f32[32,4,128]{2,1,0:T(4,128)}, u32[]{:S(2)}) copy-start(f32[32,4,128]{2,1,0:T(4,128)} %copy-done.5) | copy-start | bytes 196612
  481.8 81.8 %copy-start.8 = (f32[32,4,128]{2,1,0:T(4,128)S(1)}, f32[32,4,128]{2,1,0:T(4,128)}, u32[]{:S(2)}) copy-start(f32[32,4,128]{2,1,0:T(4,128)} %copy-done.7) | copy-start | bytes 196612
  481.8 81.8 %copy-start.10 = (f32[32,4,128]{2,1,0:T(4,128)S(1)}, f32[32,4,128]{2,1,0:T(4,128)}, u32[]{:S(2)}) copy-start(f32[32,4,128]{2,1,0:T(4,128)} %copy-done.9) | copy-start | bytes 196612
  481.8 81.8 %copy-start.21 = (pred[32]{0:T(512)(128)(4,1)S(1)}, pred[32]{0:T(512)(128)(4,1)}, u32[]{:S(2)}) copy-start(pred[32]{0:T(512)(128)(4,1)} %copy-done.20) | copy-start | bytes 100
  485.1 150.5 %all-gather.6.cloned.1.call-start = ((), (), s32[]{:S(2)}) async-start(), calls=%async_computation.8 | async-start | bytes 4718592 | tf_op jit(solution)/shard_map/all_gather | solution.py:177
  587.2 56.4 %copy-start.24 = (s32[256]{0:T(256)S(1)}, s32[256]{0:T(256)}, u32[]{:S(2)}) copy-start(s32[256]{0:T(256)} %get-tuple-element.6) | copy-start | bytes 3076
  (8 other events, 33.3 us)
Sparse Core Ops, SparseCore 0:
  158.0 60.7 reduce-scatter.2
  335.4 31.9 all-reduce.5
  370.5 40.1 all-gather.3
  416.2 62.9 all-reduce.7
  485.2 63.4 reduce-scatter.4
  563.7 71.8 all-gather.5
where the time goes:
time: 691 us; the launch traced here: 690 us
  waiting for transfers between devices  306 us (44%)
  blocking collectives  189 us (27%)
  matrix products  107 us (15%)
  other arithmetic  38.3 us (6%)
  local copies, waits for them, and re-layouts  29.4 us (4%)
  between operations  15.5 us (2%)
    all_gather x1, blocking collectives, on_device(): lax.all_gather(token_ids, 'req', axis=0, tiled=True)  109 us
    dot_general x4, matrix products, on_device(): jnp.einsum('rhk,rhkv->rhv', query_act[:, position], state_now, precision=...  82.9 us
    psum x1, waiting for transfers between devices, on_device(): lax.psum(partial_sums.astype(jnp.bfloat16), 'head').astype(jnp.float32)  63 us
    reduce_scatter x1, waiting for transfers between devices, on_device(): lax.psum_scatter(rounded(jnp.dot(activated, down_weight, preferred_elemen...  62.8 us
    reduce_scatter x1, waiting for transfers between devices, on_device(): lax.psum_scatter(jnp.where(inside[:, None], picked.astype(jnp.float32), 0...  60.3 us
    all_gather x1, waiting for transfers between devices, on_device(): lax.all_gather(full_final, 'req', axis=0, tiled=True)  48.4 us
    all_gather x1, waiting for transfers between devices, on_device(): row_piece = lax.all_gather(feed_mine, 'req', axis=0, tiled=True)  40.3 us
    pmax x1, blocking collectives, on_device(): best_value = lax.pmax(per_request, ('req', 'head'))  38.6 us
  transfers between devices with their start and end apart: 7, of which 6 were waited for; matrix products, arithmetic and copies ran while one was open for 7% of the time, Pallas kernels for 0%

commit v1 on v0

v1 whole, which is shorter than its diff:
```python
import functools

import jax
import jax.numpy as jnp
import numpy as np
from jax import lax
from jax.experimental import pallas as pl
from jax.experimental.pallas import tpu as pltpu
from jax.sharding import PartitionSpec as P

D = 2048
HEAD_DIM = 128
epsilon = 1e-06
F32 = jnp.float32
BF16 = jnp.bfloat16
VMEM = pltpu.VMEM
SMEM = pltpu.SMEM


def swap(x, axis, size, offset):
    return lax.ppermute(x, axis, [(i, i ^ offset) for i in range(size)])


def bf16_parts(x):
    high = lax.reduce_precision(x, 8, 7)
    return high.astype(BF16), (x - high).astype(BF16)


def sort_kernel(sends, order_ref, old_ref, *rest):
    outs, sems = rest[:-1], rest[-1]
    copies = []
    for k, out in enumerate(outs):
        for rank in range(sends):
            at = k * sends + rank
            copies.append(
                pltpu.make_async_copy(old_ref.at[order_ref[at]], out.at[rank], sems.at[at])
            )
    for copy in copies:
        copy.start()
    for copy in copies:
        copy.wait()


def sort_states(order, old_states, owners):
    requests = old_states.shape[0]
    sends = requests // owners
    piece = jax.ShapeDtypeStruct((sends,) + old_states.shape[1:], old_states.dtype)
    return pl.pallas_call(
        functools.partial(sort_kernel, sends),
        out_shape=[piece] * owners,
        in_specs=[pl.BlockSpec(memory_space=SMEM), pl.BlockSpec(memory_space=pl.ANY)],
        out_specs=[pl.BlockSpec(memory_space=pl.ANY)] * owners,
        scratch_shapes=[pltpu.SemaphoreType.DMA((requests,))],
    )(order, old_states)


def roll(x, by):
    return pltpu.roll(x, by % x.shape[0], 0)


def mixer_kernel(
    owners, sends, heads, classes, steps,
    me_ref, emb_ref, live_ref, gain_ref, qw_ref, fw_ref, iw_ref, floor_ref, ggain_ref, ow_ref,
    *rest,
):
    states = rest[:owners]
    own_ref, parts, kv_ref = rest[owners], rest[owners + 1 : owners + 1 + classes], rest[owners + 1 + classes]
    qhi_ref, qlo_ref, mixed_ref, part_ref = rest[owners + 2 + classes :]
    tokens = live_ref.shape[0]
    requests = tokens // steps
    group = requests // classes
    rows = group * steps
    stream = emb_ref[0:tokens, :].astype(F32)
    scale = lax.rsqrt(jnp.mean(stream * stream, axis=1, keepdims=True) + epsilon)
    normed = (stream * scale * gain_ref[...]).astype(BF16)
    query = jnp.dot(normed, qw_ref[...], preferred_element_type=F32)
    query = query * jax.nn.sigmoid(query) * HEAD_DIM ** (-0.5)
    forget_raw = jnp.dot(normed, fw_ref[...], preferred_element_type=F32)
    value = jnp.dot(normed, iw_ref[...], preferred_element_type=F32)
    floor = floor_ref[...]
    forget = jnp.where(
        live_ref[...] > 0.0, floor + (1.0 - floor) * jax.nn.sigmoid(forget_raw), 1.0
    )
    key = 1.0 - forget
    step = lax.broadcasted_iota(jnp.int32, forget.shape, 0) % steps
    upto = forget * jnp.where(step >= 1, roll(forget, 1), 1.0)
    upto = upto * jnp.where(step >= 2, roll(upto, 2), 1.0)
    after = jnp.where(step <= steps - 2, roll(forget, -1), 1.0)
    after = after * jnp.where(step <= steps - 3, roll(forget, -2), 1.0)
    after = after * jnp.where(step <= steps - 4, roll(forget, -3), 1.0)
    carried = query * upto
    high = carried.astype(BF16).astype(F32)
    qhi_ref[...] = high
    qlo_ref[...] = carried - high
    lag_key, lag_value = key, value
    local = [jnp.zeros((tokens, HEAD_DIM), F32) for _ in range(heads)]
    for lag in range(steps):
        if lag:
            lag_key = roll(lag_key, 1) * forget
            lag_value = roll(lag_value, 1)
        product = jnp.where(step >= lag, query * lag_key, 0.0)
        for head in range(heads):
            cols = slice(head * HEAD_DIM, (head + 1) * HEAD_DIM)
            weight = jnp.sum(product[:, cols], axis=1, keepdims=True)
            local[head] = local[head] + weight * lag_value[:, cols]
    for head in range(heads):
        mixed_ref[:, head * HEAD_DIM : (head + 1) * HEAD_DIM] = local[head]
    upper = lax.broadcasted_iota(jnp.int32, (8, HEAD_DIM), 0) < steps
    for tile in range(tokens // 8):
        for head in range(heads):
            cols = slice(head * HEAD_DIM, (head + 1) * HEAD_DIM)
            at = slice(tile * 8, tile * 8 + 8)
            left = jnp.concatenate([qhi_ref[at, cols], qlo_ref[at, cols]], axis=0).astype(BF16)
            got = []
            for request in (2 * tile, 2 * tile + 1):
                place = (request % group) * classes + request // group
                old = states[place // sends][place % sends, head]
                product = jnp.dot(left, old, preferred_element_type=F32)
                got.append(product[0:8] + product[8:16])
            mixed_ref[at, cols] += jnp.where(upper, got[0], got[1])
    mixed = mixed_ref[...]
    square = jnp.sum(mixed * mixed, axis=1, keepdims=True)
    part_ref[:, 0:D] = jnp.dot(
        (mixed * ggain_ref[...]).astype(BF16), ow_ref[...], preferred_element_type=F32
    )
    square_high = square.astype(BF16).astype(F32)
    lane = lax.broadcasted_iota(jnp.int32, (tokens, 128), 1)
    part_ref[:, D : D + 128] = jnp.where(lane < 64, square_high, square - square_high)
    me = me_ref[0]
    for e in range(classes):
        first = pl.multiple_of((me ^ e) * rows, rows)
        parts[e][...] = part_ref[pl.ds(first, rows), :].astype(BF16)
    own_ref[...] = emb_ref[pl.ds(pl.multiple_of(me * rows, rows), rows), :]
    both = jnp.concatenate([(key * after).astype(BF16), value.astype(BF16)], axis=0)
    shape = (2 * tokens, 2 * tokens)
    target = lax.broadcasted_iota(jnp.int32, shape, 0)
    source = lax.broadcasted_iota(jnp.int32, shape, 1)
    place, within = target // (2 * steps), target % (2 * steps)
    request = (place % classes) * group + place // classes
    wanted = request * steps + within % steps + jnp.where(within >= steps, tokens, 0)
    pick = jnp.where(source == wanted, 1.0, 0.0).astype(BF16)
    kv_ref[...] = jnp.dot(pick, both, preferred_element_type=F32).astype(BF16)


def mixer(me, emb, live, gain, qw, fw, iw, floor, ggain, ow, states, steps, classes):
    tokens = live.shape[0]
    owners, sends, heads = len(states), states[0].shape[0], states[0].shape[1]
    width = qw.shape[1]
    rows = tokens // classes
    vmem = pl.BlockSpec(memory_space=VMEM)
    return pl.pallas_call(
        functools.partial(mixer_kernel, owners, sends, heads, classes, steps),
        out_shape=[jax.ShapeDtypeStruct((rows, D), BF16)]
        + [jax.ShapeDtypeStruct((rows, D + 128), BF16)] * classes
        + [jax.ShapeDtypeStruct((2 * tokens, width), BF16)],
        in_specs=[pl.BlockSpec(memory_space=SMEM)] + [vmem] * (9 + owners),
        out_specs=[vmem] * (classes + 2),
        scratch_shapes=[
            VMEM((tokens, width), F32),
            VMEM((tokens, width), F32),
            VMEM((tokens, width), F32),
            VMEM((tokens, D + 128), F32),
        ],
        compiler_params=pltpu.CompilerParams(vmem_limit_bytes=40 << 20),
    )(me, emb, live, gain, qw, fw, iw, floor, ggain, ow, *states)


def update_kernel(owners, sends, heads, steps, slot_ref, kv_ref, *rest):
    states, out_ref = rest[:owners], rest[owners]
    diagonal = lax.broadcasted_iota(jnp.int32, (HEAD_DIM, HEAD_DIM), 0) == lax.broadcasted_iota(
        jnp.int32, (HEAD_DIM, HEAD_DIM), 1
    )
    first = lax.broadcasted_iota(jnp.int32, (2 * steps, HEAD_DIM), 0) < steps
    for k in range(owners):
        for rank in range(sends):
            place = k * sends + rank
            slot = slot_ref[place]
            for head in range(heads):
                cols = slice(head * HEAD_DIM, (head + 1) * HEAD_DIM)
                both = kv_ref[place, :, cols]
                key = jnp.where(first, both, 0.0)
                value = jnp.where(first, roll(both, steps), 0.0)
                kept = 1.0 - jnp.sum(key, axis=0, keepdims=True)
                keep = jnp.where(diagonal, kept, 0.0).astype(BF16)
                fresh = lax.dot_general(
                    key, value, (((0,), (0,)), ((), ())), preferred_element_type=F32
                )
                old = jnp.dot(keep, states[k][rank, head], preferred_element_type=F32)
                out_ref[slot, head] = (old + fresh).astype(BF16)


def update_states(slots, kv, states, steps):
    owners, sends, heads = len(states), states[0].shape[0], states[0].shape[1]
    vmem = pl.BlockSpec(memory_space=VMEM)
    return pl.pallas_call(
        functools.partial(update_kernel, owners, sends, heads, steps),
        out_shape=jax.ShapeDtypeStruct((owners * sends,) + states[0].shape[1:], BF16),
        in_specs=[pl.BlockSpec(memory_space=SMEM)] + [vmem] * (1 + owners),
        out_specs=vmem,
        compiler_params=pltpu.CompilerParams(vmem_limit_bytes=40 << 20),
    )(slots, kv, *states)


def scatter_sum(blocks, n, cut):
    outer = n // 2
    blocks = blocks.reshape((outer, 2) + blocks.shape[1:])
    first, second = blocks[..., :cut], blocks[..., cut:]
    inner_got = swap(first[:, 1], "req", n, 1)
    outer_got = [swap(second[j], "req", n, 2 * j) for j in range(1, outer)]
    first = (first[:, 0].astype(F32) + inner_got.astype(F32)).astype(BF16)
    second = sum([got.astype(F32) for got in outer_got], second[0].astype(F32)).astype(BF16)
    outer_got = [swap(first[j], "req", n, 2 * j) for j in range(1, outer)]
    inner_got = swap(second[1], "req", n, 1)
    first = sum([got.astype(F32) for got in outer_got], first[0].astype(F32))
    second = second[0].astype(F32) + inner_got.astype(F32)
    return jnp.concatenate([first, second], axis=-1)


def exchange(block, dim, n, n_head):
    if dim == "outer":
        got = [swap(block, "req", n, 2 * j) for j in range(1, n // 2)]
    elif dim == "inner":
        got = [swap(block, "req", n, 1)]
    else:
        got = [swap(block, "head", n_head, 2)]
    return jnp.stack([block] + got)


def gather_by(block, dims, order, n, n_head):
    rank = block.ndim
    for dim in dims:
        block = exchange(block, dim, n, n_head)
    at = [dims[::-1].index(dim) for dim in order]
    block = block.transpose(at + list(range(len(dims), len(dims) + rank)))
    return block.reshape((-1,) + block.shape[len(dims) :])


def on_device(
    token_ids, state_perm, token_count, tenant_bounds, old_states, embedding, mixer_gain,
    query_weight, forget_weight, input_weight, forget_floor, group_gain, output_weight, feed_gain,
    gate_weight, up_weight, down_weight, final_gain, tenant_gain, vocab_weight,
):
    requests, steps = token_ids.shape
    n = lax.axis_size("req")
    n_head = lax.axis_size("head")
    r = lax.axis_index("req")
    h = lax.axis_index("head")
    tokens = requests * steps
    everyone = requests * n
    sends = requests // n
    group = requests // n_head
    rows = group * steps
    width = D // n_head

    gate_full = lax.all_gather(gate_weight, "head", axis=0, tiled=True)
    up_full = lax.all_gather(up_weight, "head", axis=0, tiled=True)
    down_full = lax.all_gather(down_weight, "head", axis=0)
    vocab_other = swap(vocab_weight, "head", n_head, 1)

    packed = jnp.concatenate([token_ids.T, state_perm[None], token_count[None]], axis=0)
    packed = lax.all_gather(packed, "req", axis=0).transpose(1, 0, 2).reshape(steps + 2, everyone)
    every = jnp.arange(everyone, dtype=jnp.int32)
    source = packed[steps] // requests
    rank = jnp.sum(
        ((source[None, :] == source[:, None]) & (every[None, :] < every[:, None])).astype(jnp.int32),
        axis=1,
    )
    place = ((every // requests) ^ source) * sends + rank % sends
    at = (source ^ r) * requests + (place % n_head) * group + place // n_head
    chosen = (at[:, None] == every[None, :]).astype(F32)
    ordered = jnp.dot(packed.astype(F32), chosen, precision=lax.Precision.HIGHEST)
    ordered = (ordered + 0.5).astype(jnp.int32)

    ids = ordered[:steps].T.reshape(n * tokens)
    table = embedding.shape[0]
    local_ids = ids - r * table
    inside = (local_ids >= 0) & (local_ids < table)
    picked = jnp.take(embedding, jnp.clip(local_ids, 0, table - 1), axis=0, mode="clip")
    picked = jnp.where(inside[:, None], picked, jnp.zeros((), BF16)).reshape(n, tokens, width)
    embed_part = scatter_sum(picked, n, width // 2).astype(BF16)

    gains = jnp.concatenate([final_gain[None], tenant_gain], axis=0)
    gains_high, gains_low = bf16_parts(gains)
    extra = jnp.zeros((16 - 2 * gains.shape[0], width), BF16)
    embedded = lax.all_gather(
        jnp.concatenate([embed_part, gains_high, gains_low, extra], axis=0), "head", axis=1, tiled=True
    )
    gains = embedded[tokens : tokens + 5].astype(F32) + embedded[tokens + 5 : tokens + 10].astype(F32)

    old_order = (ordered[steps, :requests] - r * requests).reshape(n_head, group).T.reshape(requests)
    pieces = sort_states(old_order, old_states, n)
    live = (jnp.arange(steps)[None, :] < ordered[steps + 1, :requests][:, None]).astype(F32)
    own, *parts, kv = mixer(
        h[None], embedded, live.reshape(tokens, 1), mixer_gain[None], query_weight, forget_weight,
        input_weight, forget_floor[None], group_gain[None], output_weight, pieces, steps, n_head,
    )
    arrived = [pieces[0]] + [swap(pieces[k], "req", n, k) for k in range(1, n)]
    kv = kv.reshape(n, sends, 2 * steps, width)
    arrived_kv = jnp.stack([kv[0]] + [swap(kv[k], "req", n, k) for k in range(1, n)])

    total = parts[0].astype(F32)
    for e in range(1, n_head):
        total = total + swap(parts[e], "head", n_head, e).astype(F32)
    square = total[:, D : D + 1] + total[:, D + 127 : D + 128]
    after_mixer = own.astype(F32) + total[:, :D] * lax.rsqrt(square / D + epsilon)

    cut = D * 11 // 16
    after_mixer = after_mixer.astype(BF16)
    everything = jnp.concatenate(
        [
            gather_by(after_mixer[:, :cut], ["outer", "inner"], ["outer", "inner"], n, n_head),
            gather_by(after_mixer[:, cut:], ["inner", "outer"], ["outer", "inner"], n, n_head),
        ],
        axis=-1,
    ).reshape(n * rows, D)
    stream = everything.astype(F32)
    scale = lax.rsqrt(jnp.mean(stream * stream, axis=1, keepdims=True) + epsilon)
    feed_in = (stream * scale * feed_gain).astype(BF16)
    gate = jnp.dot(feed_in, gate_full, preferred_element_type=F32)
    up = jnp.dot(feed_in, up_full, preferred_element_type=F32)
    activated = (jax.nn.silu(gate) * up).astype(BF16)

    row = jnp.arange(n * rows, dtype=jnp.int32)
    by_owner, by_group, by_step = row // rows, (row % rows) // steps, row % steps
    if sends % n_head == 0:
        offset = by_group * n_head // sends
    else:
        offset = (by_group * n_head + h) // sends
    wanted = (by_owner ^ offset) * rows + by_group * steps + by_step
    pick = (wanted[:, None] == row[None, :]).astype(BF16)
    activated = jnp.dot(pick, activated, preferred_element_type=F32).astype(BF16)
    kept = jnp.dot(pick[:rows], everything, preferred_element_type=F32)
    down = jnp.concatenate(
        [jnp.dot(activated, down_full[b], preferred_element_type=F32).astype(BF16) for b in range(n_head)],
        axis=1,
    )
    hidden = kept + scatter_sum(down.reshape(n, rows, D), n, cut)
    mean_square = jnp.mean(hidden * hidden, axis=1, keepdims=True)

    slots = jnp.arange(requests, dtype=jnp.int32)
    source = state_perm // requests
    rank = jnp.sum(
        ((source[None, :] == source[:, None]) & (slots[None, :] < slots[:, None])).astype(jnp.int32),
        axis=1,
    )
    place = (source ^ r) * sends + rank
    slot_of = jnp.sum(jnp.where(place[None, :] == slots[:, None], slots[None, :], 0), axis=1)
    mine = jnp.sum(
        jnp.where(
            place[None, :] == (jnp.arange(group, dtype=jnp.int32) * n_head + h)[:, None],
            slots[None, :],
            0,
        ),
        axis=1,
    )
    tenant = jnp.sum(
        ((mine + r * requests)[:, None] >= tenant_bounds[None, 1:-1]).astype(jnp.int32), axis=1
    )
    tenant_rows = sum(
        jnp.where((tenant == t)[:, None], gains[1 + t][None, :], 0.0)
        for t in range(tenant_gain.shape[0])
    )
    token_gain = jnp.repeat(tenant_rows * gains[0][None, :], steps, axis=0)
    final = (hidden * lax.rsqrt(mean_square + epsilon) * token_gain).astype(BF16)

    order = ["outer", "inner", "head"]
    c1, c2 = D * 6 // 16, D * 11 // 16
    full = jnp.concatenate(
        [
            gather_by(final[:, :c1], ["outer", "inner", "head"], order, n, n_head),
            gather_by(final[:, c1:c2], ["head", "outer", "inner"], order, n, n_head),
            gather_by(final[:, c2:], ["inner", "head", "outer"], order, n, n_head),
        ],
        axis=-1,
    ).reshape(n * 2 * rows, D)
    best = jnp.maximum(
        jnp.max(jnp.dot(full, vocab_weight, preferred_element_type=F32), axis=1),
        jnp.max(jnp.dot(full, vocab_other, preferred_element_type=F32), axis=1),
    ).reshape(n, 2 * rows)
    got = best[0]
    for k in range(1, n):
        got = jnp.maximum(got, swap(best[k], "req", n, k))
    got = lax.all_gather(got, "head", axis=0).reshape(n_head, 2, rows)
    crossed = jnp.stack([got[i ^ 2, 1] for i in range(n_head)])
    best = jnp.maximum(got[:, 0], crossed).reshape(requests, steps)
    index = (place % n_head) * group + place // n_head
    match = (index[:, None] == slots[None, :])[:, :, None]
    best = jnp.sum(jnp.where(match, best[None], 0.0), axis=1)
    live = jnp.arange(steps)[None, :] < token_count[:, None]
    greatest = jnp.max(jnp.where(live, best, -1e30), axis=1)

    blocks = hidden.reshape(rows, n_head, width).transpose(1, 0, 2)
    tail = jnp.broadcast_to(mean_square, (rows, 128))
    whole = []
    for e in range(n_head):
        block = jnp.concatenate(
            [lax.dynamic_index_in_dim(blocks, h ^ e, 0, keepdims=False), tail], axis=1
        )
        whole.append(block if e == 0 else swap(block, "head", n_head, e))
    whole = jnp.stack(whole).reshape(requests, steps, width + 128)
    index = ((place % n_head) ^ h) * group + place // n_head
    whole = jnp.take(whole, index, axis=0, mode="clip")
    last = jnp.arange(steps)[None, :] == (token_count - 1)[:, None]
    last_norm = jnp.sqrt(jnp.sum(jnp.where(last, whole[:, :, width], 0.0), axis=1) + epsilon)

    new_states = update_states(
        slot_of, arrived_kv.reshape(requests, 2 * steps, width).astype(F32), arrived, steps
    )
    return whole[:, :, :width], new_states, last_norm, greatest


def solution(mesh):
    placed = (
        P("req", None),
        P("req"),
        P("req"),
        P(),
        P("req", "head", None, None),
        P("req", "head"),
        P(),
        P(None, "head"),
        P(None, "head"),
        P(None, "head"),
        P("head"),
        P("head"),
        P("head", None),
        P(),
        P("head", "req"),
        P("head", "req"),
        P("req", "head"),
        P("head"),
        P(None, "head"),
        P(None, ("req", "head")),
    )
    return jax.shard_map(
        on_device,
        mesh=mesh,
        in_specs=placed,
        out_specs=(P("req", None, "head"), P("req", "head", None, None), P("req"), P("req")),
        check_vma=False,
    )
```

time: 691 us -> 490 us (0.71)
  waiting for transfers between devices: 306 us -> 91.1 us
  blocking collectives: 189 us -> 48.4 us
  Pallas kernels: 0 us -> 138 us
  starting transfers between devices: 5.15 us -> 132 us
  matrix products: 107 us -> 18 us
  other arithmetic: 38.3 us -> 11.2 us
    pallas_call x0 -> x3, Pallas kernels: none -> 138 us  [the longest x1 129 us: sort_states(): pl.pallas_call(functools.partial(sort_kernel, sends), out_shape=[piece] *...]
    ppermute x0 -> x67, starting transfers between devices: none -> 132 us  [swap(): return lax.ppermute(x, axis, [(i, i ^ offset) for i in range(size)])]
    reduce_scatter x2 -> x0, waiting for transfers between devices: 123 us -> none  [the longest x1 62.8 us: on_device(): lax.psum_scatter(rounded(jnp.dot(activated, down_weight, preferred_elemen...]
    psum x2 -> x0, waiting for transfers between devices: 94.3 us -> none  [the longest x1 63 us: on_device(): lax.psum(partial_sums.astype(jnp.bfloat16), 'head').astype(jnp.float32)]
    ppermute x0 -> x67, waiting for transfers between devices: none -> 89.6 us  [swap(): return lax.ppermute(x, axis, [(i, i ^ offset) for i in range(size)])]
    dot_general x13 -> x10, matrix products: 107 us -> 18 us  [the longest x1 4.49 us: on_device(): jnp.dot(full, vocab_other, preferred_element_type=F32)]
    all_gather x2 -> x3, waiting for transfers between devices: 88.6 us -> 0.06 us  [the longest x1 0.02 us: on_device(): gate_full = lax.all_gather(gate_weight, 'head', axis=0, tiled=True)]
    all_gather x3 -> x2, blocking collectives: 124 us -> 42.8 us  [the longest x1 32.2 us: on_device(): lax.all_gather(packed, 'req', axis=0).transpose(1, 0, 2)]
  transfers between devices with their start and end apart: 7 -> 70, of which waited for: 6 -> 26; matrix products, arithmetic and copies ran while one was open for 7% -> 9% of each run, Pallas kernels for 0% -> 28%
where the time goes in v1:
time: 490 us; the launch traced here: 488 us
  Pallas kernels  138 us (28%)
  starting transfers between devices  132 us (27%)
  waiting for transfers between devices  91.1 us (19%)
  blocking collectives  48.4 us (10%)
  local copies, waits for them, and re-layouts  34.6 us (7%)
  matrix products  18 us (4%)
  between operations  15.5 us (3%)
  other arithmetic  11.2 us (2%)
    ppermute x67, starting transfers between devices, swap(): return lax.ppermute(x, axis, [(i, i ^ offset) for i in range(size)])  132 us
    pallas_call x1, Pallas kernels, sort_states(): pl.pallas_call(functools.partial(sort_kernel, sends), out_shape=[piece] *...  129 us
    ppermute x67, waiting for transfers between devices, swap(): return lax.ppermute(x, axis, [(i, i ^ offset) for i in range(size)])  89.6 us
    all_gather x1, blocking collectives, on_device(): lax.all_gather(packed, 'req', axis=0).transpose(1, 0, 2)  32.2 us
    unnamed x85, local copies, waits for them, and re-layouts  18.5 us
    all_gather x1, blocking collectives, on_device(): lax.all_gather(jnp.concatenate([embed_part, gains_high, gains_low, extra]...  10.6 us
  transfers between devices with their start and end apart: 70, of which 26 were waited for; matrix products, arithmetic and copies ran while one was open for 9% of the time, Pallas kernels for 28%

profile of v1, /device:TPU:0, one launch (start us, length us, event | category | flops | bytes accessed | tf_op | source)
XLA Modules:
  0.0 488.5 jit_solution(8057847686648124633)
XLA Ops:
  9.4 32.2 %all-gather.3 = s32[8,6,32]{2,1,0:T(8,128)S(1)} all-gather(s32[1,6,32]{2,1,0:T(8,128)S(1)} %add_bitcast_fusion), channel_id=2, replica_groups=mesh['req'=8,'head'=4] {'req'}, dimensions={0}, use_global_device_ids=true | all-gather | bytes 6912 | tf_op jit(solution)/shard_map/all_gather | solution.py:261
  42.9 6.7 %gather_fusion = bf16[1024,512]{1,0:T(8,128)(2,1)S(1)} fusion(bf16[4000,512]{1,0:T(8,128)(2,1)} %param.25, s32[1024]{0:T(1024)S(1)} %broadcast_clamp_fusion), kind=kCustom, calls=%fused_computation | custom fusion | bytes 2101248 | tf_op jit(solution)/shard_map/jit(_take)/gather | solution.py:278
  51.8 3.3 collective-permute-start.6
  57.4 129.3 %shard_map.219 = (bf16[4,4,128,128]{3,2,1,0:T(8,128)(2,1)}, bf16[4,4,128,128]{3,2,1,0:T(8,128)(2,1)}, bf16[4,4,128,128]{3,2,1,0:T(8,128)(2,1)}, bf16[4,4,128,128...) custom-call(s32[32]{0:T(128)} %reshape.426.order_ref, ...), custom_call_target="tpu_custom_call" | custom-call | tf_op jit(solution)/shard_map/pallas_call | solution.py:48
  204.4 2.7 collective-permute-done.3
  207.3 10.6 %all_gather.29.emb_ref = bf16[144,2048]{1,0:T(8,128)(2,1)S(1)} all-gather(bf16[144,512]{1,0:T(8,128)(2,1)S(1)} %maximum_maximum_fusion), channel_id=1, replica_groups=mesh['req'=8,'head'=4] {'head'}, dimensions={1}, use_global_device_ids=true | all-gather | bytes 737280 | tf_op jit(solution)/shard_map/all_gather | solution.py:285
  228.0 2.8 shard_map.220
  243.2 2.9 collective-permute-done.32
  248.4 2.7 collective-permute-done.33
  251.1 2.4 collective-permute-start.34
  254.1 2.7 collective-permute-done.34
  268.9 2.8 collective-permute-done.15
  279.7 37.2 %collective-permute-done.13 = bf16[32,1408]{1,0:T(8,128)(2,1)S(1)} collective-permute-done((bf16[32,1408]{1,0:T(8,128)(2,1)S(1)}, bf16[32,1408]{1,0:T(8,128)(2,1)S(1)}, u32[]{:S(2)}, u32[]{:S(2)}) %collective-permute-start.13) | collective-permute-done | bytes 90144 | tf_op jit(solution)/shard_map/ppermute | solution.py:21
  316.9 2.6 collective-permute-start.43
  319.6 38.7 %collective-permute-start.16 = (bf16[2,32,640]{2,1,0:T(8,128)(2,1)S(1)}, bf16[2,32,640]{2,1,0:T(8,128)(2,1)S(1)}, u32[]{:S(2)}, u32[]{:S(2)}) collective-permute-start(bf16[2,32,640]{2,1,0:T(8,128)(2,1)S(1)} %get-tuple-element.86), channel_id=1, source_target_pairs={{0,8},{4,12},{8,0},{12,4},{16,24},{20,28},{24,16},{28,20},{1,9},{5... | collective-permute-start | bytes 245768 | tf_op jit(solution)/shard_map/ppermute | solution.py:21
  362.9 5.5 %shard_map.221 = bf16[32,4,128,128]{3,2,1,0:T(8,128)(2,1)} custom-call(s32[32]{0:T(128)S(1)} %select_reduce_fusion.1.slot_ref, f32[32,8,512]{2,1,0:T(8,128)S(1)} %bitcast_convert_fusion.kv_ref, bf16[4,4,128,128]{3,2,1,0:T(8,128)(2,1)S(1)} %copy-done, bf16[4,4,128,128]{3,2,1,0:T(8,128)(2,1)S(1)} %collective-permute-done.37.rest_1_, ...), custom_call_target="tpu_custom_call" | custom-call | tf_op jit(solution)/shard_map/pallas_call | solution.py:195
  370.6 2.8 fusion.64
  373.5 3.1 convolution_convert_fusion
  380.8 5.7 %collective-permute-start.23 = (bf16[2,32,640]{2,1,0:T(8,128)(2,1)S(1)}, bf16[2,32,640]{2,1,0:T(8,128)(2,1)S(1)}, u32[]{:S(2)}, u32[]{:S(2)}) collective-permute-start(bf16[2,32,640]{2,1,0:T(8,128)(2,1)S(1)} %get-tuple-element.38), channel_id=1, source_target_pairs={{0,8},{4,12},{8,0},{12,4},{16,24},{20,28},{24,16},{28,20},{1,9},{5... | collective-permute-start | bytes 245768 | tf_op jit(solution)/shard_map/ppermute | solution.py:21
  390.1 6.0 %collective-permute-done.24 = bf16[2,32,640]{2,1,0:T(8,128)(2,1)S(1)} collective-permute-done((bf16[2,32,640]{2,1,0:T(8,128)(2,1)S(1)}, bf16[2,32,640]{2,1,0:T(8,128)(2,1)S(1)}, u32[]{:S(2)}, u32[]{:S(2)}) %collective-permute-start.24) | collective-permute-done | bytes 81952 | tf_op jit(solution)/shard_map/ppermute | solution.py:21
  397.3 2.5 collective-permute-done.19
  404.5 4.5 collective-permute-done.21
  416.5 2.5 collective-permute-done.49
  420.1 3.0 collective-permute-done.54
  436.0 2.4 collective-permute-start.57
  444.7 5.6 %collective-permute-done.57 = bf16[2,2,32,640]{3,2,1,0:T(8,128)(2,1)S(1)} collective-permute-done((bf16[2,2,32,640]{3,2,1,0:T(8,128)(2,1)S(1)}, bf16[2,2,32,640]{3,2,1,0:T(8,128)(2,1)S(1)}, u32[]{:S(2)}, u32[]{:S(2)}) %collective-permute-start.57) | collective-permute-done | bytes 163872 | tf_op jit(solution)/shard_map/ppermute | solution.py:21
  452.7 2.3 convolution_reduce_fusion.1
  455.1 4.5 convolution_reduce_fusion
  460.7 2.9 collective-permute-start.61
  468.9 2.8 collective-permute-start.66
  472.8 2.4 collective-permute-done.66
  475.3 5.6 %all-reduce = f32[256]{0:T(256)S(1)} all-reduce(f32[256]{0:T(256)S(1)} %maximum_dynamic-update-slice_fusion), channel_id=4, replica_groups=mesh['req'=8,'head'=4] {'head'}, use_global_device_ids=true, to_apply=%add | all-reduce | flops 256 | bytes 2048
  (333 shorter events, 129.3 us)
Async XLA Ops:
  7.2 363.3 %all-gather.8.cloned.1.call-start = ((), (), s32[]{:S(2)}) async-start(), calls=%async_computation | async-start | bytes 3604480 | tf_op jit(solution)/shard_map/all_gather | solution.py:255
  7.9 365.6 %all-gather.10.cloned.1.call-start = ((), (), s32[]{:S(2)}) async-start(), calls=%async_computation.1 | async-start | bytes 3604480 | tf_op jit(solution)/shard_map/all_gather | solution.py:256
  8.6 367.9 %all-gather.12.cloned.1.call-start = ((), (), s32[]{:S(2)}) async-start(), calls=%async_computation.2 | async-start | bytes 3604480 | tf_op jit(solution)/shard_map/all_gather | solution.py:257
  50.6 142.4 %collective-permute-start.4 = (bf16[2,128,256]{2,1,0:T(8,128)(2,1)}, bf16[2,128,256]{2,1,0:T(8,128)(2,1)}, u32[]{:S(2)}, u32[]{:S(2)}) collective-permute-start(bf16[2,128,256]{2,1,0:T(8,128)(2,1)} %get-tuple-element.41), channel_id=1, source_target_pairs={{0,8},{4,12},{8,0},{12,4},{16,24},{20,28},{24,16},{28,20},{1,9},{5... | collective-permute-start | bytes 393224 | tf_op jit(solution)/shard_map/ppermute | solution.py:21
  50.6 142.5 %collective-permute-start.5 = (bf16[2,128,256]{2,1,0:T(8,128)(2,1)}, bf16[2,128,256]{2,1,0:T(8,128)(2,1)}, u32[]{:S(2)}, u32[]{:S(2)}) collective-permute-start(bf16[2,128,256]{2,1,0:T(8,128)(2,1)} %get-tuple-element.43), channel_id=1, source_target_pairs={{0,16},{4,20},{8,24},{12,28},{16,0},{20,4},{24,8},{28,12},{1,17},{... | collective-permute-start | bytes 393224 | tf_op jit(solution)/shard_map/ppermute | solution.py:21
  51.8 141.4 %collective-permute-start.6 = (bf16[2,128,256]{2,1,0:T(8,128)(2,1)}, bf16[2,128,256]{2,1,0:T(8,128)(2,1)}, u32[]{:S(2)}, u32[]{:S(2)}) collective-permute-start(bf16[2,128,256]{2,1,0:T(8,128)(2,1)} %get-tuple-element.42), channel_id=1, source_target_pairs={{0,24},{4,28},{8,16},{12,20},{16,8},{20,12},{24,0},{28,4},{1,25},{... | collective-permute-start | bytes 393224 | tf_op jit(solution)/shard_map/ppermute | solution.py:21
  55.1 140.8 %collective-permute-start = (bf16[4,128,256]{2,1,0:T(8,128)(2,1)S(1)}, bf16[4,128,256]{2,1,0:T(8,128)(2,1)}, u32[]{:S(2)}, u32[]{:S(2)}) collective-permute-start(bf16[4,128,256]{2,1,0:T(8,128)(2,1)S(1)} %slice_bitcast_fusion.2), channel_id=1, source_target_pairs={{0,4},{4,0},{8,12},{12,8},{16,20},{20,16},{24,28},{28,24},{1,5},{5... | collective-permute-start | bytes 786440 | tf_op jit(solution)/shard_map/ppermute | solution.py:21
  186.7 85.2 %collective-permute-start.37 = (bf16[4,4,128,128]{3,2,1,0:T(8,128)(2,1)}, bf16[4,4,128,128]{3,2,1,0:T(8,128)(2,1)S(1)}, u32[]{:S(2)}, u32[]{:S(2)}) collective-permute-start(bf16[4,4,128,128]{3,2,1,0:T(8,128)(2,1)} %get-tuple-element.19.rest_1_), channel_id=1, source_target_pairs={{0,4},{4,0},{8,12},{12,8},{16,20},{20,16},{24,28},{28,24},{1,5},{5... | collective-permute-start | bytes 1572872 | tf_op jit(solution)/shard_map/ppermute | solution.py:21
  193.0 81.1 %collective-permute-start.38 = (bf16[4,4,128,128]{3,2,1,0:T(8,128)(2,1)}, bf16[4,4,128,128]{3,2,1,0:T(8,128)(2,1)}, u32[]{:S(2)}, u32[]{:S(2)}) collective-permute-start(bf16[4,4,128,128]{3,2,1,0:T(8,128)(2,1)} %get-tuple-element.20.rest_2_), channel_id=1, source_target_pairs={{0,8},{4,12},{8,0},{12,4},{16,24},{20,28},{24,16},{28,20},{1,9},{5... | collective-permute-start | bytes 1572872 | tf_op jit(solution)/shard_map/ppermute | solution.py:21
  235.8 22.7 %collective-permute-start.10 = (bf16[32,2176]{1,0:T(8,128)(2,1)}, bf16[32,2176]{1,0:T(8,128)(2,1)S(1)}, u32[]{:S(2)}, u32[]{:S(2)}) collective-permute-start(bf16[32,2176]{1,0:T(8,128)(2,1)} %copy-done.22), channel_id=1, source_target_pairs={{0,3},{1,2},{2,1},{3,0},{4,7},{5,6},{6,5},{7,4},{8,11},{9,10},{10,... | collective-permute-start | bytes 417800 | tf_op jit(solution)/shard_map/ppermute | solution.py:21
  236.4 24.2 %collective-permute-start.8 = (bf16[32,2176]{1,0:T(8,128)(2,1)}, bf16[32,2176]{1,0:T(8,128)(2,1)S(1)}, u32[]{:S(2)}, u32[]{:S(2)}) collective-permute-start(bf16[32,2176]{1,0:T(8,128)(2,1)} %copy-done.21), channel_id=1, source_target_pairs={{0,1},{1,0},{2,3},{3,2},{4,5},{5,4},{6,7},{7,6},{8,9},{9,8},{10,11... | collective-permute-start | bytes 417800 | tf_op jit(solution)/shard_map/ppermute | solution.py:21
  263.2 12.1 %collective-permute-start.11 = (bf16[32,1408]{1,0:T(8,128)(2,1)S(1)}, bf16[32,1408]{1,0:T(8,128)(2,1)S(1)}, u32[]{:S(2)}, u32[]{:S(2)}) collective-permute-start(bf16[32,1408]{1,0:T(8,128)(2,1)S(1)} %get-tuple-element.78), channel_id=1, source_target_pairs={{0,8},{4,12},{8,0},{12,4},{16,24},{20,28},{24,16},{28,20},{1,9},{5... | collective-permute-start | bytes 270344 | tf_op jit(solution)/shard_map/ppermute | solution.py:21
  264.3 12.8 %collective-permute-start.12 = (bf16[32,1408]{1,0:T(8,128)(2,1)S(1)}, bf16[32,1408]{1,0:T(8,128)(2,1)S(1)}, u32[]{:S(2)}, u32[]{:S(2)}) collective-permute-start(bf16[32,1408]{1,0:T(8,128)(2,1)S(1)} %get-tuple-element.78), channel_id=1, source_target_pairs={{0,16},{4,20},{8,24},{12,28},{16,0},{20,4},{24,8},{28,12},{1,17},{... | collective-permute-start | bytes 270344 | tf_op jit(solution)/shard_map/ppermute | solution.py:21
  271.7 48.0 %collective-permute-start.39 = (bf16[4,4,128,128]{3,2,1,0:T(8,128)(2,1)S(1)}, bf16[4,4,128,128]{3,2,1,0:T(8,128)(2,1)S(1)}, u32[]{:S(2)}, u32[]{:S(2)}) collective-permute-start(bf16[4,4,128,128]{3,2,1,0:T(8,128)(2,1)S(1)} %copy-done.14), channel_id=1, source_target_pairs={{0,12},{4,8},{8,4},{12,0},{16,28},{20,24},{24,20},{28,16},{1,13},{... | collective-permute-start | bytes 1572872 | tf_op jit(solution)/shard_map/ppermute | solution.py:21
  271.9 86.5 %collective-permute-start.40 = (bf16[4,4,128,128]{3,2,1,0:T(8,128)(2,1)S(1)}, bf16[4,4,128,128]{3,2,1,0:T(8,128)(2,1)S(1)}, u32[]{:S(2)}, u32[]{:S(2)}) collective-permute-start(bf16[4,4,128,128]{3,2,1,0:T(8,128)(2,1)S(1)} %copy-done.12), channel_id=1, source_target_pairs={{0,16},{4,20},{8,24},{12,28},{16,0},{20,4},{24,8},{28,12},{1,17},{... | collective-permute-start | bytes 1572872 | tf_op jit(solution)/shard_map/ppermute | solution.py:21
  274.1 84.8 %collective-permute-start.41 = (bf16[4,4,128,128]{3,2,1,0:T(8,128)(2,1)S(1)}, bf16[4,4,128,128]{3,2,1,0:T(8,128)(2,1)S(1)}, u32[]{:S(2)}, u32[]{:S(2)}) collective-permute-start(bf16[4,4,128,128]{3,2,1,0:T(8,128)(2,1)S(1)} %copy-done.10), channel_id=1, source_target_pairs={{0,20},{4,16},{8,28},{12,24},{16,4},{20,0},{24,12},{28,8},{1,21},{... | collective-permute-start | bytes 1572872 | tf_op jit(solution)/shard_map/ppermute | solution.py:21
  275.3 85.5 %collective-permute-start.42 = (bf16[4,4,128,128]{3,2,1,0:T(8,128)(2,1)S(1)}, bf16[4,4,128,128]{3,2,1,0:T(8,128)(2,1)S(1)}, u32[]{:S(2)}, u32[]{:S(2)}) collective-permute-start(bf16[4,4,128,128]{3,2,1,0:T(8,128)(2,1)S(1)} %copy-done.8), channel_id=1, source_target_pairs={{0,24},{4,28},{8,16},{12,20},{16,8},{20,12},{24,0},{28,4},{1,25},{... | collective-permute-start | bytes 1572872 | tf_op jit(solution)/shard_map/ppermute | solution.py:21
  277.1 39.8 %collective-permute-start.13 = (bf16[32,1408]{1,0:T(8,128)(2,1)S(1)}, bf16[32,1408]{1,0:T(8,128)(2,1)S(1)}, u32[]{:S(2)}, u32[]{:S(2)}) collective-permute-start(bf16[32,1408]{1,0:T(8,128)(2,1)S(1)} %get-tuple-element.78), channel_id=1, source_target_pairs={{0,24},{4,28},{8,16},{12,20},{16,8},{20,12},{24,0},{28,4},{1,25},{... | collective-permute-start | bytes 270344 | tf_op jit(solution)/shard_map/ppermute | solution.py:21
  316.9 45.9 %collective-permute-start.43 = (bf16[4,4,128,128]{3,2,1,0:T(8,128)(2,1)S(1)}, bf16[4,4,128,128]{3,2,1,0:T(8,128)(2,1)S(1)}, u32[]{:S(2)}, u32[]{:S(2)}) collective-permute-start(bf16[4,4,128,128]{3,2,1,0:T(8,128)(2,1)S(1)} %copy-done.6), channel_id=1, source_target_pairs={{0,28},{4,24},{8,20},{12,16},{16,12},{20,8},{24,4},{28,0},{1,29},{... | collective-permute-start | bytes 1572872 | tf_op jit(solution)/shard_map/ppermute | solution.py:21
  319.6 48.7 %collective-permute-start.16 = (bf16[2,32,640]{2,1,0:T(8,128)(2,1)S(1)}, bf16[2,32,640]{2,1,0:T(8,128)(2,1)S(1)}, u32[]{:S(2)}, u32[]{:S(2)}) collective-permute-start(bf16[2,32,640]{2,1,0:T(8,128)(2,1)S(1)} %get-tuple-element.86), channel_id=1, source_target_pairs={{0,8},{4,12},{8,0},{12,4},{16,24},{20,28},{24,16},{28,20},{1,9},{5... | collective-permute-start | bytes 245768 | tf_op jit(solution)/shard_map/ppermute | solution.py:21
  358.3 11.5 %collective-permute-start.17 = (bf16[2,32,640]{2,1,0:T(8,128)(2,1)S(1)}, bf16[2,32,640]{2,1,0:T(8,128)(2,1)S(1)}, u32[]{:S(2)}, u32[]{:S(2)}) collective-permute-start(bf16[2,32,640]{2,1,0:T(8,128)(2,1)S(1)} %get-tuple-element.86), channel_id=1, source_target_pairs={{0,16},{4,20},{8,24},{12,28},{16,0},{20,4},{24,8},{28,12},{1,17},{... | collective-permute-start | bytes 245768 | tf_op jit(solution)/shard_map/ppermute | solution.py:21
  358.9 10.9 %collective-permute-start.18 = (bf16[2,32,640]{2,1,0:T(8,128)(2,1)S(1)}, bf16[2,32,640]{2,1,0:T(8,128)(2,1)S(1)}, u32[]{:S(2)}, u32[]{:S(2)}) collective-permute-start(bf16[2,32,640]{2,1,0:T(8,128)(2,1)S(1)} %get-tuple-element.86), channel_id=1, source_target_pairs={{0,24},{4,28},{8,16},{12,20},{16,8},{20,12},{24,0},{28,4},{1,25},{... | collective-permute-start | bytes 245768 | tf_op jit(solution)/shard_map/ppermute | solution.py:21
  362.8 92.3 %collective-permute-start.59 = (bf16[2048,1000]{0,1:T(8,128)(2,1)}, bf16[2048,1000]{0,1:T(8,128)(2,1)}, u32[]{:S(2)}, u32[]{:S(2)}) collective-permute-start(bf16[2048,1000]{0,1:T(8,128)(2,1)} %param.39), channel_id=1, source_target_pairs={{0,1},{1,0},{2,3},{3,2},{4,5},{5,4},{6,7},{7,6},{8,9},{9,8},{10,11... | collective-permute-start | bytes 12288008 | tf_op jit(solution)/shard_map/ppermute | solution.py:21
  389.0 10.8 %collective-permute-start.19 = (bf16[4,32,1408]{2,1,0:T(8,128)(2,1)S(1)}, bf16[4,32,1408]{2,1,0:T(8,128)(2,1)S(1)}, u32[]{:S(2)}, u32[]{:S(2)}) collective-permute-start(bf16[4,32,1408]{2,1,0:T(8,128)(2,1)S(1)} %slice_bitcast_fusion), channel_id=1, source_target_pairs={{0,4},{4,0},{8,12},{12,8},{16,20},{20,16},{24,28},{28,24},{1,5},{5... | collective-permute-start | bytes 1081352 | tf_op jit(solution)/shard_map/ppermute | solution.py:21
  410.3 12.8 %collective-permute-start.44 = (bf16[32,768]{1,0:T(8,128)(2,1)S(1)}, bf16[32,768]{1,0:T(8,128)(2,1)S(1)}, u32[]{:S(2)}, u32[]{:S(2)}) collective-permute-start(bf16[32,768]{1,0:T(8,128)(2,1)S(1)} %get-tuple-element.72), channel_id=1, source_target_pairs={{0,8},{4,12},{8,0},{12,4},{16,24},{20,28},{24,16},{28,20},{1,9},{5... | collective-permute-start | bytes 147464 | tf_op jit(solution)/shard_map/ppermute | solution.py:21
  411.9 12.3 %collective-permute-start.45 = (bf16[32,768]{1,0:T(8,128)(2,1)S(1)}, bf16[32,768]{1,0:T(8,128)(2,1)S(1)}, u32[]{:S(2)}, u32[]{:S(2)}) collective-permute-start(bf16[32,768]{1,0:T(8,128)(2,1)S(1)} %get-tuple-element.72), channel_id=1, source_target_pairs={{0,16},{4,20},{8,24},{12,28},{16,0},{20,4},{24,8},{28,12},{1,17},{... | collective-permute-start | bytes 147464 | tf_op jit(solution)/shard_map/ppermute | solution.py:21
  412.8 12.2 %collective-permute-start.46 = (bf16[32,768]{1,0:T(8,128)(2,1)S(1)}, bf16[32,768]{1,0:T(8,128)(2,1)S(1)}, u32[]{:S(2)}, u32[]{:S(2)}) collective-permute-start(bf16[32,768]{1,0:T(8,128)(2,1)S(1)} %get-tuple-element.72), channel_id=1, source_target_pairs={{0,24},{4,28},{8,16},{12,20},{16,8},{20,12},{24,0},{28,4},{1,25},{... | collective-permute-start | bytes 147464 | tf_op jit(solution)/shard_map/ppermute | solution.py:21
  425.0 10.7 %collective-permute-start.50 = (bf16[2,32,640]{2,1,0:T(8,128)(2,1)S(1)}, bf16[2,32,640]{2,1,0:T(8,128)(2,1)S(1)}, u32[]{:S(2)}, u32[]{:S(2)}) collective-permute-start(bf16[2,32,640]{2,1,0:T(8,128)(2,1)S(1)} %get-tuple-element.82), channel_id=1, source_target_pairs={{0,8},{4,12},{8,0},{12,4},{16,24},{20,28},{24,16},{28,20},{1,9},{5... | collective-permute-start | bytes 245768 | tf_op jit(solution)/shard_map/ppermute | solution.py:21
  425.7 10.3 %collective-permute-start.51 = (bf16[2,32,640]{2,1,0:T(8,128)(2,1)S(1)}, bf16[2,32,640]{2,1,0:T(8,128)(2,1)S(1)}, u32[]{:S(2)}, u32[]{:S(2)}) collective-permute-start(bf16[2,32,640]{2,1,0:T(8,128)(2,1)S(1)} %get-tuple-element.82), channel_id=1, source_target_pairs={{0,16},{4,20},{8,24},{12,28},{16,0},{20,4},{24,8},{28,12},{1,17},{... | collective-permute-start | bytes 245768 | tf_op jit(solution)/shard_map/ppermute | solution.py:21
  436.0 14.3 %collective-permute-start.57 = (bf16[2,2,32,640]{3,2,1,0:T(8,128)(2,1)S(1)}, bf16[2,2,32,640]{3,2,1,0:T(8,128)(2,1)S(1)}, u32[]{:S(2)}, u32[]{:S(2)}) collective-permute-start(bf16[2,2,32,640]{3,2,1,0:T(8,128)(2,1)S(1)} %get-tuple-element.70), channel_id=1, source_target_pairs={{0,16},{4,20},{8,24},{12,28},{16,0},{20,4},{24,8},{28,12},{1,17},{... | collective-permute-start | bytes 491528 | tf_op jit(solution)/shard_map/ppermute | solution.py:21
  438.3 12.0 %collective-permute-start.58 = (bf16[2,2,32,640]{3,2,1,0:T(8,128)(2,1)S(1)}, bf16[2,2,32,640]{3,2,1,0:T(8,128)(2,1)S(1)}, u32[]{:S(2)}, u32[]{:S(2)}) collective-permute-start(bf16[2,2,32,640]{3,2,1,0:T(8,128)(2,1)S(1)} %get-tuple-element.70), channel_id=1, source_target_pairs={{0,24},{4,28},{8,16},{12,20},{16,8},{20,12},{24,0},{28,4},{1,25},{... | collective-permute-start | bytes 491528 | tf_op jit(solution)/shard_map/ppermute | solution.py:21
  440.3 10.2 %collective-permute-start.53 = (bf16[4,2,32,640]{3,2,1,0:T(8,128)(2,1)S(1)}, bf16[4,2,32,640]{3,2,1,0:T(8,128)(2,1)S(1)}, u32[]{:S(2)}, u32[]{:S(2)}) collective-permute-start(bf16[4,2,32,640]{3,2,1,0:T(8,128)(2,1)S(1)} %get-tuple-element.52), channel_id=1, source_target_pairs={{0,4},{4,0},{8,12},{12,8},{16,20},{20,16},{24,28},{28,24},{1,5},{5... | collective-permute-start | bytes 983048 | tf_op jit(solution)/shard_map/ppermute | solution.py:21
  (75 other events, 1322.3 us)
Sparse Core Ops, SparseCore 0:
  9.6 29.7 all-gather.7
  40.9 27.0 all-gather.9
  187.4 30.8 all-gather.11

commit v2 on v1

v2 whole, which is shorter than its diff:
```python
import functools

import jax
import jax.numpy as jnp
import numpy as np
from jax import lax
from jax.experimental import pallas as pl
from jax.experimental.pallas import tpu as pltpu
from jax.sharding import PartitionSpec as P

D = 2048
HEAD_DIM = 128
epsilon = 1e-06
F32 = jnp.float32
BF16 = jnp.bfloat16
VMEM = pltpu.VMEM
SMEM = pltpu.SMEM


def swap(x, axis, size, offset):
    return lax.ppermute(x, axis, [(i, i ^ offset) for i in range(size)])


def bf16_parts(x):
    high = lax.reduce_precision(x, 8, 7)
    return high.astype(BF16), (x - high).astype(BF16)


def sort_kernel(sends, order_ref, old_ref, *rest):
    outs, held, in_sems, out_sems = rest[:sends], rest[sends], rest[sends + 1], rest[sends + 2]
    owners = held.shape[1]

    def load(rank, owner):
        at = owner * sends + rank
        return pltpu.make_async_copy(
            old_ref.at[order_ref[at]], held.at[rank, owner], in_sems.at[rank, owner]
        )

    def store(rank):
        return pltpu.make_async_copy(held.at[rank], outs[rank], out_sems.at[rank])

    for rank in range(sends):
        for owner in range(owners):
            load(rank, owner).start()
    for rank in range(sends):
        for owner in range(owners):
            load(rank, owner).wait()
        store(rank).start()
    for rank in range(sends):
        store(rank).wait()


def sort_states(order, old_states, owners):
    requests = old_states.shape[0]
    sends = requests // owners
    piece = (owners,) + old_states.shape[1:]
    return pl.pallas_call(
        functools.partial(sort_kernel, sends),
        out_shape=[jax.ShapeDtypeStruct(piece, old_states.dtype)] * sends,
        in_specs=[pl.BlockSpec(memory_space=SMEM), pl.BlockSpec(memory_space=pl.ANY)],
        out_specs=[pl.BlockSpec(memory_space=pl.ANY)] * sends,
        scratch_shapes=[
            VMEM((sends,) + piece, old_states.dtype),
            pltpu.SemaphoreType.DMA((sends, owners)),
            pltpu.SemaphoreType.DMA((sends,)),
        ],
        compiler_params=pltpu.CompilerParams(vmem_limit_bytes=56 << 20),
    )(order, old_states)


def roll(x, by):
    return pltpu.roll(x, by % x.shape[0], 0)


def mixer_kernel(
    sends, owners, heads, classes, steps,
    me_ref, emb_ref, live_ref, gain_ref, floor_ref, ggain_ref, qw_hbm, fw_hbm, iw_hbm, ow_hbm,
    *rest,
):
    states_hbm = rest[:sends]
    own_ref, part_ref, kv_ref = rest[sends : sends + 3]
    qw_ref, fw_ref, iw_ref, ow_ref, states, qhi_ref, qlo_ref, mixed_ref, sems = rest[sends + 3 :]
    weight_pairs = ((qw_hbm, qw_ref), (fw_hbm, fw_ref), (iw_hbm, iw_ref), (ow_hbm, ow_ref))
    loads = [
        pltpu.make_async_copy(there, here, sems.at[i]) for i, (there, here) in enumerate(weight_pairs)
    ]
    state_loads = [
        pltpu.make_async_copy(states_hbm[i], states.at[i], sems.at[4 + i]) for i in range(sends)
    ]
    for load in loads[:3] + state_loads + loads[3:]:
        load.start()
    tokens = live_ref.shape[0]
    requests = tokens // steps
    group = requests // classes
    rows = group * steps
    stream = emb_ref[0:tokens, :].astype(F32)
    scale = lax.rsqrt(jnp.mean(stream * stream, axis=1, keepdims=True) + epsilon)
    normed = (stream * scale * gain_ref[...]).astype(BF16)
    loads[0].wait()
    query = jnp.dot(normed, qw_ref[...], preferred_element_type=F32)
    query = query * jax.nn.sigmoid(query) * HEAD_DIM ** (-0.5)
    loads[1].wait()
    forget_raw = jnp.dot(normed, fw_ref[...], preferred_element_type=F32)
    loads[2].wait()
    value = jnp.dot(normed, iw_ref[...], preferred_element_type=F32)
    floor = floor_ref[...]
    forget = jnp.where(
        live_ref[...] > 0.0, floor + (1.0 - floor) * jax.nn.sigmoid(forget_raw), 1.0
    )
    key = 1.0 - forget
    step = lax.broadcasted_iota(jnp.int32, forget.shape, 0) % steps
    upto = forget * jnp.where(step >= 1, roll(forget, 1), 1.0)
    upto = upto * jnp.where(step >= 2, roll(upto, 2), 1.0)
    after = jnp.where(step <= steps - 2, roll(forget, -1), 1.0)
    after = after * jnp.where(step <= steps - 3, roll(forget, -2), 1.0)
    after = after * jnp.where(step <= steps - 4, roll(forget, -3), 1.0)
    carried = query * upto
    high = carried.astype(BF16).astype(F32)
    qhi_ref[...] = high
    qlo_ref[...] = carried - high
    lag_key, lag_value = key, value
    local = [jnp.zeros((tokens, HEAD_DIM), F32) for _ in range(heads)]
    for lag in range(steps):
        if lag:
            lag_key = roll(lag_key, 1) * forget
            lag_value = roll(lag_value, 1)
        product = jnp.where(step >= lag, query * lag_key, 0.0)
        for head in range(heads):
            cols = slice(head * HEAD_DIM, (head + 1) * HEAD_DIM)
            weight = jnp.sum(product[:, cols], axis=1, keepdims=True)
            local[head] = local[head] + weight * lag_value[:, cols]
    for head in range(heads):
        mixed_ref[:, head * HEAD_DIM : (head + 1) * HEAD_DIM] = local[head]
    for load in state_loads:
        load.wait()
    here = me_ref[0]
    upper = lax.broadcasted_iota(jnp.int32, (8, HEAD_DIM), 0) < steps
    for tile in range(tokens // 8):
        for head in range(heads):
            cols = slice(head * HEAD_DIM, (head + 1) * HEAD_DIM)
            at = slice(tile * 8, tile * 8 + 8)
            left = jnp.concatenate([qhi_ref[at, cols], qlo_ref[at, cols]], axis=0).astype(BF16)
            got = []
            for request in (2 * tile, 2 * tile + 1):
                place = (request % group) * classes + request // group
                old = states[place % sends, here ^ (place // sends), head]
                product = jnp.dot(left, old, preferred_element_type=F32)
                got.append(product[0:8] + product[8:16])
            mixed_ref[at, cols] += jnp.where(upper, got[0], got[1])
    mixed = mixed_ref[...]
    square = jnp.sum(mixed * mixed, axis=1, keepdims=True)
    loads[3].wait()
    part_ref[:, 0:D] = jnp.dot(
        (mixed * ggain_ref[...]).astype(BF16), ow_ref[...], preferred_element_type=F32
    ).astype(BF16)
    square_high = square.astype(BF16).astype(F32)
    lane = lax.broadcasted_iota(jnp.int32, (tokens, 128), 1)
    part_ref[:, D : D + 128] = jnp.where(lane < 64, square_high, square - square_high).astype(BF16)
    own_ref[...] = emb_ref[pl.ds(pl.multiple_of(me_ref[1] * rows, rows), rows), :]
    both = jnp.concatenate([(key * after).astype(BF16), value.astype(BF16)], axis=0)
    shape = (2 * tokens, 2 * tokens)
    target = lax.broadcasted_iota(jnp.int32, shape, 0)
    source = lax.broadcasted_iota(jnp.int32, shape, 1)
    slot, within = target // (2 * steps), target % (2 * steps)
    place = ((slot // sends) ^ here) * sends + slot % sends
    request = (place % classes) * group + place // classes
    wanted = request * steps + within % steps + jnp.where(within >= steps, tokens, 0)
    pick = jnp.where(source == wanted, 1.0, 0.0).astype(BF16)
    kv_ref[...] = jnp.dot(pick, both, preferred_element_type=F32).astype(BF16)


def mixer(me, emb, live, gain, floor, ggain, weights, states, steps, classes):
    tokens = live.shape[0]
    sends, (owners, heads) = len(states), states[0].shape[:2]
    width = floor.shape[1]
    rows = tokens // classes
    vmem, anywhere = pl.BlockSpec(memory_space=VMEM), pl.BlockSpec(memory_space=pl.ANY)
    return pl.pallas_call(
        functools.partial(mixer_kernel, sends, owners, heads, classes, steps),
        out_shape=[
            jax.ShapeDtypeStruct((rows, D), BF16),
            jax.ShapeDtypeStruct((tokens, D + 128), BF16),
            jax.ShapeDtypeStruct((2 * tokens, width), BF16),
        ],
        in_specs=[pl.BlockSpec(memory_space=SMEM)] + [vmem] * 5 + [anywhere] * (4 + sends),
        out_specs=[vmem] * 3,
        scratch_shapes=[VMEM(w.shape, BF16) for w in weights]
        + [
            VMEM((sends,) + states[0].shape, BF16),
            VMEM((tokens, width), F32),
            VMEM((tokens, width), F32),
            VMEM((tokens, width), F32),
            pltpu.SemaphoreType.DMA((4 + sends,)),
        ],
        compiler_params=pltpu.CompilerParams(vmem_limit_bytes=56 << 20),
    )(me, emb, live, gain, floor, ggain, *weights, *states)


def update_kernel(sends, owners, heads, steps, slot_ref, kv_ref, *rest):
    states, out_ref = rest[:sends], rest[sends]
    diagonal = lax.broadcasted_iota(jnp.int32, (HEAD_DIM, HEAD_DIM), 0) == lax.broadcasted_iota(
        jnp.int32, (HEAD_DIM, HEAD_DIM), 1
    )
    first = lax.broadcasted_iota(jnp.int32, (2 * steps, HEAD_DIM), 0) < steps
    for k in range(owners):
        for rank in range(sends):
            place = k * sends + rank
            slot = slot_ref[place]
            for head in range(heads):
                cols = slice(head * HEAD_DIM, (head + 1) * HEAD_DIM)
                both = kv_ref[place, :, cols]
                key = jnp.where(first, both, 0.0)
                value = jnp.where(first, roll(both, steps), 0.0)
                kept = 1.0 - jnp.sum(key, axis=0, keepdims=True)
                keep = jnp.where(diagonal, kept, 0.0).astype(BF16)
                fresh = lax.dot_general(
                    key, value, (((0,), (0,)), ((), ())), preferred_element_type=F32
                )
                old = jnp.dot(keep, states[rank][k, head], preferred_element_type=F32)
                out_ref[slot, head] = (old + fresh).astype(BF16)


def update_states(slots, kv, states, steps):
    sends, (owners, heads) = len(states), states[0].shape[:2]
    vmem = pl.BlockSpec(memory_space=VMEM)
    return pl.pallas_call(
        functools.partial(update_kernel, sends, owners, heads, steps),
        out_shape=jax.ShapeDtypeStruct((owners * sends,) + states[0].shape[1:], BF16),
        in_specs=[pl.BlockSpec(memory_space=SMEM)] + [vmem] * (1 + sends),
        out_specs=vmem,
        compiler_params=pltpu.CompilerParams(vmem_limit_bytes=56 << 20),
    )(slots, kv, *states)


def to_all(x, axis):
    return lax.all_to_all(x, axis, split_axis=0, concat_axis=0, tiled=True)


def tied(x, *others):
    return lax.optimization_barrier((x,) + others)[0]


def on_device(
    token_ids, state_perm, token_count, tenant_bounds, old_states, embedding, mixer_gain,
    query_weight, forget_weight, input_weight, forget_floor, group_gain, output_weight, feed_gain,
    gate_weight, up_weight, down_weight, final_gain, tenant_gain, vocab_weight,
):
    requests, steps = token_ids.shape
    n = lax.axis_size("req")
    n_head = lax.axis_size("head")
    r = lax.axis_index("req")
    h = lax.axis_index("head")
    tokens = requests * steps
    everyone = requests * n
    sends = requests // n
    group = requests // n_head
    rows = group * steps
    width = D // n_head

    packed = jnp.concatenate([token_ids.T, state_perm[None], token_count[None]], axis=0)
    packed = lax.all_gather(packed, "req", axis=0).transpose(1, 0, 2).reshape(steps + 2, everyone)
    every = jnp.arange(everyone, dtype=jnp.int32)
    gate_full = lax.all_gather(tied(gate_weight, packed), "head", axis=0, tiled=True)
    up_full = lax.all_gather(tied(up_weight, packed), "head", axis=0, tiled=True)
    down_full = lax.all_gather(tied(down_weight, packed), "head", axis=0)
    source = packed[steps] // requests
    rank = jnp.sum(
        ((source[None, :] == source[:, None]) & (every[None, :] < every[:, None])).astype(jnp.int32),
        axis=1,
    )
    place = ((every // requests) ^ source) * sends + rank % sends
    at = source * requests + (place % n_head) * group + place // n_head
    chosen = (at[:, None] == every[None, :]).astype(F32)
    ordered = jnp.dot(packed.astype(F32), chosen, precision=lax.Precision.HIGHEST)
    ordered = (ordered + 0.5).astype(jnp.int32)

    ids = ordered[:steps].T.reshape(n * tokens)
    table = embedding.shape[0]
    local_ids = ids - r * table
    inside = (local_ids >= 0) & (local_ids < table)
    picked = jnp.take(embedding, jnp.clip(local_ids, 0, table - 1), axis=0, mode="clip")
    picked = jnp.where(inside[:, None], picked, jnp.zeros((), BF16)).reshape(n, tokens, width)
    embed_part = jnp.sum(to_all(picked, "req").astype(F32), axis=0).astype(BF16)
    vocab_other = swap(tied(vocab_weight, embed_part), "head", n_head, 1)

    gains = jnp.concatenate([final_gain[None], tenant_gain], axis=0)
    gains_high, gains_low = bf16_parts(gains)
    extra = jnp.zeros((16 - 2 * gains.shape[0], width), BF16)
    embedded = lax.all_gather(
        jnp.concatenate([embed_part, gains_high, gains_low, extra], axis=0), "head", axis=1, tiled=True
    )
    gains = embedded[tokens : tokens + 5].astype(F32) + embedded[tokens + 5 : tokens + 10].astype(F32)

    ordered = lax.dynamic_slice_in_dim(ordered, r * requests, requests, 1)
    old_order = (ordered[steps] - r * requests).reshape(n_head, group).T.reshape(n, sends)
    old_order = jnp.take(old_order, jnp.arange(n) ^ r, axis=0).reshape(requests)
    pieces = sort_states(old_order, old_states, n)
    live = (jnp.arange(steps)[None, :] < ordered[steps + 1][:, None]).astype(F32)
    own, parts, kv = mixer(
        jnp.stack([r, h]), embedded, live.reshape(tokens, 1), mixer_gain[None], forget_floor[None],
        group_gain[None], (query_weight, forget_weight, input_weight, output_weight), pieces,
        steps, n_head,
    )
    arrived = [
        to_all(tied(piece, embed_part), "req") for piece in pieces[: (sends + 1) // 2]
    ]

    total = jnp.sum(to_all(parts.reshape(n_head, rows, D + 128), "head").astype(F32), axis=0)
    square = total[:, D : D + 1] + total[:, D + 127 : D + 128]
    after_mixer = own.astype(F32) + total[:, :D] * lax.rsqrt(square / D + epsilon)
    after_mixer = tied(after_mixer.astype(BF16), *arrived)
    half = D // 2
    everything = jnp.concatenate(
        [lax.all_gather(after_mixer[:, at : at + half], "req", axis=0) for at in (0, half)], axis=-1
    ).reshape(n * rows, D)
    arrived_kv = to_all(tied(kv, everything).reshape(n, -1, width), "req")
    if sends >= 4:
        arrived += [to_all(tied(pieces[2], everything), "req")]
    stream = everything.astype(F32)
    scale = lax.rsqrt(jnp.mean(stream * stream, axis=1, keepdims=True) + epsilon)
    feed_in = (stream * scale * feed_gain).astype(BF16)
    gate = jnp.dot(feed_in, gate_full, preferred_element_type=F32)
    up = jnp.dot(feed_in, up_full, preferred_element_type=F32)
    activated = (jax.nn.silu(gate) * up).astype(BF16)

    row = jnp.arange(n * rows, dtype=jnp.int32)
    by_owner, by_group, by_step = row // rows, (row % rows) // steps, row % steps
    if sends % n_head == 0:
        offset = by_group * n_head // sends
    else:
        offset = (by_group * n_head + h) // sends
    wanted = (by_owner ^ offset) * rows + by_group * steps + by_step
    pick = (wanted[None, :] == row[:, None]).astype(BF16)
    activated = jnp.dot(pick, activated, preferred_element_type=F32).astype(BF16)
    mine = (wanted[None, :] == (r * rows + row[:rows])[:, None]).astype(BF16)
    kept = jnp.dot(mine, everything, preferred_element_type=F32)
    down = jnp.concatenate(
        [jnp.dot(activated, down_full[b], preferred_element_type=F32).astype(BF16) for b in range(n_head)],
        axis=1,
    )
    down = tied(down, *arrived)
    hidden = kept + jnp.sum(to_all(down.reshape(n, rows, D), "req").astype(F32), axis=0)
    mean_square = jnp.mean(hidden * hidden, axis=1, keepdims=True)

    slots = jnp.arange(requests, dtype=jnp.int32)
    source = state_perm // requests
    rank = jnp.sum(
        ((source[None, :] == source[:, None]) & (slots[None, :] < slots[:, None])).astype(jnp.int32),
        axis=1,
    )
    place = (source ^ r) * sends + rank
    natural = source * sends + rank
    slot_of = jnp.sum(jnp.where(natural[None, :] == slots[:, None], slots[None, :], 0), axis=1)
    mine = jnp.sum(
        jnp.where(
            place[None, :] == (jnp.arange(group, dtype=jnp.int32) * n_head + h)[:, None],
            slots[None, :],
            0,
        ),
        axis=1,
    )
    tenant = jnp.sum(
        ((mine + r * requests)[:, None] >= tenant_bounds[None, 1:-1]).astype(jnp.int32), axis=1
    )
    tenant_rows = sum(
        jnp.where((tenant == t)[:, None], gains[1 + t][None, :], 0.0)
        for t in range(tenant_gain.shape[0])
    )
    token_gain = jnp.repeat(tenant_rows * gains[0][None, :], steps, axis=0)
    final = (hidden * lax.rsqrt(mean_square + epsilon) * token_gain).astype(BF16)

    final = jnp.stack([final, swap(final, "head", n_head, 2)])
    quarter = D // 4
    full = jnp.concatenate(
        [
            lax.all_gather(final[:, :, at : at + quarter], "req", axis=0)
            for at in range(0, D, quarter)
        ],
        axis=-1,
    ).reshape(n * 2 * rows, D)
    if sends >= 4:
        arrived += [to_all(tied(pieces[3], full), "req")]
    best = jnp.maximum(
        jnp.max(jnp.dot(full, vocab_weight, preferred_element_type=F32), axis=1),
        jnp.max(jnp.dot(full, vocab_other, preferred_element_type=F32), axis=1),
    ).reshape(n, 2 * rows)
    got = jnp.max(to_all(best, "req"), axis=0)
    got = lax.all_gather(got, "head", axis=0).reshape(n_head, 2, rows)
    crossed = jnp.stack([got[i ^ 2, 1] for i in range(n_head)])
    best = jnp.maximum(got[:, 0], crossed).reshape(requests, steps)
    index = (place % n_head) * group + place // n_head
    match = (index[:, None] == slots[None, :])[:, :, None]
    best = jnp.sum(jnp.where(match, best[None], 0.0), axis=1)
    live = jnp.arange(steps)[None, :] < token_count[:, None]
    greatest = jnp.max(jnp.where(live, best, -1e30), axis=1)

    blocks = hidden.reshape(rows, n_head, width).transpose(1, 0, 2)
    tail = jnp.broadcast_to(mean_square[None], (n_head, rows, 128))
    whole = to_all(jnp.concatenate([blocks, tail], axis=2), "head")
    whole = whole.reshape(requests, steps, width + 128)
    whole = jnp.take(whole, (place % n_head) * group + place // n_head, axis=0, mode="clip")
    last = jnp.arange(steps)[None, :] == (token_count - 1)[:, None]
    last_norm = jnp.sqrt(jnp.sum(jnp.where(last, whole[:, :, width], 0.0), axis=1) + epsilon)

    new_states = update_states(
        slot_of, arrived_kv.reshape(requests, 2 * steps, width).astype(F32), arrived, steps
    )
    return whole[:, :, :width], new_states, last_norm, greatest


def solution(mesh):
    placed = (
        P("req", None),
        P("req"),
        P("req"),
        P(),
        P("req", "head", None, None),
        P("req", "head"),
        P(),
        P(None, "head"),
        P(None, "head"),
        P(None, "head"),
        P("head"),
        P("head"),
        P("head", None),
        P(),
        P("head", "req"),
        P("head", "req"),
        P("req", "head"),
        P("head"),
        P(None, "head"),
        P(None, ("req", "head")),
    )
    return jax.shard_map(
        on_device,
        mesh=mesh,
        in_specs=placed,
        out_specs=(P("req", None, "head"), P("req", "head", None, None), P("req"), P("req")),
        check_vma=False,
    )
```

time: 490 us -> 490 us (level)
  blocking collectives: 48.4 us -> 238 us
  Pallas kernels: 138 us -> 19.4 us
  starting transfers between devices: 132 us -> 40.3 us
  waiting for transfers between devices: 91.1 us -> 129 us
  local copies, waits for them, and re-layouts: 34.6 us -> 17.2 us
    all_gather x0 -> x6, blocking collectives: none -> 189 us  [the longest x4 126 us: on_device(): lax.all_gather(final[:, :, at:at + quarter], 'req', axis=0)]
    ppermute x67 -> x2, starting transfers between devices: 132 us -> 0.77 us  [swap(): return lax.ppermute(x, axis, [(i, i ^ offset) for i in range(size)])]
    all_to_all x0 -> x10, waiting for transfers between devices: none -> 126 us  [to_all(): return lax.all_to_all(x, axis, split_axis=0, concat_axis=0, tiled=True)]
    pallas_call x3, Pallas kernels: 138 us -> 19.4 us  [the longest x1 8.05 us: mixer(): pl.pallas_call(functools.partial(mixer_kernel, sends, owners, heads, clas...]
    ppermute x67 -> x2, waiting for transfers between devices: 89.6 us -> 0.9 us  [swap(): return lax.ppermute(x, axis, [(i, i ^ offset) for i in range(size)])]
    all_to_all x0 -> x10, starting transfers between devices: none -> 39.4 us  [to_all(): return lax.all_to_all(x, axis, split_axis=0, concat_axis=0, tiled=True)]
    unnamed x85 -> x35, local copies, waits for them, and re-layouts: 18.5 us -> 3.75 us
  transfers between devices with their start and end apart: 70 -> 15, of which waited for: 26 -> 10; matrix products, arithmetic and copies ran while one was open for 9% -> 9% of each run, Pallas kernels for 28% -> 3%
where the time goes in v2:
time: 490 us; the launch traced here: 489 us
  blocking collectives  238 us (49%)
  waiting for transfers between devices  129 us (26%)
  starting transfers between devices  40.3 us (8%)
  Pallas kernels  19.4 us (4%)
  matrix products  18.8 us (4%)
  local copies, waits for them, and re-layouts  17.2 us (4%)
  between operations  14.9 us (3%)
  other arithmetic  11.7 us (2%)
    all_to_all x10, waiting for transfers between devices, to_all(): return lax.all_to_all(x, axis, split_axis=0, concat_axis=0, tiled=True)  126 us
    all_gather x4, blocking collectives, on_device(): lax.all_gather(final[:, :, at:at + quarter], 'req', axis=0)  126 us
    all_gather x2, blocking collectives, on_device(): lax.all_gather(after_mixer[:, at:at + half], 'req', axis=0)  62.9 us
    all_to_all x10, starting transfers between devices, to_all(): return lax.all_to_all(x, axis, split_axis=0, concat_axis=0, tiled=True)  39.4 us
    all_gather x1, blocking collectives, on_device(): lax.all_gather(packed, 'req', axis=0).transpose(1, 0, 2)  32.2 us
    all_gather x1, blocking collectives, on_device(): lax.all_gather(jnp.concatenate([embed_part, gains_high, gains_low, extra]...  10.8 us
  transfers between devices with their start and end apart: 15, of which 10 were waited for; matrix products, arithmetic and copies ran while one was open for 9% of the time, Pallas kernels for 3%

profile of v2, /device:TPU:0, one launch (start us, length us, event | category | flops | bytes accessed | tf_op | source)
XLA Modules:
  0.0 489.0 jit_solution(12841056875291921103)
XLA Ops:
  7.9 32.2 %all-gather.9 = s32[8,6,32]{2,1,0:T(8,128)S(1)} all-gather(s32[1,6,32]{2,1,0:T(8,128)S(1)} %add_bitcast_fusion), channel_id=2, replica_groups=mesh['req'=8,'head'=4] {'req'}, dimensions={0}, use_global_device_ids=true | all-gather | bytes 6912 | tf_op jit(solution)/shard_map/all_gather | solution.py:261
  42.2 6.7 %gather_fusion = bf16[1024,512]{1,0:T(8,128)(2,1)S(1)} fusion(bf16[4000,512]{1,0:T(8,128)(2,1)} %param.25, s32[1024]{0:T(1024)S(1)} %broadcast_clamp_fusion), kind=kCustom, calls=%fused_computation | custom fusion | bytes 2101248 | tf_op jit(solution)/shard_map/jit(_take)/gather | solution.py:281
  50.1 5.5 %all-to-all-start = ((bf16[8,128,512]{2,1,0:T(8,128)(2,1)}), bf16[8,128,512]{2,1,0:T(8,128)(2,1)S(1)}, u32[]{:S(2)}, u32[]{:S(2)}) async-start(bf16[8,128,512]{2,1,0:T(8,128)(2,1)} %broadcast_select_fusion), calls=%async_computation | async-start | bytes 2097152 | tf_op jit(solution)/shard_map/all_to_all | solution.py:236
  57.9 4.6 shard_map.219
  63.2 12.0 %all-to-all-done = bf16[8,128,512]{2,1,0:T(8,128)(2,1)S(1)} async-done(((bf16[8,128,512]{2,1,0:T(8,128)(2,1)}), bf16[8,128,512]{2,1,0:T(8,128)(2,1)S(1)}, u32[]{:S(2)}, u32[]{:S(2)}) %all-to-all-start) | async-done | bytes 1048608 | tf_op jit(solution)/shard_map/all_to_all | solution.py:236
  75.4 10.8 %all_gather.65.emb_ref = bf16[144,2048]{1,0:T(8,128)(2,1)} all-gather(bf16[144,512]{1,0:T(8,128)(2,1)S(1)} %maximum_maximum_fusion), channel_id=1, replica_groups=mesh['req'=8,'head'=4] {'head'}, dimensions={1}, use_global_device_ids=true | all-gather | bytes 737280 | tf_op jit(solution)/shard_map/all_gather | solution.py:289
  86.2 8.1 %shard_map.220 = (bf16[32,2048]{1,0:T(8,128)(2,1)}, bf16[128,2176]{1,0:T(8,128)(2,1)}, bf16[256,512]{1,0:T(8,128)(2,1)}) custom-call(s32[2]{0:T(128)} %pad_add_fusion.me_ref, bf16[144,2048]{1,0:T(8,128)(2,1)} %all_gather.65.emb_ref, f32[128,1]{1,0:T(8,128)} %reshape.502.live_ref, f32[1,2048]{1,0:T(1,128)} %bitcast.104, f32[1,512]{1,0:T(1,128)} %bitcast.109, ...), custom_call_target="tpu_custom_call" | custom-call | tf_op jit(solution)/shard_map/pallas_call | solution.py:178
  94.2 3.5 all-to-all-start.1
  97.8 9.2 %all-to-all-done.1 = bf16[4,32,2176]{2,1,0:T(8,128)(2,1)S(1)} async-done(((bf16[4,32,2176]{2,1,0:T(8,128)(2,1)}), bf16[4,32,2176]{2,1,0:T(8,128)(2,1)S(1)}, u32[]{:S(2)}, u32[]{:S(2)}) %all-to-all-start.1) | async-done | bytes 557088 | tf_op jit(solution)/shard_map/all_to_all | solution.py:236
  106.9 3.6 all-to-all-start.2
  111.3 24.9 %all-to-all-done.2.rest_0_ = bf16[8,4,128,128]{3,2,1,0:T(8,128)(2,1)S(1)} async-done(((bf16[8,4,128,128]{3,2,1,0:T(8,128)(2,1)}), bf16[8,4,128,128]{3,2,1,0:T(8,128)(2,1)S(1)}, u32[]{:S(2)}, u32[]{:S(2)}) %all-to-all-start.2) | async-done | bytes 1048608 | tf_op jit(solution)/shard_map/all_to_all | solution.py:236
  136.2 3.6 all-to-all-start.3
  140.7 25.1 %all-to-all-done.3.rest_1_ = bf16[8,4,128,128]{3,2,1,0:T(8,128)(2,1)S(1)} async-done(((bf16[8,4,128,128]{3,2,1,0:T(8,128)(2,1)}), bf16[8,4,128,128]{3,2,1,0:T(8,128)(2,1)S(1)}, u32[]{:S(2)}, u32[]{:S(2)}) %all-to-all-start.3) | async-done | bytes 1048608 | tf_op jit(solution)/shard_map/all_to_all | solution.py:236
  165.8 31.3 %all-gather.1 = bf16[256,1024]{1,0:T(8,128)(2,1)S(1)} all-gather(bf16[32,1024]{1,0:T(8,128)(2,1)S(1)} %get-tuple-element.46), channel_id=3, replica_groups=mesh['req'=8,'head'=4] {'req'}, dimensions={0}, use_global_device_ids=true | all-gather | bytes 589824 | tf_op jit(solution)/shard_map/all_gather | solution.py:314
  197.1 31.7 %all-gather.2 = bf16[256,1024]{1,0:T(8,128)(2,1)S(1)} all-gather(bf16[32,1024]{1,0:T(8,128)(2,1)S(1)} %get-tuple-element.47), channel_id=4, replica_groups=mesh['req'=8,'head'=4] {'req'}, dimensions={0}, use_global_device_ids=true | all-gather | bytes 589824 | tf_op jit(solution)/shard_map/all_gather | solution.py:314
  229.8 4.2 all-to-all-start.4
  234.4 4.2 fusion.12
  247.0 11.9 %all-to-all-done.4.rest_2_ = bf16[8,4,128,128]{3,2,1,0:T(8,128)(2,1)S(1)} async-done(((bf16[8,4,128,128]{3,2,1,0:T(8,128)(2,1)}), bf16[8,4,128,128]{3,2,1,0:T(8,128)(2,1)S(1)}, u32[]{:S(2)}, u32[]{:S(2)}) %all-to-all-start.4) | async-done | bytes 1048608 | tf_op jit(solution)/shard_map/all_to_all | solution.py:236
  258.9 4.4 all-to-all-start.5
  265.4 17.4 %all-to-all-done.5 = bf16[8,32,2048]{2,1,0:T(8,128)(2,1)S(1)} async-done(((bf16[8,32,2048]{2,1,0:T(8,128)(2,1)}), bf16[8,32,2048]{2,1,0:T(8,128)(2,1)S(1)}, u32[]{:S(2)}, u32[]{:S(2)}) %all-to-all-start.5) | async-done | bytes 1048608 | tf_op jit(solution)/shard_map/all_to_all | solution.py:236
  288.6 32.1 %all-gather.4 = bf16[16,32,512]{2,1,0:T(8,128)(2,1)S(1)} all-gather(bf16[2,32,512]{2,1,0:T(8,128)(2,1)S(1)} %get-tuple-element.42), channel_id=6, replica_groups=mesh['req'=8,'head'=4] {'req'}, dimensions={0}, use_global_device_ids=true | all-gather | bytes 589824 | tf_op jit(solution)/shard_map/all_gather | solution.py:376
  320.7 31.5 %all-gather.5 = bf16[16,32,512]{2,1,0:T(8,128)(2,1)S(1)} all-gather(bf16[2,32,512]{2,1,0:T(8,128)(2,1)S(1)} %get-tuple-element.43), channel_id=7, replica_groups=mesh['req'=8,'head'=4] {'req'}, dimensions={0}, use_global_device_ids=true | all-gather | bytes 589824 | tf_op jit(solution)/shard_map/all_gather | solution.py:376
  352.2 31.5 %all-gather.6 = bf16[16,32,512]{2,1,0:T(8,128)(2,1)S(1)} all-gather(bf16[2,32,512]{2,1,0:T(8,128)(2,1)S(1)} %get-tuple-element.45), channel_id=8, replica_groups=mesh['req'=8,'head'=4] {'req'}, dimensions={0}, use_global_device_ids=true | all-gather | bytes 589824 | tf_op jit(solution)/shard_map/all_gather | solution.py:376
  383.7 31.2 %all-gather.7 = bf16[16,32,512]{2,1,0:T(8,128)(2,1)S(1)} all-gather(bf16[2,32,512]{2,1,0:T(8,128)(2,1)S(1)} %get-tuple-element.44), channel_id=9, replica_groups=mesh['req'=8,'head'=4] {'req'}, dimensions={0}, use_global_device_ids=true | all-gather | bytes 589824 | tf_op jit(solution)/shard_map/all_gather | solution.py:376
  419.4 4.5 convolution_reduce_fusion
  424.6 4.2 all-to-all-start.9
  429.6 5.6 %all-to-all-done.9 = f32[8,1,64]{2,1,0:T(1,128)S(1)} async-done(((f32[8,1,64]{2,1,0:T(1,128)}), f32[8,1,64]{2,1,0:T(1,128)S(1)}, u32[]{:S(2)}, u32[]{:S(2)}) %all-to-all-start.9) | async-done | bytes 2080 | tf_op jit(solution)/shard_map/all_to_all | solution.py:236
  438.7 6.7 %all-to-all-done.6 = f32[4,32,640]{2,1,0:T(8,128)S(1)} async-done(((f32[4,32,640]{2,1,0:T(8,128)}), f32[4,32,640]{2,1,0:T(8,128)S(1)}, u32[]{:S(2)}, u32[]{:S(2)}) %all-to-all-start.6) | async-done | bytes 327712 | tf_op jit(solution)/shard_map/all_to_all | solution.py:236
  445.4 3.6 all-to-all-start.8
  452.1 5.9 %all-reduce = f32[256]{0:T(256)S(1)} all-reduce(f32[256]{0:T(256)S(1)} %dynamic-update-slice), channel_id=10, replica_groups=mesh['req'=8,'head'=4] {'head'}, use_global_device_ids=true, to_apply=%add | all-reduce | flops 256 | bytes 2048
  461.3 13.4 %all-to-all-done.8.rest_3_ = bf16[8,4,128,128]{3,2,1,0:T(8,128)(2,1)S(1)} async-done(((bf16[8,4,128,128]{3,2,1,0:T(8,128)(2,1)}), bf16[8,4,128,128]{3,2,1,0:T(8,128)(2,1)S(1)}, u32[]{:S(2)}, u32[]{:S(2)}) %all-to-all-start.8) | async-done | bytes 1048608 | tf_op jit(solution)/shard_map/all_to_all | solution.py:236
  475.7 6.7 %shard_map.221 = bf16[32,4,128,128]{3,2,1,0:T(8,128)(2,1)} custom-call(s32[32]{0:T(128)} %select_reduce_fusion.1.slot_ref, f32[32,8,512]{2,1,0:T(8,128)} %convert.3.kv_ref, bf16[8,4,128,128]{3,2,1,0:T(8,128)(2,1)} %copy-done, bf16[8,4,128,128]{3,2,1,0:T(8,128)(2,1)} %copy-done.1, bf16[8,4,128,128]{3,2,1,0:T(8,128)(2,1)} %copy-done.2, ...), custom_call_target="tpu_custom_call" | custom-call | tf_op jit(solution)/shard_map/pallas_call | solution.py:226
  (152 shorter events, 42.4 us)
Async XLA Ops:
  7.2 227.3 %all-gather.14.cloned.1.call-start = ((), (), s32[]{:S(2)}) async-start(), calls=%async_computation.10 | async-start | bytes 3604480 | tf_op jit(solution)/shard_map/all_gather | solution.py:263
  40.2 198.4 %all-gather.16.cloned.1.call-start = ((), (), s32[]{:S(2)}) async-start(), calls=%async_computation.11 | async-start | bytes 3604480 | tf_op jit(solution)/shard_map/all_gather | solution.py:264
  50.1 25.1 %all-to-all-start = ((bf16[8,128,512]{2,1,0:T(8,128)(2,1)}), bf16[8,128,512]{2,1,0:T(8,128)(2,1)S(1)}, u32[]{:S(2)}, u32[]{:S(2)}) async-start(bf16[8,128,512]{2,1,0:T(8,128)(2,1)} %broadcast_select_fusion), calls=%async_computation | async-start | bytes 2097152 | tf_op jit(solution)/shard_map/all_to_all | solution.py:236
  57.9 5.2 %copy-start.7 = (f32[4,512]{1,0:T(4,128)S(1)}, f32[4,512]{1,0:T(4,128)}, u32[]{:S(2)}) copy-start(f32[4,512]{1,0:T(4,128)} %param.38) | copy-start | bytes 24580
  57.9 5.2 %copy-start.10 = (f32[512]{0:T(512)S(1)}, f32[512]{0:T(512)}, u32[]{:S(2)}) copy-start(f32[512]{0:T(512)} %param.37) | copy-start | bytes 6148
  94.2 17.0 %copy-start.14 = (s32[5]{0:T(128)S(1)}, s32[5]{0:T(128)}, u32[]{:S(2)}) copy-start(s32[5]{0:T(128)} %param.23) | copy-start | bytes 64
  94.2 12.7 %all-to-all-start.1 = ((bf16[4,32,2176]{2,1,0:T(8,128)(2,1)}), bf16[4,32,2176]{2,1,0:T(8,128)(2,1)S(1)}, u32[]{:S(2)}, u32[]{:S(2)}) async-start(bf16[4,32,2176]{2,1,0:T(8,128)(2,1)} %bitcast.92), calls=%async_computation.1 | async-start | bytes 1114112 | tf_op jit(solution)/shard_map/all_to_all | solution.py:236
  97.7 42.1 %copy-start.8 = (s32[32]{0:T(128)S(1)}, s32[32]{0:T(128)}, u32[]{:S(2)}) copy-start(s32[32]{0:T(128)} %param.21) | copy-start | bytes 388
  106.9 29.3 %all-to-all-start.2 = ((bf16[8,4,128,128]{3,2,1,0:T(8,128)(2,1)}), bf16[8,4,128,128]{3,2,1,0:T(8,128)(2,1)S(1)}, u32[]{:S(2)}, u32[]{:S(2)}) async-start(bf16[8,4,128,128]{3,2,1,0:T(8,128)(2,1)} %get-tuple-element.28.rest_0_), calls=%async_computation.2 | async-start | bytes 2097152 | tf_op jit(solution)/shard_map/all_to_all | solution.py:236
  110.5 30.1 %copy-start.6 = (bf16[32,2048]{1,0:T(8,128)(2,1)S(1)}, bf16[32,2048]{1,0:T(8,128)(2,1)}, u32[]{:S(2)}) copy-start(bf16[32,2048]{1,0:T(8,128)(2,1)} %get-tuple-element.26) | copy-start | bytes 393220
  110.5 131.4 %all-gather.18.cloned.1.call-start = ((), (), s32[]{:S(2)}) async-start(), calls=%async_computation.12 | async-start | bytes 3604480 | tf_op jit(solution)/shard_map/all_gather | solution.py:265
  136.2 60.9 %copy-start = (bf16[8,4,128,128]{3,2,1,0:T(8,128)(2,1)}, bf16[8,4,128,128]{3,2,1,0:T(8,128)(2,1)S(1)}, u32[]{:S(2)}) copy-start(bf16[8,4,128,128]{3,2,1,0:T(8,128)(2,1)S(1)} %all-to-all-done.2.rest_0_) | copy-start | bytes 3145732
  136.2 29.6 %all-to-all-start.3 = ((bf16[8,4,128,128]{3,2,1,0:T(8,128)(2,1)}), bf16[8,4,128,128]{3,2,1,0:T(8,128)(2,1)S(1)}, u32[]{:S(2)}, u32[]{:S(2)}) async-start(bf16[8,4,128,128]{3,2,1,0:T(8,128)(2,1)} %get-tuple-element.29.rest_1_), calls=%async_computation.3 | async-start | bytes 2097152 | tf_op jit(solution)/shard_map/all_to_all | solution.py:236
  165.8 64.0 %copy-start.1 = (bf16[8,4,128,128]{3,2,1,0:T(8,128)(2,1)}, bf16[8,4,128,128]{3,2,1,0:T(8,128)(2,1)S(1)}, u32[]{:S(2)}) copy-start(bf16[8,4,128,128]{3,2,1,0:T(8,128)(2,1)S(1)} %all-to-all-done.3.rest_1_) | copy-start | bytes 3145732
  229.8 4.6 copy-start.13
  229.8 29.1 %all-to-all-start.4 = ((bf16[8,4,128,128]{3,2,1,0:T(8,128)(2,1)}), bf16[8,4,128,128]{3,2,1,0:T(8,128)(2,1)S(1)}, u32[]{:S(2)}, u32[]{:S(2)}) async-start(bf16[8,4,128,128]{3,2,1,0:T(8,128)(2,1)} %get-tuple-element.34.rest_2_), calls=%async_computation.4 | async-start | bytes 2097152 | tf_op jit(solution)/shard_map/all_to_all | solution.py:236
  234.4 4.2 copy-start.4
  241.9 3.2 copy-start.12
  258.9 24.1 %copy-start.2 = (bf16[8,4,128,128]{3,2,1,0:T(8,128)(2,1)}, bf16[8,4,128,128]{3,2,1,0:T(8,128)(2,1)S(1)}, u32[]{:S(2)}) copy-start(bf16[8,4,128,128]{3,2,1,0:T(8,128)(2,1)S(1)} %all-to-all-done.4.rest_2_) | copy-start | bytes 3145732
  258.9 23.9 %all-to-all-start.5 = ((bf16[8,32,2048]{2,1,0:T(8,128)(2,1)}), bf16[8,32,2048]{2,1,0:T(8,128)(2,1)S(1)}, u32[]{:S(2)}, u32[]{:S(2)}) async-start(bf16[8,32,2048]{2,1,0:T(8,128)(2,1)} %bitcast.82), calls=%async_computation.5 | async-start | bytes 2097152 | tf_op jit(solution)/shard_map/all_to_all | solution.py:236
  263.4 155.9 %collective-permute-start.1 = (bf16[2048,1000]{0,1:T(8,128)(2,1)}, bf16[2048,1000]{0,1:T(8,128)(2,1)}, u32[]{:S(2)}, u32[]{:S(2)}) collective-permute-start(bf16[2048,1000]{0,1:T(8,128)(2,1)} %param.39), channel_id=1, source_target_pairs={{0,1},{1,0},{2,3},{3,2},{4,5},{5,4},{6,7},{7,6},{8,9},{9,8},{10,11... | collective-permute-start | bytes 12288008 | tf_op jit(solution)/shard_map/ppermute | solution.py:21
  265.4 18.0 %copy-start.5 = (f32[32,2048]{1,0:T(8,128)S(1)}, f32[32,2048]{1,0:T(8,128)}, u32[]{:S(2)}) copy-start(f32[32,2048]{1,0:T(8,128)} %reshape.445) | copy-start | bytes 786436
  283.5 5.0 %collective-permute-start = (bf16[32,2048]{1,0:T(8,128)(2,1)S(1)}, bf16[32,2048]{1,0:T(8,128)(2,1)S(1)}, u32[]{:S(2)}, u32[]{:S(2)}) collective-permute-start(bf16[32,2048]{1,0:T(8,128)(2,1)S(1)} %multiply_convert_fusion.4), channel_id=1, source_target_pairs={{0,2},{1,3},{2,0},{3,1},{4,6},{5,7},{6,4},{7,5},{8,10},{9,11},{10,... | collective-permute-start | bytes 393224 | tf_op jit(solution)/shard_map/ppermute | solution.py:21
  284.2 140.3 %all-to-all-start.7 = ((bf16[8,32,512]{2,1,0:T(8,128)(2,1)}), bf16[8,32,512]{2,1,0:T(8,128)(2,1)S(1)}, u32[]{:S(2)}, u32[]{:S(2)}) async-start(bf16[8,32,512]{2,1,0:T(8,128)(2,1)} %bitcast.23), calls=%async_computation.7 | async-start | bytes 524288 | tf_op jit(solution)/shard_map/all_to_all | solution.py:236
  414.9 2.2 copy-start.11
  423.8 25.1 %copy-start.15 = (u32[32]{0:T(128)S(1)}, u32[32]{0:T(128)}, u32[]{:S(2)}) copy-start(u32[32]{0:T(128)} %constant.189) | copy-start | bytes 388
  423.9 27.1 %copy-start.9 = (s32[32]{0:T(128)S(1)}, s32[32]{0:T(128)}, u32[]{:S(2)}) copy-start(s32[32]{0:T(128)} %param.22) | copy-start | bytes 388
  424.6 10.7 %all-to-all-start.9 = ((f32[8,1,64]{2,1,0:T(1,128)}), f32[8,1,64]{2,1,0:T(1,128)S(1)}, u32[]{:S(2)}, u32[]{:S(2)}) async-start(f32[8,1,64]{2,1,0:T(1,128)} %max.26), calls=%async_computation.9 | async-start | bytes 8192 | tf_op jit(solution)/shard_map/all_to_all | solution.py:236
  435.2 10.2 %all-to-all-start.6 = ((f32[4,32,640]{2,1,0:T(8,128)}), f32[4,32,640]{2,1,0:T(8,128)S(1)}, u32[]{:S(2)}, u32[]{:S(2)}) async-start(f32[4,32,640]{2,1,0:T(8,128)} %pad_maximum_fusion.3), calls=%async_computation.6 | async-start | bytes 655360 | tf_op jit(solution)/shard_map/all_to_all | solution.py:236
  445.4 29.3 %all-to-all-start.8 = ((bf16[8,4,128,128]{3,2,1,0:T(8,128)(2,1)}), bf16[8,4,128,128]{3,2,1,0:T(8,128)(2,1)S(1)}, u32[]{:S(2)}, u32[]{:S(2)}) async-start(bf16[8,4,128,128]{3,2,1,0:T(8,128)(2,1)} %get-tuple-element.38.rest_3_), calls=%async_computation.8 | async-start | bytes 2097152 | tf_op jit(solution)/shard_map/all_to_all | solution.py:236
  474.7 1.0 copy-start.3
Sparse Core Ops, SparseCore 0:
  40.4 27.9 all-gather.13
  69.9 29.1 all-gather.15
  112.9 27.4 all-gather.17

commit v3 on v2

--- a/solution.py
+++ b/solution.py
@@ -78,8 +78,11 @@
     *rest,
 ):
     states_hbm = rest[:sends]
-    own_ref, part_ref, kv_ref = rest[sends : sends + 3]
-    qw_ref, fw_ref, iw_ref, ow_ref, states, qhi_ref, qlo_ref, mixed_ref, sems = rest[sends + 3 :]
+    own_ref, kv_ref = rest[sends : sends + 2]
+    parts = rest[sends + 2 : sends + 2 + classes]
+    (qw_ref, fw_ref, iw_ref, ow_ref, states, qhi_ref, qlo_ref, mixed_ref, part_ref, sems) = rest[
+        sends + 2 + classes :
+    ]
     weight_pairs = ((qw_hbm, qw_ref), (fw_hbm, fw_ref), (iw_hbm, iw_ref), (ow_hbm, ow_ref))
     loads = [
         pltpu.make_async_copy(there, here, sems.at[i]) for i, (there, here) in enumerate(weight_pairs)
@@ -152,10 +155,13 @@
     loads[3].wait()
     part_ref[:, 0:D] = jnp.dot(
         (mixed * ggain_ref[...]).astype(BF16), ow_ref[...], preferred_element_type=F32
-    ).astype(BF16)
+    )
     square_high = square.astype(BF16).astype(F32)
     lane = lax.broadcasted_iota(jnp.int32, (tokens, 128), 1)
-    part_ref[:, D : D + 128] = jnp.where(lane < 64, square_high, square - square_high).astype(BF16)
+    part_ref[:, D : D + 128] = jnp.where(lane < 64, square_high, square - square_high)
+    for e in range(classes):
+        first = pl.multiple_of((me_ref[1] ^ e) * rows, rows)
+        parts[e][...] = part_ref[pl.ds(first, rows), :].astype(BF16)
     own_ref[...] = emb_ref[pl.ds(pl.multiple_of(me_ref[1] * rows, rows), rows), :]
     both = jnp.concatenate([(key * after).astype(BF16), value.astype(BF16)], axis=0)
     shape = (2 * tokens, 2 * tokens)
@@ -179,17 +185,18 @@
         functools.partial(mixer_kernel, sends, owners, heads, classes, steps),
         out_shape=[
             jax.ShapeDtypeStruct((rows, D), BF16),
-            jax.ShapeDtypeStruct((tokens, D + 128), BF16),
             jax.ShapeDtypeStruct((2 * tokens, width), BF16),
-        ],
+        ]
+        + [jax.ShapeDtypeStruct((rows, D + 128), BF16)] * classes,
         in_specs=[pl.BlockSpec(memory_space=SMEM)] + [vmem] * 5 + [anywhere] * (4 + sends),
-        out_specs=[vmem] * 3,
+        out_specs=[vmem] * (2 + classes),
         scratch_shapes=[VMEM(w.shape, BF16) for w in weights]
         + [
             VMEM((sends,) + states[0].shape, BF16),
             VMEM((tokens, width), F32),
             VMEM((tokens, width), F32),
             VMEM((tokens, width), F32),
+            VMEM((tokens, D + 128), F32),
             pltpu.SemaphoreType.DMA((4 + sends,)),
         ],
         compiler_params=pltpu.CompilerParams(vmem_limit_bytes=56 << 20),
@@ -257,12 +264,13 @@
     rows = group * steps
     width = D // n_head
 
+    gate_full = lax.all_gather(gate_weight, "head", axis=0, tiled=True)
+    up_full = lax.all_gather(up_weight, "head", axis=0, tiled=True)
+    down_full = lax.all_gather(down_weight, "head", axis=0)
+
     packed = jnp.concatenate([token_ids.T, state_perm[None], token_count[None]], axis=0)
-    packed = lax.all_gather(packed, "req", axis=0).transpose(1, 0, 2).reshape(steps + 2, everyone)
+    packed = to_all(jnp.broadcast_to(packed[None], (n,) + packed.shape), "req").transpose(1, 0, 2).reshape(steps + 2, everyone)
     every = jnp.arange(everyone, dtype=jnp.int32)
-    gate_full = lax.all_gather(tied(gate_weight, packed), "head", axis=0, tiled=True)
-    up_full = lax.all_gather(tied(up_weight, packed), "head", axis=0, tiled=True)
-    down_full = lax.all_gather(tied(down_weight, packed), "head", axis=0)
     source = packed[steps] // requests
     rank = jnp.sum(
         ((source[None, :] == source[:, None]) & (every[None, :] < every[:, None])).astype(jnp.int32),
@@ -296,26 +304,22 @@
     old_order = jnp.take(old_order, jnp.arange(n) ^ r, axis=0).reshape(requests)
     pieces = sort_states(old_order, old_states, n)
     live = (jnp.arange(steps)[None, :] < ordered[steps + 1][:, None]).astype(F32)
-    own, parts, kv = mixer(
+    own, kv, *parts = mixer(
         jnp.stack([r, h]), embedded, live.reshape(tokens, 1), mixer_gain[None], forget_floor[None],
         group_gain[None], (query_weight, forget_weight, input_weight, output_weight), pieces,
         steps, n_head,
     )
-    arrived = [
-        to_all(tied(piece, embed_part), "req") for piece in pieces[: (sends + 1) // 2]
-    ]
-
-    total = jnp.sum(to_all(parts.reshape(n_head, rows, D + 128), "head").astype(F32), axis=0)
+    arrived = [to_all(tied(pieces[0], embed_part), "req")]
+
+    total = parts[0].astype(F32)
+    for e in range(1, n_head):
+        total = total + swap(parts[e], "head", n_head, e).astype(F32)
     square = total[:, D : D + 1] + total[:, D + 127 : D + 128]
     after_mixer = own.astype(F32) + total[:, :D] * lax.rsqrt(square / D + epsilon)
-    after_mixer = tied(after_mixer.astype(BF16), *arrived)
-    half = D // 2
-    everything = jnp.concatenate(
-        [lax.all_gather(after_mixer[:, at : at + half], "req", axis=0) for at in (0, half)], axis=-1
-    ).reshape(n * rows, D)
-    arrived_kv = to_all(tied(kv, everything).reshape(n, -1, width), "req")
-    if sends >= 4:
-        arrived += [to_all(tied(pieces[2], everything), "req")]
+    after_mixer = tied(after_mixer.astype(BF16), gate_full, up_full, down_full, *arrived)
+    everything = lax.all_gather(after_mixer, "req", axis=0, tiled=True)
+    arrived += [to_all(tied(piece, after_mixer), "req") for piece in pieces[1:2]]
+    arrived_kv = to_all(tied(kv, *arrived).reshape(n, -1, width), "req")
     stream = everything.astype(F32)
     scale = lax.rsqrt(jnp.mean(stream * stream, axis=1, keepdims=True) + epsilon)
     feed_in = (stream * scale * feed_gain).astype(BF16)
@@ -338,7 +342,7 @@
         [jnp.dot(activated, down_full[b], preferred_element_type=F32).astype(BF16) for b in range(n_head)],
         axis=1,
     )
-    down = tied(down, *arrived)
+    down = tied(down, arrived_kv, *arrived)
     hidden = kept + jnp.sum(to_all(down.reshape(n, rows, D), "req").astype(F32), axis=0)
     mean_square = jnp.mean(hidden * hidden, axis=1, keepdims=True)
 
@@ -370,21 +374,14 @@
     final = (hidden * lax.rsqrt(mean_square + epsilon) * token_gain).astype(BF16)
 
     final = jnp.stack([final, swap(final, "head", n_head, 2)])
-    quarter = D // 4
-    full = jnp.concatenate(
-        [
-            lax.all_gather(final[:, :, at : at + quarter], "req", axis=0)
-            for at in range(0, D, quarter)
-        ],
-        axis=-1,
-    ).reshape(n * 2 * rows, D)
-    if sends >= 4:
-        arrived += [to_all(tied(pieces[3], full), "req")]
+    for piece in pieces[2:]:
+        arrived += [to_all(tied(piece, final, *arrived[2:]), "req")]
+    full = lax.all_gather(final, "req", axis=0, tiled=True).reshape(n * 2 * rows, D)
     best = jnp.maximum(
         jnp.max(jnp.dot(full, vocab_weight, preferred_element_type=F32), axis=1),
         jnp.max(jnp.dot(full, vocab_other, preferred_element_type=F32), axis=1),
     ).reshape(n, 2 * rows)
-    got = jnp.max(to_all(best, "req"), axis=0)
+    got = jnp.max(to_all(tied(best, *arrived), "req"), axis=0)
     got = lax.all_gather(got, "head", axis=0).reshape(n_head, 2, rows)
     crossed = jnp.stack([got[i ^ 2, 1] for i in range(n_head)])
     best = jnp.maximum(got[:, 0], crossed).reshape(requests, steps)
@@ -395,10 +392,15 @@
     greatest = jnp.max(jnp.where(live, best, -1e30), axis=1)
 
     blocks = hidden.reshape(rows, n_head, width).transpose(1, 0, 2)
-    tail = jnp.broadcast_to(mean_square[None], (n_head, rows, 128))
-    whole = to_all(jnp.concatenate([blocks, tail], axis=2), "head")
-    whole = whole.reshape(requests, steps, width + 128)
-    whole = jnp.take(whole, (place % n_head) * group + place // n_head, axis=0, mode="clip")
+    tail = jnp.broadcast_to(mean_square, (rows, 128))
+    whole = []
+    for e in range(n_head):
+        block = lax.dynamic_index_in_dim(blocks, h ^ e, 0, keepdims=False)
+        block = jnp.concatenate([block, tail], axis=1)
+        whole.append(block if e == 0 else swap(block, "head", n_head, e))
+    whole = jnp.stack(whole).reshape(requests, steps, width + 128)
+    index = ((place % n_head) ^ h) * group + place // n_head
+    whole = jnp.take(whole, index, axis=0, mode="clip")
     last = jnp.arange(steps)[None, :] == (token_count - 1)[:, None]
     last_norm = jnp.sqrt(jnp.sum(jnp.where(last, whole[:, :, width], 0.0), axis=1) + epsilon)
 

time: 490 us -> 330 us (0.67)
  blocking collectives: 238 us -> 14.8 us
  waiting for transfers between devices: 129 us -> 182 us
    all_gather x7 -> x0, blocking collectives: 221 us -> none  [the longest x4 126 us: on_device(): lax.all_gather(final[:, :, at:at + quarter], 'req', axis=0)]
    all_gather x3 -> x5, waiting for transfers between devices: 0.02 us -> 52.6 us  [the longest x1 26.9 us: on_device(): lax.all_gather(final, 'req', axis=0, tiled=True).reshape(n * 2 * rows, D)]
    ppermute x2 -> x8, waiting for transfers between devices: 0.9 us -> 14.5 us  [swap(): return lax.ppermute(x, axis, [(i, i ^ offset) for i in range(size)])]
    all_to_all x10 -> x9, waiting for transfers between devices: 126 us -> 113 us  [to_all(): return lax.all_to_all(x, axis, split_axis=0, concat_axis=0, tiled=True)]
    all_to_all x10 -> x9, starting transfers between devices: 39.4 us -> 40.2 us  [to_all(): return lax.all_to_all(x, axis, split_axis=0, concat_axis=0, tiled=True)]
  transfers between devices with their start and end apart: 15 -> 22, of which waited for: 10 -> 13; matrix products, arithmetic and copies ran while one was open for 9% -> 15% of each run, Pallas kernels for 3% -> 6%
where the time goes in v3:
time: 330 us; the launch traced here: 329 us
  waiting for transfers between devices  182 us (55%)
  starting transfers between devices  45.1 us (14%)
  matrix products  21.7 us (7%)
  Pallas kernels  19.1 us (6%)
  other arithmetic  15.4 us (5%)
  local copies, waits for them, and re-layouts  15.2 us (5%)
  between operations  15 us (5%)
  blocking collectives  14.8 us (4%)
    all_to_all x9, waiting for transfers between devices, to_all(): return lax.all_to_all(x, axis, split_axis=0, concat_axis=0, tiled=True)  113 us
    all_to_all x9, starting transfers between devices, to_all(): return lax.all_to_all(x, axis, split_axis=0, concat_axis=0, tiled=True)  40.2 us
    all_gather x1, waiting for transfers between devices, on_device(): lax.all_gather(final, 'req', axis=0, tiled=True).reshape(n * 2 * rows, D)  26.9 us
    all_gather x1, waiting for transfers between devices, on_device(): down_full = lax.all_gather(down_weight, 'head', axis=0)  21.1 us
    ppermute x8, waiting for transfers between devices, swap(): return lax.ppermute(x, axis, [(i, i ^ offset) for i in range(size)])  14.5 us
    all_gather x1, blocking collectives, on_device(): lax.all_gather(jnp.concatenate([embed_part, gains_high, gains_low, extra]...  7.99 us
    pallas_call x1, Pallas kernels, mixer(): pl.pallas_call(functools.partial(mixer_kernel, sends, owners, heads, clas...  7.97 us
    unnamed x1, blocking collectives  6.85 us
  transfers between devices with their start and end apart: 22, of which 13 were waited for; matrix products, arithmetic and copies ran while one was open for 15% of the time, Pallas kernels for 6%

profile of v3, /device:TPU:0, one launch (start us, length us, event | category | flops | bytes accessed | tf_op | source)
XLA Modules:
  0.0 328.6 jit_solution(8955505027112915659)
XLA Ops:
  9.3 7.3 %all-to-all-start = ((s32[8,1,192]{2,1,0:T(1,128)}), s32[8,1,192]{2,1,0:T(1,128)S(1)}, u32[]{:S(2)}, u32[]{:S(2)}) async-start(s32[8,1,192]{2,1,0:T(1,128)} %reshape.479), calls=%async_computation | async-start | bytes 16384 | tf_op jit(solution)/shard_map/all_to_all | solution.py:243
  18.0 5.1 %all-to-all-done = s32[8,1,192]{2,1,0:T(1,128)S(1)} async-done(((s32[8,1,192]{2,1,0:T(1,128)}), s32[8,1,192]{2,1,0:T(1,128)S(1)}, u32[]{:S(2)}, u32[]{:S(2)}) %all-to-all-start) | async-done | bytes 6176 | tf_op jit(solution)/shard_map/all_to_all | solution.py:243
  25.6 6.7 %gather_fusion = bf16[1024,512]{1,0:T(8,128)(2,1)S(1)} fusion(bf16[4000,512]{1,0:T(8,128)(2,1)} %param.25, s32[1024]{0:T(1024)S(1)} %broadcast_clamp_fusion), kind=kCustom, calls=%fused_computation | custom fusion | bytes 2101248 | tf_op jit(solution)/shard_map/jit(_take)/gather | solution.py:289
  33.6 3.6 %all-to-all-start.1 = ((bf16[8,128,512]{2,1,0:T(8,128)(2,1)}), bf16[8,128,512]{2,1,0:T(8,128)(2,1)S(1)}, u32[]{:S(2)}, u32[]{:S(2)}) async-start(bf16[8,128,512]{2,1,0:T(8,128)(2,1)} %broadcast_select_fusion), calls=%async_computation.1 | async-start | bytes 2097152 | tf_op jit(solution)/shard_map/all_to_all | solution.py:243
  40.7 4.4 %shard_map.219 = (bf16[8,4,128,128]{3,2,1,0:T(8,128)(2,1)}, bf16[8,4,128,128]{3,2,1,0:T(8,128)(2,1)}, bf16[8,4,128,128]{3,2,1,0:T(8,128)(2,1)}, bf16[8,4,128,128]{3,2,1,0:T(8,128)(2,1)}) custom-call(s32[32]{0:T(128)} %select_n.204.order_ref, bf16[32,4,128,128]{3,2,1,0:T(8,128)(2,1)} %old_ref.1), custom_call_target="tpu_custom_call" | custom-call | tf_op jit(solution)/shard_map/pallas_call | solution.py:57
  45.1 16.8 %all-to-all-done.1 = bf16[8,128,512]{2,1,0:T(8,128)(2,1)S(1)} async-done(((bf16[8,128,512]{2,1,0:T(8,128)(2,1)}), bf16[8,128,512]{2,1,0:T(8,128)(2,1)S(1)}, u32[]{:S(2)}, u32[]{:S(2)}) %all-to-all-start.1) | async-done | bytes 1048608 | tf_op jit(solution)/shard_map/all_to_all | solution.py:243
  62.0 3.6 %all-to-all-start.2 = ((bf16[8,4,128,128]{3,2,1,0:T(8,128)(2,1)}), bf16[8,4,128,128]{3,2,1,0:T(8,128)(2,1)S(1)}, u32[]{:S(2)}, u32[]{:S(2)}) async-start(bf16[8,4,128,128]{3,2,1,0:T(8,128)(2,1)} %get-tuple-element.32.rest_0_), calls=%async_computation.2 | async-start | bytes 2097152 | tf_op jit(solution)/shard_map/all_to_all | solution.py:243
  65.7 8.0 %all_gather.27.emb_ref = bf16[144,2048]{1,0:T(8,128)(2,1)} all-gather(bf16[144,512]{1,0:T(8,128)(2,1)S(1)} %maximum_maximum_fusion), channel_id=1, replica_groups=mesh['req'=8,'head'=4] {'head'}, dimensions={1}, use_global_device_ids=true | all-gather | bytes 737280 | tf_op jit(solution)/shard_map/all_gather | solution.py:297
  73.7 8.0 %shard_map.220 = (bf16[32,2048]{1,0:T(8,128)(2,1)}, bf16[256,512]{1,0:T(8,128)(2,1)}, bf16[32,2176]{1,0:T(8,128)(2,1)}, bf16[32,2176]{1,0:T(8,128)(2,1)}, bf16[3...) custom-call(s32[2]{0:T(128)} %pad_add_fusion.1.me_ref, bf16[144,2048]{1,0:T(8,128)(2,1)} %all_gather.27.emb_ref, ...), custom_call_target="tpu_custom_call" | custom-call | tf_op jit(solution)/shard_map/pallas_call | solution.py:184
  83.6 5.2 %collective-permute-done.1 = bf16[32,2176]{1,0:T(8,128)(2,1)S(1)} collective-permute-done((bf16[32,2176]{1,0:T(8,128)(2,1)}, bf16[32,2176]{1,0:T(8,128)(2,1)S(1)}, u32[]{:S(2)}, u32[]{:S(2)}) %collective-permute-start.1) | collective-permute-done | bytes 139296 | tf_op jit(solution)/shard_map/ppermute | solution.py:21
  91.4 1.7 fusion.20
  93.7 5.9 %all-to-all-start.3 = ((bf16[8,4,128,128]{3,2,1,0:T(8,128)(2,1)}), bf16[8,4,128,128]{3,2,1,0:T(8,128)(2,1)S(1)}, u32[]{:S(2)}, u32[]{:S(2)}) async-start(bf16[8,4,128,128]{3,2,1,0:T(8,128)(2,1)} %get-tuple-element.35.rest_1_), calls=%async_computation.3 | async-start | bytes 2097152 | tf_op jit(solution)/shard_map/all_to_all | solution.py:243
  99.7 34.0 %all-to-all-done.3.rest_1_ = bf16[8,4,128,128]{3,2,1,0:T(8,128)(2,1)S(1)} async-done(((bf16[8,4,128,128]{3,2,1,0:T(8,128)(2,1)}), bf16[8,4,128,128]{3,2,1,0:T(8,128)(2,1)S(1)}, u32[]{:S(2)}, u32[]{:S(2)}) %all-to-all-start.3) | async-done | bytes 1048608 | tf_op jit(solution)/shard_map/all_to_all | solution.py:243
  133.7 3.4 %all-to-all-start.4 = ((bf16[8,32,512]{2,1,0:T(8,128)(2,1)}), bf16[8,32,512]{2,1,0:T(8,128)(2,1)S(1)}, u32[]{:S(2)}, u32[]{:S(2)}) async-start(bf16[8,32,512]{2,1,0:T(8,128)(2,1)} %bitcast.16), calls=%async_computation.4 | async-start | bytes 524288 | tf_op jit(solution)/shard_map/all_to_all | solution.py:243
  137.1 4.6 %all-gather.12.cloned.1.call-done = bf16[256,2048]{1,0:T(8,128)(2,1)} async-done(((bf16[32,2048]{1,0:T(8,128)(2,1)}), bf16[256,2048]{1,0:T(8,128)(2,1)}) %all-gather.12.cloned.1.call-update) | async-done | bytes 1048592 | tf_op jit(solution)/shard_map/all_gather | solution.py:320
  143.3 4.1 %fusion.17 = f32[256,704]{0,1:T(8,128)} fusion(bf16[2048,704]{0,1:T(8,128)(2,1)} %all-gather.8.cloned.1.call-done, bf16[256,2048]{1,0:T(8,128)(2,1)} %all-gather.12.cloned.1.call-done, f32[2048]{0:T(1024)S(1)} %copy-done.11, f32[256]{0:T(256)S(1)} %add_rsqrt_fusion), kind=kOutput, calls=%fused_computation.34 | convolution fusion | flops 740294656 | bytes 4662272 | tf_op jit(solution)/shard_map/dot_general | solution.py:326
  147.4 3.2 convolution_convert_fusion
  150.7 21.1 %all-gather.16.cloned.1.call-done = bf16[2816,512]{1,0:T(8,128)(2,1)} async-done(((bf16[704,512]{1,0:T(8,128)(2,1)}), bf16[2816,512]{1,0:T(8,128)(2,1)}) %all-gather.16.cloned.1.call-update) | async-done | bytes 2883600 | tf_op jit(solution)/shard_map/all_gather | solution.py:269
  171.8 1.7 convolution_convert_fusion.1
  176.9 5.5 %all-to-all-start.5 = ((bf16[8,32,2048]{2,1,0:T(8,128)(2,1)}), bf16[8,32,2048]{2,1,0:T(8,128)(2,1)S(1)}, u32[]{:S(2)}, u32[]{:S(2)}) async-start(bf16[8,32,2048]{2,1,0:T(8,128)(2,1)} %bitcast.17), calls=%async_computation.5 | async-start | bytes 2097152 | tf_op jit(solution)/shard_map/all_to_all | solution.py:243
  183.8 24.7 %all-to-all-done.5 = bf16[8,32,2048]{2,1,0:T(8,128)(2,1)S(1)} async-done(((bf16[8,32,2048]{2,1,0:T(8,128)(2,1)}), bf16[8,32,2048]{2,1,0:T(8,128)(2,1)S(1)}, u32[]{:S(2)}, u32[]{:S(2)}) %all-to-all-start.5) | async-done | bytes 1048608 | tf_op jit(solution)/shard_map/all_to_all | solution.py:243
  209.9 4.4 %collective-permute-done.6 = bf16[32,2048]{1,0:T(8,128)(2,1)S(1)} collective-permute-done((bf16[32,2048]{1,0:T(8,128)(2,1)S(1)}, bf16[32,2048]{1,0:T(8,128)(2,1)S(1)}, u32[]{:S(2)}, u32[]{:S(2)}) %collective-permute-start.6) | collective-permute-done | bytes 131104 | tf_op jit(solution)/shard_map/ppermute | solution.py:21
  215.1 4.1 %all-to-all-start.6 = ((bf16[8,4,128,128]{3,2,1,0:T(8,128)(2,1)}), bf16[8,4,128,128]{3,2,1,0:T(8,128)(2,1)S(1)}, u32[]{:S(2)}, u32[]{:S(2)}) async-start(bf16[8,4,128,128]{3,2,1,0:T(8,128)(2,1)} %get-tuple-element.38.rest_2_), calls=%async_computation.6 | async-start | bytes 2097152 | tf_op jit(solution)/shard_map/all_to_all | solution.py:243
  221.4 32.7 %all-to-all-done.6.rest_2_ = bf16[8,4,128,128]{3,2,1,0:T(8,128)(2,1)S(1)} async-done(((bf16[8,4,128,128]{3,2,1,0:T(8,128)(2,1)}), bf16[8,4,128,128]{3,2,1,0:T(8,128)(2,1)S(1)}, u32[]{:S(2)}, u32[]{:S(2)}) %all-to-all-start.6) | async-done | bytes 1048608 | tf_op jit(solution)/shard_map/all_to_all | solution.py:243
  254.1 3.6 %all-to-all-start.7 = ((bf16[8,4,128,128]{3,2,1,0:T(8,128)(2,1)}), bf16[8,4,128,128]{3,2,1,0:T(8,128)(2,1)S(1)}, u32[]{:S(2)}, u32[]{:S(2)}) async-start(bf16[8,4,128,128]{3,2,1,0:T(8,128)(2,1)} %get-tuple-element.39.rest_3_), calls=%async_computation.7 | async-start | bytes 2097152 | tf_op jit(solution)/shard_map/all_to_all | solution.py:243
  260.9 2.6 collective-permute-done.4
  265.3 26.9 %all-gather.14.cloned.1.call-done = bf16[16,32,2048]{2,1,0:T(8,128)(2,1)} async-done(((bf16[2,32,2048]{2,1,0:T(8,128)(2,1)}), bf16[16,32,2048]{2,1,0:T(8,128)(2,1)}) %all-gather.14.cloned.1.call-update) | async-done | bytes 2097168 | tf_op jit(solution)/shard_map/all_gather | solution.py:379
  292.2 5.3 %convolution_reduce_fusion.1 = f32[512]{0:T(512)S(1)} fusion(bf16[512,2048]{1,0:T(8,128)(2,1)} %bitcast.101, bf16[2048,1000]{0,1:T(8,128)(2,1)} %param.39), kind=kOutput, calls=%fused_computation.11 | convolution fusion | flops 2097663488 | bytes 6195200 | tf_op jit(solution)/shard_map/dot_general | solution.py:381
  297.5 4.5 %convolution_reduce_fusion = f32[512]{0:T(512)S(1)} fusion(bf16[512,2048]{1,0:T(8,128)(2,1)S(1)} %bitcast.102, bf16[2048,1000]{0,1:T(8,128)(2,1)} %collective-permute-done.7), kind=kOutput, calls=%fused_computation.10 | convolution fusion | flops 2097663488 | bytes 6195200 | tf_op jit(solution)/shard_map/dot_general | solution.py:382
  302.7 3.3 all-to-all-start.8
  307.2 6.7 %shard_map.221 = bf16[32,4,128,128]{3,2,1,0:T(8,128)(2,1)} custom-call(s32[32]{0:T(128)} %select_reduce_fusion.1.slot_ref, f32[32,8,512]{2,1,0:T(8,128)} %convert.3.kv_ref, bf16[8,4,128,128]{3,2,1,0:T(8,128)(2,1)} %copy-done, bf16[8,4,128,128]{3,2,1,0:T(8,128)(2,1)} %copy-done.1, bf16[8,4,128,128]{3,2,1,0:T(8,128)(2,1)} %copy-done.2, ...), custom_call_target="tpu_custom_call" | custom-call | tf_op jit(solution)/shard_map/pallas_call | solution.py:233
  314.2 6.9 %all-reduce = f32[256]{0:T(256)S(1)} all-reduce(f32[256]{0:T(256)S(1)} %dynamic-update-slice), channel_id=3, replica_groups=mesh['req'=8,'head'=4] {'head'}, use_global_device_ids=true, to_apply=%add | all-reduce | flops 256 | bytes 2048
  (164 shorter events, 34.4 us)
Async XLA Ops:
  7.2 86.0 %all-gather.10.cloned.1.call-start = ((), (), s32[]{:S(2)}) async-start(), calls=%async_computation.10 | async-start | bytes 3604480 | tf_op jit(solution)/shard_map/all_gather | solution.py:268
  9.3 13.8 %all-to-all-start = ((s32[8,1,192]{2,1,0:T(1,128)}), s32[8,1,192]{2,1,0:T(1,128)S(1)}, u32[]{:S(2)}, u32[]{:S(2)}) async-start(s32[8,1,192]{2,1,0:T(1,128)} %reshape.479), calls=%async_computation | async-start | bytes 16384 | tf_op jit(solution)/shard_map/all_to_all | solution.py:243
  16.6 76.6 %all-gather.8.cloned.1.call-start = ((), (), s32[]{:S(2)}) async-start(), calls=%async_computation.9 | async-start | bytes 3604480 | tf_op jit(solution)/shard_map/all_gather | solution.py:267
  32.3 5.4 %copy-start.12 = (s32[5]{0:T(128)S(1)}, s32[5]{0:T(128)}, u32[]{:S(2)}) copy-start(s32[5]{0:T(128)} %param.23) | copy-start | bytes 64
  32.4 5.5 %copy-start.5 = (f32[4,512]{1,0:T(4,128)S(1)}, f32[4,512]{1,0:T(4,128)}, u32[]{:S(2)}) copy-start(f32[4,512]{1,0:T(4,128)} %param.38) | copy-start | bytes 24580
  32.4 5.5 %copy-start.8 = (f32[512]{0:T(512)S(1)}, f32[512]{0:T(512)}, u32[]{:S(2)}) copy-start(f32[512]{0:T(512)} %param.37) | copy-start | bytes 6148
  32.4 5.7 %copy-start.7 = (s32[32]{0:T(128)S(1)}, s32[32]{0:T(128)}, u32[]{:S(2)}) copy-start(s32[32]{0:T(128)} %param.21) | copy-start | bytes 388
  33.6 28.3 %all-to-all-start.1 = ((bf16[8,128,512]{2,1,0:T(8,128)(2,1)}), bf16[8,128,512]{2,1,0:T(8,128)(2,1)S(1)}, u32[]{:S(2)}, u32[]{:S(2)}) async-start(bf16[8,128,512]{2,1,0:T(8,128)(2,1)} %broadcast_select_fusion), calls=%async_computation.1 | async-start | bytes 2097152 | tf_op jit(solution)/shard_map/all_to_all | solution.py:243
  62.0 31.1 %all-to-all-start.2 = ((bf16[8,4,128,128]{3,2,1,0:T(8,128)(2,1)}), bf16[8,4,128,128]{3,2,1,0:T(8,128)(2,1)S(1)}, u32[]{:S(2)}, u32[]{:S(2)}) async-start(bf16[8,4,128,128]{3,2,1,0:T(8,128)(2,1)} %get-tuple-element.32.rest_0_), calls=%async_computation.2 | async-start | bytes 2097152 | tf_op jit(solution)/shard_map/all_to_all | solution.py:243
  65.6 76.2 %all-gather.12.cloned.1.call-start = ((), (), s32[]{:S(2)}) async-start(), calls=%async_computation.11 | async-start | bytes 1179648 | tf_op jit(solution)/shard_map/all_gather | solution.py:320
  81.7 1.9 collective-permute-start
  82.1 6.7 %collective-permute-start.1 = (bf16[32,2176]{1,0:T(8,128)(2,1)}, bf16[32,2176]{1,0:T(8,128)(2,1)S(1)}, u32[]{:S(2)}, u32[]{:S(2)}) collective-permute-start(bf16[32,2176]{1,0:T(8,128)(2,1)} %get-tuple-element.30), channel_id=1, source_target_pairs={{0,2},{1,3},{2,0},{3,1},{4,6},{5,7},{6,4},{7,5},{8,10},{9,11},{10,... | collective-permute-start | bytes 417800 | tf_op jit(solution)/shard_map/ppermute | solution.py:21
  83.0 7.3 %collective-permute-start.2 = (bf16[32,2176]{1,0:T(8,128)(2,1)}, bf16[32,2176]{1,0:T(8,128)(2,1)S(1)}, u32[]{:S(2)}, u32[]{:S(2)}) collective-permute-start(bf16[32,2176]{1,0:T(8,128)(2,1)} %get-tuple-element.31), channel_id=1, source_target_pairs={{0,3},{1,2},{2,1},{3,0},{4,7},{5,6},{6,5},{7,4},{8,11},{9,10},{10,... | collective-permute-start | bytes 417800 | tf_op jit(solution)/shard_map/ppermute | solution.py:21
  93.1 50.2 %copy-start = (bf16[8,4,128,128]{3,2,1,0:T(8,128)(2,1)}, bf16[8,4,128,128]{3,2,1,0:T(8,128)(2,1)S(1)}, u32[]{:S(2)}) copy-start(bf16[8,4,128,128]{3,2,1,0:T(8,128)(2,1)S(1)} %all-to-all-done.2.rest_0_) | copy-start | bytes 3145732
  93.2 50.2 %copy-start.11 = (f32[2048]{0:T(1024)S(1)}, f32[2048]{0:T(1024)}, u32[]{:S(2)}) copy-start(f32[2048]{0:T(1024)} %param.33) | copy-start | bytes 24580
  93.2 78.6 %all-gather.16.cloned.1.call-start = ((), (), s32[]{:S(2)}) async-start(), calls=%async_computation.13 | async-start | bytes 3604480 | tf_op jit(solution)/shard_map/all_gather | solution.py:269
  93.7 40.0 %all-to-all-start.3 = ((bf16[8,4,128,128]{3,2,1,0:T(8,128)(2,1)}), bf16[8,4,128,128]{3,2,1,0:T(8,128)(2,1)S(1)}, u32[]{:S(2)}, u32[]{:S(2)}) async-start(bf16[8,4,128,128]{3,2,1,0:T(8,128)(2,1)} %get-tuple-element.35.rest_1_), calls=%async_computation.3 | async-start | bytes 2097152 | tf_op jit(solution)/shard_map/all_to_all | solution.py:243
  133.7 13.7 %copy-start.1 = (bf16[8,4,128,128]{3,2,1,0:T(8,128)(2,1)}, bf16[8,4,128,128]{3,2,1,0:T(8,128)(2,1)S(1)}, u32[]{:S(2)}) copy-start(bf16[8,4,128,128]{3,2,1,0:T(8,128)(2,1)S(1)} %all-to-all-done.3.rest_1_) | copy-start | bytes 3145732
  133.7 43.1 %all-to-all-start.4 = ((bf16[8,32,512]{2,1,0:T(8,128)(2,1)}), bf16[8,32,512]{2,1,0:T(8,128)(2,1)S(1)}, u32[]{:S(2)}, u32[]{:S(2)}) async-start(bf16[8,32,512]{2,1,0:T(8,128)(2,1)} %bitcast.16), calls=%async_computation.4 | async-start | bytes 524288 | tf_op jit(solution)/shard_map/all_to_all | solution.py:243
  176.9 31.7 %all-to-all-start.5 = ((bf16[8,32,2048]{2,1,0:T(8,128)(2,1)}), bf16[8,32,2048]{2,1,0:T(8,128)(2,1)S(1)}, u32[]{:S(2)}, u32[]{:S(2)}) async-start(bf16[8,32,2048]{2,1,0:T(8,128)(2,1)} %bitcast.17), calls=%async_computation.5 | async-start | bytes 2097152 | tf_op jit(solution)/shard_map/all_to_all | solution.py:243
  182.4 109.8 %all-gather.14.cloned.1.call-start = ((), (), s32[]{:S(2)}) async-start(), calls=%async_computation.12 | async-start | bytes 2359296 | tf_op jit(solution)/shard_map/all_gather | solution.py:379
  209.1 10.1 %copy-start.13 = (u32[32]{0:T(128)S(1)}, u32[32]{0:T(128)}, u32[]{:S(2)}) copy-start(u32[32]{0:T(128)} %constant.202) | copy-start | bytes 388
  209.1 12.0 %copy-start.6 = (s32[32]{0:T(128)S(1)}, s32[32]{0:T(128)}, u32[]{:S(2)}) copy-start(s32[32]{0:T(128)} %param.22) | copy-start | bytes 388
  209.3 5.0 %collective-permute-start.6 = (bf16[32,2048]{1,0:T(8,128)(2,1)S(1)}, bf16[32,2048]{1,0:T(8,128)(2,1)S(1)}, u32[]{:S(2)}, u32[]{:S(2)}) collective-permute-start(bf16[32,2048]{1,0:T(8,128)(2,1)S(1)} %multiply_convert_fusion), channel_id=1, source_target_pairs={{0,2},{1,3},{2,0},{3,1},{4,6},{5,7},{6,4},{7,5},{8,10},{9,11},{10,... | collective-permute-start | bytes 393224 | tf_op jit(solution)/shard_map/ppermute | solution.py:21
  215.0 82.5 %collective-permute-start.7 = (bf16[2048,1000]{0,1:T(8,128)(2,1)}, bf16[2048,1000]{0,1:T(8,128)(2,1)}, u32[]{:S(2)}, u32[]{:S(2)}) collective-permute-start(bf16[2048,1000]{0,1:T(8,128)(2,1)} %param.39), channel_id=1, source_target_pairs={{0,1},{1,0},{2,3},{3,2},{4,5},{5,4},{6,7},{7,6},{8,9},{9,8},{10,11... | collective-permute-start | bytes 12288008 | tf_op jit(solution)/shard_map/ppermute | solution.py:21
  215.1 38.9 %all-to-all-start.6 = ((bf16[8,4,128,128]{3,2,1,0:T(8,128)(2,1)}), bf16[8,4,128,128]{3,2,1,0:T(8,128)(2,1)S(1)}, u32[]{:S(2)}, u32[]{:S(2)}) async-start(bf16[8,4,128,128]{3,2,1,0:T(8,128)(2,1)} %get-tuple-element.38.rest_2_), calls=%async_computation.6 | async-start | bytes 2097152 | tf_op jit(solution)/shard_map/all_to_all | solution.py:243
  254.1 6.8 %copy-start.2 = (bf16[8,4,128,128]{3,2,1,0:T(8,128)(2,1)}, bf16[8,4,128,128]{3,2,1,0:T(8,128)(2,1)S(1)}, u32[]{:S(2)}) copy-start(bf16[8,4,128,128]{3,2,1,0:T(8,128)(2,1)S(1)} %all-to-all-done.6.rest_2_) | copy-start | bytes 3145732
  254.1 48.6 %all-to-all-start.7 = ((bf16[8,4,128,128]{3,2,1,0:T(8,128)(2,1)}), bf16[8,4,128,128]{3,2,1,0:T(8,128)(2,1)S(1)}, u32[]{:S(2)}, u32[]{:S(2)}) async-start(bf16[8,4,128,128]{3,2,1,0:T(8,128)(2,1)} %get-tuple-element.39.rest_3_), calls=%async_computation.7 | async-start | bytes 2097152 | tf_op jit(solution)/shard_map/all_to_all | solution.py:243
  258.0 2.8 collective-permute-start.3
  258.1 5.3 %collective-permute-start.4 = (f32[32,640]{1,0:T(8,128)S(1)}, f32[32,640]{1,0:T(8,128)S(1)}, u32[]{:S(2)}, u32[]{:S(2)}) collective-permute-start(f32[32,640]{1,0:T(8,128)S(1)} %get-tuple-element.59), channel_id=1, source_target_pairs={{0,2},{1,3},{2,0},{3,1},{4,6},{5,7},{6,4},{7,5},{8,10},{9,11},{10,... | collective-permute-start | bytes 245768 | tf_op jit(solution)/shard_map/ppermute | solution.py:21
  258.7 5.5 %collective-permute-start.5 = (f32[32,640]{1,0:T(8,128)S(1)}, f32[32,640]{1,0:T(8,128)S(1)}, u32[]{:S(2)}, u32[]{:S(2)}) collective-permute-start(f32[32,640]{1,0:T(8,128)S(1)} %get-tuple-element.60), channel_id=1, source_target_pairs={{0,3},{1,2},{2,1},{3,0},{4,7},{5,6},{6,5},{7,4},{8,11},{9,10},{10,... | collective-permute-start | bytes 245768 | tf_op jit(solution)/shard_map/ppermute | solution.py:21
  302.7 11.3 %all-to-all-start.8 = ((f32[8,1,64]{2,1,0:T(1,128)}), f32[8,1,64]{2,1,0:T(1,128)S(1)}, u32[]{:S(2)}, u32[]{:S(2)}) async-start(f32[8,1,64]{2,1,0:T(1,128)} %bitcast.32), calls=%async_computation.8 | async-start | bytes 8192 | tf_op jit(solution)/shard_map/all_to_all | solution.py:243
  (4 other events, 17.1 us)
Sparse Core Ops, SparseCore 0:
  9.6 29.8 all-gather.9
  41.0 27.0 all-gather.7
  93.3 48.4 all-gather.11
  143.2 28.5 all-gather.15
  215.2 77.0 all-gather.13

commit v4 on v3

--- a/solution.py
+++ b/solution.py
@@ -27,68 +27,98 @@
 
 
 def sort_kernel(sends, order_ref, old_ref, *rest):
-    outs, held, in_sems, out_sems = rest[:sends], rest[sends], rest[sends + 1], rest[sends + 2]
-    owners = held.shape[1]
-
-    def load(rank, owner):
+    outs, (held, in_sems, out_sems) = rest[:-3], rest[-3:]
+    owners = held.shape[0]
+    spans, first = [], 0
+    for out in outs:
+        spans.append((first, out.shape[1]))
+        first += out.shape[1]
+
+    def load(owner, rank):
         at = owner * sends + rank
         return pltpu.make_async_copy(
-            old_ref.at[order_ref[at]], held.at[rank, owner], in_sems.at[rank, owner]
+            old_ref.at[order_ref[at]], held.at[owner, rank], in_sems.at[owner, rank]
         )
 
-    def store(rank):
-        return pltpu.make_async_copy(held.at[rank], outs[rank], out_sems.at[rank])
-
-    for rank in range(sends):
+    def store(part):
+        first, count = spans[part]
+        return pltpu.make_async_copy(
+            held.at[:, pl.ds(first, count)], outs[part], out_sems.at[part]
+        )
+
+    for first, count in spans:
         for owner in range(owners):
-            load(rank, owner).start()
-    for rank in range(sends):
+            for rank in range(first, first + count):
+                load(owner, rank).start()
+    for part, (first, count) in enumerate(spans):
         for owner in range(owners):
-            load(rank, owner).wait()
-        store(rank).start()
-    for rank in range(sends):
-        store(rank).wait()
-
-
-def sort_states(order, old_states, owners):
-    requests = old_states.shape[0]
-    sends = requests // owners
-    piece = (owners,) + old_states.shape[1:]
+            for rank in range(first, first + count):
+                load(owner, rank).wait()
+        store(part).start()
+    for part in range(len(outs)):
+        store(part).wait()
+
+
+def sort_states(order, old_states, owners, counts):
+    sends = sum(counts)
+    state = old_states.shape[1:]
     return pl.pallas_call(
         functools.partial(sort_kernel, sends),
-        out_shape=[jax.ShapeDtypeStruct(piece, old_states.dtype)] * sends,
+        out_shape=[
+            jax.ShapeDtypeStruct((owners, count) + state, old_states.dtype) for count in counts
+        ],
         in_specs=[pl.BlockSpec(memory_space=SMEM), pl.BlockSpec(memory_space=pl.ANY)],
-        out_specs=[pl.BlockSpec(memory_space=pl.ANY)] * sends,
+        out_specs=[pl.BlockSpec(memory_space=pl.ANY)] * len(counts),
         scratch_shapes=[
-            VMEM((sends,) + piece, old_states.dtype),
-            pltpu.SemaphoreType.DMA((sends, owners)),
-            pltpu.SemaphoreType.DMA((sends,)),
+            VMEM((owners, sends) + state, old_states.dtype),
+            pltpu.SemaphoreType.DMA((owners, sends)),
+            pltpu.SemaphoreType.DMA((len(counts),)),
         ],
         compiler_params=pltpu.CompilerParams(vmem_limit_bytes=56 << 20),
     )(order, old_states)
 
 
+def hand_on(x_ref, token_ref, out_ref):
+    pass
+
+
+def after(x, *others):
+    corners = [other.reshape((-1,) + other.shape[-2:])[0, :8, :128] for other in others]
+    anywhere = pl.BlockSpec(memory_space=pl.ANY)
+    return pl.pallas_call(
+        hand_on,
+        out_shape=jax.ShapeDtypeStruct(x.shape, x.dtype),
+        in_specs=[anywhere, anywhere],
+        out_specs=anywhere,
+        input_output_aliases={0: 0},
+    )(x, sum(corners[1:], corners[0]))
+
+
 def roll(x, by):
     return pltpu.roll(x, by % x.shape[0], 0)
 
 
 def mixer_kernel(
-    sends, owners, heads, classes, steps,
+    counts, owners, heads, classes, steps,
     me_ref, emb_ref, live_ref, gain_ref, floor_ref, ggain_ref, qw_hbm, fw_hbm, iw_hbm, ow_hbm,
     *rest,
 ):
-    states_hbm = rest[:sends]
-    own_ref, kv_ref = rest[sends : sends + 2]
-    parts = rest[sends + 2 : sends + 2 + classes]
+    pieces, sends = len(counts), sum(counts)
+    states_hbm = rest[:pieces]
+    own_ref, kv_ref = rest[pieces : pieces + 2]
+    parts = rest[pieces + 2 : pieces + 2 + classes]
     (qw_ref, fw_ref, iw_ref, ow_ref, states, qhi_ref, qlo_ref, mixed_ref, part_ref, sems) = rest[
-        sends + 2 + classes :
+        pieces + 2 + classes :
     ]
     weight_pairs = ((qw_hbm, qw_ref), (fw_hbm, fw_ref), (iw_hbm, iw_ref), (ow_hbm, ow_ref))
     loads = [
         pltpu.make_async_copy(there, here, sems.at[i]) for i, (there, here) in enumerate(weight_pairs)
     ]
     state_loads = [
-        pltpu.make_async_copy(states_hbm[i], states.at[i], sems.at[4 + i]) for i in range(sends)
+        pltpu.make_async_copy(
+            states_hbm[i], states.at[:, pl.ds(sum(counts[:i]), counts[i])], sems.at[4 + i]
+        )
+        for i in range(pieces)
     ]
     for load in loads[:3] + state_loads + loads[3:]:
         load.start()
@@ -146,7 +176,7 @@
             got = []
             for request in (2 * tile, 2 * tile + 1):
                 place = (request % group) * classes + request // group
-                old = states[place % sends, here ^ (place // sends), head]
+                old = states[here ^ (place // sends), place % sends, head]
                 product = jnp.dot(left, old, preferred_element_type=F32)
                 got.append(product[0:8] + product[8:16])
             mixed_ref[at, cols] += jnp.where(upper, got[0], got[1])
@@ -177,40 +207,44 @@
 
 def mixer(me, emb, live, gain, floor, ggain, weights, states, steps, classes):
     tokens = live.shape[0]
-    sends, (owners, heads) = len(states), states[0].shape[:2]
+    counts = tuple(piece.shape[1] for piece in states)
+    owners, _, heads = states[0].shape[:3]
     width = floor.shape[1]
     rows = tokens // classes
     vmem, anywhere = pl.BlockSpec(memory_space=VMEM), pl.BlockSpec(memory_space=pl.ANY)
     return pl.pallas_call(
-        functools.partial(mixer_kernel, sends, owners, heads, classes, steps),
+        functools.partial(mixer_kernel, counts, owners, heads, classes, steps),
         out_shape=[
             jax.ShapeDtypeStruct((rows, D), BF16),
             jax.ShapeDtypeStruct((2 * tokens, width), BF16),
         ]
         + [jax.ShapeDtypeStruct((rows, D + 128), BF16)] * classes,
-        in_specs=[pl.BlockSpec(memory_space=SMEM)] + [vmem] * 5 + [anywhere] * (4 + sends),
+        in_specs=[pl.BlockSpec(memory_space=SMEM)] + [vmem] * 5 + [anywhere] * (4 + len(states)),
         out_specs=[vmem] * (2 + classes),
         scratch_shapes=[VMEM(w.shape, BF16) for w in weights]
         + [
-            VMEM((sends,) + states[0].shape, BF16),
+            VMEM((owners, sum(counts)) + states[0].shape[2:], BF16),
             VMEM((tokens, width), F32),
             VMEM((tokens, width), F32),
             VMEM((tokens, width), F32),
             VMEM((tokens, D + 128), F32),
-            pltpu.SemaphoreType.DMA((4 + sends,)),
+            pltpu.SemaphoreType.DMA((4 + len(states),)),
         ],
         compiler_params=pltpu.CompilerParams(vmem_limit_bytes=56 << 20),
     )(me, emb, live, gain, floor, ggain, *weights, *states)
 
 
-def update_kernel(sends, owners, heads, steps, slot_ref, kv_ref, *rest):
-    states, out_ref = rest[:sends], rest[sends]
+def update_kernel(steps, slot_ref, kv_ref, *rest):
+    states, out_ref = rest[:-1], rest[-1]
+    owners, _, heads = states[0].shape[:3]
+    ranks = [(piece, i) for piece in states for i in range(piece.shape[1])]
+    sends = len(ranks)
     diagonal = lax.broadcasted_iota(jnp.int32, (HEAD_DIM, HEAD_DIM), 0) == lax.broadcasted_iota(
         jnp.int32, (HEAD_DIM, HEAD_DIM), 1
     )
     first = lax.broadcasted_iota(jnp.int32, (2 * steps, HEAD_DIM), 0) < steps
     for k in range(owners):
-        for rank in range(sends):
+        for rank, (piece, i) in enumerate(ranks):
             place = k * sends + rank
             slot = slot_ref[place]
             for head in range(heads):
@@ -223,28 +257,27 @@
                 fresh = lax.dot_general(
                     key, value, (((0,), (0,)), ((), ())), preferred_element_type=F32
                 )
-                old = jnp.dot(keep, states[rank][k, head], preferred_element_type=F32)
+                old = jnp.dot(keep, piece[k, i, head], preferred_element_type=F32)
                 out_ref[slot, head] = (old + fresh).astype(BF16)
 
 
 def update_states(slots, kv, states, steps):
-    sends, (owners, heads) = len(states), states[0].shape[:2]
     vmem = pl.BlockSpec(memory_space=VMEM)
     return pl.pallas_call(
-        functools.partial(update_kernel, sends, owners, heads, steps),
-        out_shape=jax.ShapeDtypeStruct((owners * sends,) + states[0].shape[1:], BF16),
-        in_specs=[pl.BlockSpec(memory_space=SMEM)] + [vmem] * (1 + sends),
+        functools.partial(update_kernel, steps),
+        out_shape=jax.ShapeDtypeStruct((slots.shape[0],) + states[0].shape[2:], BF16),
+        in_specs=[pl.BlockSpec(memory_space=SMEM)] + [vmem] * (1 + len(states)),
         out_specs=vmem,
         compiler_params=pltpu.CompilerParams(vmem_limit_bytes=56 << 20),
     )(slots, kv, *states)
 
 
+def dot_rows(a, b):
+    return lax.dot_general(a, b, (((1,), (1,)), ((), ())), preferred_element_type=F32)
+
+
 def to_all(x, axis):
     return lax.all_to_all(x, axis, split_axis=0, concat_axis=0, tiled=True)
-
-
-def tied(x, *others):
-    return lax.optimization_barrier((x,) + others)[0]
 
 
 def on_device(
@@ -264,8 +297,8 @@
     rows = group * steps
     width = D // n_head
 
-    gate_full = lax.all_gather(gate_weight, "head", axis=0, tiled=True)
-    up_full = lax.all_gather(up_weight, "head", axis=0, tiled=True)
+    gate_full = lax.all_gather(gate_weight.T, "head", axis=1, tiled=True)
+    up_full = lax.all_gather(up_weight.T, "head", axis=1, tiled=True)
     down_full = lax.all_gather(down_weight, "head", axis=0)
 
     packed = jnp.concatenate([token_ids.T, state_perm[None], token_count[None]], axis=0)
@@ -282,14 +315,41 @@
     ordered = jnp.dot(packed.astype(F32), chosen, precision=lax.Precision.HIGHEST)
     ordered = (ordered + 0.5).astype(jnp.int32)
 
-    ids = ordered[:steps].T.reshape(n * tokens)
+    ids = ordered[:steps].T.reshape(n, tokens)
     table = embedding.shape[0]
-    local_ids = ids - r * table
-    inside = (local_ids >= 0) & (local_ids < table)
-    picked = jnp.take(embedding, jnp.clip(local_ids, 0, table - 1), axis=0, mode="clip")
-    picked = jnp.where(inside[:, None], picked, jnp.zeros((), BF16)).reshape(n, tokens, width)
-    embed_part = jnp.sum(to_all(picked, "req").astype(F32), axis=0).astype(BF16)
-    vocab_other = swap(tied(vocab_weight, embed_part), "head", n_head, 1)
+    room = tokens // 2
+    holder = lax.div(ids, jnp.int32(table))
+    held = holder == r
+    earlier = jnp.triu(jnp.ones((tokens, tokens), BF16), 1)
+    turn = jnp.dot(held.astype(BF16), earlier, preferred_element_type=F32).astype(jnp.int32)
+    local_ids = jnp.where(held, ids - r * table, 0)
+    seat = held[:, None] & (turn[:, None] == jnp.arange(room, dtype=jnp.int32)[None, :, None])
+    wanted = jnp.sum(jnp.where(seat, local_ids[:, None], 0), axis=2).reshape(n * room)
+    got = to_all(jnp.take(embedding, wanted, axis=0, mode="clip").reshape(n, room, width), "req")
+    own_holder = lax.dynamic_index_in_dim(holder, r, 0, keepdims=False)
+    order = jnp.arange(tokens, dtype=jnp.int32)
+    own_turn = jnp.sum(
+        ((own_holder[None, :] == own_holder[:, None]) & (order[None, :] < order[:, None])).astype(
+            jnp.int32
+        ),
+        axis=1,
+    )
+    seat = jnp.where(own_turn < room, own_holder * room + own_turn, -1)
+    pick = (seat[:, None] == jnp.arange(n * room, dtype=jnp.int32)[None, :]).astype(BF16)
+    embed_part = jnp.dot(
+        pick, got.reshape(n * room, width), preferred_element_type=F32
+    ).astype(BF16)
+    owners = jnp.arange(n, dtype=jnp.int32)
+    load = jnp.sum((holder[:, None] == owners[None, :, None]).astype(jnp.int32), axis=2)
+
+    def with_rest(part):
+        rows = jnp.take(embedding, local_ids.reshape(n * tokens), axis=0, mode="clip")
+        rest = (held & (turn >= room)).reshape(n * tokens, 1)
+        rows = jnp.where(rest, rows, jnp.zeros((), BF16)).reshape(n, tokens, width)
+        return (part.astype(F32) + jnp.sum(to_all(rows, "req").astype(F32), axis=0)).astype(BF16)
+
+    embed_part = lax.cond(jnp.max(load) > room, with_rest, lambda part: part, embed_part)
+    vocab_other = swap(vocab_weight.T, "head", n_head, 1)
 
     gains = jnp.concatenate([final_gain[None], tenant_gain], axis=0)
     gains_high, gains_low = bf16_parts(gains)
@@ -302,29 +362,29 @@
     ordered = lax.dynamic_slice_in_dim(ordered, r * requests, requests, 1)
     old_order = (ordered[steps] - r * requests).reshape(n_head, group).T.reshape(n, sends)
     old_order = jnp.take(old_order, jnp.arange(n) ^ r, axis=0).reshape(requests)
-    pieces = sort_states(old_order, old_states, n)
+    counts = (1, 2, 1) if sends == 4 else (sends,)
+    pieces = sort_states(old_order, old_states, n, counts)
     live = (jnp.arange(steps)[None, :] < ordered[steps + 1][:, None]).astype(F32)
     own, kv, *parts = mixer(
         jnp.stack([r, h]), embedded, live.reshape(tokens, 1), mixer_gain[None], forget_floor[None],
         group_gain[None], (query_weight, forget_weight, input_weight, output_weight), pieces,
         steps, n_head,
     )
-    arrived = [to_all(tied(pieces[0], embed_part), "req")]
+    arrived = [to_all(pieces[0], "req")]
 
     total = parts[0].astype(F32)
     for e in range(1, n_head):
         total = total + swap(parts[e], "head", n_head, e).astype(F32)
     square = total[:, D : D + 1] + total[:, D + 127 : D + 128]
     after_mixer = own.astype(F32) + total[:, :D] * lax.rsqrt(square / D + epsilon)
-    after_mixer = tied(after_mixer.astype(BF16), gate_full, up_full, down_full, *arrived)
+    after_mixer = after(after_mixer.astype(BF16), gate_full, up_full, down_full)
     everything = lax.all_gather(after_mixer, "req", axis=0, tiled=True)
-    arrived += [to_all(tied(piece, after_mixer), "req") for piece in pieces[1:2]]
-    arrived_kv = to_all(tied(kv, *arrived).reshape(n, -1, width), "req")
+    arrived += [to_all(piece, "req") for piece in pieces[1:2]]
     stream = everything.astype(F32)
     scale = lax.rsqrt(jnp.mean(stream * stream, axis=1, keepdims=True) + epsilon)
     feed_in = (stream * scale * feed_gain).astype(BF16)
-    gate = jnp.dot(feed_in, gate_full, preferred_element_type=F32)
-    up = jnp.dot(feed_in, up_full, preferred_element_type=F32)
+    gate = dot_rows(feed_in, gate_full)
+    up = dot_rows(feed_in, up_full)
     activated = (jax.nn.silu(gate) * up).astype(BF16)
 
     row = jnp.arange(n * rows, dtype=jnp.int32)
@@ -342,7 +402,7 @@
         [jnp.dot(activated, down_full[b], preferred_element_type=F32).astype(BF16) for b in range(n_head)],
         axis=1,
     )
-    down = tied(down, arrived_kv, *arrived)
+    down = after(down, *arrived)
     hidden = kept + jnp.sum(to_all(down.reshape(n, rows, D), "req").astype(F32), axis=0)
     mean_square = jnp.mean(hidden * hidden, axis=1, keepdims=True)
 
@@ -374,14 +434,14 @@
     final = (hidden * lax.rsqrt(mean_square + epsilon) * token_gain).astype(BF16)
 
     final = jnp.stack([final, swap(final, "head", n_head, 2)])
-    for piece in pieces[2:]:
-        arrived += [to_all(tied(piece, final, *arrived[2:]), "req")]
+    arrived += [to_all(after(piece, final), "req") for piece in pieces[2:]]
+    arrived_kv = to_all(after(kv, final).reshape(n, -1, width), "req")
     full = lax.all_gather(final, "req", axis=0, tiled=True).reshape(n * 2 * rows, D)
     best = jnp.maximum(
-        jnp.max(jnp.dot(full, vocab_weight, preferred_element_type=F32), axis=1),
-        jnp.max(jnp.dot(full, vocab_other, preferred_element_type=F32), axis=1),
+        jnp.max(dot_rows(full, vocab_weight.T), axis=1),
+        jnp.max(dot_rows(full, vocab_other), axis=1),
     ).reshape(n, 2 * rows)
-    got = jnp.max(to_all(tied(best, *arrived), "req"), axis=0)
+    got = jnp.max(to_all(best, "req"), axis=0)
     got = lax.all_gather(got, "head", axis=0).reshape(n_head, 2, rows)
     crossed = jnp.stack([got[i ^ 2, 1] for i in range(n_head)])
     best = jnp.maximum(got[:, 0], crossed).reshape(requests, steps)

time: 330 us -> 311 us (0.942)
  waiting for transfers between devices: 182 us -> 163 us
  starting transfers between devices: 45.1 us -> 38.5 us
  blocking collectives: 14.8 us -> 18.6 us
    all_to_all x9 -> x8, waiting for transfers between devices: 113 us -> 86.3 us  [to_all(): return lax.all_to_all(x, axis, split_axis=0, concat_axis=0, tiled=True)]
    all_gather x1, waiting for transfers between devices: 21.1 us -> 0.01 us  [on_device(): down_full = lax.all_gather(down_weight, 'head', axis=0)]
    all_gather x1, waiting for transfers between devices: 4.64 us -> 25 us  [on_device(): everything = lax.all_gather(after_mixer, 'req', axis=0, tiled=True)]
    all_gather x1, waiting for transfers between devices: 26.9 us -> 35.3 us  [on_device(): lax.all_gather(final, 'req', axis=0, tiled=True).reshape(n * 2 * rows, D)]
    all_to_all x9 -> x8, starting transfers between devices: 40.2 us -> 32.9 us  [to_all(): return lax.all_to_all(x, axis, split_axis=0, concat_axis=0, tiled=True)]
    all_gather x1, blocking collectives: 7.99 us -> 11.8 us  [on_device(): lax.all_gather(jnp.concatenate([embed_part, gains_high, gains_low, extra]...]
    dot_general x3 -> x5, matrix products: 13.8 us -> 14.2 us  [the longest x3 13.8 us: dot_rows(): lax.dot_general(a, b, (((1,), (1,)), ((), ())), preferred_element_type=F32)]
    pallas_call x2 -> x6, Pallas kernels: 14.7 us -> 14.8 us  [the longest x1 8.04 us: mixer(): pl.pallas_call(functools.partial(mixer_kernel, counts, owners, heads, cla...]
  transfers between devices with their start and end apart: 22 -> 21, of which waited for: 13 -> 13; matrix products, arithmetic and copies ran while one was open for 15% -> 12% of each run, Pallas kernels for 6% -> 6%
where the time goes in v4:
time: 311 us; the launch traced here: 310 us
  waiting for transfers between devices  163 us (52%)
  starting transfers between devices  38.5 us (12%)
  matrix products  23.1 us (7%)
  Pallas kernels  19.4 us (6%)
  blocking collectives  18.6 us (6%)
  other arithmetic  16.6 us (5%)
  between operations  15.7 us (5%)
  local copies, waits for them, and re-layouts  14.3 us (5%)
    all_to_all x8, waiting for transfers between devices, to_all(): return lax.all_to_all(x, axis, split_axis=0, concat_axis=0, tiled=True)  86.3 us
    all_gather x1, waiting for transfers between devices, on_device(): lax.all_gather(final, 'req', axis=0, tiled=True).reshape(n * 2 * rows, D)  35.3 us
    all_to_all x8, starting transfers between devices, to_all(): return lax.all_to_all(x, axis, split_axis=0, concat_axis=0, tiled=True)  32.9 us
    all_gather x1, waiting for transfers between devices, on_device(): everything = lax.all_gather(after_mixer, 'req', axis=0, tiled=True)  25 us
    ppermute x8, waiting for transfers between devices, swap(): return lax.ppermute(x, axis, [(i, i ^ offset) for i in range(size)])  14.7 us
    dot_general x3, matrix products, dot_rows(): lax.dot_general(a, b, (((1,), (1,)), ((), ())), preferred_element_type=F32)  13.8 us
    all_gather x1, blocking collectives, on_device(): lax.all_gather(jnp.concatenate([embed_part, gains_high, gains_low, extra]...  11.8 us
    pallas_call x1, Pallas kernels, mixer(): pl.pallas_call(functools.partial(mixer_kernel, counts, owners, heads, cla...  8.04 us
  transfers between devices with their start and end apart: 21, of which 13 were waited for; matrix products, arithmetic and copies ran while one was open for 12% of the time, Pallas kernels for 6%

profile of v4, /device:TPU:0, one launch (start us, length us, event | category | flops | bytes accessed | tf_op | source)
XLA Modules:
  0.0 309.7 jit_solution(13197867457578030978)
XLA Ops:
  10.1 7.3 %all-to-all-start.1 = ((s32[8,1,192]{2,1,0:T(1,128)}), s32[8,1,192]{2,1,0:T(1,128)S(1)}, u32[]{:S(2)}, u32[]{:S(2)}) async-start(s32[8,1,192]{2,1,0:T(1,128)} %reshape.540), calls=%async_computation.1 | async-start | bytes 16384 | tf_op jit(solution)/shard_map/all_to_all | solution.py:280
  18.7 5.1 %all-to-all-done.1 = s32[8,1,192]{2,1,0:T(1,128)S(1)} async-done(((s32[8,1,192]{2,1,0:T(1,128)}), s32[8,1,192]{2,1,0:T(1,128)S(1)}, u32[]{:S(2)}, u32[]{:S(2)}) %all-to-all-start.1) | async-done | bytes 6176 | tf_op jit(solution)/shard_map/all_to_all | solution.py:280
  26.5 5.4 %gather_fusion.1 = bf16[512,512]{1,0:T(8,128)(2,1)} fusion(bf16[4000,512]{1,0:T(8,128)(2,1)} %param.27, s32[1024]{0:T(1024)S(1)} %pad_clamp_fusion.2), kind=kCustom, calls=%fused_computation.1 | custom fusion | bytes 1050624 | tf_op jit(solution)/shard_map/jit(_take)/gather | solution.py:328
  31.9 3.5 %all-to-all-start.2 = ((bf16[8,64,512]{2,1,0:T(8,128)(2,1)}), bf16[8,64,512]{2,1,0:T(8,128)(2,1)S(1)}, u32[]{:S(2)}, u32[]{:S(2)}) async-start(bf16[8,64,512]{2,1,0:T(8,128)(2,1)} %bitcast.10), calls=%async_computation.2 | async-start | bytes 1048576 | tf_op jit(solution)/shard_map/all_to_all | solution.py:280
  38.4 4.6 %shard_map.219 = (bf16[8,1,4,128,128]{4,3,2,1,0:T(8,128)(2,1)}, bf16[8,2,4,128,128]{4,3,2,1,0:T(8,128)(2,1)}, bf16[8,1,4,128,128]{4,3,2,1,0:T(8,128)(2,1)}) custom-call(s32[32]{0:T(128)} %select_n.239.order_ref, bf16[32,4,128,128]{3,2,1,0:T(8,128)(2,1)} %old_ref.1), custom_call_target="tpu_custom_call" | custom-call | tf_op jit(solution)/shard_map/pallas_call | solution.py:65
  43.2 5.4 %all-to-all-done.2 = bf16[8,64,512]{2,1,0:T(8,128)(2,1)S(1)} async-done(((bf16[8,64,512]{2,1,0:T(8,128)(2,1)}), bf16[8,64,512]{2,1,0:T(8,128)(2,1)S(1)}, u32[]{:S(2)}, u32[]{:S(2)}) %all-to-all-start.2) | async-done | bytes 524320 | tf_op jit(solution)/shard_map/all_to_all | solution.py:280
  48.9 3.8 %all-to-all-start.3 = ((bf16[8,1,4,128,128]{4,3,2,1,0:T(8,128)(2,1)}), bf16[8,1,4,128,128]{4,3,2,1,0:T(8,128)(2,1)S(1)}, u32[]{:S(2)}, u32[]{:S(2)}) async-start(bf16[8,1,4,128,128]{4,3,2,1,0:T(8,128)(2,1)} %get-tuple-element.41.rest_0_), calls=%async_computation.3 | async-start | bytes 2097152 | tf_op jit(solution)/shard_map/all_to_all | solution.py:280
  54.3 23.6 %all-to-all-done.3.rest_0_ = bf16[8,1,4,128,128]{4,3,2,1,0:T(8,128)(2,1)S(1)} async-done(((bf16[8,1,4,128,128]{4,3,2,1,0:T(8,128)(2,1)}), bf16[8,1,4,128,128]{4,3,2,1,0:T(8,128)(2,1)S(1)}, u32[]{:S(2)}, u32[]{:S(2)}) %all-to-all-start.3) | async-done | bytes 1048608 | tf_op jit(solution)/shard_map/all_to_all | solution.py:280
  77.9 3.6 %all-to-all-start.4 = ((bf16[8,2,4,128,128]{4,3,2,1,0:T(8,128)(2,1)}), bf16[8,2,4,128,128]{4,3,2,1,0:T(8,128)(2,1)S(1)}, u32[]{:S(2)}, u32[]{:S(2)}) async-start(bf16[8,2,4,128,128]{4,3,2,1,0:T(8,128)(2,1)} %get-tuple-element.42.rest_1_), calls=%async_computation.4 | async-start | bytes 4194304 | tf_op jit(solution)/shard_map/all_to_all | solution.py:280
  81.7 11.8 %all_gather.27.emb_ref = bf16[144,2048]{1,0:T(8,128)(2,1)} all-gather(bf16[144,512]{1,0:T(8,128)(2,1)S(1)} %maximum_maximum_fusion), channel_id=1, replica_groups=mesh['req'=8,'head'=4] {'head'}, dimensions={1}, use_global_device_ids=true | all-gather | bytes 737280 | tf_op jit(solution)/shard_map/all_gather | solution.py:357
  93.5 8.0 %shard_map.220 = (bf16[32,2048]{1,0:T(8,128)(2,1)}, bf16[256,512]{1,0:T(8,128)(2,1)}, bf16[32,2176]{1,0:T(8,128)(2,1)}, bf16[32,2176]{1,0:T(8,128)(2,1)}, bf16[3...) custom-call(s32[2]{0:T(128)} %pad_add_fusion.1.me_ref, bf16[144,2048]{1,0:T(8,128)(2,1)} %all_gather.27.emb_ref, ...), custom_call_target="tpu_custom_call" | custom-call | tf_op jit(solution)/shard_map/pallas_call | solution.py:215
  103.5 5.2 %collective-permute-done.1 = bf16[32,2176]{1,0:T(8,128)(2,1)S(1)} collective-permute-done((bf16[32,2176]{1,0:T(8,128)(2,1)}, bf16[32,2176]{1,0:T(8,128)(2,1)S(1)}, u32[]{:S(2)}, u32[]{:S(2)}) %collective-permute-start.1) | collective-permute-done | bytes 139296 | tf_op jit(solution)/shard_map/ppermute | solution.py:21
  111.3 1.7 fusion.20.x_ref
  114.3 17.6 %all-to-all-done.4.rest_1_ = bf16[8,2,4,128,128]{4,3,2,1,0:T(8,128)(2,1)S(1)} async-done(((bf16[8,2,4,128,128]{4,3,2,1,0:T(8,128)(2,1)}), bf16[8,2,4,128,128]{4,3,2,1,0:T(8,128)(2,1)S(1)}, u32[]{:S(2)}, u32[]{:S(2)}) %all-to-all-start.4) | async-done | bytes 2097184 | tf_op jit(solution)/shard_map/all_to_all | solution.py:280
  132.5 25.0 %all-gather.12.cloned.1.call-done = bf16[256,2048]{1,0:T(8,128)(2,1)} async-done(((bf16[32,2048]{1,0:T(8,128)(2,1)}), bf16[256,2048]{1,0:T(8,128)(2,1)}) %all-gather.12.cloned.1.call-update) | async-done | bytes 1048592 | tf_op jit(solution)/shard_map/all_gather | solution.py:381
  159.1 4.1 %fusion.17 = f32[256,704]{0,1:T(8,128)} fusion(bf16[704,2048]{1,0:T(8,128)(2,1)} %all-gather.8.cloned.1.call-done, bf16[256,2048]{1,0:T(8,128)(2,1)} %all-gather.12.cloned.1.call-done, f32[2048]{0:T(1024)S(1)} %copy-done.10, f32[256]{0:T(256)S(1)} %add_rsqrt_fusion), kind=kOutput, calls=%fused_computation.41 | convolution fusion | flops 740294656 | bytes 4662272 | tf_op jit(solution)/shard_map/dot_general | solution.py:276
  163.2 4.0 %convolution_convert_fusion = bf16[256,704]{0,1:T(8,128)(2,1)} fusion(bf16[704,2048]{1,0:T(8,128)(2,1)} %all-gather.10.cloned.1.call-done, f32[256,704]{0,1:T(8,128)} %fusion.17, bf16[256,2048]{1,0:T(8,128)(2,1)S(1)} %copy-done.3, f32[2048]{0:T(1024)S(1)} %copy-done.10, f32[256]{0:T(256)S(1)} %add_rsqrt_fusion, s32[256]{0:T(256)S(1)} %fusion.47), kind=kOutput, calls=%fused_computation.20 | convolution fusion | flops 833896448 | bytes 5023744 | tf_op jit(solution)/shard_map/dot_general | solution.py:398
  167.2 1.8 convolution_convert_fusion.2
  172.5 3.6 %all-to-all-start.5 = ((bf16[8,32,2048]{2,1,0:T(8,128)(2,1)}), bf16[8,32,2048]{2,1,0:T(8,128)(2,1)S(1)}, u32[]{:S(2)}, u32[]{:S(2)}) async-start(bf16[8,32,2048]{2,1,0:T(8,128)(2,1)} %bitcast.99), calls=%async_computation.5 | async-start | bytes 2097152 | tf_op jit(solution)/shard_map/all_to_all | solution.py:280
  177.4 23.8 %all-to-all-done.5 = bf16[8,32,2048]{2,1,0:T(8,128)(2,1)S(1)} async-done(((bf16[8,32,2048]{2,1,0:T(8,128)(2,1)}), bf16[8,32,2048]{2,1,0:T(8,128)(2,1)S(1)}, u32[]{:S(2)}, u32[]{:S(2)}) %all-to-all-start.5) | async-done | bytes 1048608 | tf_op jit(solution)/shard_map/all_to_all | solution.py:280
  203.5 3.5 %collective-permute-done.6 = bf16[32,2048]{1,0:T(8,128)(2,1)S(1)} collective-permute-done((bf16[32,2048]{1,0:T(8,128)(2,1)S(1)}, bf16[32,2048]{1,0:T(8,128)(2,1)S(1)}, u32[]{:S(2)}, u32[]{:S(2)}) %collective-permute-start.6) | collective-permute-done | bytes 131104 | tf_op jit(solution)/shard_map/ppermute | solution.py:21
  208.4 3.8 %all-to-all-start.6 = ((bf16[8,32,512]{2,1,0:T(8,128)(2,1)}), bf16[8,32,512]{2,1,0:T(8,128)(2,1)S(1)}, u32[]{:S(2)}, u32[]{:S(2)}) async-start(bf16[8,32,512]{2,1,0:T(8,128)(2,1)} %bitcast.105), calls=%async_computation.6 | async-start | bytes 524288 | tf_op jit(solution)/shard_map/all_to_all | solution.py:280
  214.5 10.6 %all-to-all-done.6 = bf16[8,32,512]{2,1,0:T(8,128)(2,1)S(1)} async-done(((bf16[8,32,512]{2,1,0:T(8,128)(2,1)}), bf16[8,32,512]{2,1,0:T(8,128)(2,1)S(1)}, u32[]{:S(2)}, u32[]{:S(2)}) %all-to-all-start.6) | async-done | bytes 262176 | tf_op jit(solution)/shard_map/all_to_all | solution.py:280
  225.1 4.0 %all-to-all-start.7 = ((bf16[8,1,4,128,128]{4,3,2,1,0:T(8,128)(2,1)}), bf16[8,1,4,128,128]{4,3,2,1,0:T(8,128)(2,1)S(1)}, u32[]{:S(2)}, u32[]{:S(2)}) async-start(bf16[8,1,4,128,128]{4,3,2,1,0:T(8,128)(2,1)} %shard_map.224), calls=%async_computation.7 | async-start | bytes 2097152 | tf_op jit(solution)/shard_map/all_to_all | solution.py:280
  229.6 1.7 collective-permute-start.4
  231.5 3.2 %collective-permute-done.4 = f32[32,640]{1,0:T(8,128)S(1)} collective-permute-done((f32[32,640]{1,0:T(8,128)S(1)}, f32[32,640]{1,0:T(8,128)S(1)}, u32[]{:S(2)}, u32[]{:S(2)}) %collective-permute-start.4) | collective-permute-done | bytes 81952 | tf_op jit(solution)/shard_map/ppermute | solution.py:21
  237.1 35.3 %all-gather.14.cloned.1.call-done = bf16[16,32,2048]{2,1,0:T(8,128)(2,1)} async-done(((bf16[2,32,2048]{2,1,0:T(8,128)(2,1)}), bf16[16,32,2048]{2,1,0:T(8,128)(2,1)}) %all-gather.14.cloned.1.call-update) | async-done | bytes 2097168 | tf_op jit(solution)/shard_map/all_gather | solution.py:439
  272.4 5.3 %convolution_reduce_fusion.1 = f32[512]{0:T(512)S(1)} fusion(bf16[512,2048]{1,0:T(8,128)(2,1)} %bitcast.136, bf16[2048,1000]{0,1:T(8,128)(2,1)} %param.41), kind=kOutput, calls=%fused_computation.17 | convolution fusion | flops 2097663488 | bytes 6195200 | tf_op jit(solution)/shard_map/dot_general | solution.py:276
  277.7 4.5 %convolution_reduce_fusion = f32[512]{0:T(512)S(1)} fusion(bf16[512,2048]{1,0:T(8,128)(2,1)S(1)} %bitcast.137, bf16[1000,2048]{1,0:T(8,128)(2,1)} %collective-permute-done.7), kind=kOutput, calls=%fused_computation.16 | convolution fusion | flops 2097663488 | bytes 6195200 | tf_op jit(solution)/shard_map/dot_general | solution.py:276
  282.9 3.3 %all-to-all-start.8 = ((f32[8,1,64]{2,1,0:T(1,128)}), f32[8,1,64]{2,1,0:T(1,128)S(1)}, u32[]{:S(2)}, u32[]{:S(2)}) async-start(f32[8,1,64]{2,1,0:T(1,128)} %max.22), calls=%async_computation.8 | async-start | bytes 8192 | tf_op jit(solution)/shard_map/all_to_all | solution.py:280
  288.3 6.7 %shard_map.225 = bf16[32,4,128,128]{3,2,1,0:T(8,128)(2,1)} custom-call(s32[32]{0:T(128)} %select_reduce_fusion.2.slot_ref, f32[32,8,512]{2,1,0:T(8,128)} %convert.2.kv_ref, bf16[8,1,4,128,128]{4,3,2,1,0:T(8,128)(2,1)} %copy-done.1, bf16[8,2,4,128,128]{4,3,2,1,0:T(8,128)(2,1)} %copy-done, bf16[8,1,4,128,128]{4,3,2,1,0:T(8,128)(2,1)} %copy-done.2), custom_call_target="tpu_custom_call" | custom-call | tf_op jit(solution)/shard_map/pallas_call | solution.py:266
  295.3 6.8 %all-reduce = f32[256]{0:T(256)S(1)} all-reduce(f32[256]{0:T(256)S(1)} %dynamic-update-slice), channel_id=3, replica_groups=mesh['req'=8,'head'=4] {'head'}, use_global_device_ids=true, to_apply=%add | all-reduce | flops 256 | bytes 2048
  (175 shorter events, 36.3 us)
Async XLA Ops:
  7.2 10.9 %copy-start.6 = (s32[32]{0:T(128)S(1)}, s32[32]{0:T(128)}, u32[]{:S(2)}) copy-start(s32[32]{0:T(128)} %param.23) | copy-start | bytes 388
  7.2 11.2 %copy-start.11 = (s32[5]{0:T(128)S(1)}, s32[5]{0:T(128)}, u32[]{:S(2)}) copy-start(s32[5]{0:T(128)} %param.25) | copy-start | bytes 64
  7.2 105.8 %all-gather.16.cloned.1.call-start = ((), (), s32[]{:S(2)}) async-start(), calls=%async_computation.13 | async-start | bytes 3604480 | tf_op jit(solution)/shard_map/all_gather | solution.py:302
  7.9 105.0 %all-gather.8.cloned.1.call-start = ((), (), s32[]{:S(2)}) async-start(), calls=%async_computation.9 | async-start | bytes 3604480 | tf_op jit(solution)/shard_map/all_gather | solution.py:300
  10.1 13.8 %all-to-all-start.1 = ((s32[8,1,192]{2,1,0:T(1,128)}), s32[8,1,192]{2,1,0:T(1,128)S(1)}, u32[]{:S(2)}, u32[]{:S(2)}) async-start(s32[8,1,192]{2,1,0:T(1,128)} %reshape.540), calls=%async_computation.1 | async-start | bytes 16384 | tf_op jit(solution)/shard_map/all_to_all | solution.py:280
  17.3 95.6 %all-gather.10.cloned.1.call-start = ((), (), s32[]{:S(2)}) async-start(), calls=%async_computation.10 | async-start | bytes 3604480 | tf_op jit(solution)/shard_map/all_gather | solution.py:301
  31.9 16.7 %all-to-all-start.2 = ((bf16[8,64,512]{2,1,0:T(8,128)(2,1)}), bf16[8,64,512]{2,1,0:T(8,128)(2,1)S(1)}, u32[]{:S(2)}, u32[]{:S(2)}) async-start(bf16[8,64,512]{2,1,0:T(8,128)(2,1)} %bitcast.10), calls=%async_computation.2 | async-start | bytes 1048576 | tf_op jit(solution)/shard_map/all_to_all | solution.py:280
  48.9 4.6 %copy-start.4 = (f32[4,512]{1,0:T(4,128)S(1)}, f32[4,512]{1,0:T(4,128)}, u32[]{:S(2)}) copy-start(f32[4,512]{1,0:T(4,128)} %param.40) | copy-start | bytes 24580
  48.9 4.6 %copy-start.7 = (f32[512]{0:T(512)S(1)}, f32[512]{0:T(512)}, u32[]{:S(2)}) copy-start(f32[512]{0:T(512)} %param.39) | copy-start | bytes 6148
  48.9 29.0 %all-to-all-start.3 = ((bf16[8,1,4,128,128]{4,3,2,1,0:T(8,128)(2,1)}), bf16[8,1,4,128,128]{4,3,2,1,0:T(8,128)(2,1)S(1)}, u32[]{:S(2)}, u32[]{:S(2)}) async-start(bf16[8,1,4,128,128]{4,3,2,1,0:T(8,128)(2,1)} %get-tuple-element.41.rest_0_), calls=%async_computation.3 | async-start | bytes 2097152 | tf_op jit(solution)/shard_map/all_to_all | solution.py:280
  77.9 54.0 %copy-start.1 = (bf16[8,1,4,128,128]{4,3,2,1,0:T(8,128)(2,1)}, bf16[8,1,4,128,128]{4,3,2,1,0:T(8,128)(2,1)S(1)}, u32[]{:S(2)}) copy-start(bf16[8,1,4,128,128]{4,3,2,1,0:T(8,128)(2,1)S(1)} %all-to-all-done.3.rest_0_) | copy-start | bytes 3145732
  77.9 54.0 %all-to-all-start.4 = ((bf16[8,2,4,128,128]{4,3,2,1,0:T(8,128)(2,1)}), bf16[8,2,4,128,128]{4,3,2,1,0:T(8,128)(2,1)S(1)}, u32[]{:S(2)}, u32[]{:S(2)}) async-start(bf16[8,2,4,128,128]{4,3,2,1,0:T(8,128)(2,1)} %get-tuple-element.42.rest_1_), calls=%async_computation.4 | async-start | bytes 4194304 | tf_op jit(solution)/shard_map/all_to_all | solution.py:280
  81.5 76.0 %all-gather.12.cloned.1.call-start = ((), (), s32[]{:S(2)}) async-start(), calls=%async_computation.11 | async-start | bytes 1179648 | tf_op jit(solution)/shard_map/all_gather | solution.py:381
  101.5 57.6 %copy-start.10 = (f32[2048]{0:T(1024)S(1)}, f32[2048]{0:T(1024)}, u32[]{:S(2)}) copy-start(f32[2048]{0:T(1024)} %param.35) | copy-start | bytes 24580
  101.5 1.9 collective-permute-start
  101.9 6.7 %collective-permute-start.1 = (bf16[32,2176]{1,0:T(8,128)(2,1)}, bf16[32,2176]{1,0:T(8,128)(2,1)S(1)}, u32[]{:S(2)}, u32[]{:S(2)}) collective-permute-start(bf16[32,2176]{1,0:T(8,128)(2,1)} %get-tuple-element.47), channel_id=1, source_target_pairs={{0,2},{1,3},{2,0},{3,1},{4,6},{5,7},{6,4},{7,5},{8,10},{9,11},{10,... | collective-permute-start | bytes 417800 | tf_op jit(solution)/shard_map/ppermute | solution.py:21
  103.3 6.9 %collective-permute-start.2 = (bf16[32,2176]{1,0:T(8,128)(2,1)}, bf16[32,2176]{1,0:T(8,128)(2,1)S(1)}, u32[]{:S(2)}, u32[]{:S(2)}) collective-permute-start(bf16[32,2176]{1,0:T(8,128)(2,1)} %get-tuple-element.48), channel_id=1, source_target_pairs={{0,3},{1,2},{2,1},{3,0},{4,7},{5,6},{6,5},{7,4},{8,11},{9,10},{10,... | collective-permute-start | bytes 417800 | tf_op jit(solution)/shard_map/ppermute | solution.py:21
  131.9 31.3 %copy-start = (bf16[8,2,4,128,128]{4,3,2,1,0:T(8,128)(2,1)}, bf16[8,2,4,128,128]{4,3,2,1,0:T(8,128)(2,1)S(1)}, u32[]{:S(2)}) copy-start(bf16[8,2,4,128,128]{4,3,2,1,0:T(8,128)(2,1)S(1)} %all-to-all-done.4.rest_1_) | copy-start | bytes 6291460
  172.5 28.7 %all-to-all-start.5 = ((bf16[8,32,2048]{2,1,0:T(8,128)(2,1)}), bf16[8,32,2048]{2,1,0:T(8,128)(2,1)S(1)}, u32[]{:S(2)}, u32[]{:S(2)}) async-start(bf16[8,32,2048]{2,1,0:T(8,128)(2,1)} %bitcast.99), calls=%async_computation.5 | async-start | bytes 2097152 | tf_op jit(solution)/shard_map/all_to_all | solution.py:280
  176.1 96.3 %all-gather.14.cloned.1.call-start = ((), (), s32[]{:S(2)}) async-start(), calls=%async_computation.12 | async-start | bytes 2359296 | tf_op jit(solution)/shard_map/all_gather | solution.py:439
  177.4 30.4 %copy-start.5 = (s32[32]{0:T(128)S(1)}, s32[32]{0:T(128)}, u32[]{:S(2)}) copy-start(s32[32]{0:T(128)} %param.24) | copy-start | bytes 388
  201.4 11.5 %copy-start.12 = (u32[32]{0:T(128)S(1)}, u32[32]{0:T(128)}, u32[]{:S(2)}) copy-start(u32[32]{0:T(128)} %constant.217) | copy-start | bytes 388
  202.0 5.0 %collective-permute-start.6 = (bf16[32,2048]{1,0:T(8,128)(2,1)S(1)}, bf16[32,2048]{1,0:T(8,128)(2,1)S(1)}, u32[]{:S(2)}, u32[]{:S(2)}) collective-permute-start(bf16[32,2048]{1,0:T(8,128)(2,1)S(1)} %multiply_convert_fusion), channel_id=1, source_target_pairs={{0,2},{1,3},{2,0},{3,1},{4,6},{5,7},{6,4},{7,5},{8,10},{9,11},{10,... | collective-permute-start | bytes 393224 | tf_op jit(solution)/shard_map/ppermute | solution.py:21
  207.8 69.9 %collective-permute-start.7 = (bf16[1000,2048]{1,0:T(8,128)(2,1)}, bf16[1000,2048]{1,0:T(8,128)(2,1)}, u32[]{:S(2)}, u32[]{:S(2)}) collective-permute-start(bf16[1000,2048]{1,0:T(8,128)(2,1)} %bitcast.135), channel_id=1, source_target_pairs={{0,1},{1,0},{2,3},{3,2},{4,5},{5,4},{6,7},{7,6},{8,9},{9,8},{10,11... | collective-permute-start | bytes 12288008 | tf_op jit(solution)/shard_map/ppermute | solution.py:21
  208.4 16.6 %all-to-all-start.6 = ((bf16[8,32,512]{2,1,0:T(8,128)(2,1)}), bf16[8,32,512]{2,1,0:T(8,128)(2,1)S(1)}, u32[]{:S(2)}, u32[]{:S(2)}) async-start(bf16[8,32,512]{2,1,0:T(8,128)(2,1)} %bitcast.105), calls=%async_computation.6 | async-start | bytes 524288 | tf_op jit(solution)/shard_map/all_to_all | solution.py:280
  225.1 57.8 %all-to-all-start.7 = ((bf16[8,1,4,128,128]{4,3,2,1,0:T(8,128)(2,1)}), bf16[8,1,4,128,128]{4,3,2,1,0:T(8,128)(2,1)S(1)}, u32[]{:S(2)}, u32[]{:S(2)}) async-start(bf16[8,1,4,128,128]{4,3,2,1,0:T(8,128)(2,1)} %shard_map.224), calls=%async_computation.7 | async-start | bytes 2097152 | tf_op jit(solution)/shard_map/all_to_all | solution.py:280
  229.5 1.9 collective-permute-start.3
  229.6 5.0 %collective-permute-start.4 = (f32[32,640]{1,0:T(8,128)S(1)}, f32[32,640]{1,0:T(8,128)S(1)}, u32[]{:S(2)}, u32[]{:S(2)}) collective-permute-start(f32[32,640]{1,0:T(8,128)S(1)} %get-tuple-element.69), channel_id=1, source_target_pairs={{0,2},{1,3},{2,0},{3,1},{4,6},{5,7},{6,4},{7,5},{8,10},{9,11},{10,... | collective-permute-start | bytes 245768 | tf_op jit(solution)/shard_map/ppermute | solution.py:21
  231.3 4.7 %collective-permute-start.5 = (f32[32,640]{1,0:T(8,128)S(1)}, f32[32,640]{1,0:T(8,128)S(1)}, u32[]{:S(2)}, u32[]{:S(2)}) collective-permute-start(f32[32,640]{1,0:T(8,128)S(1)} %get-tuple-element.70), channel_id=1, source_target_pairs={{0,3},{1,2},{2,1},{3,0},{4,7},{5,6},{6,5},{7,4},{8,11},{9,10},{10,... | collective-permute-start | bytes 245768 | tf_op jit(solution)/shard_map/ppermute | solution.py:21
  272.4 5.3 %copy-start.9 = (bf16[16,32,2048]{2,1,0:T(8,128)(2,1)S(1)}, bf16[16,32,2048]{2,1,0:T(8,128)(2,1)}, u32[]{:S(2)}) copy-start(bf16[16,32,2048]{2,1,0:T(8,128)(2,1)} %all-gather.14.cloned.1.call-done) | copy-start | bytes 6291460
  282.9 5.4 %copy-start.2 = (bf16[8,1,4,128,128]{4,3,2,1,0:T(8,128)(2,1)}, bf16[8,1,4,128,128]{4,3,2,1,0:T(8,128)(2,1)S(1)}, u32[]{:S(2)}) copy-start(bf16[8,1,4,128,128]{4,3,2,1,0:T(8,128)(2,1)S(1)} %all-to-all-done.7.rest_2_) | copy-start | bytes 3145732
  282.9 12.2 %all-to-all-start.8 = ((f32[8,1,64]{2,1,0:T(1,128)}), f32[8,1,64]{2,1,0:T(1,128)S(1)}, u32[]{:S(2)}, u32[]{:S(2)}) async-start(f32[8,1,64]{2,1,0:T(1,128)} %max.22), calls=%async_computation.8 | async-start | bytes 8192 | tf_op jit(solution)/shard_map/all_to_all | solution.py:280
  (3 other events, 10.9 us)
Sparse Core Ops, SparseCore 0:
  9.6 29.7 all-gather.15
  40.9 27.0 all-gather.7
  69.6 30.1 all-gather.9
  114.4 43.1 all-gather.11
  207.9 64.5 all-gather.13

commit v5 on v4

--- a/solution.py
+++ b/solution.py
@@ -272,6 +272,40 @@
     )(slots, kv, *states)
 
 
+def greatest_kernel(full_hbm, *rest):
+    count = (len(rest) - 3) // 2
+    there, best_ref, full_ref, here, sems = (
+        rest[:count], rest[count], rest[count + 1], rest[count + 2 : -1], rest[-1]
+    )
+    loads = [pltpu.make_async_copy(full_hbm, full_ref, sems.at[count])]
+    loads += [pltpu.make_async_copy(there[i], here[i], sems.at[i]) for i in range(count)]
+    for load in loads:
+        load.start()
+    loads[0].wait()
+    best = None
+    for i in range(count):
+        loads[1 + i].wait()
+        height = here[i].shape[0]
+        for first in range(0, height, 256):
+            entries = dot_rows(here[i][first : min(first + 256, height), :], full_ref[...])
+            top = jnp.max(entries, axis=0, keepdims=True)
+            best = top if best is None else jnp.maximum(best, top)
+    best_ref[...] = best
+
+
+def greatest_entries(full, *tables):
+    anywhere = pl.BlockSpec(memory_space=pl.ANY)
+    return pl.pallas_call(
+        greatest_kernel,
+        out_shape=jax.ShapeDtypeStruct((1, full.shape[0]), F32),
+        in_specs=[anywhere] * (1 + len(tables)),
+        out_specs=pl.BlockSpec(memory_space=VMEM),
+        scratch_shapes=[VMEM(x.shape, BF16) for x in (full,) + tables]
+        + [pltpu.SemaphoreType.DMA((1 + len(tables),))],
+        compiler_params=pltpu.CompilerParams(vmem_limit_bytes=48 << 20),
+    )(full, *tables)
+
+
 def dot_rows(a, b):
     return lax.dot_general(a, b, (((1,), (1,)), ((), ())), preferred_element_type=F32)
 
@@ -362,7 +396,7 @@
     ordered = lax.dynamic_slice_in_dim(ordered, r * requests, requests, 1)
     old_order = (ordered[steps] - r * requests).reshape(n_head, group).T.reshape(n, sends)
     old_order = jnp.take(old_order, jnp.arange(n) ^ r, axis=0).reshape(requests)
-    counts = (1, 2, 1) if sends == 4 else (sends,)
+    counts = (2, 2) if sends == 4 else (sends,)
     pieces = sort_states(old_order, old_states, n, counts)
     live = (jnp.arange(steps)[None, :] < ordered[steps + 1][:, None]).astype(F32)
     own, kv, *parts = mixer(
@@ -379,7 +413,7 @@
     after_mixer = own.astype(F32) + total[:, :D] * lax.rsqrt(square / D + epsilon)
     after_mixer = after(after_mixer.astype(BF16), gate_full, up_full, down_full)
     everything = lax.all_gather(after_mixer, "req", axis=0, tiled=True)
-    arrived += [to_all(piece, "req") for piece in pieces[1:2]]
+    arrived += [to_all(after(piece, after_mixer), "req") for piece in pieces[1:]]
     stream = everything.astype(F32)
     scale = lax.rsqrt(jnp.mean(stream * stream, axis=1, keepdims=True) + epsilon)
     feed_in = (stream * scale * feed_gain).astype(BF16)
@@ -434,13 +468,9 @@
     final = (hidden * lax.rsqrt(mean_square + epsilon) * token_gain).astype(BF16)
 
     final = jnp.stack([final, swap(final, "head", n_head, 2)])
-    arrived += [to_all(after(piece, final), "req") for piece in pieces[2:]]
     arrived_kv = to_all(after(kv, final).reshape(n, -1, width), "req")
     full = lax.all_gather(final, "req", axis=0, tiled=True).reshape(n * 2 * rows, D)
-    best = jnp.maximum(
-        jnp.max(dot_rows(full, vocab_weight.T), axis=1),
-        jnp.max(dot_rows(full, vocab_other), axis=1),
-    ).reshape(n, 2 * rows)
+    best = greatest_entries(full, vocab_weight.T, vocab_other).reshape(n, 2 * rows)
     got = jnp.max(to_all(best, "req"), axis=0)
     got = lax.all_gather(got, "head", axis=0).reshape(n_head, 2, rows)
     crossed = jnp.stack([got[i ^ 2, 1] for i in range(n_head)])

time: 311 us -> 305 us (0.981)
  matrix products: 23.1 us -> 12.3 us
  local copies, waits for them, and re-layouts: 14.3 us -> 19.9 us
  Pallas kernels: 19.4 us -> 24.9 us
  waiting for transfers between devices: 163 us -> 159 us
    all_to_all x8 -> x7, waiting for transfers between devices: 86.3 us -> 35.1 us  [to_all(): return lax.all_to_all(x, axis, split_axis=0, concat_axis=0, tiled=True)]
    all_gather x1, waiting for transfers between devices: 25 us -> 56.2 us  [on_device(): everything = lax.all_gather(after_mixer, 'req', axis=0, tiled=True)]
    all_gather x1, waiting for transfers between devices: 0.01 us -> 13.4 us  [on_device(): down_full = lax.all_gather(down_weight, 'head', axis=0)]
    dot_general x3 -> x1, matrix products: 13.8 us -> 4.11 us  [dot_rows(): lax.dot_general(a, b, (((1,), (1,)), ((), ())), preferred_element_type=F32)]
    pallas_call x0 -> x1, Pallas kernels: none -> 5.38 us  [greatest_entries(): pl.pallas_call(greatest_kernel, out_shape=jax.ShapeDtypeStruct((1, full.s...]
    unnamed x37 -> x33, local copies, waits for them, and re-layouts: 1.68 us -> 5.41 us
    all_to_all x8 -> x7, starting transfers between devices: 32.9 us -> 31.7 us  [to_all(): return lax.all_to_all(x, axis, split_axis=0, concat_axis=0, tiled=True)]
  transfers between devices with their start and end apart: 21 -> 20, of which waited for: 13 -> 11; matrix products, arithmetic and copies ran while one was open for 12% -> 14% of each run, Pallas kernels for 6% -> 8%
where the time goes in v5:
time: 305 us; the launch traced here: 304 us
  waiting for transfers between devices  159 us (52%)
  starting transfers between devices  37.7 us (12%)
  Pallas kernels  24.9 us (8%)
  local copies, waits for them, and re-layouts  19.9 us (7%)
  other arithmetic  17.8 us (6%)
  blocking collectives  17.3 us (6%)
  between operations  15.7 us (5%)
  matrix products  12.3 us (4%)
    all_gather x1, waiting for transfers between devices, on_device(): everything = lax.all_gather(after_mixer, 'req', axis=0, tiled=True)  56.2 us
    all_gather x1, waiting for transfers between devices, on_device(): lax.all_gather(final, 'req', axis=0, tiled=True).reshape(n * 2 * rows, D)  36.6 us
    all_to_all x7, waiting for transfers between devices, to_all(): return lax.all_to_all(x, axis, split_axis=0, concat_axis=0, tiled=True)  35.1 us
    all_to_all x7, starting transfers between devices, to_all(): return lax.all_to_all(x, axis, split_axis=0, concat_axis=0, tiled=True)  31.7 us
    ppermute x8, waiting for transfers between devices, swap(): return lax.ppermute(x, axis, [(i, i ^ offset) for i in range(size)])  15.2 us
    all_gather x1, waiting for transfers between devices, on_device(): down_full = lax.all_gather(down_weight, 'head', axis=0)  13.4 us
    all_gather x1, blocking collectives, on_device(): lax.all_gather(jnp.concatenate([embed_part, gains_high, gains_low, extra]...  11.6 us
    pallas_call x1, Pallas kernels, mixer(): pl.pallas_call(functools.partial(mixer_kernel, counts, owners, heads, cla...  8.11 us
  transfers between devices with their start and end apart: 20, of which 11 were waited for; matrix products, arithmetic and copies ran while one was open for 14% of the time, Pallas kernels for 8%

profile of v5, /device:TPU:0, one launch (start us, length us, event | category | flops | bytes accessed | tf_op | source)
XLA Modules:
  0.0 304.3 jit_solution(10484708849418554312)
XLA Ops:
  10.1 7.3 %all-to-all-start.1 = ((s32[8,1,192]{2,1,0:T(1,128)}), s32[8,1,192]{2,1,0:T(1,128)S(1)}, u32[]{:S(2)}, u32[]{:S(2)}) async-start(s32[8,1,192]{2,1,0:T(1,128)} %reshape.532), calls=%async_computation.1 | async-start | bytes 16384 | tf_op jit(solution)/shard_map/all_to_all | solution.py:314
  18.7 5.1 %all-to-all-done.1 = s32[8,1,192]{2,1,0:T(1,128)S(1)} async-done(((s32[8,1,192]{2,1,0:T(1,128)}), s32[8,1,192]{2,1,0:T(1,128)S(1)}, u32[]{:S(2)}, u32[]{:S(2)}) %all-to-all-start.1) | async-done | bytes 6176 | tf_op jit(solution)/shard_map/all_to_all | solution.py:314
  26.5 5.4 %gather_fusion.1 = bf16[512,512]{1,0:T(8,128)(2,1)} fusion(bf16[4000,512]{1,0:T(8,128)(2,1)} %param.27, s32[1024]{0:T(1024)S(1)} %pad_clamp_fusion.2), kind=kCustom, calls=%fused_computation.1 | custom fusion | bytes 1050624 | tf_op jit(solution)/shard_map/jit(_take)/gather | solution.py:362
  31.9 3.5 %all-to-all-start.2 = ((bf16[8,64,512]{2,1,0:T(8,128)(2,1)}), bf16[8,64,512]{2,1,0:T(8,128)(2,1)S(1)}, u32[]{:S(2)}, u32[]{:S(2)}) async-start(bf16[8,64,512]{2,1,0:T(8,128)(2,1)} %bitcast.10), calls=%async_computation.2 | async-start | bytes 1048576 | tf_op jit(solution)/shard_map/all_to_all | solution.py:314
  38.5 4.6 %shard_map.219 = (bf16[8,2,4,128,128]{4,3,2,1,0:T(8,128)(2,1)}, bf16[8,2,4,128,128]{4,3,2,1,0:T(8,128)(2,1)}) custom-call(s32[32]{0:T(128)} %select_n.239.order_ref, bf16[32,4,128,128]{3,2,1,0:T(8,128)(2,1)} %old_ref.1), custom_call_target="tpu_custom_call" | custom-call | tf_op jit(solution)/shard_map/pallas_call | solution.py:65
  43.3 5.3 %all-to-all-done.2 = bf16[8,64,512]{2,1,0:T(8,128)(2,1)S(1)} async-done(((bf16[8,64,512]{2,1,0:T(8,128)(2,1)}), bf16[8,64,512]{2,1,0:T(8,128)(2,1)S(1)}, u32[]{:S(2)}, u32[]{:S(2)}) %all-to-all-start.2) | async-done | bytes 524320 | tf_op jit(solution)/shard_map/all_to_all | solution.py:314
  48.9 3.8 %all-to-all-start.3 = ((bf16[8,2,4,128,128]{4,3,2,1,0:T(8,128)(2,1)}), bf16[8,2,4,128,128]{4,3,2,1,0:T(8,128)(2,1)S(1)}, u32[]{:S(2)}, u32[]{:S(2)}) async-start(bf16[8,2,4,128,128]{4,3,2,1,0:T(8,128)(2,1)} %get-tuple-element.40.rest_0_), calls=%async_computation.3 | async-start | bytes 4194304 | tf_op jit(solution)/shard_map/all_to_all | solution.py:314
  54.4 11.6 %all_gather.27.emb_ref = bf16[144,2048]{1,0:T(8,128)(2,1)} all-gather(bf16[144,512]{1,0:T(8,128)(2,1)S(1)} %maximum_maximum_fusion), channel_id=1, replica_groups=mesh['req'=8,'head'=4] {'head'}, dimensions={1}, use_global_device_ids=true | all-gather | bytes 737280 | tf_op jit(solution)/shard_map/all_gather | solution.py:391
  66.0 8.1 %shard_map.220 = (bf16[32,2048]{1,0:T(8,128)(2,1)}, bf16[256,512]{1,0:T(8,128)(2,1)}, bf16[32,2176]{1,0:T(8,128)(2,1)}, bf16[32,2176]{1,0:T(8,128)(2,1)}, bf16[3...) custom-call(s32[2]{0:T(128)} %pad_add_fusion.1.me_ref, bf16[144,2048]{1,0:T(8,128)(2,1)} %all_gather.27.emb_ref, ...), custom_call_target="tpu_custom_call" | custom-call | tf_op jit(solution)/shard_map/pallas_call | solution.py:215
  76.2 3.7 %collective-permute-done.2 = bf16[32,2176]{1,0:T(8,128)(2,1)S(1)} collective-permute-done((bf16[32,2176]{1,0:T(8,128)(2,1)}, bf16[32,2176]{1,0:T(8,128)(2,1)S(1)}, u32[]{:S(2)}, u32[]{:S(2)}) %collective-permute-start.2) | collective-permute-done | bytes 139296 | tf_op jit(solution)/shard_map/ppermute | solution.py:21
  79.9 4.3 %collective-permute-done.1 = bf16[32,2176]{1,0:T(8,128)(2,1)S(1)} collective-permute-done((bf16[32,2176]{1,0:T(8,128)(2,1)}, bf16[32,2176]{1,0:T(8,128)(2,1)S(1)}, u32[]{:S(2)}, u32[]{:S(2)}) %collective-permute-start.1) | collective-permute-done | bytes 139296 | tf_op jit(solution)/shard_map/ppermute | solution.py:21
  85.3 1.7 fusion.20.x_ref
  87.0 13.4 %all-gather.16.cloned.1.call-done = bf16[2816,512]{1,0:T(8,128)(2,1)} async-done(((bf16[704,512]{1,0:T(8,128)(2,1)}), bf16[2816,512]{1,0:T(8,128)(2,1)}) %all-gather.16.cloned.1.call-update) | async-done | bytes 2883600 | tf_op jit(solution)/shard_map/all_gather | solution.py:336
  102.9 6.0 %all-to-all-start.4 = ((bf16[8,2,4,128,128]{4,3,2,1,0:T(8,128)(2,1)}), bf16[8,2,4,128,128]{4,3,2,1,0:T(8,128)(2,1)}, u32[]{:S(2)}, u32[]{:S(2)}) async-start(bf16[8,2,4,128,128]{4,3,2,1,0:T(8,128)(2,1)} %shard_map.222), calls=%async_computation.4 | async-start | bytes 4194304 | tf_op jit(solution)/shard_map/all_to_all | solution.py:314
  108.9 56.2 %all-gather.12.cloned.1.call-done = bf16[256,2048]{1,0:T(8,128)(2,1)} async-done(((bf16[32,2048]{1,0:T(8,128)(2,1)}), bf16[256,2048]{1,0:T(8,128)(2,1)}) %all-gather.12.cloned.1.call-update) | async-done | bytes 1048592 | tf_op jit(solution)/shard_map/all_gather | solution.py:415
  165.1 1.5 fusion
  166.7 4.1 %fusion.17 = f32[256,704]{0,1:T(8,128)} fusion(bf16[704,2048]{1,0:T(8,128)(2,1)} %all-gather.8.cloned.1.call-done, bf16[256,2048]{1,0:T(8,128)(2,1)} %all-gather.12.cloned.1.call-done, f32[2048]{0:T(1024)S(1)} %copy-done.9, f32[256]{0:T(256)S(1)} %add_rsqrt_fusion), kind=kOutput, calls=%fused_computation.39 | convolution fusion | flops 740294656 | bytes 4662272 | tf_op jit(solution)/shard_map/dot_general | solution.py:310
  170.8 3.2 %convolution_convert_fusion = bf16[256,704]{0,1:T(8,128)(2,1)S(1)} fusion(bf16[704,2048]{1,0:T(8,128)(2,1)} %all-gather.10.cloned.1.call-done, f32[256,704]{0,1:T(8,128)} %fusion.17, bf16[256,2048]{1,0:T(8,128)(2,1)S(1)} %copy-done.3, f32[2048]{0:T(1024)S(1)} %copy-done.9, f32[256]{0:T(256)S(1)} %add_rsqrt_fusion, s32[256]{0:T(256)S(1)} %fusion.47), kind=kOutput, calls=%fused_computation.18 | convolution fusion | flops 833896448 | bytes 5023744 | tf_op jit(solution)/shard_map/dot_general | solution.py:432
  174.0 1.7 convolution_convert_fusion.1
  180.4 3.6 %all-to-all-start.5 = ((bf16[8,32,2048]{2,1,0:T(8,128)(2,1)}), bf16[8,32,2048]{2,1,0:T(8,128)(2,1)S(1)}, u32[]{:S(2)}, u32[]{:S(2)}) async-start(bf16[8,32,2048]{2,1,0:T(8,128)(2,1)} %bitcast.101), calls=%async_computation.5 | async-start | bytes 2097152 | tf_op jit(solution)/shard_map/all_to_all | solution.py:314
  185.3 24.6 %all-to-all-done.5 = bf16[8,32,2048]{2,1,0:T(8,128)(2,1)S(1)} async-done(((bf16[8,32,2048]{2,1,0:T(8,128)(2,1)}), bf16[8,32,2048]{2,1,0:T(8,128)(2,1)S(1)}, u32[]{:S(2)}, u32[]{:S(2)}) %all-to-all-start.5) | async-done | bytes 1048608 | tf_op jit(solution)/shard_map/all_to_all | solution.py:314
  210.7 1.8 collective-permute-start.6
  212.4 3.3 %collective-permute-done.6 = bf16[32,2048]{1,0:T(8,128)(2,1)S(1)} collective-permute-done((bf16[32,2048]{1,0:T(8,128)(2,1)S(1)}, bf16[32,2048]{1,0:T(8,128)(2,1)S(1)}, u32[]{:S(2)}, u32[]{:S(2)}) %collective-permute-start.6) | collective-permute-done | bytes 131104 | tf_op jit(solution)/shard_map/ppermute | solution.py:21
  219.5 4.1 %all-to-all-start.6 = ((bf16[8,32,512]{2,1,0:T(8,128)(2,1)}), bf16[8,32,512]{2,1,0:T(8,128)(2,1)S(1)}, u32[]{:S(2)}, u32[]{:S(2)}) async-start(bf16[8,32,512]{2,1,0:T(8,128)(2,1)} %bitcast.107), calls=%async_computation.6 | async-start | bytes 524288 | tf_op jit(solution)/shard_map/all_to_all | solution.py:314
  225.6 2.8 collective-permute-done.5
  230.6 36.6 %all-gather.14.cloned.1.call-done = bf16[16,32,2048]{2,1,0:T(8,128)(2,1)} async-done(((bf16[2,32,2048]{2,1,0:T(8,128)(2,1)}), bf16[16,32,2048]{2,1,0:T(8,128)(2,1)}) %all-gather.14.cloned.1.call-update) | async-done | bytes 2097168 | tf_op jit(solution)/shard_map/all_gather | solution.py:472
  267.3 2.2 copy-done
  269.5 1.6 copy-done.1
  271.0 5.4 %shard_map.226 = f32[1,512]{1,0:T(1,128)S(1)} custom-call(bf16[512,2048]{1,0:T(8,128)(2,1)S(1)} %bitcast.100, bf16[1000,2048]{1,0:T(8,128)(2,1)S(1)} %bitcast.99, bf16[1000,2048]{1,0:T(8,128)(2,1)} %collective-permute-done.7.rest_1_), custom_call_target="tpu_custom_call" | custom-call | tf_op jit(solution)/shard_map/pallas_call | solution.py:298
  278.3 3.6 %all-to-all-start.7 = ((f32[8,1,64]{2,1,0:T(1,128)}), f32[8,1,64]{2,1,0:T(1,128)S(1)}, u32[]{:S(2)}, u32[]{:S(2)}) async-start(f32[8,1,64]{2,1,0:T(1,128)} %bitcast.48), calls=%async_computation.7 | async-start | bytes 8192 | tf_op jit(solution)/shard_map/all_to_all | solution.py:314
  283.9 6.8 %shard_map.225 = bf16[32,4,128,128]{3,2,1,0:T(8,128)(2,1)} custom-call(s32[32]{0:T(128)} %select_reduce_fusion.2.slot_ref, f32[32,8,512]{2,1,0:T(8,128)} %convert.2.kv_ref, bf16[8,2,4,128,128]{4,3,2,1,0:T(8,128)(2,1)} %copy-done.2, bf16[8,2,4,128,128]{4,3,2,1,0:T(8,128)(2,1)} %all-to-all-done.4.rest_1_), custom_call_target="tpu_custom_call" | custom-call | tf_op jit(solution)/shard_map/pallas_call | solution.py:266
  291.0 5.7 %all-reduce = f32[256]{0:T(256)S(1)} all-reduce(f32[256]{0:T(256)S(1)} %dynamic-update-slice), channel_id=3, replica_groups=mesh['req'=8,'head'=4] {'head'}, use_global_device_ids=true, to_apply=%add | all-reduce | flops 256 | bytes 2048
  (170 shorter events, 36.3 us)
Async XLA Ops:
  7.2 10.9 %copy-start.6 = (s32[32]{0:T(128)S(1)}, s32[32]{0:T(128)}, u32[]{:S(2)}) copy-start(s32[32]{0:T(128)} %param.23) | copy-start | bytes 388
  7.2 11.2 %copy-start.10 = (s32[5]{0:T(128)S(1)}, s32[5]{0:T(128)}, u32[]{:S(2)}) copy-start(s32[5]{0:T(128)} %param.25) | copy-start | bytes 64
  7.2 79.8 %all-gather.10.cloned.1.call-start = ((), (), s32[]{:S(2)}) async-start(), calls=%async_computation.9 | async-start | bytes 3604480 | tf_op jit(solution)/shard_map/all_gather | solution.py:335
  7.9 79.1 %all-gather.8.cloned.1.call-start = ((), (), s32[]{:S(2)}) async-start(), calls=%async_computation.8 | async-start | bytes 3604480 | tf_op jit(solution)/shard_map/all_gather | solution.py:334
  10.1 13.8 %all-to-all-start.1 = ((s32[8,1,192]{2,1,0:T(1,128)}), s32[8,1,192]{2,1,0:T(1,128)S(1)}, u32[]{:S(2)}, u32[]{:S(2)}) async-start(s32[8,1,192]{2,1,0:T(1,128)} %reshape.532), calls=%async_computation.1 | async-start | bytes 16384 | tf_op jit(solution)/shard_map/all_to_all | solution.py:314
  17.3 83.0 %all-gather.16.cloned.1.call-start = ((), (), s32[]{:S(2)}) async-start(), calls=%async_computation.12 | async-start | bytes 3604480 | tf_op jit(solution)/shard_map/all_gather | solution.py:336
  31.9 16.7 %all-to-all-start.2 = ((bf16[8,64,512]{2,1,0:T(8,128)(2,1)}), bf16[8,64,512]{2,1,0:T(8,128)(2,1)S(1)}, u32[]{:S(2)}, u32[]{:S(2)}) async-start(bf16[8,64,512]{2,1,0:T(8,128)(2,1)} %bitcast.10), calls=%async_computation.2 | async-start | bytes 1048576 | tf_op jit(solution)/shard_map/all_to_all | solution.py:314
  48.9 4.6 %copy-start.4 = (f32[4,512]{1,0:T(4,128)S(1)}, f32[4,512]{1,0:T(4,128)}, u32[]{:S(2)}) copy-start(f32[4,512]{1,0:T(4,128)} %param.40) | copy-start | bytes 24580
  48.9 4.6 %copy-start.7 = (f32[512]{0:T(512)S(1)}, f32[512]{0:T(512)}, u32[]{:S(2)}) copy-start(f32[512]{0:T(512)} %param.39) | copy-start | bytes 6148
  48.9 54.0 %all-to-all-start.3 = ((bf16[8,2,4,128,128]{4,3,2,1,0:T(8,128)(2,1)}), bf16[8,2,4,128,128]{4,3,2,1,0:T(8,128)(2,1)S(1)}, u32[]{:S(2)}, u32[]{:S(2)}) async-start(bf16[8,2,4,128,128]{4,3,2,1,0:T(8,128)(2,1)} %get-tuple-element.40.rest_0_), calls=%async_computation.3 | async-start | bytes 4194304 | tf_op jit(solution)/shard_map/all_to_all | solution.py:314
  52.7 112.4 %all-gather.12.cloned.1.call-start = ((), (), s32[]{:S(2)}) async-start(), calls=%async_computation.10 | async-start | bytes 1179648 | tf_op jit(solution)/shard_map/all_gather | solution.py:415
  74.1 5.8 %collective-permute-start.2 = (bf16[32,2176]{1,0:T(8,128)(2,1)}, bf16[32,2176]{1,0:T(8,128)(2,1)S(1)}, u32[]{:S(2)}, u32[]{:S(2)}) collective-permute-start(bf16[32,2176]{1,0:T(8,128)(2,1)} %get-tuple-element.46), channel_id=1, source_target_pairs={{0,3},{1,2},{2,1},{3,0},{4,7},{5,6},{6,5},{7,4},{8,11},{9,10},{10,... | collective-permute-start | bytes 417800 | tf_op jit(solution)/shard_map/ppermute | solution.py:21
  75.3 8.9 %collective-permute-start.1 = (bf16[32,2176]{1,0:T(8,128)(2,1)}, bf16[32,2176]{1,0:T(8,128)(2,1)S(1)}, u32[]{:S(2)}, u32[]{:S(2)}) collective-permute-start(bf16[32,2176]{1,0:T(8,128)(2,1)} %get-tuple-element.45), channel_id=1, source_target_pairs={{0,2},{1,3},{2,0},{3,1},{4,6},{5,7},{6,4},{7,5},{8,10},{9,11},{10,... | collective-permute-start | bytes 417800 | tf_op jit(solution)/shard_map/ppermute | solution.py:21
  76.2 8.0 %collective-permute-start = (bf16[32,2176]{1,0:T(8,128)(2,1)}, bf16[32,2176]{1,0:T(8,128)(2,1)S(1)}, u32[]{:S(2)}, u32[]{:S(2)}) collective-permute-start(bf16[32,2176]{1,0:T(8,128)(2,1)} %get-tuple-element.44), channel_id=1, source_target_pairs={{0,1},{1,0},{2,3},{3,2},{4,5},{5,4},{6,7},{7,6},{8,9},{9,8},{10,11... | collective-permute-start | bytes 417800 | tf_op jit(solution)/shard_map/ppermute | solution.py:21
  102.9 63.7 %copy-start.9 = (f32[2048]{0:T(1024)S(1)}, f32[2048]{0:T(1024)}, u32[]{:S(2)}) copy-start(f32[2048]{0:T(1024)} %param.35) | copy-start | bytes 24580
  102.9 76.2 %copy-start.2 = (bf16[8,2,4,128,128]{4,3,2,1,0:T(8,128)(2,1)}, bf16[8,2,4,128,128]{4,3,2,1,0:T(8,128)(2,1)S(1)}, u32[]{:S(2)}) copy-start(bf16[8,2,4,128,128]{4,3,2,1,0:T(8,128)(2,1)S(1)} %all-to-all-done.3.rest_0_) | copy-start | bytes 6291460
  102.9 76.2 %all-to-all-start.4 = ((bf16[8,2,4,128,128]{4,3,2,1,0:T(8,128)(2,1)}), bf16[8,2,4,128,128]{4,3,2,1,0:T(8,128)(2,1)}, u32[]{:S(2)}, u32[]{:S(2)}) async-start(bf16[8,2,4,128,128]{4,3,2,1,0:T(8,128)(2,1)} %shard_map.222), calls=%async_computation.4 | async-start | bytes 4194304 | tf_op jit(solution)/shard_map/all_to_all | solution.py:314
  166.7 4.1 %copy-start.3 = (bf16[256,2048]{1,0:T(8,128)(2,1)S(1)}, bf16[256,2048]{1,0:T(8,128)(2,1)}, u32[]{:S(2)}) copy-start(bf16[256,2048]{1,0:T(8,128)(2,1)} %all-gather.12.cloned.1.call-done) | copy-start | bytes 3145732
  174.0 3.2 %copy-start.8 = (bf16[2816,512]{1,0:T(8,128)(2,1)S(1)}, bf16[2816,512]{1,0:T(8,128)(2,1)}, u32[]{:S(2)}) copy-start(bf16[2816,512]{1,0:T(8,128)(2,1)} %all-gather.16.cloned.1.call-done) | copy-start | bytes 8650756
  180.4 29.6 %all-to-all-start.5 = ((bf16[8,32,2048]{2,1,0:T(8,128)(2,1)}), bf16[8,32,2048]{2,1,0:T(8,128)(2,1)S(1)}, u32[]{:S(2)}, u32[]{:S(2)}) async-start(bf16[8,32,2048]{2,1,0:T(8,128)(2,1)} %bitcast.101), calls=%async_computation.5 | async-start | bytes 2097152 | tf_op jit(solution)/shard_map/all_to_all | solution.py:314
  183.9 83.4 %all-gather.14.cloned.1.call-start = ((), (), s32[]{:S(2)}) async-start(), calls=%async_computation.11 | async-start | bytes 2359296 | tf_op jit(solution)/shard_map/all_gather | solution.py:472
  184.0 46.7 %collective-permute-start.7 = (bf16[1000,2048]{1,0:T(8,128)(2,1)}, bf16[1000,2048]{1,0:T(8,128)(2,1)}, u32[]{:S(2)}, u32[]{:S(2)}) collective-permute-start(bf16[1000,2048]{1,0:T(8,128)(2,1)} %bitcast.98), channel_id=1, source_target_pairs={{0,1},{1,0},{2,3},{3,2},{4,5},{5,4},{6,7},{7,6},{8,9},{9,8},{10,11... | collective-permute-start | bytes 12288008 | tf_op jit(solution)/shard_map/ppermute | solution.py:21
  185.3 31.2 %copy-start.11 = (u32[32]{0:T(128)S(1)}, u32[32]{0:T(128)}, u32[]{:S(2)}) copy-start(u32[32]{0:T(128)} %constant.217) | copy-start | bytes 388
  185.3 33.1 %copy-start.5 = (s32[32]{0:T(128)S(1)}, s32[32]{0:T(128)}, u32[]{:S(2)}) copy-start(s32[32]{0:T(128)} %param.24) | copy-start | bytes 388
  210.7 5.0 %collective-permute-start.6 = (bf16[32,2048]{1,0:T(8,128)(2,1)S(1)}, bf16[32,2048]{1,0:T(8,128)(2,1)S(1)}, u32[]{:S(2)}, u32[]{:S(2)}) collective-permute-start(bf16[32,2048]{1,0:T(8,128)(2,1)S(1)} %multiply_convert_fusion), channel_id=1, source_target_pairs={{0,2},{1,3},{2,0},{3,1},{4,6},{5,7},{6,4},{7,5},{8,10},{9,11},{10,... | collective-permute-start | bytes 393224 | tf_op jit(solution)/shard_map/ppermute | solution.py:21
  219.5 58.8 %all-to-all-start.6 = ((bf16[8,32,512]{2,1,0:T(8,128)(2,1)}), bf16[8,32,512]{2,1,0:T(8,128)(2,1)S(1)}, u32[]{:S(2)}, u32[]{:S(2)}) async-start(bf16[8,32,512]{2,1,0:T(8,128)(2,1)} %bitcast.107), calls=%async_computation.6 | async-start | bytes 524288 | tf_op jit(solution)/shard_map/all_to_all | solution.py:314
  223.7 4.7 %collective-permute-start.5 = (f32[32,640]{1,0:T(8,128)S(1)}, f32[32,640]{1,0:T(8,128)S(1)}, u32[]{:S(2)}, u32[]{:S(2)}) collective-permute-start(f32[32,640]{1,0:T(8,128)S(1)} %get-tuple-element.68), channel_id=1, source_target_pairs={{0,3},{1,2},{2,1},{3,0},{4,7},{5,6},{6,5},{7,4},{8,11},{9,10},{10,... | collective-permute-start | bytes 245768 | tf_op jit(solution)/shard_map/ppermute | solution.py:21
  223.8 5.8 %collective-permute-start.4 = (f32[32,640]{1,0:T(8,128)S(1)}, f32[32,640]{1,0:T(8,128)S(1)}, u32[]{:S(2)}, u32[]{:S(2)}) collective-permute-start(f32[32,640]{1,0:T(8,128)S(1)} %get-tuple-element.67), channel_id=1, source_target_pairs={{0,2},{1,3},{2,0},{3,1},{4,6},{5,7},{6,4},{7,5},{8,10},{9,11},{10,... | collective-permute-start | bytes 245768 | tf_op jit(solution)/shard_map/ppermute | solution.py:21
  224.9 4.7 %collective-permute-start.3 = (f32[32,640]{1,0:T(8,128)S(1)}, f32[32,640]{1,0:T(8,128)S(1)}, u32[]{:S(2)}, u32[]{:S(2)}) collective-permute-start(f32[32,640]{1,0:T(8,128)S(1)} %get-tuple-element.66), channel_id=1, source_target_pairs={{0,1},{1,0},{2,3},{3,2},{4,5},{5,4},{6,7},{7,6},{8,9},{9,8},{10,11... | collective-permute-start | bytes 245768 | tf_op jit(solution)/shard_map/ppermute | solution.py:21
  267.3 2.2 copy-start
  269.5 1.6 copy-start.1
  278.3 12.5 %all-to-all-start.7 = ((f32[8,1,64]{2,1,0:T(1,128)}), f32[8,1,64]{2,1,0:T(1,128)S(1)}, u32[]{:S(2)}, u32[]{:S(2)}) async-start(f32[8,1,64]{2,1,0:T(1,128)} %bitcast.48), calls=%async_computation.7 | async-start | bytes 8192 | tf_op jit(solution)/shard_map/all_to_all | solution.py:314
Sparse Core Ops, SparseCore 0:
  9.6 29.7 all-gather.9
  40.9 30.2 all-gather.7
  72.8 27.5 all-gather.15
  102.3 62.7 all-gather.11
  216.6 50.6 all-gather.13

commit v6 on v4

--- a/solution.py
+++ b/solution.py
@@ -78,20 +78,19 @@
     )(order, old_states)
 
 
-def hand_on(x_ref, token_ref, out_ref):
+def hand_on(*refs):
     pass
 
 
 def after(x, *others):
-    corners = [other.reshape((-1,) + other.shape[-2:])[0, :8, :128] for other in others]
     anywhere = pl.BlockSpec(memory_space=pl.ANY)
     return pl.pallas_call(
         hand_on,
         out_shape=jax.ShapeDtypeStruct(x.shape, x.dtype),
-        in_specs=[anywhere, anywhere],
+        in_specs=[anywhere] * (1 + len(others)),
         out_specs=anywhere,
         input_output_aliases={0: 0},
-    )(x, sum(corners[1:], corners[0]))
+    )(x, *others)
 
 
 def roll(x, by):
@@ -276,6 +275,98 @@
     return lax.dot_general(a, b, (((1,), (1,)), ((), ())), preferred_element_type=F32)
 
 
+def feed_kernel(
+    x_hbm, weights_hbm, pick_ref, mine_ref, gain_ref, down_ref, kept_ref, x, weights, feed, act, sems
+):
+    blocks, height, depth = weights.shape
+    units = height // 3
+    loads = [pltpu.make_async_copy(x_hbm, x, sems.at[3])]
+    for i in range(3):
+        span = pl.ds(i * units, units)
+        loads.append(
+            pltpu.make_async_copy(weights_hbm.at[:, span], weights.at[:, span], sems.at[i])
+        )
+    for load in loads:
+        load.start()
+    loads[0].wait()
+    stream = x[...].astype(F32)
+    scale = lax.rsqrt(jnp.mean(stream * stream, axis=1, keepdims=True) + epsilon)
+    feed[...] = (stream * scale * gain_ref[...]).astype(BF16)
+    kept_ref[...] = jnp.dot(mine_ref[...], x[...], preferred_element_type=F32).astype(BF16)
+    loads[1].wait()
+    loads[2].wait()
+    for first in range(0, units, 256):
+        last = min(first + 256, units)
+        gate = up = 0.0
+        for b in range(blocks):
+            part = feed[:, b * depth : (b + 1) * depth]
+            gate += dot_rows(part, weights[b, first:last, :])
+            up += dot_rows(part, weights[b, units + first : units + last, :])
+        act[:, first:last] = (gate * jax.nn.sigmoid(gate) * up).astype(BF16)
+    placed = jnp.dot(pick_ref[...], act[...], preferred_element_type=F32).astype(BF16)
+    loads[3].wait()
+    for b in range(blocks):
+        down_ref[:, b * depth : (b + 1) * depth] = jnp.dot(
+            placed, weights[b, 2 * units :, :], preferred_element_type=F32
+        ).astype(BF16)
+
+
+def feed_forward(x, weights, pick, mine, gain):
+    vmem, anywhere = pl.BlockSpec(memory_space=VMEM), pl.BlockSpec(memory_space=pl.ANY)
+    tokens, width = x.shape
+    return pl.pallas_call(
+        feed_kernel,
+        out_shape=[
+            jax.ShapeDtypeStruct((tokens, width), BF16),
+            jax.ShapeDtypeStruct((mine.shape[0], width), BF16),
+        ],
+        in_specs=[anywhere] * 2 + [vmem] * 3,
+        out_specs=[vmem] * 2,
+        scratch_shapes=[
+            VMEM(x.shape, BF16),
+            VMEM(weights.shape, BF16),
+            VMEM(x.shape, BF16),
+            VMEM((tokens, weights.shape[1] // 3), BF16),
+            pltpu.SemaphoreType.DMA((4,)),
+        ],
+        compiler_params=pltpu.CompilerParams(vmem_limit_bytes=58 << 20),
+    )(x, weights, pick, mine, gain)
+
+
+def greatest_kernel(states_hbm, full_hbm, own_hbm, other_hbm, best_ref, full, own, other, sems):
+    loads = [
+        pltpu.make_async_copy(there, here, sems.at[i])
+        for i, (there, here) in enumerate(((full_hbm, full), (own_hbm, own), (other_hbm, other)))
+    ]
+    for load in loads:
+        load.start()
+    loads[0].wait()
+    best = None
+    for i, table in enumerate((own, other)):
+        loads[1 + i].wait()
+        height = table.shape[0]
+        for first in range(0, height, 256):
+            entries = dot_rows(table[first : min(first + 256, height), :], full[...])
+            top = jnp.max(entries, axis=0, keepdims=True)
+            best = top if best is None else jnp.maximum(best, top)
+    width = best_ref.shape[1]
+    for k in range(best_ref.shape[0]):
+        best_ref[k : k + 1, :] = best[:, k * width : (k + 1) * width]
+
+
+def greatest_entries(blocks, states, full, own, other):
+    anywhere = pl.BlockSpec(memory_space=pl.ANY)
+    return pl.pallas_call(
+        greatest_kernel,
+        out_shape=jax.ShapeDtypeStruct((blocks, full.shape[0] // blocks), F32),
+        in_specs=[anywhere] * 4,
+        out_specs=pl.BlockSpec(memory_space=VMEM),
+        scratch_shapes=[VMEM(x.shape, BF16) for x in (full, own, other)]
+        + [pltpu.SemaphoreType.DMA((3,))],
+        compiler_params=pltpu.CompilerParams(vmem_limit_bytes=58 << 20),
+    )(states, full, own, other)
+
+
 def to_all(x, axis):
     return lax.all_to_all(x, axis, split_axis=0, concat_axis=0, tiled=True)
 
@@ -297,9 +388,8 @@
     rows = group * steps
     width = D // n_head
 
-    gate_full = lax.all_gather(gate_weight.T, "head", axis=1, tiled=True)
-    up_full = lax.all_gather(up_weight.T, "head", axis=1, tiled=True)
-    down_full = lax.all_gather(down_weight, "head", axis=0)
+    feed_weights = jnp.concatenate([gate_weight.T, up_weight.T, down_weight], axis=0)
+    feed_weights = lax.all_gather(feed_weights, "head", axis=0)
 
     packed = jnp.concatenate([token_ids.T, state_perm[None], token_count[None]], axis=0)
     packed = to_all(jnp.broadcast_to(packed[None], (n,) + packed.shape), "req").transpose(1, 0, 2).reshape(steps + 2, everyone)
@@ -362,7 +452,7 @@
     ordered = lax.dynamic_slice_in_dim(ordered, r * requests, requests, 1)
     old_order = (ordered[steps] - r * requests).reshape(n_head, group).T.reshape(n, sends)
     old_order = jnp.take(old_order, jnp.arange(n) ^ r, axis=0).reshape(requests)
-    counts = (1, 2, 1) if sends == 4 else (sends,)
+    counts = (1, 1, 1, 1) if sends == 4 else (sends,)
     pieces = sort_states(old_order, old_states, n, counts)
     live = (jnp.arange(steps)[None, :] < ordered[steps + 1][:, None]).astype(F32)
     own, kv, *parts = mixer(
@@ -377,15 +467,10 @@
         total = total + swap(parts[e], "head", n_head, e).astype(F32)
     square = total[:, D : D + 1] + total[:, D + 127 : D + 128]
     after_mixer = own.astype(F32) + total[:, :D] * lax.rsqrt(square / D + epsilon)
-    after_mixer = after(after_mixer.astype(BF16), gate_full, up_full, down_full)
+    after_mixer = after(after_mixer.astype(BF16), feed_weights)
     everything = lax.all_gather(after_mixer, "req", axis=0, tiled=True)
-    arrived += [to_all(piece, "req") for piece in pieces[1:2]]
-    stream = everything.astype(F32)
-    scale = lax.rsqrt(jnp.mean(stream * stream, axis=1, keepdims=True) + epsilon)
-    feed_in = (stream * scale * feed_gain).astype(BF16)
-    gate = dot_rows(feed_in, gate_full)
-    up = dot_rows(feed_in, up_full)
-    activated = (jax.nn.silu(gate) * up).astype(BF16)
+    for piece in pieces[1:3]:
+        arrived += [to_all(after(piece, after_mixer, *arrived[1:]), "req")]
 
     row = jnp.arange(n * rows, dtype=jnp.int32)
     by_owner, by_group, by_step = row // rows, (row % rows) // steps, row % steps
@@ -395,15 +480,10 @@
         offset = (by_group * n_head + h) // sends
     wanted = (by_owner ^ offset) * rows + by_group * steps + by_step
     pick = (wanted[None, :] == row[:, None]).astype(BF16)
-    activated = jnp.dot(pick, activated, preferred_element_type=F32).astype(BF16)
     mine = (wanted[None, :] == (r * rows + row[:rows])[:, None]).astype(BF16)
-    kept = jnp.dot(mine, everything, preferred_element_type=F32)
-    down = jnp.concatenate(
-        [jnp.dot(activated, down_full[b], preferred_element_type=F32).astype(BF16) for b in range(n_head)],
-        axis=1,
-    )
+    down, kept = feed_forward(everything, feed_weights, pick, mine, feed_gain[None])
     down = after(down, *arrived)
-    hidden = kept + jnp.sum(to_all(down.reshape(n, rows, D), "req").astype(F32), axis=0)
+    hidden = kept.astype(F32) + jnp.sum(to_all(down.reshape(n, rows, D), "req").astype(F32), axis=0)
     mean_square = jnp.mean(hidden * hidden, axis=1, keepdims=True)
 
     slots = jnp.arange(requests, dtype=jnp.int32)
@@ -434,13 +514,13 @@
     final = (hidden * lax.rsqrt(mean_square + epsilon) * token_gain).astype(BF16)
 
     final = jnp.stack([final, swap(final, "head", n_head, 2)])
-    arrived += [to_all(after(piece, final), "req") for piece in pieces[2:]]
+    arrived += [to_all(after(piece, final), "req") for piece in pieces[3:]]
     arrived_kv = to_all(after(kv, final).reshape(n, -1, width), "req")
     full = lax.all_gather(final, "req", axis=0, tiled=True).reshape(n * 2 * rows, D)
-    best = jnp.maximum(
-        jnp.max(dot_rows(full, vocab_weight.T), axis=1),
-        jnp.max(dot_rows(full, vocab_other), axis=1),
-    ).reshape(n, 2 * rows)
+    new_states = update_states(
+        slot_of, arrived_kv.reshape(requests, 2 * steps, width).astype(F32), arrived, steps
+    )
+    best = greatest_entries(n, new_states, full, vocab_weight.T, vocab_other)
     got = jnp.max(to_all(best, "req"), axis=0)
     got = lax.all_gather(got, "head", axis=0).reshape(n_head, 2, rows)
     crossed = jnp.stack([got[i ^ 2, 1] for i in range(n_head)])
@@ -464,9 +544,6 @@
     last = jnp.arange(steps)[None, :] == (token_count - 1)[:, None]
     last_norm = jnp.sqrt(jnp.sum(jnp.where(last, whole[:, :, width], 0.0), axis=1) + epsilon)
 
-    new_states = update_states(
-        slot_of, arrived_kv.reshape(requests, 2 * steps, width).astype(F32), arrived, steps
-    )
     return whole[:, :, :width], new_states, last_norm, greatest
 
 

time: 311 us -> 328 us (1.055)
  blocking collectives: 18.6 us -> 49.1 us
  matrix products: 23.1 us -> 0.62 us
  Pallas kernels: 19.4 us -> 35.4 us
  waiting for transfers between devices: 163 us -> 155 us
    all_gather x1, waiting for transfers between devices: 35.3 us -> 0.01 us  [on_device(): lax.all_gather(final, 'req', axis=0, tiled=True).reshape(n * 2 * rows, D)]
    all_to_all x0 -> x1, blocking collectives: none -> 31.7 us  [to_all(): return lax.all_to_all(x, axis, split_axis=0, concat_axis=0, tiled=True)]
    all_to_all x8, waiting for transfers between devices: 86.3 us -> 109 us  [to_all(): return lax.all_to_all(x, axis, split_axis=0, concat_axis=0, tiled=True)]
    dot_general x9 -> x0, matrix products: 22.4 us -> none  [the longest x3 13.8 us: dot_rows(): lax.dot_general(a, b, (((1,), (1,)), ((), ())), preferred_element_type=F32)]
    pallas_call x0 -> x2, Pallas kernels: none -> 16.2 us  [the longest x1 8.22 us: greatest_entries(): pl.pallas_call(greatest_kernel, out_shape=jax.ShapeDtypeStruct((blocks, f...]
    all_gather x1, waiting for transfers between devices: 25 us -> 28.4 us  [on_device(): everything = lax.all_gather(after_mixer, 'req', axis=0, tiled=True)]
  transfers between devices with their start and end apart: 21 -> 19, of which waited for: 13 -> 13; matrix products, arithmetic and copies ran while one was open for 12% -> 8% of each run, Pallas kernels for 6% -> 8%
where the time goes in v6:
time: 328 us; the launch traced here: 327 us
  waiting for transfers between devices  155 us (47%)
  blocking collectives  49.1 us (15%)
  starting transfers between devices  40.7 us (12%)
  Pallas kernels  35.4 us (11%)
  other arithmetic  15.9 us (5%)
  between operations  15.6 us (5%)
  local copies, waits for them, and re-layouts  15 us (5%)
    all_to_all x8, waiting for transfers between devices, to_all(): return lax.all_to_all(x, axis, split_axis=0, concat_axis=0, tiled=True)  109 us
    all_to_all x8, starting transfers between devices, to_all(): return lax.all_to_all(x, axis, split_axis=0, concat_axis=0, tiled=True)  35.4 us
    all_to_all x1, blocking collectives, to_all(): return lax.all_to_all(x, axis, split_axis=0, concat_axis=0, tiled=True)  31.7 us
    all_gather x1, waiting for transfers between devices, on_device(): everything = lax.all_gather(after_mixer, 'req', axis=0, tiled=True)  28.4 us
    ppermute x8, waiting for transfers between devices, swap(): return lax.ppermute(x, axis, [(i, i ^ offset) for i in range(size)])  16.4 us
    all_gather x1, blocking collectives, on_device(): lax.all_gather(jnp.concatenate([embed_part, gains_high, gains_low, extra]...  11.6 us
    pallas_call x1, Pallas kernels, greatest_entries(): pl.pallas_call(greatest_kernel, out_shape=jax.ShapeDtypeStruct((blocks, f...  8.22 us
    pallas_call x1, Pallas kernels, mixer(): pl.pallas_call(functools.partial(mixer_kernel, counts, owners, heads, cla...  8.06 us
  transfers between devices with their start and end apart: 19, of which 13 were waited for; matrix products, arithmetic and copies ran while one was open for 8% of the time, Pallas kernels for 8%

profile of v6, /device:TPU:0, one launch (start us, length us, event | category | flops | bytes accessed | tf_op | source)
XLA Modules:
  0.0 326.9 jit_solution(5499397474789273474)
XLA Ops:
  7.3 3.0 pad_maximum_fusion
  11.1 7.3 %all-to-all-start.1 = ((s32[8,1,192]{2,1,0:T(1,128)}), s32[8,1,192]{2,1,0:T(1,128)S(1)}, u32[]{:S(2)}, u32[]{:S(2)}) async-start(s32[8,1,192]{2,1,0:T(1,128)} %reshape.485), calls=%async_computation.1 | async-start | bytes 16384 | tf_op jit(solution)/shard_map/all_to_all | solution.py:371
  19.7 5.1 %all-to-all-done.1 = s32[8,1,192]{2,1,0:T(1,128)S(1)} async-done(((s32[8,1,192]{2,1,0:T(1,128)}), s32[8,1,192]{2,1,0:T(1,128)S(1)}, u32[]{:S(2)}, u32[]{:S(2)}) %all-to-all-start.1) | async-done | bytes 6176 | tf_op jit(solution)/shard_map/all_to_all | solution.py:371
  27.5 5.4 %gather_fusion.1 = bf16[512,512]{1,0:T(8,128)(2,1)} fusion(bf16[4000,512]{1,0:T(8,128)(2,1)} %param.27, s32[1024]{0:T(1024)S(1)} %pad_clamp_fusion.2), kind=kCustom, calls=%fused_computation.1 | custom fusion | bytes 1050624 | tf_op jit(solution)/shard_map/jit(_take)/gather | solution.py:418
  32.9 3.5 %all-to-all-start.2 = ((bf16[8,64,512]{2,1,0:T(8,128)(2,1)}), bf16[8,64,512]{2,1,0:T(8,128)(2,1)S(1)}, u32[]{:S(2)}, u32[]{:S(2)}) async-start(bf16[8,64,512]{2,1,0:T(8,128)(2,1)} %bitcast.10), calls=%async_computation.2 | async-start | bytes 1048576 | tf_op jit(solution)/shard_map/all_to_all | solution.py:371
  40.1 4.4 %shard_map.219 = (bf16[8,1,4,128,128]{4,3,2,1,0:T(8,128)(2,1)}, bf16[8,1,4,128,128]{4,3,2,1,0:T(8,128)(2,1)}, bf16[8,1,4,128,128]{4,3,2,1,0:T(8,128)(2,1)}, bf16[8,1,4,128,128]{4,3,2,1,0:T(8,128)(2,1)}) custom-call(s32[32]{0:T(128)} %select_n.235.order_ref, bf16[32,4,128,128]{3,2,1,0:T(8,128)(2,1)} %old_ref.1), custom_call_target="tpu_custom_call" | custom-call | tf_op jit(solution)/shard_map/pallas_call | solution.py:65
  44.7 5.0 %all-to-all-done.2 = bf16[8,64,512]{2,1,0:T(8,128)(2,1)S(1)} async-done(((bf16[8,64,512]{2,1,0:T(8,128)(2,1)}), bf16[8,64,512]{2,1,0:T(8,128)(2,1)S(1)}, u32[]{:S(2)}, u32[]{:S(2)}) %all-to-all-start.2) | async-done | bytes 524320 | tf_op jit(solution)/shard_map/all_to_all | solution.py:371
  50.2 11.6 %all_gather.21.emb_ref = bf16[144,2048]{1,0:T(8,128)(2,1)} all-gather(bf16[144,512]{1,0:T(8,128)(2,1)S(1)} %maximum_maximum_fusion), channel_id=1, replica_groups=mesh['req'=8,'head'=4] {'head'}, dimensions={1}, use_global_device_ids=true | all-gather | bytes 737280 | tf_op jit(solution)/shard_map/all_gather | solution.py:447
  61.8 8.1 %shard_map.220 = (bf16[32,2048]{1,0:T(8,128)(2,1)}, bf16[256,512]{1,0:T(8,128)(2,1)}, bf16[32,2176]{1,0:T(8,128)(2,1)}, bf16[32,2176]{1,0:T(8,128)(2,1)}, bf16[3...) custom-call(s32[2]{0:T(128)} %pad_add_fusion.1.me_ref, bf16[144,2048]{1,0:T(8,128)(2,1)} %all_gather.21.emb_ref, ...), custom_call_target="tpu_custom_call" | custom-call | tf_op jit(solution)/shard_map/pallas_call | solution.py:214
  71.8 5.8 %collective-permute-done.1 = bf16[32,2176]{1,0:T(8,128)(2,1)S(1)} collective-permute-done((bf16[32,2176]{1,0:T(8,128)(2,1)}, bf16[32,2176]{1,0:T(8,128)(2,1)S(1)}, u32[]{:S(2)}, u32[]{:S(2)}) %collective-permute-start.1) | collective-permute-done | bytes 139296 | tf_op jit(solution)/shard_map/ppermute | solution.py:21
  77.6 2.5 collective-permute-done.2
  81.2 1.7 fusion.2.refs_0_
  82.9 31.7 %all_to_all.54.refs_2_.rest_1_ = bf16[8,1,4,128,128]{4,3,2,1,0:T(8,128)(2,1)} all-to-all(bf16[8,1,4,128,128]{4,3,2,1,0:T(8,128)(2,1)} %shard_map.223), channel_id=1, replica_groups=mesh['req'=8,'head'=4] {'req'}, dimensions={0} | all-to-all | bytes 2097152 | tf_op jit(solution)/shard_map/all_to_all | solution.py:371
  114.6 3.6 %all-to-all-start.3 = ((bf16[8,1,4,128,128]{4,3,2,1,0:T(8,128)(2,1)}), bf16[8,1,4,128,128]{4,3,2,1,0:T(8,128)(2,1)S(1)}, u32[]{:S(2)}, u32[]{:S(2)}) async-start(bf16[8,1,4,128,128]{4,3,2,1,0:T(8,128)(2,1)} %get-tuple-element.44.rest_0_), calls=%async_computation.3 | async-start | bytes 2097152 | tf_op jit(solution)/shard_map/all_to_all | solution.py:371
  119.0 29.0 %all-to-all-done.3.refs_1_.rest_0_ = bf16[8,1,4,128,128]{4,3,2,1,0:T(8,128)(2,1)S(1)} async-done(((bf16[8,1,4,128,128]{4,3,2,1,0:T(8,128)(2,1)}), bf16[8,1,4,128,128]{4,3,2,1,0:T(8,128)(2,1)S(1)}, u32[]{:S(2)}, u32[]{:S(2)}) %all-to-all-start.3) | async-done | bytes 1048608 | tf_op jit(solution)/shard_map/all_to_all | solution.py:371
  148.0 3.7 %all-to-all-start.5 = ((bf16[8,1,4,128,128]{4,3,2,1,0:T(8,128)(2,1)}), bf16[8,1,4,128,128]{4,3,2,1,0:T(8,128)(2,1)S(1)}, u32[]{:S(2)}, u32[]{:S(2)}) async-start(bf16[8,1,4,128,128]{4,3,2,1,0:T(8,128)(2,1)} %shard_map.224), calls=%async_computation.5 | async-start | bytes 2097152 | tf_op jit(solution)/shard_map/all_to_all | solution.py:371
  153.2 28.4 %all-gather.6.cloned.1.call-done.x_hbm = bf16[256,2048]{1,0:T(8,128)(2,1)} async-done(((bf16[32,2048]{1,0:T(8,128)(2,1)}), bf16[256,2048]{1,0:T(8,128)(2,1)}) %all-gather.6.cloned.1.call-update) | async-done | bytes 1048592 | tf_op jit(solution)/shard_map/all_gather | solution.py:471
  181.6 8.0 %shard_map.222 = (bf16[256,2048]{1,0:T(8,128)(2,1)}, bf16[32,2048]{1,0:T(8,128)(2,1)}) custom-call(bf16[256,2048]{1,0:T(8,128)(2,1)} %all-gather.6.cloned.1.call-done.x_hbm, bf16[4,2112,512]{2,1,0:T(8,128)(2,1)} %bitcast.82, bf16[256,256]{1,0:T(8,128)(2,1)} %fusion.5.pick_ref, bf16[32,256]{1,0:T(8,128)(2,1)} %compare_convert_fusion.mine_ref, f32[1,2048]{1,0:T(1,128)} %bitcast.110), custom_call_target="tpu_custom_call" | custom-call | tf_op jit(solution)/shard_map/pallas_call | solution.py:317
  190.6 3.7 %all-to-all-start.6 = ((bf16[8,32,2048]{2,1,0:T(8,128)(2,1)}), bf16[8,32,2048]{2,1,0:T(8,128)(2,1)S(1)}, u32[]{:S(2)}, u32[]{:S(2)}) async-start(bf16[8,32,2048]{2,1,0:T(8,128)(2,1)} %bitcast.83), calls=%async_computation.6 | async-start | bytes 2097152 | tf_op jit(solution)/shard_map/all_to_all | solution.py:371
  195.7 24.8 %all-to-all-done.6 = bf16[8,32,2048]{2,1,0:T(8,128)(2,1)S(1)} async-done(((bf16[8,32,2048]{2,1,0:T(8,128)(2,1)}), bf16[8,32,2048]{2,1,0:T(8,128)(2,1)S(1)}, u32[]{:S(2)}, u32[]{:S(2)}) %all-to-all-start.6) | async-done | bytes 1048608 | tf_op jit(solution)/shard_map/all_to_all | solution.py:371
  220.9 1.2 collective-permute-start.6
  222.1 3.8 %collective-permute-done.6 = bf16[32,2048]{1,0:T(8,128)(2,1)S(1)} collective-permute-done((bf16[32,2048]{1,0:T(8,128)(2,1)S(1)}, bf16[32,2048]{1,0:T(8,128)(2,1)S(1)}, u32[]{:S(2)}, u32[]{:S(2)}) %collective-permute-start.6) | collective-permute-done | bytes 131104 | tf_op jit(solution)/shard_map/ppermute | solution.py:21
  226.7 4.1 %all-to-all-start.7 = ((bf16[8,32,512]{2,1,0:T(8,128)(2,1)}), bf16[8,32,512]{2,1,0:T(8,128)(2,1)S(1)}, u32[]{:S(2)}, u32[]{:S(2)}) async-start(bf16[8,32,512]{2,1,0:T(8,128)(2,1)} %bitcast.89), calls=%async_computation.7 | async-start | bytes 524288 | tf_op jit(solution)/shard_map/all_to_all | solution.py:371
  230.8 11.3 %all-to-all-done.7 = bf16[8,32,512]{2,1,0:T(8,128)(2,1)S(1)} async-done(((bf16[8,32,512]{2,1,0:T(8,128)(2,1)}), bf16[8,32,512]{2,1,0:T(8,128)(2,1)S(1)}, u32[]{:S(2)}, u32[]{:S(2)}) %all-to-all-start.7) | async-done | bytes 262176 | tf_op jit(solution)/shard_map/all_to_all | solution.py:371
  242.1 4.1 %all-to-all-start.8 = ((bf16[8,1,4,128,128]{4,3,2,1,0:T(8,128)(2,1)}), bf16[8,1,4,128,128]{4,3,2,1,0:T(8,128)(2,1)S(1)}, u32[]{:S(2)}, u32[]{:S(2)}) async-start(bf16[8,1,4,128,128]{4,3,2,1,0:T(8,128)(2,1)} %shard_map.227), calls=%async_computation.8 | async-start | bytes 2097152 | tf_op jit(solution)/shard_map/all_to_all | solution.py:371
  250.7 3.4 %collective-permute-done.4 = f32[32,640]{1,0:T(8,128)S(1)} collective-permute-done((f32[32,640]{1,0:T(8,128)S(1)}, f32[32,640]{1,0:T(8,128)S(1)}, u32[]{:S(2)}, u32[]{:S(2)}) %collective-permute-start.4) | collective-permute-done | bytes 81952 | tf_op jit(solution)/shard_map/ppermute | solution.py:21
  256.9 28.6 %all-to-all-done.8.rest_3_ = bf16[8,1,4,128,128]{4,3,2,1,0:T(8,128)(2,1)S(1)} async-done(((bf16[8,1,4,128,128]{4,3,2,1,0:T(8,128)(2,1)}), bf16[8,1,4,128,128]{4,3,2,1,0:T(8,128)(2,1)S(1)}, u32[]{:S(2)}, u32[]{:S(2)}) %all-to-all-start.8) | async-done | bytes 1048608 | tf_op jit(solution)/shard_map/all_to_all | solution.py:371
  286.4 6.7 %shard_map.228.states_hbm = bf16[32,4,128,128]{3,2,1,0:T(8,128)(2,1)} custom-call(s32[32]{0:T(128)} %select_reduce_fusion.2.slot_ref, f32[32,8,512]{2,1,0:T(8,128)} %convert.2.kv_ref, bf16[8,1,4,128,128]{4,3,2,1,0:T(8,128)(2,1)} %copy-done, bf16[8,1,4,128,128]{4,3,2,1,0:T(8,128)(2,1)} %all_to_all.54.refs_2_.rest_1_, bf16[8,1,4,128,128]{4,3,2,1,0:T(8,128)(2,1)} %copy-done.1, ...), custom_call_target="tpu_custom_call" | custom-call | tf_op jit(solution)/shard_map/pallas_call | solution.py:265
  293.2 8.2 %shard_map.229 = f32[8,64]{1,0:T(8,128)} custom-call(bf16[32,4,128,128]{3,2,1,0:T(8,128)(2,1)} %shard_map.228.states_hbm, bf16[512,2048]{1,0:T(8,128)(2,1)} %bitcast.88, bf16[1000,2048]{1,0:T(8,128)(2,1)} %bitcast.86, bf16[1000,2048]{1,0:T(8,128)(2,1)} %collective-permute-done.7.other_hbm), custom_call_target="tpu_custom_call" | custom-call | tf_op jit(solution)/shard_map/pallas_call | solution.py:359
  301.4 5.4 %all-to-all-start.9 = ((f32[8,1,64]{2,1,0:T(1,128)}), f32[8,1,64]{2,1,0:T(1,128)S(1)}, u32[]{:S(2)}, u32[]{:S(2)}) async-start(f32[8,1,64]{2,1,0:T(1,128)} %bitcast.108), calls=%async_computation.9 | async-start | bytes 8192 | tf_op jit(solution)/shard_map/all_to_all | solution.py:371
  308.1 5.2 %all-to-all-done.9 = f32[8,1,64]{2,1,0:T(1,128)S(1)} async-done(((f32[8,1,64]{2,1,0:T(1,128)}), f32[8,1,64]{2,1,0:T(1,128)S(1)}, u32[]{:S(2)}, u32[]{:S(2)}) %all-to-all-start.9) | async-done | bytes 2080 | tf_op jit(solution)/shard_map/all_to_all | solution.py:371
  313.6 5.8 %all-reduce = f32[256]{0:T(256)S(1)} all-reduce(f32[256]{0:T(256)S(1)} %dynamic-update-slice), channel_id=3, replica_groups=mesh['req'=8,'head'=4] {'head'}, use_global_device_ids=true, to_apply=%add | all-reduce | flops 256 | bytes 2048
  (155 shorter events, 27.1 us)
Async XLA Ops:
  7.2 3.2 copy-start.6
  7.2 3.2 copy-start.7
  7.2 3.2 copy-start.5
  7.2 11.1 %copy-start.9 = (s32[5]{0:T(128)S(1)}, s32[5]{0:T(128)}, u32[]{:S(2)}) copy-start(s32[5]{0:T(128)} %param.25) | copy-start | bytes 64
  7.2 11.2 %copy-start.8 = (f32[512]{0:T(512)S(1)}, f32[512]{0:T(512)}, u32[]{:S(2)}) copy-start(f32[512]{0:T(512)} %param.39) | copy-start | bytes 6148
  7.2 11.2 %copy-start.4 = (f32[4,512]{1,0:T(4,128)S(1)}, f32[4,512]{1,0:T(4,128)}, u32[]{:S(2)}) copy-start(f32[4,512]{1,0:T(4,128)} %param.40) | copy-start | bytes 24580
  7.2 75.7 %all-gather.10.cloned.1.call-start = ((), (), s32[]{:S(2)}) async-start(), calls=%async_computation.12 | async-start | bytes 10813440 | tf_op jit(solution)/shard_map/all_gather | solution.py:392
  11.1 13.8 %all-to-all-start.1 = ((s32[8,1,192]{2,1,0:T(1,128)}), s32[8,1,192]{2,1,0:T(1,128)S(1)}, u32[]{:S(2)}, u32[]{:S(2)}) async-start(s32[8,1,192]{2,1,0:T(1,128)} %reshape.485), calls=%async_computation.1 | async-start | bytes 16384 | tf_op jit(solution)/shard_map/all_to_all | solution.py:371
  32.9 16.9 %all-to-all-start.2 = ((bf16[8,64,512]{2,1,0:T(8,128)(2,1)}), bf16[8,64,512]{2,1,0:T(8,128)(2,1)S(1)}, u32[]{:S(2)}, u32[]{:S(2)}) async-start(bf16[8,64,512]{2,1,0:T(8,128)(2,1)} %bitcast.10), calls=%async_computation.2 | async-start | bytes 1048576 | tf_op jit(solution)/shard_map/all_to_all | solution.py:371
  69.9 1.9 collective-permute-start
  70.2 7.4 %collective-permute-start.1 = (bf16[32,2176]{1,0:T(8,128)(2,1)}, bf16[32,2176]{1,0:T(8,128)(2,1)S(1)}, u32[]{:S(2)}, u32[]{:S(2)}) collective-permute-start(bf16[32,2176]{1,0:T(8,128)(2,1)} %get-tuple-element.51), channel_id=1, source_target_pairs={{0,2},{1,3},{2,0},{3,1},{4,6},{5,7},{6,4},{7,5},{8,10},{9,11},{10,... | collective-permute-start | bytes 417800 | tf_op jit(solution)/shard_map/ppermute | solution.py:21
  71.4 8.7 %collective-permute-start.2 = (bf16[32,2176]{1,0:T(8,128)(2,1)}, bf16[32,2176]{1,0:T(8,128)(2,1)S(1)}, u32[]{:S(2)}, u32[]{:S(2)}) collective-permute-start(bf16[32,2176]{1,0:T(8,128)(2,1)} %get-tuple-element.52), channel_id=1, source_target_pairs={{0,3},{1,2},{2,1},{3,0},{4,7},{5,6},{6,5},{7,4},{8,11},{9,10},{10,... | collective-permute-start | bytes 417800 | tf_op jit(solution)/shard_map/ppermute | solution.py:21
  114.6 33.4 %all-to-all-start.3 = ((bf16[8,1,4,128,128]{4,3,2,1,0:T(8,128)(2,1)}), bf16[8,1,4,128,128]{4,3,2,1,0:T(8,128)(2,1)S(1)}, u32[]{:S(2)}, u32[]{:S(2)}) async-start(bf16[8,1,4,128,128]{4,3,2,1,0:T(8,128)(2,1)} %get-tuple-element.44.rest_0_), calls=%async_computation.3 | async-start | bytes 2097152 | tf_op jit(solution)/shard_map/all_to_all | solution.py:371
  118.2 63.3 %all-gather.6.cloned.1.call-start = ((), (), s32[]{:S(2)}) async-start(), calls=%async_computation.10 | async-start | bytes 1179648 | tf_op jit(solution)/shard_map/all_gather | solution.py:471
  148.0 41.5 %copy-start = (bf16[8,1,4,128,128]{4,3,2,1,0:T(8,128)(2,1)}, bf16[8,1,4,128,128]{4,3,2,1,0:T(8,128)(2,1)S(1)}, u32[]{:S(2)}) copy-start(bf16[8,1,4,128,128]{4,3,2,1,0:T(8,128)(2,1)S(1)} %all-to-all-done.3.refs_1_.rest_0_) | copy-start | bytes 3145732
  148.0 41.5 %all-to-all-start.5 = ((bf16[8,1,4,128,128]{4,3,2,1,0:T(8,128)(2,1)}), bf16[8,1,4,128,128]{4,3,2,1,0:T(8,128)(2,1)S(1)}, u32[]{:S(2)}, u32[]{:S(2)}) async-start(bf16[8,1,4,128,128]{4,3,2,1,0:T(8,128)(2,1)} %shard_map.224), calls=%async_computation.5 | async-start | bytes 2097152 | tf_op jit(solution)/shard_map/all_to_all | solution.py:371
  189.6 1.0 copy-start.1
  190.6 30.0 %copy-start.3 = (bf16[32,2048]{1,0:T(8,128)(2,1)S(1)}, bf16[32,2048]{1,0:T(8,128)(2,1)}, u32[]{:S(2)}) copy-start(bf16[32,2048]{1,0:T(8,128)(2,1)} %get-tuple-element.53) | copy-start | bytes 393220
  190.6 29.9 %all-to-all-start.6 = ((bf16[8,32,2048]{2,1,0:T(8,128)(2,1)}), bf16[8,32,2048]{2,1,0:T(8,128)(2,1)S(1)}, u32[]{:S(2)}, u32[]{:S(2)}) async-start(bf16[8,32,2048]{2,1,0:T(8,128)(2,1)} %bitcast.83), calls=%async_computation.6 | async-start | bytes 2097152 | tf_op jit(solution)/shard_map/all_to_all | solution.py:371
  194.3 98.9 %all-gather.8.cloned.1.call-start = ((), (), s32[]{:S(2)}) async-start(), calls=%async_computation.11 | async-start | bytes 2359296 | tf_op jit(solution)/shard_map/all_gather | solution.py:519
  194.3 98.9 %collective-permute-start.7 = (bf16[1000,2048]{1,0:T(8,128)(2,1)}, bf16[1000,2048]{1,0:T(8,128)(2,1)}, u32[]{:S(2)}, u32[]{:S(2)}) collective-permute-start(bf16[1000,2048]{1,0:T(8,128)(2,1)} %bitcast.85), channel_id=1, source_target_pairs={{0,1},{1,0},{2,3},{3,2},{4,5},{5,4},{6,7},{7,6},{8,9},{9,8},{10,11... | collective-permute-start | bytes 12288008 | tf_op jit(solution)/shard_map/ppermute | solution.py:21
  220.6 25.6 %copy-start.10 = (u32[32]{0:T(128)S(1)}, u32[32]{0:T(128)}, u32[]{:S(2)}) copy-start(u32[32]{0:T(128)} %constant.211) | copy-start | bytes 388
  220.9 5.0 %collective-permute-start.6 = (bf16[32,2048]{1,0:T(8,128)(2,1)S(1)}, bf16[32,2048]{1,0:T(8,128)(2,1)S(1)}, u32[]{:S(2)}, u32[]{:S(2)}) collective-permute-start(bf16[32,2048]{1,0:T(8,128)(2,1)S(1)} %multiply_convert_fusion), channel_id=1, source_target_pairs={{0,2},{1,3},{2,0},{3,1},{4,6},{5,7},{6,4},{7,5},{8,10},{9,11},{10,... | collective-permute-start | bytes 393224 | tf_op jit(solution)/shard_map/ppermute | solution.py:21
  226.7 15.4 %all-to-all-start.7 = ((bf16[8,32,512]{2,1,0:T(8,128)(2,1)}), bf16[8,32,512]{2,1,0:T(8,128)(2,1)S(1)}, u32[]{:S(2)}, u32[]{:S(2)}) async-start(bf16[8,32,512]{2,1,0:T(8,128)(2,1)} %bitcast.89), calls=%async_computation.7 | async-start | bytes 524288 | tf_op jit(solution)/shard_map/all_to_all | solution.py:371
  242.1 43.4 %all-to-all-start.8 = ((bf16[8,1,4,128,128]{4,3,2,1,0:T(8,128)(2,1)}), bf16[8,1,4,128,128]{4,3,2,1,0:T(8,128)(2,1)S(1)}, u32[]{:S(2)}, u32[]{:S(2)}) async-start(bf16[8,1,4,128,128]{4,3,2,1,0:T(8,128)(2,1)} %shard_map.227), calls=%async_computation.8 | async-start | bytes 2097152 | tf_op jit(solution)/shard_map/all_to_all | solution.py:371
  248.8 1.9 collective-permute-start.3
  248.8 5.3 %collective-permute-start.4 = (f32[32,640]{1,0:T(8,128)S(1)}, f32[32,640]{1,0:T(8,128)S(1)}, u32[]{:S(2)}, u32[]{:S(2)}) collective-permute-start(f32[32,640]{1,0:T(8,128)S(1)} %get-tuple-element.77), channel_id=1, source_target_pairs={{0,2},{1,3},{2,0},{3,1},{4,6},{5,7},{6,4},{7,5},{8,10},{9,11},{10,... | collective-permute-start | bytes 245768 | tf_op jit(solution)/shard_map/ppermute | solution.py:21
  249.8 5.2 %collective-permute-start.5 = (f32[32,640]{1,0:T(8,128)S(1)}, f32[32,640]{1,0:T(8,128)S(1)}, u32[]{:S(2)}, u32[]{:S(2)}) collective-permute-start(f32[32,640]{1,0:T(8,128)S(1)} %get-tuple-element.78), channel_id=1, source_target_pairs={{0,3},{1,2},{2,1},{3,0},{4,7},{5,6},{6,5},{7,4},{8,11},{9,10},{10,... | collective-permute-start | bytes 245768 | tf_op jit(solution)/shard_map/ppermute | solution.py:21
  285.5 1.0 copy-start.2
  301.4 11.9 %all-to-all-start.9 = ((f32[8,1,64]{2,1,0:T(1,128)}), f32[8,1,64]{2,1,0:T(1,128)S(1)}, u32[]{:S(2)}, u32[]{:S(2)}) async-start(f32[8,1,64]{2,1,0:T(1,128)} %bitcast.108), calls=%async_computation.9 | async-start | bytes 8192 | tf_op jit(solution)/shard_map/all_to_all | solution.py:371
Sparse Core Ops, SparseCore 0:
  10.4 66.7 all-gather.9
  121.2 60.2 all-gather.5
  226.8 61.2 all-gather.7

commit v7 on v6

--- a/solution.py
+++ b/solution.py
@@ -333,7 +333,7 @@
     )(x, weights, pick, mine, gain)
 
 
-def greatest_kernel(states_hbm, full_hbm, own_hbm, other_hbm, best_ref, full, own, other, sems):
+def greatest_kernel(full_hbm, own_hbm, other_hbm, best_ref, full, own, other, sems):
     loads = [
         pltpu.make_async_copy(there, here, sems.at[i])
         for i, (there, here) in enumerate(((full_hbm, full), (own_hbm, own), (other_hbm, other)))
@@ -354,17 +354,17 @@
         best_ref[k : k + 1, :] = best[:, k * width : (k + 1) * width]
 
 
-def greatest_entries(blocks, states, full, own, other):
+def greatest_entries(blocks, full, own, other):
     anywhere = pl.BlockSpec(memory_space=pl.ANY)
     return pl.pallas_call(
         greatest_kernel,
         out_shape=jax.ShapeDtypeStruct((blocks, full.shape[0] // blocks), F32),
-        in_specs=[anywhere] * 4,
+        in_specs=[anywhere] * 3,
         out_specs=pl.BlockSpec(memory_space=VMEM),
         scratch_shapes=[VMEM(x.shape, BF16) for x in (full, own, other)]
         + [pltpu.SemaphoreType.DMA((3,))],
         compiler_params=pltpu.CompilerParams(vmem_limit_bytes=58 << 20),
-    )(states, full, own, other)
+    )(full, own, other)
 
 
 def to_all(x, axis):
@@ -452,7 +452,7 @@
     ordered = lax.dynamic_slice_in_dim(ordered, r * requests, requests, 1)
     old_order = (ordered[steps] - r * requests).reshape(n_head, group).T.reshape(n, sends)
     old_order = jnp.take(old_order, jnp.arange(n) ^ r, axis=0).reshape(requests)
-    counts = (1, 1, 1, 1) if sends == 4 else (sends,)
+    counts = (2, 2) if sends == 4 else (sends,)
     pieces = sort_states(old_order, old_states, n, counts)
     live = (jnp.arange(steps)[None, :] < ordered[steps + 1][:, None]).astype(F32)
     own, kv, *parts = mixer(
@@ -469,8 +469,8 @@
     after_mixer = own.astype(F32) + total[:, :D] * lax.rsqrt(square / D + epsilon)
     after_mixer = after(after_mixer.astype(BF16), feed_weights)
     everything = lax.all_gather(after_mixer, "req", axis=0, tiled=True)
-    for piece in pieces[1:3]:
-        arrived += [to_all(after(piece, after_mixer, *arrived[1:]), "req")]
+    for piece in pieces[1:]:
+        arrived += [to_all(after(piece, after_mixer, *arrived), "req")]
 
     row = jnp.arange(n * rows, dtype=jnp.int32)
     by_owner, by_group, by_step = row // rows, (row % rows) // steps, row % steps
@@ -514,13 +514,12 @@
     final = (hidden * lax.rsqrt(mean_square + epsilon) * token_gain).astype(BF16)
 
     final = jnp.stack([final, swap(final, "head", n_head, 2)])
-    arrived += [to_all(after(piece, final), "req") for piece in pieces[3:]]
     arrived_kv = to_all(after(kv, final).reshape(n, -1, width), "req")
     full = lax.all_gather(final, "req", axis=0, tiled=True).reshape(n * 2 * rows, D)
     new_states = update_states(
         slot_of, arrived_kv.reshape(requests, 2 * steps, width).astype(F32), arrived, steps
     )
-    best = greatest_entries(n, new_states, full, vocab_weight.T, vocab_other)
+    best = greatest_entries(n, full, vocab_weight.T, vocab_other)
     got = jnp.max(to_all(best, "req"), axis=0)
     got = lax.all_gather(got, "head", axis=0).reshape(n_head, 2, rows)
     crossed = jnp.stack([got[i ^ 2, 1] for i in range(n_head)])

time: 328 us -> 300 us (0.915)
  blocking collectives: 49.1 us -> 17.5 us
  waiting for transfers between devices: 155 us -> 163 us
  starting transfers between devices: 40.7 us -> 35 us
    all_to_all x8 -> x7, waiting for transfers between devices: 109 us -> 50 us  [to_all(): return lax.all_to_all(x, axis, split_axis=0, concat_axis=0, tiled=True)]
    all_gather x1, waiting for transfers between devices: 0.01 us -> 37.4 us  [on_device(): lax.all_gather(final, 'req', axis=0, tiled=True).reshape(n * 2 * rows, D)]
    all_to_all x1 -> x0, blocking collectives: 31.7 us -> none  [to_all(): return lax.all_to_all(x, axis, split_axis=0, concat_axis=0, tiled=True)]
    all_gather x1, waiting for transfers between devices: 28.4 us -> 59.9 us  [on_device(): everything = lax.all_gather(after_mixer, 'req', axis=0, tiled=True)]
    all_to_all x8 -> x7, starting transfers between devices: 35.4 us -> 29.3 us  [to_all(): return lax.all_to_all(x, axis, split_axis=0, concat_axis=0, tiled=True)]
  transfers between devices with their start and end apart: 19 -> 18, of which waited for: 13 -> 11; matrix products, arithmetic and copies ran while one was open for 8% -> 8% of each run, Pallas kernels for 8% -> 12%
where the time goes in v7:
time: 300 us; the launch traced here: 299 us
  waiting for transfers between devices  163 us (54%)
  Pallas kernels  35.7 us (12%)
  starting transfers between devices  35 us (12%)
  blocking collectives  17.5 us (6%)
  local copies, waits for them, and re-layouts  16.3 us (5%)
  other arithmetic  15.8 us (5%)
  between operations  15.6 us (5%)
    all_gather x1, waiting for transfers between devices, on_device(): everything = lax.all_gather(after_mixer, 'req', axis=0, tiled=True)  59.9 us
    all_to_all x7, waiting for transfers between devices, to_all(): return lax.all_to_all(x, axis, split_axis=0, concat_axis=0, tiled=True)  50 us
    all_gather x1, waiting for transfers between devices, on_device(): lax.all_gather(final, 'req', axis=0, tiled=True).reshape(n * 2 * rows, D)  37.4 us
    all_to_all x7, starting transfers between devices, to_all(): return lax.all_to_all(x, axis, split_axis=0, concat_axis=0, tiled=True)  29.3 us
    ppermute x8, waiting for transfers between devices, swap(): return lax.ppermute(x, axis, [(i, i ^ offset) for i in range(size)])  14.6 us
    all_gather x1, blocking collectives, on_device(): lax.all_gather(jnp.concatenate([embed_part, gains_high, gains_low, extra]...  11.6 us
    pallas_call x1, Pallas kernels, greatest_entries(): pl.pallas_call(greatest_kernel, out_shape=jax.ShapeDtypeStruct((blocks, f...  8.21 us
    pallas_call x1, Pallas kernels, mixer(): pl.pallas_call(functools.partial(mixer_kernel, counts, owners, heads, cla...  8.14 us
  transfers between devices with their start and end apart: 18, of which 11 were waited for; matrix products, arithmetic and copies ran while one was open for 8% of the time, Pallas kernels for 12%

profile of v7, /device:TPU:0, one launch (start us, length us, event | category | flops | bytes accessed | tf_op | source)
XLA Modules:
  0.0 299.1 jit_solution(15289478407299892666)
XLA Ops:
  7.2 3.0 %pad_maximum_fusion = bf16[2112,512]{1,0:T(8,128)(2,1)} fusion(bf16[704,512]{1,0:T(8,128)(2,1)} %param.38, bf16[704,512]{1,0:T(8,128)(2,1)} %bitcast.91, bf16[704,512]{1,0:T(8,128)(2,1)} %bitcast.92), kind=kLoop, calls=%fused_computation.9 | loop fusion | flops 6488064 | bytes 4325376 | tf_op jit(solution)/shard_map/concatenate | solution.py:391
  11.6 7.3 %all-to-all-start.1 = ((s32[8,1,192]{2,1,0:T(1,128)}), s32[8,1,192]{2,1,0:T(1,128)S(1)}, u32[]{:S(2)}, u32[]{:S(2)}) async-start(s32[8,1,192]{2,1,0:T(1,128)} %reshape.485), calls=%async_computation.1 | async-start | bytes 16384 | tf_op jit(solution)/shard_map/all_to_all | solution.py:371
  19.5 5.9 %all-to-all-done.1 = s32[8,1,192]{2,1,0:T(1,128)S(1)} async-done(((s32[8,1,192]{2,1,0:T(1,128)}), s32[8,1,192]{2,1,0:T(1,128)S(1)}, u32[]{:S(2)}, u32[]{:S(2)}) %all-to-all-start.1) | async-done | bytes 6176 | tf_op jit(solution)/shard_map/all_to_all | solution.py:371
  28.1 5.4 %gather_fusion.1 = bf16[512,512]{1,0:T(8,128)(2,1)} fusion(bf16[4000,512]{1,0:T(8,128)(2,1)} %param.27, s32[1024]{0:T(1024)S(1)} %pad_clamp_fusion.2), kind=kCustom, calls=%fused_computation.1 | custom fusion | bytes 1050624 | tf_op jit(solution)/shard_map/jit(_take)/gather | solution.py:418
  33.4 3.5 %all-to-all-start.2 = ((bf16[8,64,512]{2,1,0:T(8,128)(2,1)}), bf16[8,64,512]{2,1,0:T(8,128)(2,1)S(1)}, u32[]{:S(2)}, u32[]{:S(2)}) async-start(bf16[8,64,512]{2,1,0:T(8,128)(2,1)} %bitcast.10), calls=%async_computation.2 | async-start | bytes 1048576 | tf_op jit(solution)/shard_map/all_to_all | solution.py:371
  39.9 4.6 %shard_map.219 = (bf16[8,2,4,128,128]{4,3,2,1,0:T(8,128)(2,1)}, bf16[8,2,4,128,128]{4,3,2,1,0:T(8,128)(2,1)}) custom-call(s32[32]{0:T(128)} %select_n.235.order_ref, bf16[32,4,128,128]{3,2,1,0:T(8,128)(2,1)} %old_ref.1), custom_call_target="tpu_custom_call" | custom-call | tf_op jit(solution)/shard_map/pallas_call | solution.py:65
  44.8 5.4 %all-to-all-done.2 = bf16[8,64,512]{2,1,0:T(8,128)(2,1)S(1)} async-done(((bf16[8,64,512]{2,1,0:T(8,128)(2,1)}), bf16[8,64,512]{2,1,0:T(8,128)(2,1)S(1)}, u32[]{:S(2)}, u32[]{:S(2)}) %all-to-all-start.2) | async-done | bytes 524320 | tf_op jit(solution)/shard_map/all_to_all | solution.py:371
  50.5 3.8 %all-to-all-start.3 = ((bf16[8,2,4,128,128]{4,3,2,1,0:T(8,128)(2,1)}), bf16[8,2,4,128,128]{4,3,2,1,0:T(8,128)(2,1)S(1)}, u32[]{:S(2)}, u32[]{:S(2)}) async-start(bf16[8,2,4,128,128]{4,3,2,1,0:T(8,128)(2,1)} %get-tuple-element.42.rest_0_), calls=%async_computation.3 | async-start | bytes 4194304 | tf_op jit(solution)/shard_map/all_to_all | solution.py:371
  55.9 11.6 %all_gather.21.emb_ref = bf16[144,2048]{1,0:T(8,128)(2,1)} all-gather(bf16[144,512]{1,0:T(8,128)(2,1)S(1)} %maximum_maximum_fusion), channel_id=1, replica_groups=mesh['req'=8,'head'=4] {'head'}, dimensions={1}, use_global_device_ids=true | all-gather | bytes 737280 | tf_op jit(solution)/shard_map/all_gather | solution.py:447
  67.5 8.1 %shard_map.220 = (bf16[32,2048]{1,0:T(8,128)(2,1)}, bf16[256,512]{1,0:T(8,128)(2,1)}, bf16[32,2176]{1,0:T(8,128)(2,1)}, bf16[32,2176]{1,0:T(8,128)(2,1)}, bf16[3...) custom-call(s32[2]{0:T(128)} %pad_add_fusion.1.me_ref, bf16[144,2048]{1,0:T(8,128)(2,1)} %all_gather.21.emb_ref, ...), custom_call_target="tpu_custom_call" | custom-call | tf_op jit(solution)/shard_map/pallas_call | solution.py:214
  76.0 1.1 collective-permute-start.1
  77.5 5.1 %collective-permute-done.1 = bf16[32,2176]{1,0:T(8,128)(2,1)S(1)} collective-permute-done((bf16[32,2176]{1,0:T(8,128)(2,1)}, bf16[32,2176]{1,0:T(8,128)(2,1)S(1)}, u32[]{:S(2)}, u32[]{:S(2)}) %collective-permute-start.1) | collective-permute-done | bytes 139296 | tf_op jit(solution)/shard_map/ppermute | solution.py:21
  82.7 1.6 collective-permute-done.2
  85.4 1.7 fusion.2.refs_0_
  87.1 14.6 %all-to-all-done.3.refs_2_.refs_1_.rest_0_ = bf16[8,2,4,128,128]{4,3,2,1,0:T(8,128)(2,1)S(1)} async-done(((bf16[8,2,4,128,128]{4,3,2,1,0:T(8,128)(2,1)}), bf16[8,2,4,128,128]{4,3,2,1,0:T(8,128)(2,1)S(1)}, u32[]{:S(2)}, u32[]{:S(2)}) %all-to-all-start.3) | async-done | bytes 2097184 | tf_op jit(solution)/shard_map/all_to_all | solution.py:371
  101.7 1.3 copy-done
  103.1 3.6 %all-to-all-start.4 = ((bf16[8,2,4,128,128]{4,3,2,1,0:T(8,128)(2,1)}), bf16[8,2,4,128,128]{4,3,2,1,0:T(8,128)(2,1)S(1)}, u32[]{:S(2)}, u32[]{:S(2)}) async-start(bf16[8,2,4,128,128]{4,3,2,1,0:T(8,128)(2,1)} %shard_map.223), calls=%async_computation.4 | async-start | bytes 4194304 | tf_op jit(solution)/shard_map/all_to_all | solution.py:371
  108.8 59.9 %all-gather.6.cloned.1.call-done.x_hbm = bf16[256,2048]{1,0:T(8,128)(2,1)} async-done(((bf16[32,2048]{1,0:T(8,128)(2,1)}), bf16[256,2048]{1,0:T(8,128)(2,1)}) %all-gather.6.cloned.1.call-update) | async-done | bytes 1048592 | tf_op jit(solution)/shard_map/all_gather | solution.py:471
  168.8 8.0 %shard_map.222 = (bf16[256,2048]{1,0:T(8,128)(2,1)}, bf16[32,2048]{1,0:T(8,128)(2,1)}) custom-call(bf16[256,2048]{1,0:T(8,128)(2,1)} %all-gather.6.cloned.1.call-done.x_hbm, bf16[4,2112,512]{2,1,0:T(8,128)(2,1)} %bitcast.82, bf16[256,256]{1,0:T(8,128)(2,1)} %fusion.5.pick_ref, bf16[32,256]{1,0:T(8,128)(2,1)} %compare_convert_fusion.mine_ref, f32[1,2048]{1,0:T(1,128)} %bitcast.110), custom_call_target="tpu_custom_call" | custom-call | tf_op jit(solution)/shard_map/pallas_call | solution.py:317
  176.8 1.3 copy-done.1
  178.1 3.9 %all-to-all-start.5 = ((bf16[8,32,2048]{2,1,0:T(8,128)(2,1)}), bf16[8,32,2048]{2,1,0:T(8,128)(2,1)S(1)}, u32[]{:S(2)}, u32[]{:S(2)}) async-start(bf16[8,32,2048]{2,1,0:T(8,128)(2,1)} %bitcast.84), calls=%async_computation.5 | async-start | bytes 2097152 | tf_op jit(solution)/shard_map/all_to_all | solution.py:371
  183.4 24.1 %all-to-all-done.5 = bf16[8,32,2048]{2,1,0:T(8,128)(2,1)S(1)} async-done(((bf16[8,32,2048]{2,1,0:T(8,128)(2,1)}), bf16[8,32,2048]{2,1,0:T(8,128)(2,1)S(1)}, u32[]{:S(2)}, u32[]{:S(2)}) %all-to-all-start.5) | async-done | bytes 1048608 | tf_op jit(solution)/shard_map/all_to_all | solution.py:371
  207.9 1.5 collective-permute-start.6
  209.4 3.5 %collective-permute-done.6 = bf16[32,2048]{1,0:T(8,128)(2,1)S(1)} collective-permute-done((bf16[32,2048]{1,0:T(8,128)(2,1)S(1)}, bf16[32,2048]{1,0:T(8,128)(2,1)S(1)}, u32[]{:S(2)}, u32[]{:S(2)}) %collective-permute-start.6) | collective-permute-done | bytes 131104 | tf_op jit(solution)/shard_map/ppermute | solution.py:21
  216.1 3.8 %all-to-all-start.6 = ((bf16[8,32,512]{2,1,0:T(8,128)(2,1)}), bf16[8,32,512]{2,1,0:T(8,128)(2,1)S(1)}, u32[]{:S(2)}, u32[]{:S(2)}) async-start(bf16[8,32,512]{2,1,0:T(8,128)(2,1)} %bitcast.89), calls=%async_computation.6 | async-start | bytes 524288 | tf_op jit(solution)/shard_map/all_to_all | solution.py:371
  220.1 1.5 collective-permute-start.4
  222.0 3.3 %collective-permute-done.4 = f32[32,640]{1,0:T(8,128)S(1)} collective-permute-done((f32[32,640]{1,0:T(8,128)S(1)}, f32[32,640]{1,0:T(8,128)S(1)}, u32[]{:S(2)}, u32[]{:S(2)}) %collective-permute-start.4) | collective-permute-done | bytes 81952 | tf_op jit(solution)/shard_map/ppermute | solution.py:21
  227.5 37.4 %all-gather.8.cloned.1.call-done = bf16[16,32,2048]{2,1,0:T(8,128)(2,1)} async-done(((bf16[2,32,2048]{2,1,0:T(8,128)(2,1)}), bf16[16,32,2048]{2,1,0:T(8,128)(2,1)}) %all-gather.8.cloned.1.call-update) | async-done | bytes 2097168 | tf_op jit(solution)/shard_map/all_gather | solution.py:518
  264.9 8.2 %shard_map.227 = f32[8,64]{1,0:T(8,128)} custom-call(bf16[512,2048]{1,0:T(8,128)(2,1)} %bitcast.88, bf16[1000,2048]{1,0:T(8,128)(2,1)} %bitcast.86, bf16[1000,2048]{1,0:T(8,128)(2,1)} %collective-permute-done.7.other_hbm), custom_call_target="tpu_custom_call" | custom-call | tf_op jit(solution)/shard_map/pallas_call | solution.py:359
  273.1 3.3 %all-to-all-start.7 = ((f32[8,1,64]{2,1,0:T(1,128)}), f32[8,1,64]{2,1,0:T(1,128)S(1)}, u32[]{:S(2)}, u32[]{:S(2)}) async-start(f32[8,1,64]{2,1,0:T(1,128)} %bitcast.108), calls=%async_computation.7 | async-start | bytes 8192 | tf_op jit(solution)/shard_map/all_to_all | solution.py:371
  278.5 6.8 %shard_map.226 = bf16[32,4,128,128]{3,2,1,0:T(8,128)(2,1)} custom-call(s32[32]{0:T(128)} %select_reduce_fusion.2.slot_ref, f32[32,8,512]{2,1,0:T(8,128)} %convert.2.kv_ref, bf16[8,2,4,128,128]{4,3,2,1,0:T(8,128)(2,1)} %copy-done, bf16[8,2,4,128,128]{4,3,2,1,0:T(8,128)(2,1)} %copy-done.1), custom_call_target="tpu_custom_call" | custom-call | tf_op jit(solution)/shard_map/pallas_call | solution.py:265
  285.6 6.0 %all-reduce = f32[256]{0:T(256)S(1)} all-reduce(f32[256]{0:T(256)S(1)} %dynamic-update-slice), channel_id=3, replica_groups=mesh['req'=8,'head'=4] {'head'}, use_global_device_ids=true, to_apply=%add | all-reduce | flops 256 | bytes 2048
  (148 shorter events, 23.2 us)
Async XLA Ops:
  7.2 79.9 %all-gather.10.cloned.1.call-start = ((), (), s32[]{:S(2)}) async-start(), calls=%async_computation.10 | async-start | bytes 10813440 | tf_op jit(solution)/shard_map/all_gather | solution.py:392
  10.2 0.7 copy-start.4
  10.2 0.7 copy-start.5
  10.2 0.7 copy-start.6
  10.2 8.7 %copy-start.8 = (s32[5]{0:T(128)S(1)}, s32[5]{0:T(128)}, u32[]{:S(2)}) copy-start(s32[5]{0:T(128)} %param.25) | copy-start | bytes 64
  11.6 13.8 %all-to-all-start.1 = ((s32[8,1,192]{2,1,0:T(1,128)}), s32[8,1,192]{2,1,0:T(1,128)S(1)}, u32[]{:S(2)}, u32[]{:S(2)}) async-start(s32[8,1,192]{2,1,0:T(1,128)} %reshape.485), calls=%async_computation.1 | async-start | bytes 16384 | tf_op jit(solution)/shard_map/all_to_all | solution.py:371
  33.4 16.8 %all-to-all-start.2 = ((bf16[8,64,512]{2,1,0:T(8,128)(2,1)}), bf16[8,64,512]{2,1,0:T(8,128)(2,1)S(1)}, u32[]{:S(2)}, u32[]{:S(2)}) async-start(bf16[8,64,512]{2,1,0:T(8,128)(2,1)} %bitcast.10), calls=%async_computation.2 | async-start | bytes 1048576 | tf_op jit(solution)/shard_map/all_to_all | solution.py:371
  50.5 4.5 %copy-start.3 = (f32[4,512]{1,0:T(4,128)S(1)}, f32[4,512]{1,0:T(4,128)}, u32[]{:S(2)}) copy-start(f32[4,512]{1,0:T(4,128)} %param.40) | copy-start | bytes 24580
  50.5 4.5 %copy-start.7 = (f32[512]{0:T(512)S(1)}, f32[512]{0:T(512)}, u32[]{:S(2)}) copy-start(f32[512]{0:T(512)} %param.39) | copy-start | bytes 6148
  50.5 51.2 %all-to-all-start.3 = ((bf16[8,2,4,128,128]{4,3,2,1,0:T(8,128)(2,1)}), bf16[8,2,4,128,128]{4,3,2,1,0:T(8,128)(2,1)S(1)}, u32[]{:S(2)}, u32[]{:S(2)}) async-start(bf16[8,2,4,128,128]{4,3,2,1,0:T(8,128)(2,1)} %get-tuple-element.42.rest_0_), calls=%async_computation.3 | async-start | bytes 4194304 | tf_op jit(solution)/shard_map/all_to_all | solution.py:371
  75.6 1.9 collective-permute-start
  76.0 6.7 %collective-permute-start.1 = (bf16[32,2176]{1,0:T(8,128)(2,1)}, bf16[32,2176]{1,0:T(8,128)(2,1)S(1)}, u32[]{:S(2)}, u32[]{:S(2)}) collective-permute-start(bf16[32,2176]{1,0:T(8,128)(2,1)} %get-tuple-element.47), channel_id=1, source_target_pairs={{0,2},{1,3},{2,0},{3,1},{4,6},{5,7},{6,4},{7,5},{8,10},{9,11},{10,... | collective-permute-start | bytes 417800 | tf_op jit(solution)/shard_map/ppermute | solution.py:21
  77.1 7.2 %collective-permute-start.2 = (bf16[32,2176]{1,0:T(8,128)(2,1)}, bf16[32,2176]{1,0:T(8,128)(2,1)S(1)}, u32[]{:S(2)}, u32[]{:S(2)}) collective-permute-start(bf16[32,2176]{1,0:T(8,128)(2,1)} %get-tuple-element.48), channel_id=1, source_target_pairs={{0,3},{1,2},{2,1},{3,0},{4,7},{5,6},{6,5},{7,4},{8,11},{9,10},{10,... | collective-permute-start | bytes 417800 | tf_op jit(solution)/shard_map/ppermute | solution.py:21
  101.7 1.3 copy-start
  103.1 73.7 %all-to-all-start.4 = ((bf16[8,2,4,128,128]{4,3,2,1,0:T(8,128)(2,1)}), bf16[8,2,4,128,128]{4,3,2,1,0:T(8,128)(2,1)S(1)}, u32[]{:S(2)}, u32[]{:S(2)}) async-start(bf16[8,2,4,128,128]{4,3,2,1,0:T(8,128)(2,1)} %shard_map.223), calls=%async_computation.4 | async-start | bytes 4194304 | tf_op jit(solution)/shard_map/all_to_all | solution.py:371
  106.7 62.1 %all-gather.6.cloned.1.call-start = ((), (), s32[]{:S(2)}) async-start(), calls=%async_computation.8 | async-start | bytes 1179648 | tf_op jit(solution)/shard_map/all_gather | solution.py:471
  176.7 1.3 copy-start.1
  178.1 29.5 %copy-start.2 = (bf16[32,2048]{1,0:T(8,128)(2,1)S(1)}, bf16[32,2048]{1,0:T(8,128)(2,1)}, u32[]{:S(2)}) copy-start(bf16[32,2048]{1,0:T(8,128)(2,1)} %get-tuple-element.49) | copy-start | bytes 393220
  178.1 29.4 %all-to-all-start.5 = ((bf16[8,32,2048]{2,1,0:T(8,128)(2,1)}), bf16[8,32,2048]{2,1,0:T(8,128)(2,1)S(1)}, u32[]{:S(2)}, u32[]{:S(2)}) async-start(bf16[8,32,2048]{2,1,0:T(8,128)(2,1)} %bitcast.84), calls=%async_computation.5 | async-start | bytes 2097152 | tf_op jit(solution)/shard_map/all_to_all | solution.py:371
  182.0 82.9 %all-gather.8.cloned.1.call-start = ((), (), s32[]{:S(2)}) async-start(), calls=%async_computation.9 | async-start | bytes 2359296 | tf_op jit(solution)/shard_map/all_gather | solution.py:518
  182.1 45.4 %collective-permute-start.7 = (bf16[1000,2048]{1,0:T(8,128)(2,1)}, bf16[1000,2048]{1,0:T(8,128)(2,1)}, u32[]{:S(2)}, u32[]{:S(2)}) collective-permute-start(bf16[1000,2048]{1,0:T(8,128)(2,1)} %bitcast.85), channel_id=1, source_target_pairs={{0,1},{1,0},{2,3},{3,2},{4,5},{5,4},{6,7},{7,6},{8,9},{9,8},{10,11... | collective-permute-start | bytes 12288008 | tf_op jit(solution)/shard_map/ppermute | solution.py:21
  183.2 30.4 %copy-start.9 = (u32[32]{0:T(128)S(1)}, u32[32]{0:T(128)}, u32[]{:S(2)}) copy-start(u32[32]{0:T(128)} %constant.211) | copy-start | bytes 388
  207.9 5.0 %collective-permute-start.6 = (bf16[32,2048]{1,0:T(8,128)(2,1)S(1)}, bf16[32,2048]{1,0:T(8,128)(2,1)S(1)}, u32[]{:S(2)}, u32[]{:S(2)}) collective-permute-start(bf16[32,2048]{1,0:T(8,128)(2,1)S(1)} %multiply_convert_fusion), channel_id=1, source_target_pairs={{0,2},{1,3},{2,0},{3,1},{4,6},{5,7},{6,4},{7,5},{8,10},{9,11},{10,... | collective-permute-start | bytes 393224 | tf_op jit(solution)/shard_map/ppermute | solution.py:21
  216.1 57.0 %all-to-all-start.6 = ((bf16[8,32,512]{2,1,0:T(8,128)(2,1)}), bf16[8,32,512]{2,1,0:T(8,128)(2,1)S(1)}, u32[]{:S(2)}, u32[]{:S(2)}) async-start(bf16[8,32,512]{2,1,0:T(8,128)(2,1)} %bitcast.89), calls=%async_computation.6 | async-start | bytes 524288 | tf_op jit(solution)/shard_map/all_to_all | solution.py:371
  220.1 1.9 collective-permute-start.3
  220.1 5.2 %collective-permute-start.4 = (f32[32,640]{1,0:T(8,128)S(1)}, f32[32,640]{1,0:T(8,128)S(1)}, u32[]{:S(2)}, u32[]{:S(2)}) collective-permute-start(f32[32,640]{1,0:T(8,128)S(1)} %get-tuple-element.73), channel_id=1, source_target_pairs={{0,2},{1,3},{2,0},{3,1},{4,6},{5,7},{6,4},{7,5},{8,10},{9,11},{10,... | collective-permute-start | bytes 245768 | tf_op jit(solution)/shard_map/ppermute | solution.py:21
  221.7 4.7 %collective-permute-start.5 = (f32[32,640]{1,0:T(8,128)S(1)}, f32[32,640]{1,0:T(8,128)S(1)}, u32[]{:S(2)}, u32[]{:S(2)}) collective-permute-start(f32[32,640]{1,0:T(8,128)S(1)} %get-tuple-element.74), channel_id=1, source_target_pairs={{0,3},{1,2},{2,1},{3,0},{4,7},{5,6},{6,5},{7,4},{8,11},{9,10},{10,... | collective-permute-start | bytes 245768 | tf_op jit(solution)/shard_map/ppermute | solution.py:21
  273.1 12.2 %all-to-all-start.7 = ((f32[8,1,64]{2,1,0:T(1,128)}), f32[8,1,64]{2,1,0:T(1,128)S(1)}, u32[]{:S(2)}, u32[]{:S(2)}) async-start(f32[8,1,64]{2,1,0:T(1,128)} %bitcast.108), calls=%async_computation.7 | async-start | bytes 8192 | tf_op jit(solution)/shard_map/all_to_all | solution.py:371
Sparse Core Ops, SparseCore 0:
  10.4 65.6 all-gather.9
  109.7 59.0 all-gather.5
  213.8 51.0 all-gather.7

commit v8 on v7

--- a/solution.py
+++ b/solution.py
@@ -367,6 +367,16 @@
     )(full, own, other)
 
 
+def in_order(own, other, r):
+    even = r % 2 == 0
+    return jnp.stack([jnp.where(even, own, other), jnp.where(even, other, own)])
+
+
+def gather_outer(x, n):
+    groups = [list(range(first, n, 2)) for first in (0, 1)]
+    return lax.all_gather(x, "req", axis=0, tiled=True, axis_index_groups=groups)
+
+
 def to_all(x, axis):
     return lax.all_to_all(x, axis, split_axis=0, concat_axis=0, tiled=True)
 
@@ -468,9 +478,10 @@
     square = total[:, D : D + 1] + total[:, D + 127 : D + 128]
     after_mixer = own.astype(F32) + total[:, :D] * lax.rsqrt(square / D + epsilon)
     after_mixer = after(after_mixer.astype(BF16), feed_weights)
-    everything = lax.all_gather(after_mixer, "req", axis=0, tiled=True)
+    pair = in_order(after_mixer, swap(after_mixer, "req", n, 1), r)
+    everything = gather_outer(pair.reshape(2 * rows, D), n)
     for piece in pieces[1:]:
-        arrived += [to_all(after(piece, after_mixer, *arrived), "req")]
+        arrived += [to_all(after(piece, after_mixer[:8, :128]), "req")]
 
     row = jnp.arange(n * rows, dtype=jnp.int32)
     by_owner, by_group, by_step = row // rows, (row % rows) // steps, row % steps
@@ -513,9 +524,12 @@
     token_gain = jnp.repeat(tenant_rows * gains[0][None, :], steps, axis=0)
     final = (hidden * lax.rsqrt(mean_square + epsilon) * token_gain).astype(BF16)
 
-    final = jnp.stack([final, swap(final, "head", n_head, 2)])
+    both = [(i * n_head + j, (i ^ 1) * n_head + (j ^ 2)) for i in range(n) for j in range(n_head)]
+    here = jnp.stack([final, swap(final, "head", n_head, 2)])
+    there = jnp.stack([swap(final, "req", n, 1), lax.ppermute(final, ("req", "head"), both)])
+    pair = in_order(here, there, r)
     arrived_kv = to_all(after(kv, final).reshape(n, -1, width), "req")
-    full = lax.all_gather(final, "req", axis=0, tiled=True).reshape(n * 2 * rows, D)
+    full = gather_outer(pair, n).reshape(n * 2 * rows, D)
     new_states = update_states(
         slot_of, arrived_kv.reshape(requests, 2 * steps, width).astype(F32), arrived, steps
     )

time: 300 us -> 303 us (1.010)
  starting transfers between devices: 35 us -> 39.5 us
    all_gather x2, waiting for transfers between devices: 97.4 us -> 75.4 us  [gather_outer(): lax.all_gather(x, 'req', axis=0, tiled=True, axis_index_groups=groups)]
    ppermute x8 -> x10, waiting for transfers between devices: 14.6 us -> 33.5 us  [swap(): return lax.ppermute(x, axis, [(i, i ^ offset) for i in range(size)])]
    ppermute x8 -> x10, starting transfers between devices: 5.48 us -> 8.76 us  [swap(): return lax.ppermute(x, axis, [(i, i ^ offset) for i in range(size)])]
  transfers between devices with their start and end apart: 18 -> 21, of which waited for: 11 -> 14; matrix products, arithmetic and copies ran while one was open for 8% -> 9% of each run, Pallas kernels for 12% -> 12%
where the time goes in v8:
time: 303 us; the launch traced here: 302 us
  waiting for transfers between devices  160 us (53%)
  starting transfers between devices  39.5 us (13%)
  Pallas kernels  35.7 us (12%)
  blocking collectives  18.3 us (6%)
  other arithmetic  16.8 us (6%)
  between operations  15.6 us (5%)
  local copies, waits for them, and re-layouts  15 us (5%)
    all_gather x2, waiting for transfers between devices, gather_outer(): lax.all_gather(x, 'req', axis=0, tiled=True, axis_index_groups=groups)  75.4 us
    all_to_all x7, waiting for transfers between devices, to_all(): return lax.all_to_all(x, axis, split_axis=0, concat_axis=0, tiled=True)  49.5 us
    ppermute x10, waiting for transfers between devices, swap(): return lax.ppermute(x, axis, [(i, i ^ offset) for i in range(size)])  33.5 us
    all_to_all x7, starting transfers between devices, to_all(): return lax.all_to_all(x, axis, split_axis=0, concat_axis=0, tiled=True)  29.9 us
    all_gather x1, blocking collectives, on_device(): lax.all_gather(jnp.concatenate([embed_part, gains_high, gains_low, extra]...  11.6 us
    ppermute x10, starting transfers between devices, swap(): return lax.ppermute(x, axis, [(i, i ^ offset) for i in range(size)])  8.76 us
    pallas_call x1, Pallas kernels, greatest_entries(): pl.pallas_call(greatest_kernel, out_shape=jax.ShapeDtypeStruct((blocks, f...  8.21 us
    pallas_call x1, Pallas kernels, mixer(): pl.pallas_call(functools.partial(mixer_kernel, counts, owners, heads, cla...  8.13 us
  transfers between devices with their start and end apart: 21, of which 14 were waited for; matrix products, arithmetic and copies ran while one was open for 9% of the time, Pallas kernels for 12%

profile of v8, /device:TPU:0, one launch (start us, length us, event | category | flops | bytes accessed | tf_op | source)
XLA Modules:
  0.0 301.9 jit_solution(8791566235636490484)
XLA Ops:
  7.2 3.0 %pad_maximum_fusion = bf16[2112,512]{1,0:T(8,128)(2,1)} fusion(bf16[704,512]{1,0:T(8,128)(2,1)} %param.38, bf16[704,512]{1,0:T(8,128)(2,1)} %bitcast.100, bf16[704,512]{1,0:T(8,128)(2,1)} %bitcast.101), kind=kLoop, calls=%fused_computation.9 | loop fusion | flops 6488064 | bytes 4325376 | tf_op jit(solution)/shard_map/concatenate | solution.py:401
  11.6 7.3 %all-to-all-start.1 = ((s32[8,1,192]{2,1,0:T(1,128)}), s32[8,1,192]{2,1,0:T(1,128)S(1)}, u32[]{:S(2)}, u32[]{:S(2)}) async-start(s32[8,1,192]{2,1,0:T(1,128)} %reshape.607), calls=%async_computation.1 | async-start | bytes 16384 | tf_op jit(solution)/shard_map/all_to_all | solution.py:381
  19.5 5.9 %all-to-all-done.1 = s32[8,1,192]{2,1,0:T(1,128)S(1)} async-done(((s32[8,1,192]{2,1,0:T(1,128)}), s32[8,1,192]{2,1,0:T(1,128)S(1)}, u32[]{:S(2)}, u32[]{:S(2)}) %all-to-all-start.1) | async-done | bytes 6176 | tf_op jit(solution)/shard_map/all_to_all | solution.py:381
  28.1 5.4 %gather_fusion.1 = bf16[512,512]{1,0:T(8,128)(2,1)} fusion(bf16[4000,512]{1,0:T(8,128)(2,1)} %param.27, s32[1024]{0:T(1024)S(1)} %pad_clamp_fusion.2), kind=kCustom, calls=%fused_computation.1 | custom fusion | bytes 1050624 | tf_op jit(solution)/shard_map/jit(_take)/gather | solution.py:428
  33.4 3.5 %all-to-all-start.2 = ((bf16[8,64,512]{2,1,0:T(8,128)(2,1)}), bf16[8,64,512]{2,1,0:T(8,128)(2,1)S(1)}, u32[]{:S(2)}, u32[]{:S(2)}) async-start(bf16[8,64,512]{2,1,0:T(8,128)(2,1)} %bitcast.10), calls=%async_computation.2 | async-start | bytes 1048576 | tf_op jit(solution)/shard_map/all_to_all | solution.py:381
  40.0 4.6 %shard_map.219 = (bf16[8,2,4,128,128]{4,3,2,1,0:T(8,128)(2,1)}, bf16[8,2,4,128,128]{4,3,2,1,0:T(8,128)(2,1)}) custom-call(s32[32]{0:T(128)} %select_n.283.order_ref, bf16[32,4,128,128]{3,2,1,0:T(8,128)(2,1)} %old_ref.1), custom_call_target="tpu_custom_call" | custom-call | tf_op jit(solution)/shard_map/pallas_call | solution.py:65
  44.8 5.4 %all-to-all-done.2 = bf16[8,64,512]{2,1,0:T(8,128)(2,1)S(1)} async-done(((bf16[8,64,512]{2,1,0:T(8,128)(2,1)}), bf16[8,64,512]{2,1,0:T(8,128)(2,1)S(1)}, u32[]{:S(2)}, u32[]{:S(2)}) %all-to-all-start.2) | async-done | bytes 524320 | tf_op jit(solution)/shard_map/all_to_all | solution.py:381
  50.5 3.8 %all-to-all-start.3 = ((bf16[8,2,4,128,128]{4,3,2,1,0:T(8,128)(2,1)}), bf16[8,2,4,128,128]{4,3,2,1,0:T(8,128)(2,1)S(1)}, u32[]{:S(2)}, u32[]{:S(2)}) async-start(bf16[8,2,4,128,128]{4,3,2,1,0:T(8,128)(2,1)} %get-tuple-element.42.rest_0_), calls=%async_computation.3 | async-start | bytes 4194304 | tf_op jit(solution)/shard_map/all_to_all | solution.py:381
  55.9 11.6 %all_gather.21.emb_ref = bf16[144,2048]{1,0:T(8,128)(2,1)} all-gather(bf16[144,512]{1,0:T(8,128)(2,1)S(1)} %maximum_maximum_fusion), channel_id=1, replica_groups=mesh['req'=8,'head'=4] {'head'}, dimensions={1}, use_global_device_ids=true | all-gather | bytes 737280 | tf_op jit(solution)/shard_map/all_gather | solution.py:457
  67.5 8.1 %shard_map.220 = (bf16[32,2048]{1,0:T(8,128)(2,1)}, bf16[256,512]{1,0:T(8,128)(2,1)}, bf16[32,2176]{1,0:T(8,128)(2,1)}, bf16[32,2176]{1,0:T(8,128)(2,1)}, bf16[3...) custom-call(s32[2]{0:T(128)} %pad_add_fusion.1.me_ref, bf16[144,2048]{1,0:T(8,128)(2,1)} %all_gather.21.emb_ref, ...), custom_call_target="tpu_custom_call" | custom-call | tf_op jit(solution)/shard_map/pallas_call | solution.py:214
  77.5 5.1 %collective-permute-done.1 = bf16[32,2176]{1,0:T(8,128)(2,1)S(1)} collective-permute-done((bf16[32,2176]{1,0:T(8,128)(2,1)}, bf16[32,2176]{1,0:T(8,128)(2,1)S(1)}, u32[]{:S(2)}, u32[]{:S(2)}) %collective-permute-start.1) | collective-permute-done | bytes 139296 | tf_op jit(solution)/shard_map/ppermute | solution.py:21
  85.4 1.7 fusion.2.refs_0_
  88.3 13.4 %all-to-all-done.3.refs_1_.rest_0_ = bf16[8,2,4,128,128]{4,3,2,1,0:T(8,128)(2,1)S(1)} async-done(((bf16[8,2,4,128,128]{4,3,2,1,0:T(8,128)(2,1)}), bf16[8,2,4,128,128]{4,3,2,1,0:T(8,128)(2,1)S(1)}, u32[]{:S(2)}, u32[]{:S(2)}) %all-to-all-start.3) | async-done | bytes 2097184 | tf_op jit(solution)/shard_map/all_to_all | solution.py:381
  101.7 4.3 %all-to-all-start.4 = ((bf16[8,2,4,128,128]{4,3,2,1,0:T(8,128)(2,1)}), bf16[8,2,4,128,128]{4,3,2,1,0:T(8,128)(2,1)}, u32[]{:S(2)}, u32[]{:S(2)}) async-start(bf16[8,2,4,128,128]{4,3,2,1,0:T(8,128)(2,1)} %shard_map.223), calls=%async_computation.4 | async-start | bytes 4194304 | tf_op jit(solution)/shard_map/all_to_all | solution.py:381
  106.3 1.7 collective-permute-start.3
  108.0 18.5 %collective-permute-done.3 = bf16[32,2048]{1,0:T(8,128)(2,1)S(1)} collective-permute-done((bf16[32,2048]{1,0:T(8,128)(2,1)S(1)}, bf16[32,2048]{1,0:T(8,128)(2,1)S(1)}, u32[]{:S(2)}, u32[]{:S(2)}) %collective-permute-start.3) | collective-permute-done | bytes 131104 | tf_op jit(solution)/shard_map/ppermute | solution.py:21
  128.7 40.6 %all-gather.6.cloned.1.call-done.x_hbm = bf16[256,2048]{1,0:T(8,128)(2,1)} async-done(((bf16[64,2048]{1,0:T(8,128)(2,1)}), bf16[256,2048]{1,0:T(8,128)(2,1)}) %all-gather.6.cloned.1.call-update) | async-done | bytes 1048592 | tf_op jit(solution)/shard_map/all_gather | solution.py:377
  169.3 8.0 %shard_map.222 = (bf16[256,2048]{1,0:T(8,128)(2,1)}, bf16[32,2048]{1,0:T(8,128)(2,1)}) custom-call(bf16[256,2048]{1,0:T(8,128)(2,1)} %all-gather.6.cloned.1.call-done.x_hbm, bf16[4,2112,512]{2,1,0:T(8,128)(2,1)} %bitcast.89, bf16[256,256]{1,0:T(8,128)(2,1)} %fusion.5.pick_ref, bf16[32,256]{1,0:T(8,128)(2,1)} %compare_convert_fusion.mine_ref, f32[1,2048]{1,0:T(1,128)} %bitcast.120), custom_call_target="tpu_custom_call" | custom-call | tf_op jit(solution)/shard_map/pallas_call | solution.py:317
  177.3 3.7 %all-to-all-start.5 = ((bf16[8,32,2048]{2,1,0:T(8,128)(2,1)}), bf16[8,32,2048]{2,1,0:T(8,128)(2,1)S(1)}, u32[]{:S(2)}, u32[]{:S(2)}) async-start(bf16[8,32,2048]{2,1,0:T(8,128)(2,1)} %bitcast.91), calls=%async_computation.5 | async-start | bytes 2097152 | tf_op jit(solution)/shard_map/all_to_all | solution.py:381
  182.4 24.8 %all-to-all-done.5 = bf16[8,32,2048]{2,1,0:T(8,128)(2,1)S(1)} async-done(((bf16[8,32,2048]{2,1,0:T(8,128)(2,1)}), bf16[8,32,2048]{2,1,0:T(8,128)(2,1)S(1)}, u32[]{:S(2)}, u32[]{:S(2)}) %all-to-all-start.5) | async-done | bytes 1048608 | tf_op jit(solution)/shard_map/all_to_all | solution.py:381
  207.6 1.6 collective-permute-start.7
  211.2 1.7 collective-permute-done.7
  212.9 2.2 collective-permute-done.8
  215.0 1.9 collective-permute-done.9
  220.1 3.8 %all-to-all-start.6 = ((bf16[8,32,512]{2,1,0:T(8,128)(2,1)}), bf16[8,32,512]{2,1,0:T(8,128)(2,1)S(1)}, u32[]{:S(2)}, u32[]{:S(2)}) async-start(bf16[8,32,512]{2,1,0:T(8,128)(2,1)} %bitcast.98), calls=%async_computation.6 | async-start | bytes 524288 | tf_op jit(solution)/shard_map/all_to_all | solution.py:381
  224.4 1.6 collective-permute-start.5
  226.3 3.2 %collective-permute-done.5 = f32[32,640]{1,0:T(8,128)S(1)} collective-permute-done((f32[32,640]{1,0:T(8,128)S(1)}, f32[32,640]{1,0:T(8,128)S(1)}, u32[]{:S(2)}, u32[]{:S(2)}) %collective-permute-start.5) | collective-permute-done | bytes 81952 | tf_op jit(solution)/shard_map/ppermute | solution.py:21
  231.8 34.9 %all-gather.8.cloned.1.call-done = bf16[8,2,32,2048]{3,2,1,0:T(8,128)(2,1)} async-done(((bf16[2,2,32,2048]{3,2,1,0:T(8,128)(2,1)}), bf16[8,2,32,2048]{3,2,1,0:T(8,128)(2,1)}) %all-gather.8.cloned.1.call-update) | async-done | bytes 2097168 | tf_op jit(solution)/shard_map/all_gather | solution.py:377
  266.7 8.2 %shard_map.227 = f32[8,64]{1,0:T(8,128)} custom-call(bf16[512,2048]{1,0:T(8,128)(2,1)} %bitcast.95, bf16[1000,2048]{1,0:T(8,128)(2,1)} %bitcast.93, bf16[1000,2048]{1,0:T(8,128)(2,1)} %collective-permute-done.10.other_hbm), custom_call_target="tpu_custom_call" | custom-call | tf_op jit(solution)/shard_map/pallas_call | solution.py:359
  274.9 3.5 %all-to-all-start.7 = ((f32[8,1,64]{2,1,0:T(1,128)}), f32[8,1,64]{2,1,0:T(1,128)S(1)}, u32[]{:S(2)}, u32[]{:S(2)}) async-start(f32[8,1,64]{2,1,0:T(1,128)} %bitcast.118), calls=%async_computation.7 | async-start | bytes 8192 | tf_op jit(solution)/shard_map/all_to_all | solution.py:381
  280.5 6.8 %shard_map.226 = bf16[32,4,128,128]{3,2,1,0:T(8,128)(2,1)} custom-call(s32[32]{0:T(128)} %select_reduce_fusion.2.slot_ref, f32[32,8,512]{2,1,0:T(8,128)} %convert.2.kv_ref, bf16[8,2,4,128,128]{4,3,2,1,0:T(8,128)(2,1)} %copy-done, bf16[8,2,4,128,128]{4,3,2,1,0:T(8,128)(2,1)} %all-to-all-done.4.refs_2_.rest_1_), custom_call_target="tpu_custom_call" | custom-call | tf_op jit(solution)/shard_map/pallas_call | solution.py:265
  287.6 6.7 %all-reduce = f32[256]{0:T(256)S(1)} all-reduce(f32[256]{0:T(256)S(1)} %dynamic-update-slice), channel_id=3, replica_groups=mesh['req'=8,'head'=4] {'head'}, use_global_device_ids=true, to_apply=%add | all-reduce | flops 256 | bytes 2048
  (160 shorter events, 29.8 us)
Async XLA Ops:
  7.2 79.9 %all-gather.10.cloned.1.call-start = ((), (), s32[]{:S(2)}) async-start(), calls=%async_computation.10 | async-start | bytes 10813440 | tf_op jit(solution)/shard_map/all_gather | solution.py:402
  10.2 0.7 copy-start.5
  10.2 0.7 copy-start.6
  10.2 0.7 copy-start.7
  10.2 8.7 %copy-start.9 = (s32[5]{0:T(128)S(1)}, s32[5]{0:T(128)}, u32[]{:S(2)}) copy-start(s32[5]{0:T(128)} %param.25) | copy-start | bytes 64
  11.6 13.8 %all-to-all-start.1 = ((s32[8,1,192]{2,1,0:T(1,128)}), s32[8,1,192]{2,1,0:T(1,128)S(1)}, u32[]{:S(2)}, u32[]{:S(2)}) async-start(s32[8,1,192]{2,1,0:T(1,128)} %reshape.607), calls=%async_computation.1 | async-start | bytes 16384 | tf_op jit(solution)/shard_map/all_to_all | solution.py:381
  33.4 16.8 %all-to-all-start.2 = ((bf16[8,64,512]{2,1,0:T(8,128)(2,1)}), bf16[8,64,512]{2,1,0:T(8,128)(2,1)S(1)}, u32[]{:S(2)}, u32[]{:S(2)}) async-start(bf16[8,64,512]{2,1,0:T(8,128)(2,1)} %bitcast.10), calls=%async_computation.2 | async-start | bytes 1048576 | tf_op jit(solution)/shard_map/all_to_all | solution.py:381
  50.5 4.5 %copy-start.4 = (f32[4,512]{1,0:T(4,128)S(1)}, f32[4,512]{1,0:T(4,128)}, u32[]{:S(2)}) copy-start(f32[4,512]{1,0:T(4,128)} %param.40) | copy-start | bytes 24580
  50.5 4.5 %copy-start.8 = (f32[512]{0:T(512)S(1)}, f32[512]{0:T(512)}, u32[]{:S(2)}) copy-start(f32[512]{0:T(512)} %param.39) | copy-start | bytes 6148
  50.5 51.2 %all-to-all-start.3 = ((bf16[8,2,4,128,128]{4,3,2,1,0:T(8,128)(2,1)}), bf16[8,2,4,128,128]{4,3,2,1,0:T(8,128)(2,1)S(1)}, u32[]{:S(2)}, u32[]{:S(2)}) async-start(bf16[8,2,4,128,128]{4,3,2,1,0:T(8,128)(2,1)} %get-tuple-element.42.rest_0_), calls=%async_computation.3 | async-start | bytes 4194304 | tf_op jit(solution)/shard_map/all_to_all | solution.py:381
  75.6 1.9 collective-permute-start
  75.9 6.7 %collective-permute-start.1 = (bf16[32,2176]{1,0:T(8,128)(2,1)}, bf16[32,2176]{1,0:T(8,128)(2,1)S(1)}, u32[]{:S(2)}, u32[]{:S(2)}) collective-permute-start(bf16[32,2176]{1,0:T(8,128)(2,1)} %get-tuple-element.47), channel_id=1, source_target_pairs={{0,2},{1,3},{2,0},{3,1},{4,6},{5,7},{6,4},{7,5},{8,10},{9,11},{10,... | collective-permute-start | bytes 417800 | tf_op jit(solution)/shard_map/ppermute | solution.py:21
  77.1 7.2 %collective-permute-start.2 = (bf16[32,2176]{1,0:T(8,128)(2,1)}, bf16[32,2176]{1,0:T(8,128)(2,1)S(1)}, u32[]{:S(2)}, u32[]{:S(2)}) collective-permute-start(bf16[32,2176]{1,0:T(8,128)(2,1)} %get-tuple-element.48), channel_id=1, source_target_pairs={{0,3},{1,2},{2,1},{3,0},{4,7},{5,6},{6,5},{7,4},{8,11},{9,10},{10,... | collective-permute-start | bytes 417800 | tf_op jit(solution)/shard_map/ppermute | solution.py:21
  88.3 18.0 %copy-start.1 = (bf16[32,2048]{1,0:T(8,128)(2,1)S(1)}, bf16[32,2048]{1,0:T(8,128)(2,1)}, u32[]{:S(2)}) copy-start(bf16[32,2048]{1,0:T(8,128)(2,1)} %shard_map.221) | copy-start | bytes 393220
  101.7 24.8 %copy-start = (bf16[8,2,4,128,128]{4,3,2,1,0:T(8,128)(2,1)}, bf16[8,2,4,128,128]{4,3,2,1,0:T(8,128)(2,1)S(1)}, u32[]{:S(2)}) copy-start(bf16[8,2,4,128,128]{4,3,2,1,0:T(8,128)(2,1)S(1)} %all-to-all-done.3.refs_1_.rest_0_) | copy-start | bytes 6291460
  101.7 75.5 %all-to-all-start.4 = ((bf16[8,2,4,128,128]{4,3,2,1,0:T(8,128)(2,1)}), bf16[8,2,4,128,128]{4,3,2,1,0:T(8,128)(2,1)}, u32[]{:S(2)}, u32[]{:S(2)}) async-start(bf16[8,2,4,128,128]{4,3,2,1,0:T(8,128)(2,1)} %shard_map.223), calls=%async_computation.4 | async-start | bytes 4194304 | tf_op jit(solution)/shard_map/all_to_all | solution.py:381
  106.1 63.2 %all-gather.6.cloned.1.call-start = ((), (), s32[]{:S(2)}) async-start(), calls=%async_computation.8 | async-start | bytes 1310720 | tf_op jit(solution)/shard_map/all_gather | solution.py:377
  106.3 20.2 %collective-permute-start.3 = (bf16[32,2048]{1,0:T(8,128)(2,1)S(1)}, bf16[32,2048]{1,0:T(8,128)(2,1)S(1)}, u32[]{:S(2)}, u32[]{:S(2)}) collective-permute-start(bf16[32,2048]{1,0:T(8,128)(2,1)S(1)} %copy-done.1), channel_id=1, source_target_pairs={{0,4},{4,0},{8,12},{12,8},{16,20},{20,16},{24,28},{28,24},{1,5},{5... | collective-permute-start | bytes 393224 | tf_op jit(solution)/shard_map/ppermute | solution.py:21
  177.3 30.1 %copy-start.3 = (bf16[32,2048]{1,0:T(8,128)(2,1)S(1)}, bf16[32,2048]{1,0:T(8,128)(2,1)}, u32[]{:S(2)}) copy-start(bf16[32,2048]{1,0:T(8,128)(2,1)} %get-tuple-element.49) | copy-start | bytes 393220
  177.3 29.9 %all-to-all-start.5 = ((bf16[8,32,2048]{2,1,0:T(8,128)(2,1)}), bf16[8,32,2048]{2,1,0:T(8,128)(2,1)S(1)}, u32[]{:S(2)}, u32[]{:S(2)}) async-start(bf16[8,32,2048]{2,1,0:T(8,128)(2,1)} %bitcast.91), calls=%async_computation.5 | async-start | bytes 2097152 | tf_op jit(solution)/shard_map/all_to_all | solution.py:381
  181.0 85.7 %all-gather.8.cloned.1.call-start = ((), (), s32[]{:S(2)}) async-start(), calls=%async_computation.9 | async-start | bytes 2621440 | tf_op jit(solution)/shard_map/all_gather | solution.py:377
  181.1 50.7 %collective-permute-start.10 = (bf16[1000,2048]{1,0:T(8,128)(2,1)}, bf16[1000,2048]{1,0:T(8,128)(2,1)}, u32[]{:S(2)}, u32[]{:S(2)}) collective-permute-start(bf16[1000,2048]{1,0:T(8,128)(2,1)} %bitcast.92), channel_id=1, source_target_pairs={{0,1},{1,0},{2,3},{3,2},{4,5},{5,4},{6,7},{7,6},{8,9},{9,8},{10,11... | collective-permute-start | bytes 12288008 | tf_op jit(solution)/shard_map/ppermute | solution.py:21
  207.3 10.5 %copy-start.10 = (u32[32]{0:T(128)S(1)}, u32[32]{0:T(128)}, u32[]{:S(2)}) copy-start(u32[32]{0:T(128)} %constant.222) | copy-start | bytes 388
  207.6 12.5 %copy-start.2 = (bf16[32,2048]{1,0:T(8,128)(2,1)}, bf16[32,2048]{1,0:T(8,128)(2,1)S(1)}, u32[]{:S(2)}) copy-start(bf16[32,2048]{1,0:T(8,128)(2,1)S(1)} %multiply_convert_fusion.refs_1_) | copy-start | bytes 393220
  207.6 5.2 %collective-permute-start.7 = (bf16[32,2048]{1,0:T(8,128)(2,1)S(1)}, bf16[32,2048]{1,0:T(8,128)(2,1)S(1)}, u32[]{:S(2)}, u32[]{:S(2)}) collective-permute-start(bf16[32,2048]{1,0:T(8,128)(2,1)S(1)} %multiply_convert_fusion.refs_1_), channel_id=1, source_target_pairs={{0,2},{1,3},{2,0},{3,1},{4,6},{5,7},{6,4},{7,5},{8,10},{9,11},{10,... | collective-permute-start | bytes 393224 | tf_op jit(solution)/shard_map/ppermute | solution.py:21
  209.3 5.7 %collective-permute-start.8 = (bf16[32,2048]{1,0:T(8,128)(2,1)S(1)}, bf16[32,2048]{1,0:T(8,128)(2,1)S(1)}, u32[]{:S(2)}, u32[]{:S(2)}) collective-permute-start(bf16[32,2048]{1,0:T(8,128)(2,1)S(1)} %multiply_convert_fusion.refs_1_), channel_id=1, source_target_pairs={{0,4},{4,0},{8,12},{12,8},{16,20},{20,16},{24,28},{28,24},{1,5},{5... | collective-permute-start | bytes 393224 | tf_op jit(solution)/shard_map/ppermute | solution.py:21
  210.7 6.3 %collective-permute-start.9 = (bf16[32,2048]{1,0:T(8,128)(2,1)S(1)}, bf16[32,2048]{1,0:T(8,128)(2,1)S(1)}, u32[]{:S(2)}, u32[]{:S(2)}) collective-permute-start(bf16[32,2048]{1,0:T(8,128)(2,1)S(1)} %multiply_convert_fusion.refs_1_), channel_id=1, source_target_pairs={{0,6},{1,7},{2,4},{3,5},{4,2},{5,3},{6,0},{7,1},{8,14},{9,15},{10,... | collective-permute-start | bytes 393224 | tf_op jit(solution)/shard_map/ppermute | solution.py:529
  220.1 54.8 %all-to-all-start.6 = ((bf16[8,32,512]{2,1,0:T(8,128)(2,1)}), bf16[8,32,512]{2,1,0:T(8,128)(2,1)S(1)}, u32[]{:S(2)}, u32[]{:S(2)}) async-start(bf16[8,32,512]{2,1,0:T(8,128)(2,1)} %bitcast.98), calls=%async_computation.6 | async-start | bytes 524288 | tf_op jit(solution)/shard_map/all_to_all | solution.py:381
  224.3 1.9 collective-permute-start.4
  224.4 5.1 %collective-permute-start.5 = (f32[32,640]{1,0:T(8,128)S(1)}, f32[32,640]{1,0:T(8,128)S(1)}, u32[]{:S(2)}, u32[]{:S(2)}) collective-permute-start(f32[32,640]{1,0:T(8,128)S(1)} %get-tuple-element.77), channel_id=1, source_target_pairs={{0,2},{1,3},{2,0},{3,1},{4,6},{5,7},{6,4},{7,5},{8,10},{9,11},{10,... | collective-permute-start | bytes 245768 | tf_op jit(solution)/shard_map/ppermute | solution.py:21
  226.0 4.7 %collective-permute-start.6 = (f32[32,640]{1,0:T(8,128)S(1)}, f32[32,640]{1,0:T(8,128)S(1)}, u32[]{:S(2)}, u32[]{:S(2)}) collective-permute-start(f32[32,640]{1,0:T(8,128)S(1)} %get-tuple-element.78), channel_id=1, source_target_pairs={{0,3},{1,2},{2,1},{3,0},{4,7},{5,6},{6,5},{7,4},{8,11},{9,10},{10,... | collective-permute-start | bytes 245768 | tf_op jit(solution)/shard_map/ppermute | solution.py:21
  274.9 12.4 %all-to-all-start.7 = ((f32[8,1,64]{2,1,0:T(1,128)}), f32[8,1,64]{2,1,0:T(1,128)S(1)}, u32[]{:S(2)}, u32[]{:S(2)}) async-start(f32[8,1,64]{2,1,0:T(1,128)} %bitcast.118), calls=%async_computation.7 | async-start | bytes 8192 | tf_op jit(solution)/shard_map/all_to_all | solution.py:381
Sparse Core Ops, SparseCore 0:
  10.4 65.6 all-gather.9
  127.4 41.8 all-gather.5
  218.0 48.6 all-gather.7

commit v9 on v7

--- a/solution.py
+++ b/solution.py
@@ -367,6 +367,24 @@
     )(full, own, other)
 
 
+def exchange(block, dim, n, n_head):
+    if dim == "outer":
+        got = [swap(block, "req", n, 2 * j) for j in range(1, n // 2)]
+    elif dim == "inner":
+        got = [swap(block, "req", n, 1)]
+    else:
+        got = [swap(block, "head", n_head, 2)]
+    return jnp.stack([block] + got)
+
+
+def gather_by(block, dims, n, n_head):
+    rank = block.ndim
+    for dim in dims:
+        block = exchange(block, dim, n, n_head)
+    at = [dims[::-1].index(dim) for dim in ("outer", "inner", "cross")]
+    return block.transpose(at + list(range(len(dims), len(dims) + rank)))
+
+
 def to_all(x, axis):
     return lax.all_to_all(x, axis, split_axis=0, concat_axis=0, tiled=True)
 
@@ -469,8 +487,8 @@
     after_mixer = own.astype(F32) + total[:, :D] * lax.rsqrt(square / D + epsilon)
     after_mixer = after(after_mixer.astype(BF16), feed_weights)
     everything = lax.all_gather(after_mixer, "req", axis=0, tiled=True)
-    for piece in pieces[1:]:
-        arrived += [to_all(after(piece, after_mixer, *arrived), "req")]
+    arrived += [to_all(after(piece, after_mixer[:8, :128]), "req") for piece in pieces[1:]]
+    arrived_kv = to_all(kv.reshape(n, -1, width), "req")
 
     row = jnp.arange(n * rows, dtype=jnp.int32)
     by_owner, by_group, by_step = row // rows, (row % rows) // steps, row % steps
@@ -482,7 +500,7 @@
     pick = (wanted[None, :] == row[:, None]).astype(BF16)
     mine = (wanted[None, :] == (r * rows + row[:rows])[:, None]).astype(BF16)
     down, kept = feed_forward(everything, feed_weights, pick, mine, feed_gain[None])
-    down = after(down, *arrived)
+    down = after(down, arrived_kv, *arrived)
     hidden = kept.astype(F32) + jnp.sum(to_all(down.reshape(n, rows, D), "req").astype(F32), axis=0)
     mean_square = jnp.mean(hidden * hidden, axis=1, keepdims=True)
 
@@ -513,13 +531,20 @@
     token_gain = jnp.repeat(tenant_rows * gains[0][None, :], steps, axis=0)
     final = (hidden * lax.rsqrt(mean_square + epsilon) * token_gain).astype(BF16)
 
-    final = jnp.stack([final, swap(final, "head", n_head, 2)])
-    arrived_kv = to_all(after(kv, final).reshape(n, -1, width), "req")
-    full = lax.all_gather(final, "req", axis=0, tiled=True).reshape(n * 2 * rows, D)
+    c1, c2 = D * 7 // 16, D * 13 // 16
+    full = jnp.concatenate(
+        [
+            gather_by(final[:, :c1], ("outer", "inner", "cross"), n, n_head),
+            gather_by(final[:, c1:c2], ("cross", "outer", "inner"), n, n_head),
+            gather_by(final[:, c2:], ("inner", "cross", "outer"), n, n_head),
+        ],
+        axis=-1,
+    ).reshape(n * 2 * rows, D)
     new_states = update_states(
         slot_of, arrived_kv.reshape(requests, 2 * steps, width).astype(F32), arrived, steps
     )
     best = greatest_entries(n, full, vocab_weight.T, vocab_other)
+    best = jnp.take(best, jnp.arange(n) ^ r, axis=0)
     got = jnp.max(to_all(best, "req"), axis=0)
     got = lax.all_gather(got, "head", axis=0).reshape(n_head, 2, rows)
     crossed = jnp.stack([got[i ^ 2, 1] for i in range(n_head)])

time: 300 us -> 315 us (1.050)
  blocking collectives: 17.5 us -> 31 us
  waiting for transfers between devices: 163 us -> 152 us
  starting transfers between devices: 35 us -> 45.8 us
    all_gather x1 -> x0, waiting for transfers between devices: 37.4 us -> none  [on_device(): lax.all_gather(final, 'req', axis=0, tiled=True).reshape(n * 2 * rows, D)]
    all_to_all x7 -> x6, waiting for transfers between devices: 50 us -> 68.3 us  [to_all(): return lax.all_to_all(x, axis, split_axis=0, concat_axis=0, tiled=True)]
    ppermute x8 -> x22, starting transfers between devices: 5.48 us -> 19.4 us  [swap(): return lax.ppermute(x, axis, [(i, i ^ offset) for i in range(size)])]
    all_to_all x0 -> x1, blocking collectives: none -> 13.7 us  [to_all(): return lax.all_to_all(x, axis, split_axis=0, concat_axis=0, tiled=True)]
    ppermute x8 -> x22, waiting for transfers between devices: 14.6 us -> 25.2 us  [swap(): return lax.ppermute(x, axis, [(i, i ^ offset) for i in range(size)])]
    all_to_all x7 -> x6, starting transfers between devices: 29.3 us -> 26.1 us  [to_all(): return lax.all_to_all(x, axis, split_axis=0, concat_axis=0, tiled=True)]
  transfers between devices with their start and end apart: 18 -> 30, of which waited for: 11 -> 17; matrix products, arithmetic and copies ran while one was open for 8% -> 8% of each run, Pallas kernels for 12% -> 9%
where the time goes in v9:
time: 315 us; the launch traced here: 314 us
  waiting for transfers between devices  152 us (48%)
  starting transfers between devices  45.8 us (15%)
  Pallas kernels  35.7 us (11%)
  blocking collectives  31 us (10%)
  local copies, waits for them, and re-layouts  17.6 us (6%)
  between operations  16.1 us (5%)
  other arithmetic  15.3 us (5%)
    all_to_all x6, waiting for transfers between devices, to_all(): return lax.all_to_all(x, axis, split_axis=0, concat_axis=0, tiled=True)  68.3 us
    all_gather x1, waiting for transfers between devices, on_device(): everything = lax.all_gather(after_mixer, 'req', axis=0, tiled=True)  57.9 us
    all_to_all x6, starting transfers between devices, to_all(): return lax.all_to_all(x, axis, split_axis=0, concat_axis=0, tiled=True)  26.1 us
    ppermute x22, waiting for transfers between devices, swap(): return lax.ppermute(x, axis, [(i, i ^ offset) for i in range(size)])  25.2 us
    ppermute x22, starting transfers between devices, swap(): return lax.ppermute(x, axis, [(i, i ^ offset) for i in range(size)])  19.4 us
    all_to_all x1, blocking collectives, to_all(): return lax.all_to_all(x, axis, split_axis=0, concat_axis=0, tiled=True)  13.7 us
    all_gather x1, blocking collectives, on_device(): lax.all_gather(jnp.concatenate([embed_part, gains_high, gains_low, extra]...  11.6 us
    pallas_call x1, Pallas kernels, greatest_entries(): pl.pallas_call(greatest_kernel, out_shape=jax.ShapeDtypeStruct((blocks, f...  8.22 us
  transfers between devices with their start and end apart: 30, of which 17 were waited for; matrix products, arithmetic and copies ran while one was open for 8% of the time, Pallas kernels for 9%

profile of v9, /device:TPU:0, one launch (start us, length us, event | category | flops | bytes accessed | tf_op | source)
XLA Modules:
  0.0 313.7 jit_solution(10011742288049515472)
XLA Ops:
  7.2 3.0 pad_maximum_fusion
  11.6 7.3 %all-to-all-start.1 = ((s32[8,1,192]{2,1,0:T(1,128)}), s32[8,1,192]{2,1,0:T(1,128)S(1)}, u32[]{:S(2)}, u32[]{:S(2)}) async-start(s32[8,1,192]{2,1,0:T(1,128)} %reshape.516), calls=%async_computation.1 | async-start | bytes 16384 | tf_op jit(solution)/shard_map/all_to_all | solution.py:389
  19.6 5.8 %all-to-all-done.1 = s32[8,1,192]{2,1,0:T(1,128)S(1)} async-done(((s32[8,1,192]{2,1,0:T(1,128)}), s32[8,1,192]{2,1,0:T(1,128)S(1)}, u32[]{:S(2)}, u32[]{:S(2)}) %all-to-all-start.1) | async-done | bytes 6176 | tf_op jit(solution)/shard_map/all_to_all | solution.py:389
  28.1 5.3 %gather_fusion.1 = bf16[512,512]{1,0:T(8,128)(2,1)} fusion(bf16[4000,512]{1,0:T(8,128)(2,1)} %param.27, s32[1024]{0:T(1024)S(1)} %pad_clamp_fusion.2), kind=kCustom, calls=%fused_computation.1 | custom fusion | bytes 1050624 | tf_op jit(solution)/shard_map/jit(_take)/gather | solution.py:436
  33.4 3.5 %all-to-all-start.2 = ((bf16[8,64,512]{2,1,0:T(8,128)(2,1)}), bf16[8,64,512]{2,1,0:T(8,128)(2,1)S(1)}, u32[]{:S(2)}, u32[]{:S(2)}) async-start(bf16[8,64,512]{2,1,0:T(8,128)(2,1)} %bitcast.10), calls=%async_computation.2 | async-start | bytes 1048576 | tf_op jit(solution)/shard_map/all_to_all | solution.py:389
  40.7 4.5 %shard_map.219 = (bf16[8,2,4,128,128]{4,3,2,1,0:T(8,128)(2,1)}, bf16[8,2,4,128,128]{4,3,2,1,0:T(8,128)(2,1)}) custom-call(s32[32]{0:T(128)} %select_n.248.order_ref, bf16[32,4,128,128]{3,2,1,0:T(8,128)(2,1)} %old_ref.1), custom_call_target="tpu_custom_call" | custom-call | tf_op jit(solution)/shard_map/pallas_call | solution.py:65
  45.4 4.8 %all-to-all-done.2 = bf16[8,64,512]{2,1,0:T(8,128)(2,1)S(1)} async-done(((bf16[8,64,512]{2,1,0:T(8,128)(2,1)}), bf16[8,64,512]{2,1,0:T(8,128)(2,1)S(1)}, u32[]{:S(2)}, u32[]{:S(2)}) %all-to-all-start.2) | async-done | bytes 524320 | tf_op jit(solution)/shard_map/all_to_all | solution.py:389
  50.6 11.6 %all_gather.18.emb_ref = bf16[144,2048]{1,0:T(8,128)(2,1)} all-gather(bf16[144,512]{1,0:T(8,128)(2,1)S(1)} %maximum_maximum_fusion), channel_id=1, replica_groups=mesh['req'=8,'head'=4] {'head'}, dimensions={1}, use_global_device_ids=true | all-gather | bytes 737280 | tf_op jit(solution)/shard_map/all_gather | solution.py:465
  62.2 8.1 %shard_map.220 = (bf16[32,2048]{1,0:T(8,128)(2,1)}, bf16[256,512]{1,0:T(8,128)(2,1)}, bf16[32,2176]{1,0:T(8,128)(2,1)}, bf16[32,2176]{1,0:T(8,128)(2,1)}, bf16[3...) custom-call(s32[2]{0:T(128)} %pad_add_fusion.1.me_ref, bf16[144,2048]{1,0:T(8,128)(2,1)} %all_gather.18.emb_ref, ...), custom_call_target="tpu_custom_call" | custom-call | tf_op jit(solution)/shard_map/pallas_call | solution.py:214
  70.3 13.7 %all_to_all.41.refs_1_ = bf16[8,32,512]{2,1,0:T(8,128)(2,1)} all-to-all(bf16[8,32,512]{2,1,0:T(8,128)(2,1)} %bitcast.130), channel_id=1, replica_groups=mesh['req'=8,'head'=4] {'req'}, dimensions={0} | all-to-all | bytes 524288 | tf_op jit(solution)/shard_map/all_to_all | solution.py:389
  84.0 3.7 %all-to-all-start.4 = ((bf16[8,2,4,128,128]{4,3,2,1,0:T(8,128)(2,1)}), bf16[8,2,4,128,128]{4,3,2,1,0:T(8,128)(2,1)S(1)}, u32[]{:S(2)}, u32[]{:S(2)}) async-start(bf16[8,2,4,128,128]{4,3,2,1,0:T(8,128)(2,1)} %get-tuple-element.42.rest_0_), calls=%async_computation.4 | async-start | bytes 4194304 | tf_op jit(solution)/shard_map/all_to_all | solution.py:389
  89.8 4.7 %collective-permute-done.1 = bf16[32,2176]{1,0:T(8,128)(2,1)S(1)} collective-permute-done((bf16[32,2176]{1,0:T(8,128)(2,1)S(1)}, bf16[32,2176]{1,0:T(8,128)(2,1)S(1)}, u32[]{:S(2)}, u32[]{:S(2)}) %collective-permute-start.1) | collective-permute-done | bytes 139296 | tf_op jit(solution)/shard_map/ppermute | solution.py:21
  94.4 2.1 collective-permute-done.2
  98.8 37.4 %all-to-all-done.4.refs_2_.rest_0_ = bf16[8,2,4,128,128]{4,3,2,1,0:T(8,128)(2,1)S(1)} async-done(((bf16[8,2,4,128,128]{4,3,2,1,0:T(8,128)(2,1)}), bf16[8,2,4,128,128]{4,3,2,1,0:T(8,128)(2,1)S(1)}, u32[]{:S(2)}, u32[]{:S(2)}) %all-to-all-start.4) | async-done | bytes 2097184 | tf_op jit(solution)/shard_map/all_to_all | solution.py:389
  136.2 4.4 %all-to-all-start.5 = ((bf16[8,2,4,128,128]{4,3,2,1,0:T(8,128)(2,1)}), bf16[8,2,4,128,128]{4,3,2,1,0:T(8,128)(2,1)}, u32[]{:S(2)}, u32[]{:S(2)}) async-start(bf16[8,2,4,128,128]{4,3,2,1,0:T(8,128)(2,1)} %shard_map.223), calls=%async_computation.5 | async-start | bytes 4194304 | tf_op jit(solution)/shard_map/all_to_all | solution.py:389
  143.8 57.9 %all-gather.5.cloned.1.call-done.x_hbm = bf16[256,2048]{1,0:T(8,128)(2,1)} async-done(((bf16[32,2048]{1,0:T(8,128)(2,1)}), bf16[256,2048]{1,0:T(8,128)(2,1)}) %all-gather.5.cloned.1.call-update) | async-done | bytes 1048592 | tf_op jit(solution)/shard_map/all_gather | solution.py:489
  201.7 8.0 %shard_map.222 = (bf16[256,2048]{1,0:T(8,128)(2,1)}, bf16[32,2048]{1,0:T(8,128)(2,1)}) custom-call(bf16[256,2048]{1,0:T(8,128)(2,1)} %all-gather.5.cloned.1.call-done.x_hbm, bf16[4,2112,512]{2,1,0:T(8,128)(2,1)} %bitcast.117, bf16[256,256]{1,0:T(8,128)(2,1)} %fusion.5.pick_ref, bf16[32,256]{1,0:T(8,128)(2,1)} %compare_convert_fusion.mine_ref, ...), custom_call_target="tpu_custom_call" | custom-call | tf_op jit(solution)/shard_map/pallas_call | solution.py:317
  209.7 3.9 %all-to-all-start.6 = ((bf16[8,32,2048]{2,1,0:T(8,128)(2,1)}), bf16[8,32,2048]{2,1,0:T(8,128)(2,1)S(1)}, u32[]{:S(2)}, u32[]{:S(2)}) async-start(bf16[8,32,2048]{2,1,0:T(8,128)(2,1)} %bitcast.119), calls=%async_computation.6 | async-start | bytes 2097152 | tf_op jit(solution)/shard_map/all_to_all | solution.py:389
  217.2 6.8 %shard_map.225 = bf16[32,4,128,128]{3,2,1,0:T(8,128)(2,1)} custom-call(s32[32]{0:T(128)} %select_reduce_fusion.2.slot_ref, f32[32,8,512]{2,1,0:T(8,128)} %convert.2.kv_ref, bf16[8,2,4,128,128]{4,3,2,1,0:T(8,128)(2,1)} %copy-done, bf16[8,2,4,128,128]{4,3,2,1,0:T(8,128)(2,1)} %all-to-all-done.5.refs_3_.rest_1_), custom_call_target="tpu_custom_call" | custom-call | tf_op jit(solution)/shard_map/pallas_call | solution.py:265
  224.1 15.2 %all-to-all-done.6 = bf16[8,32,2048]{2,1,0:T(8,128)(2,1)S(1)} async-done(((bf16[8,32,2048]{2,1,0:T(8,128)(2,1)}), bf16[8,32,2048]{2,1,0:T(8,128)(2,1)S(1)}, u32[]{:S(2)}, u32[]{:S(2)}) %all-to-all-start.6) | async-done | bytes 1048608 | tf_op jit(solution)/shard_map/all_to_all | solution.py:389
  239.7 1.5 collective-permute-start.7
  241.3 2.8 collective-permute-start.8
  246.0 2.2 collective-permute-done.16
  254.6 3.6 %collective-permute-done.9 = bf16[4,32,896]{2,1,0:T(8,128)(2,1)S(1)} collective-permute-done((bf16[4,32,896]{2,1,0:T(8,128)(2,1)S(1)}, bf16[4,32,896]{2,1,0:T(8,128)(2,1)S(1)}, u32[]{:S(2)}, u32[]{:S(2)}) %collective-permute-start.9) | collective-permute-done | bytes 229408 | tf_op jit(solution)/shard_map/ppermute | solution.py:21
  261.3 3.4 %collective-permute-done.14 = bf16[2,32,768]{2,1,0:T(8,128)(2,1)S(1)} collective-permute-done((bf16[2,32,768]{2,1,0:T(8,128)(2,1)S(1)}, bf16[2,32,768]{2,1,0:T(8,128)(2,1)S(1)}, u32[]{:S(2)}, u32[]{:S(2)}) %collective-permute-start.14) | collective-permute-done | bytes 98336 | tf_op jit(solution)/shard_map/ppermute | solution.py:21
  267.6 1.7 collective-permute-start.15
  272.7 2.6 collective-permute-done.19
  275.3 2.9 collective-permute-done.20
  280.1 8.2 %shard_map.226 = f32[8,64]{1,0:T(8,128)} custom-call(bf16[512,2048]{1,0:T(8,128)(2,1)} %bitcast.118, bf16[1000,2048]{1,0:T(8,128)(2,1)} %bitcast.122, bf16[1000,2048]{1,0:T(8,128)(2,1)} %collective-permute-done.21.other_hbm), custom_call_target="tpu_custom_call" | custom-call | tf_op jit(solution)/shard_map/pallas_call | solution.py:359
  290.3 3.3 %all-to-all-start.7 = ((f32[8,1,64]{2,1,0:T(1,128)}), f32[8,1,64]{2,1,0:T(1,128)S(1)}, u32[]{:S(2)}, u32[]{:S(2)}) async-start(f32[8,1,64]{2,1,0:T(1,128)} %bitcast.66), calls=%async_computation.7 | async-start | bytes 8192 | tf_op jit(solution)/shard_map/all_to_all | solution.py:389
  294.8 5.2 %all-to-all-done.7 = f32[8,1,64]{2,1,0:T(1,128)S(1)} async-done(((f32[8,1,64]{2,1,0:T(1,128)}), f32[8,1,64]{2,1,0:T(1,128)S(1)}, u32[]{:S(2)}, u32[]{:S(2)}) %all-to-all-start.7) | async-done | bytes 2080 | tf_op jit(solution)/shard_map/all_to_all | solution.py:389
  300.2 5.6 %all-reduce = f32[256]{0:T(256)S(1)} all-reduce(f32[256]{0:T(256)S(1)} %dynamic-update-slice), channel_id=3, replica_groups=mesh['req'=8,'head'=4] {'head'}, use_global_device_ids=true, to_apply=%add | all-reduce | flops 256 | bytes 2048
  (195 shorter events, 42.9 us)
Async XLA Ops:
  7.2 90.4 %all-gather.7.cloned.1.call-start = ((), (), s32[]{:S(2)}) async-start(), calls=%async_computation.9 | async-start | bytes 10813440 | tf_op jit(solution)/shard_map/all_gather | solution.py:410
  11.6 13.8 %all-to-all-start.1 = ((s32[8,1,192]{2,1,0:T(1,128)}), s32[8,1,192]{2,1,0:T(1,128)S(1)}, u32[]{:S(2)}, u32[]{:S(2)}) async-start(s32[8,1,192]{2,1,0:T(1,128)} %reshape.516), calls=%async_computation.1 | async-start | bytes 16384 | tf_op jit(solution)/shard_map/all_to_all | solution.py:389
  33.4 16.8 %all-to-all-start.2 = ((bf16[8,64,512]{2,1,0:T(8,128)(2,1)}), bf16[8,64,512]{2,1,0:T(8,128)(2,1)S(1)}, u32[]{:S(2)}, u32[]{:S(2)}) async-start(bf16[8,64,512]{2,1,0:T(8,128)(2,1)} %bitcast.10), calls=%async_computation.2 | async-start | bytes 1048576 | tf_op jit(solution)/shard_map/all_to_all | solution.py:389
  84.0 52.2 %all-to-all-start.4 = ((bf16[8,2,4,128,128]{4,3,2,1,0:T(8,128)(2,1)}), bf16[8,2,4,128,128]{4,3,2,1,0:T(8,128)(2,1)S(1)}, u32[]{:S(2)}, u32[]{:S(2)}) async-start(bf16[8,2,4,128,128]{4,3,2,1,0:T(8,128)(2,1)} %get-tuple-element.42.rest_0_), calls=%async_computation.4 | async-start | bytes 4194304 | tf_op jit(solution)/shard_map/all_to_all | solution.py:389
  87.8 1.9 collective-permute-start
  87.9 6.5 %collective-permute-start.1 = (bf16[32,2176]{1,0:T(8,128)(2,1)S(1)}, bf16[32,2176]{1,0:T(8,128)(2,1)S(1)}, u32[]{:S(2)}, u32[]{:S(2)}) collective-permute-start(bf16[32,2176]{1,0:T(8,128)(2,1)S(1)} %copy-done.11), channel_id=1, source_target_pairs={{0,2},{1,3},{2,0},{3,1},{4,6},{5,7},{6,4},{7,5},{8,10},{9,11},{10,... | collective-permute-start | bytes 417800 | tf_op jit(solution)/shard_map/ppermute | solution.py:21
  89.2 7.3 %collective-permute-start.2 = (bf16[32,2176]{1,0:T(8,128)(2,1)S(1)}, bf16[32,2176]{1,0:T(8,128)(2,1)S(1)}, u32[]{:S(2)}, u32[]{:S(2)}) collective-permute-start(bf16[32,2176]{1,0:T(8,128)(2,1)S(1)} %copy-done.10), channel_id=1, source_target_pairs={{0,3},{1,2},{2,1},{3,0},{4,7},{5,6},{6,5},{7,4},{8,11},{9,10},{10,... | collective-permute-start | bytes 417800 | tf_op jit(solution)/shard_map/ppermute | solution.py:21
  98.8 42.6 %copy-start.13 = (s32[5]{0:T(128)S(1)}, s32[5]{0:T(128)}, u32[]{:S(2)}) copy-start(s32[5]{0:T(128)} %param.25) | copy-start | bytes 64
  136.2 73.5 %all-to-all-start.5 = ((bf16[8,2,4,128,128]{4,3,2,1,0:T(8,128)(2,1)}), bf16[8,2,4,128,128]{4,3,2,1,0:T(8,128)(2,1)}, u32[]{:S(2)}, u32[]{:S(2)}) async-start(bf16[8,2,4,128,128]{4,3,2,1,0:T(8,128)(2,1)} %shard_map.223), calls=%async_computation.5 | async-start | bytes 4194304 | tf_op jit(solution)/shard_map/all_to_all | solution.py:389
  140.6 61.1 %all-gather.5.cloned.1.call-start = ((), (), s32[]{:S(2)}) async-start(), calls=%async_computation.8 | async-start | bytes 1179648 | tf_op jit(solution)/shard_map/all_gather | solution.py:489
  140.8 139.3 %collective-permute-start.21 = (bf16[1000,2048]{1,0:T(8,128)(2,1)}, bf16[1000,2048]{1,0:T(8,128)(2,1)}, u32[]{:S(2)}, u32[]{:S(2)}) collective-permute-start(bf16[1000,2048]{1,0:T(8,128)(2,1)} %bitcast.121), channel_id=1, source_target_pairs={{0,1},{1,0},{2,3},{3,2},{4,5},{5,4},{6,7},{7,6},{8,9},{9,8},{10,11... | collective-permute-start | bytes 12288008 | tf_op jit(solution)/shard_map/ppermute | solution.py:21
  209.7 29.5 %all-to-all-start.6 = ((bf16[8,32,2048]{2,1,0:T(8,128)(2,1)}), bf16[8,32,2048]{2,1,0:T(8,128)(2,1)S(1)}, u32[]{:S(2)}, u32[]{:S(2)}) async-start(bf16[8,32,2048]{2,1,0:T(8,128)(2,1)} %bitcast.119), calls=%async_computation.6 | async-start | bytes 2097152 | tf_op jit(solution)/shard_map/all_to_all | solution.py:389
  217.2 22.1 %copy-start.4 = (bf16[32,2048]{1,0:T(8,128)(2,1)S(1)}, bf16[32,2048]{1,0:T(8,128)(2,1)}, u32[]{:S(2)}) copy-start(bf16[32,2048]{1,0:T(8,128)(2,1)} %get-tuple-element.49) | copy-start | bytes 393220
  239.7 9.8 %collective-permute-start.6 = (bf16[32,896]{1,0:T(8,128)(2,1)S(1)}, bf16[32,896]{1,0:T(8,128)(2,1)S(1)}, u32[]{:S(2)}, u32[]{:S(2)}) collective-permute-start(bf16[32,896]{1,0:T(8,128)(2,1)S(1)} %get-tuple-element.73), channel_id=1, source_target_pairs={{0,8},{4,12},{8,0},{12,4},{16,24},{20,28},{24,16},{28,20},{1,9},{5... | collective-permute-start | bytes 172040 | tf_op jit(solution)/shard_map/ppermute | solution.py:21
  239.7 9.8 %collective-permute-start.7 = (bf16[32,896]{1,0:T(8,128)(2,1)S(1)}, bf16[32,896]{1,0:T(8,128)(2,1)S(1)}, u32[]{:S(2)}, u32[]{:S(2)}) collective-permute-start(bf16[32,896]{1,0:T(8,128)(2,1)S(1)} %get-tuple-element.73), channel_id=1, source_target_pairs={{0,16},{4,20},{8,24},{12,28},{16,0},{20,4},{24,8},{28,12},{1,17},{... | collective-permute-start | bytes 172040 | tf_op jit(solution)/shard_map/ppermute | solution.py:21
  241.3 9.1 %collective-permute-start.8 = (bf16[32,896]{1,0:T(8,128)(2,1)S(1)}, bf16[32,896]{1,0:T(8,128)(2,1)S(1)}, u32[]{:S(2)}, u32[]{:S(2)}) collective-permute-start(bf16[32,896]{1,0:T(8,128)(2,1)S(1)} %get-tuple-element.73), channel_id=1, source_target_pairs={{0,24},{4,28},{8,16},{12,20},{16,8},{20,12},{24,0},{28,4},{1,25},{... | collective-permute-start | bytes 172040 | tf_op jit(solution)/shard_map/ppermute | solution.py:21
  244.3 3.9 %collective-permute-start.16 = (bf16[32,384]{1,0:T(8,128)(2,1)S(1)}, bf16[32,384]{1,0:T(8,128)(2,1)S(1)}, u32[]{:S(2)}, u32[]{:S(2)}) collective-permute-start(bf16[32,384]{1,0:T(8,128)(2,1)S(1)} %get-tuple-element.77), channel_id=1, source_target_pairs={{0,4},{4,0},{8,12},{12,8},{16,20},{20,16},{24,28},{28,24},{1,5},{5... | collective-permute-start | bytes 73736 | tf_op jit(solution)/shard_map/ppermute | solution.py:21
  248.2 4.1 %collective-permute-start.11 = (bf16[32,768]{1,0:T(8,128)(2,1)S(1)}, bf16[32,768]{1,0:T(8,128)(2,1)S(1)}, u32[]{:S(2)}, u32[]{:S(2)}) collective-permute-start(bf16[32,768]{1,0:T(8,128)(2,1)S(1)} %get-tuple-element.75), channel_id=1, source_target_pairs={{0,2},{1,3},{2,0},{3,1},{4,6},{5,7},{6,4},{7,5},{8,10},{9,11},{10,... | collective-permute-start | bytes 147464 | tf_op jit(solution)/shard_map/ppermute | solution.py:21
  249.4 16.6 %collective-permute-start.3 = (f32[32,640]{1,0:T(8,128)S(1)}, f32[32,640]{1,0:T(8,128)S(1)}, u32[]{:S(2)}, u32[]{:S(2)}) collective-permute-start(f32[32,640]{1,0:T(8,128)S(1)} %get-tuple-element.90), channel_id=1, source_target_pairs={{0,1},{1,0},{2,3},{3,2},{4,5},{5,4},{6,7},{7,6},{8,9},{9,8},{10,11... | collective-permute-start | bytes 245768 | tf_op jit(solution)/shard_map/ppermute | solution.py:21
  249.5 4.2 %collective-permute-start.17 = (bf16[2,32,384]{2,1,0:T(8,128)(2,1)S(1)}, bf16[2,32,384]{2,1,0:T(8,128)(2,1)S(1)}, u32[]{:S(2)}, u32[]{:S(2)}) collective-permute-start(bf16[2,32,384]{2,1,0:T(8,128)(2,1)S(1)} %get-tuple-element.88), channel_id=1, source_target_pairs={{0,2},{1,3},{2,0},{3,1},{4,6},{5,7},{6,4},{7,5},{8,10},{9,11},{10,... | collective-permute-start | bytes 147464 | tf_op jit(solution)/shard_map/ppermute | solution.py:21
  250.5 7.7 %collective-permute-start.9 = (bf16[4,32,896]{2,1,0:T(8,128)(2,1)S(1)}, bf16[4,32,896]{2,1,0:T(8,128)(2,1)S(1)}, u32[]{:S(2)}, u32[]{:S(2)}) collective-permute-start(bf16[4,32,896]{2,1,0:T(8,128)(2,1)S(1)} %get-tuple-element.71), channel_id=1, source_target_pairs={{0,4},{4,0},{8,12},{12,8},{16,20},{20,16},{24,28},{28,24},{1,5},{5... | collective-permute-start | bytes 688136 | tf_op jit(solution)/shard_map/ppermute | solution.py:21
  252.3 6.9 %collective-permute-start.12 = (bf16[2,32,768]{2,1,0:T(8,128)(2,1)S(1)}, bf16[2,32,768]{2,1,0:T(8,128)(2,1)S(1)}, u32[]{:S(2)}, u32[]{:S(2)}) collective-permute-start(bf16[2,32,768]{2,1,0:T(8,128)(2,1)S(1)} %get-tuple-element.79), channel_id=1, source_target_pairs={{0,8},{4,12},{8,0},{12,4},{16,24},{20,28},{24,16},{28,20},{1,9},{5... | collective-permute-start | bytes 294920 | tf_op jit(solution)/shard_map/ppermute | solution.py:21
  253.7 7.7 %collective-permute-start.13 = (bf16[2,32,768]{2,1,0:T(8,128)(2,1)S(1)}, bf16[2,32,768]{2,1,0:T(8,128)(2,1)S(1)}, u32[]{:S(2)}, u32[]{:S(2)}) collective-permute-start(bf16[2,32,768]{2,1,0:T(8,128)(2,1)S(1)} %get-tuple-element.79), channel_id=1, source_target_pairs={{0,16},{4,20},{8,24},{12,28},{16,0},{20,4},{24,8},{28,12},{1,17},{... | collective-permute-start | bytes 294920 | tf_op jit(solution)/shard_map/ppermute | solution.py:21
  258.2 6.5 %collective-permute-start.14 = (bf16[2,32,768]{2,1,0:T(8,128)(2,1)S(1)}, bf16[2,32,768]{2,1,0:T(8,128)(2,1)S(1)}, u32[]{:S(2)}, u32[]{:S(2)}) collective-permute-start(bf16[2,32,768]{2,1,0:T(8,128)(2,1)S(1)} %get-tuple-element.79), channel_id=1, source_target_pairs={{0,24},{4,28},{8,16},{12,20},{16,8},{20,12},{24,0},{28,4},{1,25},{... | collective-permute-start | bytes 294920 | tf_op jit(solution)/shard_map/ppermute | solution.py:21
  259.3 7.5 %collective-permute-start.4 = (f32[32,640]{1,0:T(8,128)S(1)}, f32[32,640]{1,0:T(8,128)S(1)}, u32[]{:S(2)}, u32[]{:S(2)}) collective-permute-start(f32[32,640]{1,0:T(8,128)S(1)} %get-tuple-element.91), channel_id=1, source_target_pairs={{0,2},{1,3},{2,0},{3,1},{4,6},{5,7},{6,4},{7,5},{8,10},{9,11},{10,... | collective-permute-start | bytes 245768 | tf_op jit(solution)/shard_map/ppermute | solution.py:21
  261.3 6.3 %collective-permute-start.5 = (f32[32,640]{1,0:T(8,128)S(1)}, f32[32,640]{1,0:T(8,128)S(1)}, u32[]{:S(2)}, u32[]{:S(2)}) collective-permute-start(f32[32,640]{1,0:T(8,128)S(1)} %get-tuple-element.92), channel_id=1, source_target_pairs={{0,3},{1,2},{2,1},{3,0},{4,7},{5,6},{6,5},{7,4},{8,11},{9,10},{10,... | collective-permute-start | bytes 245768 | tf_op jit(solution)/shard_map/ppermute | solution.py:21
  264.7 13.5 %collective-permute-start.10 = (bf16[2,4,32,896]{3,2,1,0:T(8,128)(2,1)S(1)}, bf16[2,4,32,896]{3,2,1,0:T(8,128)(2,1)S(1)}, u32[]{:S(2)}, u32[]{:S(2)}) collective-permute-start(bf16[2,4,32,896]{3,2,1,0:T(8,128)(2,1)S(1)} %get-tuple-element.63), channel_id=1, source_target_pairs={{0,2},{1,3},{2,0},{3,1},{4,6},{5,7},{6,4},{7,5},{8,10},{9,11},{10,... | collective-permute-start | bytes 1376264 | tf_op jit(solution)/shard_map/ppermute | solution.py:21
  266.0 5.5 %collective-permute-start.18 = (bf16[2,2,32,384]{3,2,1,0:T(8,128)(2,1)}, bf16[2,2,32,384]{3,2,1,0:T(8,128)(2,1)S(1)}, u32[]{:S(2)}, u32[]{:S(2)}) collective-permute-start(bf16[2,2,32,384]{3,2,1,0:T(8,128)(2,1)} %get-tuple-element.81), channel_id=1, source_target_pairs={{0,8},{4,12},{8,0},{12,4},{16,24},{20,28},{24,16},{28,20},{1,9},{5... | collective-permute-start | bytes 294920 | tf_op jit(solution)/shard_map/ppermute | solution.py:21
  266.7 8.5 %collective-permute-start.19 = (bf16[2,2,32,384]{3,2,1,0:T(8,128)(2,1)}, bf16[2,2,32,384]{3,2,1,0:T(8,128)(2,1)S(1)}, u32[]{:S(2)}, u32[]{:S(2)}) collective-permute-start(bf16[2,2,32,384]{3,2,1,0:T(8,128)(2,1)} %get-tuple-element.81), channel_id=1, source_target_pairs={{0,16},{4,20},{8,24},{12,28},{16,0},{20,4},{24,8},{28,12},{1,17},{... | collective-permute-start | bytes 294920 | tf_op jit(solution)/shard_map/ppermute | solution.py:21
  267.6 10.7 %collective-permute-start.15 = (bf16[4,2,32,768]{3,2,1,0:T(8,128)(2,1)S(1)}, bf16[4,2,32,768]{3,2,1,0:T(8,128)(2,1)S(1)}, u32[]{:S(2)}, u32[]{:S(2)}) collective-permute-start(bf16[4,2,32,768]{3,2,1,0:T(8,128)(2,1)S(1)} %get-tuple-element.65), channel_id=1, source_target_pairs={{0,4},{4,0},{8,12},{12,8},{16,20},{20,16},{24,28},{28,24},{1,5},{5... | collective-permute-start | bytes 1179656 | tf_op jit(solution)/shard_map/ppermute | solution.py:21
  271.5 6.6 %collective-permute-start.20 = (bf16[2,2,32,384]{3,2,1,0:T(8,128)(2,1)}, bf16[2,2,32,384]{3,2,1,0:T(8,128)(2,1)S(1)}, u32[]{:S(2)}, u32[]{:S(2)}) collective-permute-start(bf16[2,2,32,384]{3,2,1,0:T(8,128)(2,1)} %get-tuple-element.81), channel_id=1, source_target_pairs={{0,24},{4,28},{8,16},{12,20},{16,8},{20,12},{24,0},{28,4},{1,25},{... | collective-permute-start | bytes 294920 | tf_op jit(solution)/shard_map/ppermute | solution.py:21
  290.3 9.7 %all-to-all-start.7 = ((f32[8,1,64]{2,1,0:T(1,128)}), f32[8,1,64]{2,1,0:T(1,128)S(1)}, u32[]{:S(2)}, u32[]{:S(2)}) async-start(f32[8,1,64]{2,1,0:T(1,128)} %bitcast.66), calls=%async_computation.7 | async-start | bytes 8192 | tf_op jit(solution)/shard_map/all_to_all | solution.py:389
  (13 other events, 73.1 us)
Sparse Core Ops, SparseCore 0:
  10.4 65.6 all-gather.6
  144.1 57.5 all-gather.4

commit v10 on v9

--- a/solution.py
+++ b/solution.py
@@ -329,6 +329,9 @@
             VMEM((tokens, weights.shape[1] // 3), BF16),
             pltpu.SemaphoreType.DMA((4,)),
         ],
+        cost_estimate=pl.CostEstimate(
+            flops=32 * tokens * weights.size, bytes_accessed=2 * weights.size, transcendentals=0
+        ),
         compiler_params=pltpu.CompilerParams(vmem_limit_bytes=58 << 20),
     )(x, weights, pick, mine, gain)
 
@@ -488,7 +491,7 @@
     after_mixer = after(after_mixer.astype(BF16), feed_weights)
     everything = lax.all_gather(after_mixer, "req", axis=0, tiled=True)
     arrived += [to_all(after(piece, after_mixer[:8, :128]), "req") for piece in pieces[1:]]
-    arrived_kv = to_all(kv.reshape(n, -1, width), "req")
+    arrived_kv = to_all(after(kv, arrived[-1]).reshape(n, -1, width), "req")
 
     row = jnp.arange(n * rows, dtype=jnp.int32)
     by_owner, by_group, by_step = row // rows, (row % rows) // steps, row % steps

time: 315 us -> 322 us (1.022)
  blocking collectives: 31 us -> 71.4 us
  waiting for transfers between devices: 152 us -> 115 us
    all_gather x1, waiting for transfers between devices: 57.9 us -> 0.01 us  [on_device(): everything = lax.all_gather(after_mixer, 'req', axis=0, tiled=True)]
    all_to_all x1, blocking collectives: 13.7 us -> 54.1 us  [to_all(): return lax.all_to_all(x, axis, split_axis=0, concat_axis=0, tiled=True)]
    all_to_all x6, waiting for transfers between devices: 68.3 us -> 88.8 us  [to_all(): return lax.all_to_all(x, axis, split_axis=0, concat_axis=0, tiled=True)]
where the time goes in v10:
time: 322 us; the launch traced here: 321 us
  waiting for transfers between devices  115 us (36%)
  blocking collectives  71.4 us (22%)
  starting transfers between devices  47.4 us (15%)
  Pallas kernels  35.7 us (11%)
  local copies, waits for them, and re-layouts  18.3 us (6%)
  other arithmetic  17.1 us (5%)
  between operations  16 us (5%)
    all_to_all x6, waiting for transfers between devices, to_all(): return lax.all_to_all(x, axis, split_axis=0, concat_axis=0, tiled=True)  88.8 us
    all_to_all x1, blocking collectives, to_all(): return lax.all_to_all(x, axis, split_axis=0, concat_axis=0, tiled=True)  54.1 us
    all_to_all x6, starting transfers between devices, to_all(): return lax.all_to_all(x, axis, split_axis=0, concat_axis=0, tiled=True)  28.5 us
    ppermute x22, waiting for transfers between devices, swap(): return lax.ppermute(x, axis, [(i, i ^ offset) for i in range(size)])  25.4 us
    ppermute x22, starting transfers between devices, swap(): return lax.ppermute(x, axis, [(i, i ^ offset) for i in range(size)])  18.8 us
    all_gather x1, blocking collectives, on_device(): lax.all_gather(jnp.concatenate([embed_part, gains_high, gains_low, extra]...  11.6 us
    pallas_call x1, Pallas kernels, greatest_entries(): pl.pallas_call(greatest_kernel, out_shape=jax.ShapeDtypeStruct((blocks, f...  8.22 us
    pallas_call x1, Pallas kernels, mixer(): pl.pallas_call(functools.partial(mixer_kernel, counts, owners, heads, cla...  8.1 us
  transfers between devices with their start and end apart: 30, of which 17 were waited for; matrix products, arithmetic and copies ran while one was open for 8% of the time, Pallas kernels for 9%

profile of v10, /device:TPU:0, one launch (start us, length us, event | category | flops | bytes accessed | tf_op | source)
XLA Modules:
  0.0 321.2 jit_solution(14724792574726102538)
XLA Ops:
  7.2 3.0 pad_maximum_fusion
  11.6 7.3 %all-to-all-start.1 = ((s32[8,1,192]{2,1,0:T(1,128)}), s32[8,1,192]{2,1,0:T(1,128)S(1)}, u32[]{:S(2)}, u32[]{:S(2)}) async-start(s32[8,1,192]{2,1,0:T(1,128)} %reshape.516), calls=%async_computation.1 | async-start | bytes 16384 | tf_op jit(solution)/shard_map/all_to_all | solution.py:392
  19.7 5.8 %all-to-all-done.1 = s32[8,1,192]{2,1,0:T(1,128)S(1)} async-done(((s32[8,1,192]{2,1,0:T(1,128)}), s32[8,1,192]{2,1,0:T(1,128)S(1)}, u32[]{:S(2)}, u32[]{:S(2)}) %all-to-all-start.1) | async-done | bytes 6176 | tf_op jit(solution)/shard_map/all_to_all | solution.py:392
  28.1 5.3 %gather_fusion.1 = bf16[512,512]{1,0:T(8,128)(2,1)} fusion(bf16[4000,512]{1,0:T(8,128)(2,1)} %param.27, s32[1024]{0:T(1024)S(1)} %pad_clamp_fusion.2), kind=kCustom, calls=%fused_computation.1 | custom fusion | bytes 1050624 | tf_op jit(solution)/shard_map/jit(_take)/gather | solution.py:439
  33.4 3.5 %all-to-all-start.2 = ((bf16[8,64,512]{2,1,0:T(8,128)(2,1)}), bf16[8,64,512]{2,1,0:T(8,128)(2,1)S(1)}, u32[]{:S(2)}, u32[]{:S(2)}) async-start(bf16[8,64,512]{2,1,0:T(8,128)(2,1)} %bitcast.10), calls=%async_computation.2 | async-start | bytes 1048576 | tf_op jit(solution)/shard_map/all_to_all | solution.py:392
  40.7 4.6 %shard_map.219 = (bf16[8,2,4,128,128]{4,3,2,1,0:T(8,128)(2,1)}, bf16[8,2,4,128,128]{4,3,2,1,0:T(8,128)(2,1)}) custom-call(s32[32]{0:T(128)} %select_n.248.order_ref, bf16[32,4,128,128]{3,2,1,0:T(8,128)(2,1)} %old_ref.1), custom_call_target="tpu_custom_call" | custom-call | tf_op jit(solution)/shard_map/pallas_call | solution.py:65
  45.5 4.7 %all-to-all-done.2 = bf16[8,64,512]{2,1,0:T(8,128)(2,1)S(1)} async-done(((bf16[8,64,512]{2,1,0:T(8,128)(2,1)}), bf16[8,64,512]{2,1,0:T(8,128)(2,1)S(1)}, u32[]{:S(2)}, u32[]{:S(2)}) %all-to-all-start.2) | async-done | bytes 524320 | tf_op jit(solution)/shard_map/all_to_all | solution.py:392
  50.6 11.6 %all_gather.18.emb_ref = bf16[144,2048]{1,0:T(8,128)(2,1)} all-gather(bf16[144,512]{1,0:T(8,128)(2,1)S(1)} %maximum_maximum_fusion), channel_id=1, replica_groups=mesh['req'=8,'head'=4] {'head'}, dimensions={1}, use_global_device_ids=true | all-gather | bytes 737280 | tf_op jit(solution)/shard_map/all_gather | solution.py:468
  62.2 8.1 %shard_map.220 = (bf16[32,2048]{1,0:T(8,128)(2,1)}, bf16[256,512]{1,0:T(8,128)(2,1)}, bf16[32,2176]{1,0:T(8,128)(2,1)}, bf16[32,2176]{1,0:T(8,128)(2,1)}, bf16[3...) custom-call(s32[2]{0:T(128)} %pad_add_fusion.1.me_ref, bf16[144,2048]{1,0:T(8,128)(2,1)} %all_gather.18.emb_ref, ...), custom_call_target="tpu_custom_call" | custom-call | tf_op jit(solution)/shard_map/pallas_call | solution.py:214
  72.2 5.3 %collective-permute-done.1 = bf16[32,2176]{1,0:T(8,128)(2,1)S(1)} collective-permute-done((bf16[32,2176]{1,0:T(8,128)(2,1)}, bf16[32,2176]{1,0:T(8,128)(2,1)S(1)}, u32[]{:S(2)}, u32[]{:S(2)}) %collective-permute-start.1) | collective-permute-done | bytes 139296 | tf_op jit(solution)/shard_map/ppermute | solution.py:21
  77.5 2.4 collective-permute-done.2
  81.1 1.7 fusion.2.refs_0_
  84.0 54.1 %all_to_all.41.refs_1_.refs_3_.rest_1_ = bf16[8,2,4,128,128]{4,3,2,1,0:T(8,128)(2,1)} all-to-all(bf16[8,2,4,128,128]{4,3,2,1,0:T(8,128)(2,1)} %shard_map.223), channel_id=1, replica_groups=mesh['req'=8,'head'=4] {'req'}, dimensions={0} | all-to-all | bytes 4194304 | tf_op jit(solution)/shard_map/all_to_all | solution.py:392
  138.1 3.8 %all-to-all-start.5 = ((bf16[8,2,4,128,128]{4,3,2,1,0:T(8,128)(2,1)}), bf16[8,2,4,128,128]{4,3,2,1,0:T(8,128)(2,1)S(1)}, u32[]{:S(2)}, u32[]{:S(2)}) async-start(bf16[8,2,4,128,128]{4,3,2,1,0:T(8,128)(2,1)} %get-tuple-element.42.rest_0_), calls=%async_computation.5 | async-start | bytes 4194304 | tf_op jit(solution)/shard_map/all_to_all | solution.py:392
  145.1 57.3 %all-to-all-done.5.refs_2_.rest_0_ = bf16[8,2,4,128,128]{4,3,2,1,0:T(8,128)(2,1)S(1)} async-done(((bf16[8,2,4,128,128]{4,3,2,1,0:T(8,128)(2,1)}), bf16[8,2,4,128,128]{4,3,2,1,0:T(8,128)(2,1)S(1)}, u32[]{:S(2)}, u32[]{:S(2)}) %all-to-all-start.5) | async-done | bytes 2097184 | tf_op jit(solution)/shard_map/all_to_all | solution.py:392
  202.4 3.7 %all-to-all-start.4 = ((bf16[8,32,512]{2,1,0:T(8,128)(2,1)}), bf16[8,32,512]{2,1,0:T(8,128)(2,1)S(1)}, u32[]{:S(2)}, u32[]{:S(2)}) async-start(bf16[8,32,512]{2,1,0:T(8,128)(2,1)} %bitcast.125), calls=%async_computation.4 | async-start | bytes 524288 | tf_op jit(solution)/shard_map/all_to_all | solution.py:392
  206.1 8.0 %shard_map.222 = (bf16[256,2048]{1,0:T(8,128)(2,1)}, bf16[32,2048]{1,0:T(8,128)(2,1)}) custom-call(bf16[256,2048]{1,0:T(8,128)(2,1)} %all-gather.5.cloned.1.call-done.x_hbm, bf16[4,2112,512]{2,1,0:T(8,128)(2,1)} %bitcast.117, bf16[256,256]{1,0:T(8,128)(2,1)} %fusion.5.pick_ref, bf16[32,256]{1,0:T(8,128)(2,1)} %compare_convert_fusion.mine_ref, ...), custom_call_target="tpu_custom_call" | custom-call | flops 35433480192 | bytes 8650752 | tf_op jit(solution)/shard_map/pallas_call | solution.py:317
  215.6 5.3 %all-to-all-start.6 = ((bf16[8,32,2048]{2,1,0:T(8,128)(2,1)}), bf16[8,32,2048]{2,1,0:T(8,128)(2,1)S(1)}, u32[]{:S(2)}, u32[]{:S(2)}) async-start(bf16[8,32,2048]{2,1,0:T(8,128)(2,1)} %bitcast.119), calls=%async_computation.6 | async-start | bytes 2097152 | tf_op jit(solution)/shard_map/all_to_all | solution.py:392
  224.4 6.8 %shard_map.226 = bf16[32,4,128,128]{3,2,1,0:T(8,128)(2,1)} custom-call(s32[32]{0:T(128)} %select_reduce_fusion.2.slot_ref, f32[32,8,512]{2,1,0:T(8,128)} %convert.2.kv_ref, bf16[8,2,4,128,128]{4,3,2,1,0:T(8,128)(2,1)} %copy-done, bf16[8,2,4,128,128]{4,3,2,1,0:T(8,128)(2,1)} %all_to_all.41.refs_1_.refs_3_.rest_1_), custom_call_target="tpu_custom_call" | custom-call | tf_op jit(solution)/shard_map/pallas_call | solution.py:265
  231.2 15.0 %all-to-all-done.6 = bf16[8,32,2048]{2,1,0:T(8,128)(2,1)S(1)} async-done(((bf16[8,32,2048]{2,1,0:T(8,128)(2,1)}), bf16[8,32,2048]{2,1,0:T(8,128)(2,1)S(1)}, u32[]{:S(2)}, u32[]{:S(2)}) %all-to-all-start.6) | async-done | bytes 1048608 | tf_op jit(solution)/shard_map/all_to_all | solution.py:392
  248.3 2.9 collective-permute-start.8
  253.0 2.2 collective-permute-done.16
  255.4 2.1 collective-permute-start.17
  262.0 3.2 %collective-permute-done.9 = bf16[4,32,896]{2,1,0:T(8,128)(2,1)S(1)} collective-permute-done((bf16[4,32,896]{2,1,0:T(8,128)(2,1)S(1)}, bf16[4,32,896]{2,1,0:T(8,128)(2,1)S(1)}, u32[]{:S(2)}, u32[]{:S(2)}) %collective-permute-start.9) | collective-permute-done | bytes 229408 | tf_op jit(solution)/shard_map/ppermute | solution.py:21
  268.0 3.7 %collective-permute-done.14 = bf16[2,32,768]{2,1,0:T(8,128)(2,1)S(1)} collective-permute-done((bf16[2,32,768]{2,1,0:T(8,128)(2,1)S(1)}, bf16[2,32,768]{2,1,0:T(8,128)(2,1)S(1)}, u32[]{:S(2)}, u32[]{:S(2)}) %collective-permute-start.14) | collective-permute-done | bytes 98336 | tf_op jit(solution)/shard_map/ppermute | solution.py:21
  273.6 1.7 collective-permute-start.15
  277.0 1.7 collective-permute-start.20
  279.8 3.9 %collective-permute-done.20 = bf16[2,2,32,384]{3,2,1,0:T(8,128)(2,1)S(1)} collective-permute-done((bf16[2,2,32,384]{3,2,1,0:T(8,128)(2,1)}, bf16[2,2,32,384]{3,2,1,0:T(8,128)(2,1)S(1)}, u32[]{:S(2)}, u32[]{:S(2)}) %collective-permute-start.20) | collective-permute-done | bytes 98336 | tf_op jit(solution)/shard_map/ppermute | solution.py:21
  285.8 8.2 %shard_map.227 = f32[8,64]{1,0:T(8,128)} custom-call(bf16[512,2048]{1,0:T(8,128)(2,1)} %bitcast.118, bf16[1000,2048]{1,0:T(8,128)(2,1)} %bitcast.122, bf16[1000,2048]{1,0:T(8,128)(2,1)} %collective-permute-done.21.other_hbm), custom_call_target="tpu_custom_call" | custom-call | tf_op jit(solution)/shard_map/pallas_call | solution.py:362
  295.9 5.0 %all-to-all-start.7 = ((f32[8,1,64]{2,1,0:T(1,128)}), f32[8,1,64]{2,1,0:T(1,128)S(1)}, u32[]{:S(2)}, u32[]{:S(2)}) async-start(f32[8,1,64]{2,1,0:T(1,128)} %bitcast.66), calls=%async_computation.7 | async-start | bytes 8192 | tf_op jit(solution)/shard_map/all_to_all | solution.py:392
  302.2 5.2 %all-to-all-done.7 = f32[8,1,64]{2,1,0:T(1,128)S(1)} async-done(((f32[8,1,64]{2,1,0:T(1,128)}), f32[8,1,64]{2,1,0:T(1,128)S(1)}, u32[]{:S(2)}, u32[]{:S(2)}) %all-to-all-start.7) | async-done | bytes 2080 | tf_op jit(solution)/shard_map/all_to_all | solution.py:392
  307.7 5.6 %all-reduce = f32[256]{0:T(256)S(1)} all-reduce(f32[256]{0:T(256)S(1)} %dynamic-update-slice), channel_id=3, replica_groups=mesh['req'=8,'head'=4] {'head'}, use_global_device_ids=true, to_apply=%add | all-reduce | flops 256 | bytes 2048
  (188 shorter events, 42.3 us)
Async XLA Ops:
  7.2 75.6 %all-gather.7.cloned.1.call-start = ((), (), s32[]{:S(2)}) async-start(), calls=%async_computation.9 | async-start | bytes 10813440 | tf_op jit(solution)/shard_map/all_gather | solution.py:413
  11.6 13.8 %all-to-all-start.1 = ((s32[8,1,192]{2,1,0:T(1,128)}), s32[8,1,192]{2,1,0:T(1,128)S(1)}, u32[]{:S(2)}, u32[]{:S(2)}) async-start(s32[8,1,192]{2,1,0:T(1,128)} %reshape.516), calls=%async_computation.1 | async-start | bytes 16384 | tf_op jit(solution)/shard_map/all_to_all | solution.py:392
  33.4 16.8 %all-to-all-start.2 = ((bf16[8,64,512]{2,1,0:T(8,128)(2,1)}), bf16[8,64,512]{2,1,0:T(8,128)(2,1)S(1)}, u32[]{:S(2)}, u32[]{:S(2)}) async-start(bf16[8,64,512]{2,1,0:T(8,128)(2,1)} %bitcast.10), calls=%async_computation.2 | async-start | bytes 1048576 | tf_op jit(solution)/shard_map/all_to_all | solution.py:392
  70.3 1.9 collective-permute-start
  70.7 6.9 %collective-permute-start.1 = (bf16[32,2176]{1,0:T(8,128)(2,1)}, bf16[32,2176]{1,0:T(8,128)(2,1)S(1)}, u32[]{:S(2)}, u32[]{:S(2)}) collective-permute-start(bf16[32,2176]{1,0:T(8,128)(2,1)} %get-tuple-element.47), channel_id=1, source_target_pairs={{0,2},{1,3},{2,0},{3,1},{4,6},{5,7},{6,4},{7,5},{8,10},{9,11},{10,... | collective-permute-start | bytes 417800 | tf_op jit(solution)/shard_map/ppermute | solution.py:21
  71.9 8.1 %collective-permute-start.2 = (bf16[32,2176]{1,0:T(8,128)(2,1)}, bf16[32,2176]{1,0:T(8,128)(2,1)S(1)}, u32[]{:S(2)}, u32[]{:S(2)}) collective-permute-start(bf16[32,2176]{1,0:T(8,128)(2,1)} %get-tuple-element.48), channel_id=1, source_target_pairs={{0,3},{1,2},{2,1},{3,0},{4,7},{5,6},{6,5},{7,4},{8,11},{9,10},{10,... | collective-permute-start | bytes 417800 | tf_op jit(solution)/shard_map/ppermute | solution.py:21
  138.1 64.2 %all-to-all-start.5 = ((bf16[8,2,4,128,128]{4,3,2,1,0:T(8,128)(2,1)}), bf16[8,2,4,128,128]{4,3,2,1,0:T(8,128)(2,1)S(1)}, u32[]{:S(2)}, u32[]{:S(2)}) async-start(bf16[8,2,4,128,128]{4,3,2,1,0:T(8,128)(2,1)} %get-tuple-element.42.rest_0_), calls=%async_computation.5 | async-start | bytes 4194304 | tf_op jit(solution)/shard_map/all_to_all | solution.py:392
  141.9 64.2 %all-gather.5.cloned.1.call-start = ((), (), s32[]{:S(2)}) async-start(), calls=%async_computation.8 | async-start | bytes 1179648 | tf_op jit(solution)/shard_map/all_gather | solution.py:492
  142.0 143.8 %collective-permute-start.21 = (bf16[1000,2048]{1,0:T(8,128)(2,1)}, bf16[1000,2048]{1,0:T(8,128)(2,1)}, u32[]{:S(2)}, u32[]{:S(2)}) collective-permute-start(bf16[1000,2048]{1,0:T(8,128)(2,1)} %bitcast.121), channel_id=1, source_target_pairs={{0,1},{1,0},{2,3},{3,2},{4,5},{5,4},{6,7},{7,6},{8,9},{9,8},{10,11... | collective-permute-start | bytes 12288008 | tf_op jit(solution)/shard_map/ppermute | solution.py:21
  202.4 11.7 %copy-start = (bf16[8,2,4,128,128]{4,3,2,1,0:T(8,128)(2,1)}, bf16[8,2,4,128,128]{4,3,2,1,0:T(8,128)(2,1)S(1)}, u32[]{:S(2)}) copy-start(bf16[8,2,4,128,128]{4,3,2,1,0:T(8,128)(2,1)S(1)} %all-to-all-done.5.refs_2_.rest_0_) | copy-start | bytes 6291460
  202.4 12.6 %all-to-all-start.4 = ((bf16[8,32,512]{2,1,0:T(8,128)(2,1)}), bf16[8,32,512]{2,1,0:T(8,128)(2,1)S(1)}, u32[]{:S(2)}, u32[]{:S(2)}) async-start(bf16[8,32,512]{2,1,0:T(8,128)(2,1)} %bitcast.125), calls=%async_computation.4 | async-start | bytes 524288 | tf_op jit(solution)/shard_map/all_to_all | solution.py:392
  215.6 30.7 %all-to-all-start.6 = ((bf16[8,32,2048]{2,1,0:T(8,128)(2,1)}), bf16[8,32,2048]{2,1,0:T(8,128)(2,1)S(1)}, u32[]{:S(2)}, u32[]{:S(2)}) async-start(bf16[8,32,2048]{2,1,0:T(8,128)(2,1)} %bitcast.119), calls=%async_computation.6 | async-start | bytes 2097152 | tf_op jit(solution)/shard_map/all_to_all | solution.py:392
  224.4 22.0 %copy-start.3 = (bf16[32,2048]{1,0:T(8,128)(2,1)S(1)}, bf16[32,2048]{1,0:T(8,128)(2,1)}, u32[]{:S(2)}) copy-start(bf16[32,2048]{1,0:T(8,128)(2,1)} %get-tuple-element.49) | copy-start | bytes 393220
  246.7 8.6 %collective-permute-start.6 = (bf16[32,896]{1,0:T(8,128)(2,1)S(1)}, bf16[32,896]{1,0:T(8,128)(2,1)S(1)}, u32[]{:S(2)}, u32[]{:S(2)}) collective-permute-start(bf16[32,896]{1,0:T(8,128)(2,1)S(1)} %get-tuple-element.73), channel_id=1, source_target_pairs={{0,8},{4,12},{8,0},{12,4},{16,24},{20,28},{24,16},{28,20},{1,9},{5... | collective-permute-start | bytes 172040 | tf_op jit(solution)/shard_map/ppermute | solution.py:21
  246.8 8.6 %collective-permute-start.7 = (bf16[32,896]{1,0:T(8,128)(2,1)S(1)}, bf16[32,896]{1,0:T(8,128)(2,1)S(1)}, u32[]{:S(2)}, u32[]{:S(2)}) collective-permute-start(bf16[32,896]{1,0:T(8,128)(2,1)S(1)} %get-tuple-element.73), channel_id=1, source_target_pairs={{0,16},{4,20},{8,24},{12,28},{16,0},{20,4},{24,8},{28,12},{1,17},{... | collective-permute-start | bytes 172040 | tf_op jit(solution)/shard_map/ppermute | solution.py:21
  248.3 9.2 %collective-permute-start.8 = (bf16[32,896]{1,0:T(8,128)(2,1)S(1)}, bf16[32,896]{1,0:T(8,128)(2,1)S(1)}, u32[]{:S(2)}, u32[]{:S(2)}) collective-permute-start(bf16[32,896]{1,0:T(8,128)(2,1)S(1)} %get-tuple-element.73), channel_id=1, source_target_pairs={{0,24},{4,28},{8,16},{12,20},{16,8},{20,12},{24,0},{28,4},{1,25},{... | collective-permute-start | bytes 172040 | tf_op jit(solution)/shard_map/ppermute | solution.py:21
  251.4 3.9 %collective-permute-start.16 = (bf16[32,384]{1,0:T(8,128)(2,1)S(1)}, bf16[32,384]{1,0:T(8,128)(2,1)S(1)}, u32[]{:S(2)}, u32[]{:S(2)}) collective-permute-start(bf16[32,384]{1,0:T(8,128)(2,1)S(1)} %get-tuple-element.77), channel_id=1, source_target_pairs={{0,4},{4,0},{8,12},{12,8},{16,20},{20,16},{24,28},{28,24},{1,5},{5... | collective-permute-start | bytes 73736 | tf_op jit(solution)/shard_map/ppermute | solution.py:21
  255.2 4.5 %collective-permute-start.11 = (bf16[32,768]{1,0:T(8,128)(2,1)S(1)}, bf16[32,768]{1,0:T(8,128)(2,1)S(1)}, u32[]{:S(2)}, u32[]{:S(2)}) collective-permute-start(bf16[32,768]{1,0:T(8,128)(2,1)S(1)} %get-tuple-element.75), channel_id=1, source_target_pairs={{0,2},{1,3},{2,0},{3,1},{4,6},{5,7},{6,4},{7,5},{8,10},{9,11},{10,... | collective-permute-start | bytes 147464 | tf_op jit(solution)/shard_map/ppermute | solution.py:21
  255.3 16.8 %collective-permute-start.3 = (f32[32,640]{1,0:T(8,128)S(1)}, f32[32,640]{1,0:T(8,128)S(1)}, u32[]{:S(2)}, u32[]{:S(2)}) collective-permute-start(f32[32,640]{1,0:T(8,128)S(1)} %get-tuple-element.90), channel_id=1, source_target_pairs={{0,1},{1,0},{2,3},{3,2},{4,5},{5,4},{6,7},{7,6},{8,9},{9,8},{10,11... | collective-permute-start | bytes 245768 | tf_op jit(solution)/shard_map/ppermute | solution.py:21
  255.4 4.9 %collective-permute-start.17 = (bf16[2,32,384]{2,1,0:T(8,128)(2,1)S(1)}, bf16[2,32,384]{2,1,0:T(8,128)(2,1)S(1)}, u32[]{:S(2)}, u32[]{:S(2)}) collective-permute-start(bf16[2,32,384]{2,1,0:T(8,128)(2,1)S(1)} %get-tuple-element.88), channel_id=1, source_target_pairs={{0,2},{1,3},{2,0},{3,1},{4,6},{5,7},{6,4},{7,5},{8,10},{9,11},{10,... | collective-permute-start | bytes 147464 | tf_op jit(solution)/shard_map/ppermute | solution.py:21
  257.5 7.7 %collective-permute-start.9 = (bf16[4,32,896]{2,1,0:T(8,128)(2,1)S(1)}, bf16[4,32,896]{2,1,0:T(8,128)(2,1)S(1)}, u32[]{:S(2)}, u32[]{:S(2)}) collective-permute-start(bf16[4,32,896]{2,1,0:T(8,128)(2,1)S(1)} %get-tuple-element.71), channel_id=1, source_target_pairs={{0,4},{4,0},{8,12},{12,8},{16,20},{20,16},{24,28},{28,24},{1,5},{5... | collective-permute-start | bytes 688136 | tf_op jit(solution)/shard_map/ppermute | solution.py:21
  259.8 6.4 %collective-permute-start.12 = (bf16[2,32,768]{2,1,0:T(8,128)(2,1)S(1)}, bf16[2,32,768]{2,1,0:T(8,128)(2,1)S(1)}, u32[]{:S(2)}, u32[]{:S(2)}) collective-permute-start(bf16[2,32,768]{2,1,0:T(8,128)(2,1)S(1)} %get-tuple-element.79), channel_id=1, source_target_pairs={{0,8},{4,12},{8,0},{12,4},{16,24},{20,28},{24,16},{28,20},{1,9},{5... | collective-permute-start | bytes 294920 | tf_op jit(solution)/shard_map/ppermute | solution.py:21
  260.3 7.7 %collective-permute-start.13 = (bf16[2,32,768]{2,1,0:T(8,128)(2,1)S(1)}, bf16[2,32,768]{2,1,0:T(8,128)(2,1)S(1)}, u32[]{:S(2)}, u32[]{:S(2)}) collective-permute-start(bf16[2,32,768]{2,1,0:T(8,128)(2,1)S(1)} %get-tuple-element.79), channel_id=1, source_target_pairs={{0,16},{4,20},{8,24},{12,28},{16,0},{20,4},{24,8},{28,12},{1,17},{... | collective-permute-start | bytes 294920 | tf_op jit(solution)/shard_map/ppermute | solution.py:21
  265.2 6.5 %collective-permute-start.14 = (bf16[2,32,768]{2,1,0:T(8,128)(2,1)S(1)}, bf16[2,32,768]{2,1,0:T(8,128)(2,1)S(1)}, u32[]{:S(2)}, u32[]{:S(2)}) collective-permute-start(bf16[2,32,768]{2,1,0:T(8,128)(2,1)S(1)} %get-tuple-element.79), channel_id=1, source_target_pairs={{0,24},{4,28},{8,16},{12,20},{16,8},{20,12},{24,0},{28,4},{1,25},{... | collective-permute-start | bytes 294920 | tf_op jit(solution)/shard_map/ppermute | solution.py:21
  266.2 6.6 %collective-permute-start.4 = (f32[32,640]{1,0:T(8,128)S(1)}, f32[32,640]{1,0:T(8,128)S(1)}, u32[]{:S(2)}, u32[]{:S(2)}) collective-permute-start(f32[32,640]{1,0:T(8,128)S(1)} %get-tuple-element.91), channel_id=1, source_target_pairs={{0,2},{1,3},{2,0},{3,1},{4,6},{5,7},{6,4},{7,5},{8,10},{9,11},{10,... | collective-permute-start | bytes 245768 | tf_op jit(solution)/shard_map/ppermute | solution.py:21
  268.0 5.7 %collective-permute-start.5 = (f32[32,640]{1,0:T(8,128)S(1)}, f32[32,640]{1,0:T(8,128)S(1)}, u32[]{:S(2)}, u32[]{:S(2)}) collective-permute-start(f32[32,640]{1,0:T(8,128)S(1)} %get-tuple-element.92), channel_id=1, source_target_pairs={{0,3},{1,2},{2,1},{3,0},{4,7},{5,6},{6,5},{7,4},{8,11},{9,10},{10,... | collective-permute-start | bytes 245768 | tf_op jit(solution)/shard_map/ppermute | solution.py:21
  271.7 12.1 %collective-permute-start.10 = (bf16[2,4,32,896]{3,2,1,0:T(8,128)(2,1)S(1)}, bf16[2,4,32,896]{3,2,1,0:T(8,128)(2,1)S(1)}, u32[]{:S(2)}, u32[]{:S(2)}) collective-permute-start(bf16[2,4,32,896]{3,2,1,0:T(8,128)(2,1)S(1)} %get-tuple-element.63), channel_id=1, source_target_pairs={{0,2},{1,3},{2,0},{3,1},{4,6},{5,7},{6,4},{7,5},{8,10},{9,11},{10,... | collective-permute-start | bytes 1376264 | tf_op jit(solution)/shard_map/ppermute | solution.py:21
  272.1 4.9 %collective-permute-start.18 = (bf16[2,2,32,384]{3,2,1,0:T(8,128)(2,1)}, bf16[2,2,32,384]{3,2,1,0:T(8,128)(2,1)S(1)}, u32[]{:S(2)}, u32[]{:S(2)}) collective-permute-start(bf16[2,2,32,384]{3,2,1,0:T(8,128)(2,1)} %get-tuple-element.81), channel_id=1, source_target_pairs={{0,8},{4,12},{8,0},{12,4},{16,24},{20,28},{24,16},{28,20},{1,9},{5... | collective-permute-start | bytes 294920 | tf_op jit(solution)/shard_map/ppermute | solution.py:21
  272.9 7.0 %collective-permute-start.19 = (bf16[2,2,32,384]{3,2,1,0:T(8,128)(2,1)}, bf16[2,2,32,384]{3,2,1,0:T(8,128)(2,1)S(1)}, u32[]{:S(2)}, u32[]{:S(2)}) collective-permute-start(bf16[2,2,32,384]{3,2,1,0:T(8,128)(2,1)} %get-tuple-element.81), channel_id=1, source_target_pairs={{0,16},{4,20},{8,24},{12,28},{16,0},{20,4},{24,8},{28,12},{1,17},{... | collective-permute-start | bytes 294920 | tf_op jit(solution)/shard_map/ppermute | solution.py:21
  273.6 10.3 %collective-permute-start.15 = (bf16[4,2,32,768]{3,2,1,0:T(8,128)(2,1)S(1)}, bf16[4,2,32,768]{3,2,1,0:T(8,128)(2,1)S(1)}, u32[]{:S(2)}, u32[]{:S(2)}) collective-permute-start(bf16[4,2,32,768]{3,2,1,0:T(8,128)(2,1)S(1)} %get-tuple-element.65), channel_id=1, source_target_pairs={{0,4},{4,0},{8,12},{12,8},{16,20},{20,16},{24,28},{28,24},{1,5},{5... | collective-permute-start | bytes 1179656 | tf_op jit(solution)/shard_map/ppermute | solution.py:21
  277.0 6.7 %collective-permute-start.20 = (bf16[2,2,32,384]{3,2,1,0:T(8,128)(2,1)}, bf16[2,2,32,384]{3,2,1,0:T(8,128)(2,1)S(1)}, u32[]{:S(2)}, u32[]{:S(2)}) collective-permute-start(bf16[2,2,32,384]{3,2,1,0:T(8,128)(2,1)} %get-tuple-element.81), channel_id=1, source_target_pairs={{0,24},{4,28},{8,16},{12,20},{16,8},{20,12},{24,0},{28,4},{1,25},{... | collective-permute-start | bytes 294920 | tf_op jit(solution)/shard_map/ppermute | solution.py:21
  295.9 11.5 %all-to-all-start.7 = ((f32[8,1,64]{2,1,0:T(1,128)}), f32[8,1,64]{2,1,0:T(1,128)S(1)}, u32[]{:S(2)}, u32[]{:S(2)}) async-start(f32[8,1,64]{2,1,0:T(1,128)} %bitcast.66), calls=%async_computation.7 | async-start | bytes 8192 | tf_op jit(solution)/shard_map/all_to_all | solution.py:392
  (9 other events, 37.9 us)
Sparse Core Ops, SparseCore 0:
  10.4 66.1 all-gather.6
  144.9 58.0 all-gather.4

commit v11 on v9

--- a/solution.py
+++ b/solution.py
@@ -82,7 +82,7 @@
     pass
 
 
-def after(x, *others):
+def after(x, *others, flops=0):
     anywhere = pl.BlockSpec(memory_space=pl.ANY)
     return pl.pallas_call(
         hand_on,
@@ -90,6 +90,7 @@
         in_specs=[anywhere] * (1 + len(others)),
         out_specs=anywhere,
         input_output_aliases={0: 0},
+        cost_estimate=pl.CostEstimate(flops=flops, bytes_accessed=0, transcendentals=0),
     )(x, *others)
 
 
@@ -487,8 +488,10 @@
     after_mixer = own.astype(F32) + total[:, :D] * lax.rsqrt(square / D + epsilon)
     after_mixer = after(after_mixer.astype(BF16), feed_weights)
     everything = lax.all_gather(after_mixer, "req", axis=0, tiled=True)
-    arrived += [to_all(after(piece, after_mixer[:8, :128]), "req") for piece in pieces[1:]]
-    arrived_kv = to_all(kv.reshape(n, -1, width), "req")
+    for piece in pieces[1:]:
+        piece = after(piece, after_mixer, *arrived, flops=50_000_000_000)
+        arrived += [to_all(piece, "req")]
+    arrived_kv = to_all(after(kv, arrived[-1]).reshape(n, -1, width), "req")
 
     row = jnp.arange(n * rows, dtype=jnp.int32)
     by_owner, by_group, by_step = row // rows, (row % rows) // steps, row % steps

time: 315 us -> 290 us (0.921)
  waiting for transfers between devices: 152 us -> 130 us
  blocking collectives: 31 us -> 17.2 us
  starting transfers between devices: 45.8 us -> 51.9 us
    all_gather x1, waiting for transfers between devices: 57.9 us -> 0.01 us  [on_device(): everything = lax.all_gather(after_mixer, 'req', axis=0, tiled=True)]
    all_to_all x6 -> x7, waiting for transfers between devices: 68.3 us -> 105 us  [to_all(): return lax.all_to_all(x, axis, split_axis=0, concat_axis=0, tiled=True)]
    all_to_all x1 -> x0, blocking collectives: 13.7 us -> none  [to_all(): return lax.all_to_all(x, axis, split_axis=0, concat_axis=0, tiled=True)]
    all_to_all x6 -> x7, starting transfers between devices: 26.1 us -> 31.6 us  [to_all(): return lax.all_to_all(x, axis, split_axis=0, concat_axis=0, tiled=True)]
    unnamed x37 -> x31, local copies, waits for them, and re-layouts: 2.31 us -> 5.61 us
  transfers between devices with their start and end apart: 30 -> 31, of which waited for: 17 -> 17; matrix products, arithmetic and copies ran while one was open for 8% -> 9% of each run, Pallas kernels for 9% -> 10%
where the time goes in v11:
time: 290 us; the launch traced here: 289 us
  waiting for transfers between devices  130 us (45%)
  starting transfers between devices  51.9 us (18%)
  Pallas kernels  35.7 us (12%)
  local copies, waits for them, and re-layouts  19.7 us (7%)
  blocking collectives  17.2 us (6%)
  other arithmetic  17.1 us (6%)
  between operations  16 us (6%)
    all_to_all x7, waiting for transfers between devices, to_all(): return lax.all_to_all(x, axis, split_axis=0, concat_axis=0, tiled=True)  105 us
    all_to_all x7, starting transfers between devices, to_all(): return lax.all_to_all(x, axis, split_axis=0, concat_axis=0, tiled=True)  31.6 us
    ppermute x22, waiting for transfers between devices, swap(): return lax.ppermute(x, axis, [(i, i ^ offset) for i in range(size)])  24.8 us
    ppermute x22, starting transfers between devices, swap(): return lax.ppermute(x, axis, [(i, i ^ offset) for i in range(size)])  20.2 us
    all_gather x1, blocking collectives, on_device(): lax.all_gather(jnp.concatenate([embed_part, gains_high, gains_low, extra]...  11.6 us
    pallas_call x1, Pallas kernels, greatest_entries(): pl.pallas_call(greatest_kernel, out_shape=jax.ShapeDtypeStruct((blocks, f...  8.21 us
    pallas_call x1, Pallas kernels, mixer(): pl.pallas_call(functools.partial(mixer_kernel, counts, owners, heads, cla...  8.14 us
    pallas_call x1, Pallas kernels, feed_forward(): pl.pallas_call(feed_kernel, out_shape=[jax.ShapeDtypeStruct((tokens, widt...  7.97 us
  transfers between devices with their start and end apart: 31, of which 17 were waited for; matrix products, arithmetic and copies ran while one was open for 9% of the time, Pallas kernels for 10%

profile of v11, /device:TPU:0, one launch (start us, length us, event | category | flops | bytes accessed | tf_op | source)
XLA Modules:
  0.0 288.6 jit_solution(7819840707692461261)
XLA Ops:
  7.2 3.0 %pad_maximum_fusion = bf16[2112,512]{1,0:T(8,128)(2,1)} fusion(bf16[704,512]{1,0:T(8,128)(2,1)} %param.38, bf16[704,512]{1,0:T(8,128)(2,1)} %bitcast.126, bf16[704,512]{1,0:T(8,128)(2,1)} %bitcast.127), kind=kLoop, calls=%fused_computation.10 | loop fusion | flops 6488064 | bytes 4325376 | tf_op jit(solution)/shard_map/concatenate | solution.py:410
  11.6 7.3 %all-to-all-start.1 = ((s32[8,1,192]{2,1,0:T(1,128)}), s32[8,1,192]{2,1,0:T(1,128)S(1)}, u32[]{:S(2)}, u32[]{:S(2)}) async-start(s32[8,1,192]{2,1,0:T(1,128)} %reshape.516), calls=%async_computation.1 | async-start | bytes 16384 | tf_op jit(solution)/shard_map/all_to_all | solution.py:390
  18.9 6.5 %all-to-all-done.1 = s32[8,1,192]{2,1,0:T(1,128)S(1)} async-done(((s32[8,1,192]{2,1,0:T(1,128)}), s32[8,1,192]{2,1,0:T(1,128)S(1)}, u32[]{:S(2)}, u32[]{:S(2)}) %all-to-all-start.1) | async-done | bytes 6176 | tf_op jit(solution)/shard_map/all_to_all | solution.py:390
  28.1 5.3 %gather_fusion.1 = bf16[512,512]{1,0:T(8,128)(2,1)} fusion(bf16[4000,512]{1,0:T(8,128)(2,1)} %param.27, s32[1024]{0:T(1024)S(1)} %pad_clamp_fusion.2), kind=kCustom, calls=%fused_computation.1 | custom fusion | bytes 1050624 | tf_op jit(solution)/shard_map/jit(_take)/gather | solution.py:437
  33.4 3.5 %all-to-all-start.2 = ((bf16[8,64,512]{2,1,0:T(8,128)(2,1)}), bf16[8,64,512]{2,1,0:T(8,128)(2,1)S(1)}, u32[]{:S(2)}, u32[]{:S(2)}) async-start(bf16[8,64,512]{2,1,0:T(8,128)(2,1)} %bitcast.10), calls=%async_computation.2 | async-start | bytes 1048576 | tf_op jit(solution)/shard_map/all_to_all | solution.py:390
  39.9 4.5 %shard_map.219 = (bf16[8,2,4,128,128]{4,3,2,1,0:T(8,128)(2,1)}, bf16[8,2,4,128,128]{4,3,2,1,0:T(8,128)(2,1)}) custom-call(s32[32]{0:T(128)} %select_n.248.order_ref, bf16[32,4,128,128]{3,2,1,0:T(8,128)(2,1)} %old_ref.1), custom_call_target="tpu_custom_call" | custom-call | tf_op jit(solution)/shard_map/pallas_call | solution.py:65
  44.7 5.5 %all-to-all-done.2 = bf16[8,64,512]{2,1,0:T(8,128)(2,1)S(1)} async-done(((bf16[8,64,512]{2,1,0:T(8,128)(2,1)}), bf16[8,64,512]{2,1,0:T(8,128)(2,1)S(1)}, u32[]{:S(2)}, u32[]{:S(2)}) %all-to-all-start.2) | async-done | bytes 524320 | tf_op jit(solution)/shard_map/all_to_all | solution.py:390
  50.5 3.8 %all-to-all-start.3 = ((bf16[8,2,4,128,128]{4,3,2,1,0:T(8,128)(2,1)}), bf16[8,2,4,128,128]{4,3,2,1,0:T(8,128)(2,1)S(1)}, u32[]{:S(2)}, u32[]{:S(2)}) async-start(bf16[8,2,4,128,128]{4,3,2,1,0:T(8,128)(2,1)} %get-tuple-element.42.rest_0_), calls=%async_computation.3 | async-start | bytes 4194304 | tf_op jit(solution)/shard_map/all_to_all | solution.py:390
  55.8 11.6 %all_gather.18.emb_ref = bf16[144,2048]{1,0:T(8,128)(2,1)} all-gather(bf16[144,512]{1,0:T(8,128)(2,1)S(1)} %maximum_maximum_fusion), channel_id=1, replica_groups=mesh['req'=8,'head'=4] {'head'}, dimensions={1}, use_global_device_ids=true | all-gather | bytes 737280 | tf_op jit(solution)/shard_map/all_gather | solution.py:466
  67.4 8.1 %shard_map.220 = (bf16[32,2048]{1,0:T(8,128)(2,1)}, bf16[256,512]{1,0:T(8,128)(2,1)}, bf16[32,2176]{1,0:T(8,128)(2,1)}, bf16[32,2176]{1,0:T(8,128)(2,1)}, bf16[3...) custom-call(s32[2]{0:T(128)} %pad_add_fusion.1.me_ref, bf16[144,2048]{1,0:T(8,128)(2,1)} %all_gather.18.emb_ref, ...), custom_call_target="tpu_custom_call" | custom-call | tf_op jit(solution)/shard_map/pallas_call | solution.py:215
  77.5 5.1 %collective-permute-done.1 = bf16[32,2176]{1,0:T(8,128)(2,1)S(1)} collective-permute-done((bf16[32,2176]{1,0:T(8,128)(2,1)}, bf16[32,2176]{1,0:T(8,128)(2,1)S(1)}, u32[]{:S(2)}, u32[]{:S(2)}) %collective-permute-start.1) | collective-permute-done | bytes 139296 | tf_op jit(solution)/shard_map/ppermute | solution.py:21
  87.0 14.7 %all-to-all-done.3.refs_2_.rest_0_ = bf16[8,2,4,128,128]{4,3,2,1,0:T(8,128)(2,1)S(1)} async-done(((bf16[8,2,4,128,128]{4,3,2,1,0:T(8,128)(2,1)}), bf16[8,2,4,128,128]{4,3,2,1,0:T(8,128)(2,1)S(1)}, u32[]{:S(2)}, u32[]{:S(2)}) %all-to-all-start.3) | async-done | bytes 2097184 | tf_op jit(solution)/shard_map/all_to_all | solution.py:390
  103.0 3.8 %all-to-all-start.4 = ((bf16[8,2,4,128,128]{4,3,2,1,0:T(8,128)(2,1)}), bf16[8,2,4,128,128]{4,3,2,1,0:T(8,128)(2,1)S(1)}, u32[]{:S(2)}, u32[]{:S(2)}) async-start(bf16[8,2,4,128,128]{4,3,2,1,0:T(8,128)(2,1)} %shard_map.223), calls=%async_computation.4 | async-start | bytes 4194304 | tf_op jit(solution)/shard_map/all_to_all | solution.py:390
  108.6 58.4 %all-to-all-done.4.refs_1_.refs_3_.rest_1_ = bf16[8,2,4,128,128]{4,3,2,1,0:T(8,128)(2,1)S(1)} async-done(((bf16[8,2,4,128,128]{4,3,2,1,0:T(8,128)(2,1)}), bf16[8,2,4,128,128]{4,3,2,1,0:T(8,128)(2,1)S(1)}, u32[]{:S(2)}, u32[]{:S(2)}) %all-to-all-start.4) | async-done | bytes 2097184 | tf_op jit(solution)/shard_map/all_to_all | solution.py:390
  168.2 3.8 %all-to-all-start.5 = ((bf16[8,32,512]{2,1,0:T(8,128)(2,1)}), bf16[8,32,512]{2,1,0:T(8,128)(2,1)S(1)}, u32[]{:S(2)}, u32[]{:S(2)}) async-start(bf16[8,32,512]{2,1,0:T(8,128)(2,1)} %bitcast.125), calls=%async_computation.5 | async-start | bytes 524288 | tf_op jit(solution)/shard_map/all_to_all | solution.py:390
  173.4 8.0 %shard_map.222 = (bf16[256,2048]{1,0:T(8,128)(2,1)}, bf16[32,2048]{1,0:T(8,128)(2,1)}) custom-call(bf16[256,2048]{1,0:T(8,128)(2,1)} %all-gather.5.cloned.1.call-done.x_hbm, bf16[4,2112,512]{2,1,0:T(8,128)(2,1)} %bitcast.117, bf16[256,256]{1,0:T(8,128)(2,1)} %fusion.5.pick_ref, bf16[32,256]{1,0:T(8,128)(2,1)} %compare_convert_fusion.mine_ref, ...), custom_call_target="tpu_custom_call" | custom-call | tf_op jit(solution)/shard_map/pallas_call | solution.py:318
  182.1 6.1 %all-to-all-start.6 = ((bf16[8,32,2048]{2,1,0:T(8,128)(2,1)}), bf16[8,32,2048]{2,1,0:T(8,128)(2,1)S(1)}, u32[]{:S(2)}, u32[]{:S(2)}) async-start(bf16[8,32,2048]{2,1,0:T(8,128)(2,1)} %bitcast.119), calls=%async_computation.6 | async-start | bytes 2097152 | tf_op jit(solution)/shard_map/all_to_all | solution.py:390
  191.8 6.8 %shard_map.226 = bf16[32,4,128,128]{3,2,1,0:T(8,128)(2,1)} custom-call(s32[32]{0:T(128)} %select_reduce_fusion.2.slot_ref, f32[32,8,512]{2,1,0:T(8,128)} %convert.2.kv_ref, bf16[8,2,4,128,128]{4,3,2,1,0:T(8,128)(2,1)} %copy-done.1, bf16[8,2,4,128,128]{4,3,2,1,0:T(8,128)(2,1)} %copy-done), custom_call_target="tpu_custom_call" | custom-call | tf_op jit(solution)/shard_map/pallas_call | solution.py:266
  198.6 15.2 %all-to-all-done.6 = bf16[8,32,2048]{2,1,0:T(8,128)(2,1)S(1)} async-done(((bf16[8,32,2048]{2,1,0:T(8,128)(2,1)}), bf16[8,32,2048]{2,1,0:T(8,128)(2,1)S(1)}, u32[]{:S(2)}, u32[]{:S(2)}) %all-to-all-start.6) | async-done | bytes 1048608 | tf_op jit(solution)/shard_map/all_to_all | solution.py:390
  215.7 2.9 %collective-permute-start.8 = (bf16[32,896]{1,0:T(8,128)(2,1)S(1)}, bf16[32,896]{1,0:T(8,128)(2,1)S(1)}, u32[]{:S(2)}, u32[]{:S(2)}) collective-permute-start(bf16[32,896]{1,0:T(8,128)(2,1)S(1)} %get-tuple-element.73), channel_id=1, source_target_pairs={{0,24},{4,28},{8,16},{12,20},{16,8},{20,12},{24,0},{28,4},{1,25},{... | collective-permute-start | bytes 172040 | tf_op jit(solution)/shard_map/ppermute | solution.py:21
  220.5 2.2 collective-permute-done.16
  222.7 1.8 collective-permute-start.11
  226.9 1.9 collective-permute-done.17
  229.4 3.3 %collective-permute-done.9 = bf16[4,32,896]{2,1,0:T(8,128)(2,1)S(1)} collective-permute-done((bf16[4,32,896]{2,1,0:T(8,128)(2,1)S(1)}, bf16[4,32,896]{2,1,0:T(8,128)(2,1)S(1)}, u32[]{:S(2)}, u32[]{:S(2)}) %collective-permute-start.9) | collective-permute-done | bytes 229408 | tf_op jit(solution)/shard_map/ppermute | solution.py:21
  233.8 1.8 collective-permute-start.4
  236.2 3.1 %collective-permute-done.14 = bf16[2,32,768]{2,1,0:T(8,128)(2,1)S(1)} collective-permute-done((bf16[2,32,768]{2,1,0:T(8,128)(2,1)S(1)}, bf16[2,32,768]{2,1,0:T(8,128)(2,1)S(1)}, u32[]{:S(2)}, u32[]{:S(2)}) %collective-permute-start.14) | collective-permute-done | bytes 98336 | tf_op jit(solution)/shard_map/ppermute | solution.py:21
  247.7 2.1 collective-permute-done.19
  249.8 3.2 %collective-permute-done.20 = bf16[2,2,32,384]{3,2,1,0:T(8,128)(2,1)S(1)} collective-permute-done((bf16[2,2,32,384]{3,2,1,0:T(8,128)(2,1)}, bf16[2,2,32,384]{3,2,1,0:T(8,128)(2,1)S(1)}, u32[]{:S(2)}, u32[]{:S(2)}) %collective-permute-start.20) | collective-permute-done | bytes 98336 | tf_op jit(solution)/shard_map/ppermute | solution.py:21
  255.0 8.2 %shard_map.227 = f32[8,64]{1,0:T(8,128)} custom-call(bf16[512,2048]{1,0:T(8,128)(2,1)} %bitcast.118, bf16[1000,2048]{1,0:T(8,128)(2,1)} %bitcast.122, bf16[1000,2048]{1,0:T(8,128)(2,1)} %collective-permute-done.21.other_hbm), custom_call_target="tpu_custom_call" | custom-call | tf_op jit(solution)/shard_map/pallas_call | solution.py:360
  265.1 3.3 %all-to-all-start.7 = ((f32[8,1,64]{2,1,0:T(1,128)}), f32[8,1,64]{2,1,0:T(1,128)S(1)}, u32[]{:S(2)}, u32[]{:S(2)}) async-start(f32[8,1,64]{2,1,0:T(1,128)} %bitcast.66), calls=%async_computation.7 | async-start | bytes 8192 | tf_op jit(solution)/shard_map/all_to_all | solution.py:390
  269.7 5.2 %all-to-all-done.7 = f32[8,1,64]{2,1,0:T(1,128)S(1)} async-done(((f32[8,1,64]{2,1,0:T(1,128)}), f32[8,1,64]{2,1,0:T(1,128)S(1)}, u32[]{:S(2)}, u32[]{:S(2)}) %all-to-all-start.7) | async-done | bytes 2080 | tf_op jit(solution)/shard_map/all_to_all | solution.py:390
  275.2 5.6 %all-reduce = f32[256]{0:T(256)S(1)} all-reduce(f32[256]{0:T(256)S(1)} %dynamic-update-slice), channel_id=3, replica_groups=mesh['req'=8,'head'=4] {'head'}, use_global_device_ids=true, to_apply=%add | all-reduce | flops 256 | bytes 2048
  (190 shorter events, 47.1 us)
Async XLA Ops:
  7.2 79.9 %all-gather.7.cloned.1.call-start = ((), (), s32[]{:S(2)}) async-start(), calls=%async_computation.9 | async-start | bytes 10813440 | tf_op jit(solution)/shard_map/all_gather | solution.py:411
  11.6 13.8 %all-to-all-start.1 = ((s32[8,1,192]{2,1,0:T(1,128)}), s32[8,1,192]{2,1,0:T(1,128)S(1)}, u32[]{:S(2)}, u32[]{:S(2)}) async-start(s32[8,1,192]{2,1,0:T(1,128)} %reshape.516), calls=%async_computation.1 | async-start | bytes 16384 | tf_op jit(solution)/shard_map/all_to_all | solution.py:390
  33.4 16.8 %all-to-all-start.2 = ((bf16[8,64,512]{2,1,0:T(8,128)(2,1)}), bf16[8,64,512]{2,1,0:T(8,128)(2,1)S(1)}, u32[]{:S(2)}, u32[]{:S(2)}) async-start(bf16[8,64,512]{2,1,0:T(8,128)(2,1)} %bitcast.10), calls=%async_computation.2 | async-start | bytes 1048576 | tf_op jit(solution)/shard_map/all_to_all | solution.py:390
  50.5 51.2 %all-to-all-start.3 = ((bf16[8,2,4,128,128]{4,3,2,1,0:T(8,128)(2,1)}), bf16[8,2,4,128,128]{4,3,2,1,0:T(8,128)(2,1)S(1)}, u32[]{:S(2)}, u32[]{:S(2)}) async-start(bf16[8,2,4,128,128]{4,3,2,1,0:T(8,128)(2,1)} %get-tuple-element.42.rest_0_), calls=%async_computation.3 | async-start | bytes 4194304 | tf_op jit(solution)/shard_map/all_to_all | solution.py:390
  75.6 1.9 collective-permute-start
  75.9 6.7 %collective-permute-start.1 = (bf16[32,2176]{1,0:T(8,128)(2,1)}, bf16[32,2176]{1,0:T(8,128)(2,1)S(1)}, u32[]{:S(2)}, u32[]{:S(2)}) collective-permute-start(bf16[32,2176]{1,0:T(8,128)(2,1)} %get-tuple-element.47), channel_id=1, source_target_pairs={{0,2},{1,3},{2,0},{3,1},{4,6},{5,7},{6,4},{7,5},{8,10},{9,11},{10,... | collective-permute-start | bytes 417800 | tf_op jit(solution)/shard_map/ppermute | solution.py:21
  77.1 7.2 %collective-permute-start.2 = (bf16[32,2176]{1,0:T(8,128)(2,1)}, bf16[32,2176]{1,0:T(8,128)(2,1)S(1)}, u32[]{:S(2)}, u32[]{:S(2)}) collective-permute-start(bf16[32,2176]{1,0:T(8,128)(2,1)} %get-tuple-element.48), channel_id=1, source_target_pairs={{0,3},{1,2},{2,1},{3,0},{4,7},{5,6},{6,5},{7,4},{8,11},{9,10},{10,... | collective-permute-start | bytes 417800 | tf_op jit(solution)/shard_map/ppermute | solution.py:21
  103.0 63.9 %all-to-all-start.4 = ((bf16[8,2,4,128,128]{4,3,2,1,0:T(8,128)(2,1)}), bf16[8,2,4,128,128]{4,3,2,1,0:T(8,128)(2,1)S(1)}, u32[]{:S(2)}, u32[]{:S(2)}) async-start(bf16[8,2,4,128,128]{4,3,2,1,0:T(8,128)(2,1)} %shard_map.223), calls=%async_computation.4 | async-start | bytes 4194304 | tf_op jit(solution)/shard_map/all_to_all | solution.py:390
  106.8 66.7 %all-gather.5.cloned.1.call-start = ((), (), s32[]{:S(2)}) async-start(), calls=%async_computation.8 | async-start | bytes 1179648 | tf_op jit(solution)/shard_map/all_gather | solution.py:490
  106.8 148.2 %collective-permute-start.21 = (bf16[1000,2048]{1,0:T(8,128)(2,1)}, bf16[1000,2048]{1,0:T(8,128)(2,1)}, u32[]{:S(2)}, u32[]{:S(2)}) collective-permute-start(bf16[1000,2048]{1,0:T(8,128)(2,1)} %bitcast.121), channel_id=1, source_target_pairs={{0,1},{1,0},{2,3},{3,2},{4,5},{5,4},{6,7},{7,6},{8,9},{9,8},{10,11... | collective-permute-start | bytes 12288008 | tf_op jit(solution)/shard_map/ppermute | solution.py:21
  168.2 13.2 %all-to-all-start.5 = ((bf16[8,32,512]{2,1,0:T(8,128)(2,1)}), bf16[8,32,512]{2,1,0:T(8,128)(2,1)S(1)}, u32[]{:S(2)}, u32[]{:S(2)}) async-start(bf16[8,32,512]{2,1,0:T(8,128)(2,1)} %bitcast.125), calls=%async_computation.5 | async-start | bytes 524288 | tf_op jit(solution)/shard_map/all_to_all | solution.py:390
  182.1 31.6 %all-to-all-start.6 = ((bf16[8,32,2048]{2,1,0:T(8,128)(2,1)}), bf16[8,32,2048]{2,1,0:T(8,128)(2,1)S(1)}, u32[]{:S(2)}, u32[]{:S(2)}) async-start(bf16[8,32,2048]{2,1,0:T(8,128)(2,1)} %bitcast.119), calls=%async_computation.6 | async-start | bytes 2097152 | tf_op jit(solution)/shard_map/all_to_all | solution.py:390
  191.8 22.1 %copy-start.4 = (bf16[32,2048]{1,0:T(8,128)(2,1)S(1)}, bf16[32,2048]{1,0:T(8,128)(2,1)}, u32[]{:S(2)}) copy-start(bf16[32,2048]{1,0:T(8,128)(2,1)} %get-tuple-element.49) | copy-start | bytes 393220
  214.2 10.3 %collective-permute-start.6 = (bf16[32,896]{1,0:T(8,128)(2,1)S(1)}, bf16[32,896]{1,0:T(8,128)(2,1)S(1)}, u32[]{:S(2)}, u32[]{:S(2)}) collective-permute-start(bf16[32,896]{1,0:T(8,128)(2,1)S(1)} %get-tuple-element.73), channel_id=1, source_target_pairs={{0,8},{4,12},{8,0},{12,4},{16,24},{20,28},{24,16},{28,20},{1,9},{5... | collective-permute-start | bytes 172040 | tf_op jit(solution)/shard_map/ppermute | solution.py:21
  214.3 10.3 %collective-permute-start.7 = (bf16[32,896]{1,0:T(8,128)(2,1)S(1)}, bf16[32,896]{1,0:T(8,128)(2,1)S(1)}, u32[]{:S(2)}, u32[]{:S(2)}) collective-permute-start(bf16[32,896]{1,0:T(8,128)(2,1)S(1)} %get-tuple-element.73), channel_id=1, source_target_pairs={{0,16},{4,20},{8,24},{12,28},{16,0},{20,4},{24,8},{28,12},{1,17},{... | collective-permute-start | bytes 172040 | tf_op jit(solution)/shard_map/ppermute | solution.py:21
  215.7 9.2 %collective-permute-start.8 = (bf16[32,896]{1,0:T(8,128)(2,1)S(1)}, bf16[32,896]{1,0:T(8,128)(2,1)S(1)}, u32[]{:S(2)}, u32[]{:S(2)}) collective-permute-start(bf16[32,896]{1,0:T(8,128)(2,1)S(1)} %get-tuple-element.73), channel_id=1, source_target_pairs={{0,24},{4,28},{8,16},{12,20},{16,8},{20,12},{24,0},{28,4},{1,25},{... | collective-permute-start | bytes 172040 | tf_op jit(solution)/shard_map/ppermute | solution.py:21
  218.8 3.9 %collective-permute-start.16 = (bf16[32,384]{1,0:T(8,128)(2,1)S(1)}, bf16[32,384]{1,0:T(8,128)(2,1)S(1)}, u32[]{:S(2)}, u32[]{:S(2)}) collective-permute-start(bf16[32,384]{1,0:T(8,128)(2,1)S(1)} %get-tuple-element.77), channel_id=1, source_target_pairs={{0,4},{4,0},{8,12},{12,8},{16,20},{20,16},{24,28},{28,24},{1,5},{5... | collective-permute-start | bytes 73736 | tf_op jit(solution)/shard_map/ppermute | solution.py:21
  222.7 4.1 %collective-permute-start.11 = (bf16[32,768]{1,0:T(8,128)(2,1)S(1)}, bf16[32,768]{1,0:T(8,128)(2,1)S(1)}, u32[]{:S(2)}, u32[]{:S(2)}) collective-permute-start(bf16[32,768]{1,0:T(8,128)(2,1)S(1)} %get-tuple-element.75), channel_id=1, source_target_pairs={{0,2},{1,3},{2,0},{3,1},{4,6},{5,7},{6,4},{7,5},{8,10},{9,11},{10,... | collective-permute-start | bytes 147464 | tf_op jit(solution)/shard_map/ppermute | solution.py:21
  224.5 16.5 %collective-permute-start.3 = (f32[32,640]{1,0:T(8,128)S(1)}, f32[32,640]{1,0:T(8,128)S(1)}, u32[]{:S(2)}, u32[]{:S(2)}) collective-permute-start(f32[32,640]{1,0:T(8,128)S(1)} %get-tuple-element.90), channel_id=1, source_target_pairs={{0,1},{1,0},{2,3},{3,2},{4,5},{5,4},{6,7},{7,6},{8,9},{9,8},{10,11... | collective-permute-start | bytes 245768 | tf_op jit(solution)/shard_map/ppermute | solution.py:21
  224.6 4.2 %collective-permute-start.17 = (bf16[2,32,384]{2,1,0:T(8,128)(2,1)S(1)}, bf16[2,32,384]{2,1,0:T(8,128)(2,1)S(1)}, u32[]{:S(2)}, u32[]{:S(2)}) collective-permute-start(bf16[2,32,384]{2,1,0:T(8,128)(2,1)S(1)} %get-tuple-element.88), channel_id=1, source_target_pairs={{0,2},{1,3},{2,0},{3,1},{4,6},{5,7},{6,4},{7,5},{8,10},{9,11},{10,... | collective-permute-start | bytes 147464 | tf_op jit(solution)/shard_map/ppermute | solution.py:21
  225.0 7.8 %collective-permute-start.9 = (bf16[4,32,896]{2,1,0:T(8,128)(2,1)S(1)}, bf16[4,32,896]{2,1,0:T(8,128)(2,1)S(1)}, u32[]{:S(2)}, u32[]{:S(2)}) collective-permute-start(bf16[4,32,896]{2,1,0:T(8,128)(2,1)S(1)} %get-tuple-element.71), channel_id=1, source_target_pairs={{0,4},{4,0},{8,12},{12,8},{16,20},{20,16},{24,28},{28,24},{1,5},{5... | collective-permute-start | bytes 688136 | tf_op jit(solution)/shard_map/ppermute | solution.py:21
  226.8 6.9 %collective-permute-start.12 = (bf16[2,32,768]{2,1,0:T(8,128)(2,1)S(1)}, bf16[2,32,768]{2,1,0:T(8,128)(2,1)S(1)}, u32[]{:S(2)}, u32[]{:S(2)}) collective-permute-start(bf16[2,32,768]{2,1,0:T(8,128)(2,1)S(1)} %get-tuple-element.79), channel_id=1, source_target_pairs={{0,8},{4,12},{8,0},{12,4},{16,24},{20,28},{24,16},{28,20},{1,9},{5... | collective-permute-start | bytes 294920 | tf_op jit(solution)/shard_map/ppermute | solution.py:21
  228.8 7.4 %collective-permute-start.13 = (bf16[2,32,768]{2,1,0:T(8,128)(2,1)S(1)}, bf16[2,32,768]{2,1,0:T(8,128)(2,1)S(1)}, u32[]{:S(2)}, u32[]{:S(2)}) collective-permute-start(bf16[2,32,768]{2,1,0:T(8,128)(2,1)S(1)} %get-tuple-element.79), channel_id=1, source_target_pairs={{0,16},{4,20},{8,24},{12,28},{16,0},{20,4},{24,8},{28,12},{1,17},{... | collective-permute-start | bytes 294920 | tf_op jit(solution)/shard_map/ppermute | solution.py:21
  232.7 6.5 %collective-permute-start.14 = (bf16[2,32,768]{2,1,0:T(8,128)(2,1)S(1)}, bf16[2,32,768]{2,1,0:T(8,128)(2,1)S(1)}, u32[]{:S(2)}, u32[]{:S(2)}) collective-permute-start(bf16[2,32,768]{2,1,0:T(8,128)(2,1)S(1)} %get-tuple-element.79), channel_id=1, source_target_pairs={{0,24},{4,28},{8,16},{12,20},{16,8},{20,12},{24,0},{28,4},{1,25},{... | collective-permute-start | bytes 294920 | tf_op jit(solution)/shard_map/ppermute | solution.py:21
  233.8 7.4 %collective-permute-start.4 = (f32[32,640]{1,0:T(8,128)S(1)}, f32[32,640]{1,0:T(8,128)S(1)}, u32[]{:S(2)}, u32[]{:S(2)}) collective-permute-start(f32[32,640]{1,0:T(8,128)S(1)} %get-tuple-element.91), channel_id=1, source_target_pairs={{0,2},{1,3},{2,0},{3,1},{4,6},{5,7},{6,4},{7,5},{8,10},{9,11},{10,... | collective-permute-start | bytes 245768 | tf_op jit(solution)/shard_map/ppermute | solution.py:21
  236.2 6.5 %collective-permute-start.5 = (f32[32,640]{1,0:T(8,128)S(1)}, f32[32,640]{1,0:T(8,128)S(1)}, u32[]{:S(2)}, u32[]{:S(2)}) collective-permute-start(f32[32,640]{1,0:T(8,128)S(1)} %get-tuple-element.92), channel_id=1, source_target_pairs={{0,3},{1,2},{2,1},{3,0},{4,7},{5,6},{6,5},{7,4},{8,11},{9,10},{10,... | collective-permute-start | bytes 245768 | tf_op jit(solution)/shard_map/ppermute | solution.py:21
  239.3 13.8 %collective-permute-start.10 = (bf16[2,4,32,896]{3,2,1,0:T(8,128)(2,1)S(1)}, bf16[2,4,32,896]{3,2,1,0:T(8,128)(2,1)S(1)}, u32[]{:S(2)}, u32[]{:S(2)}) collective-permute-start(bf16[2,4,32,896]{3,2,1,0:T(8,128)(2,1)S(1)} %get-tuple-element.63), channel_id=1, source_target_pairs={{0,2},{1,3},{2,0},{3,1},{4,6},{5,7},{6,4},{7,5},{8,10},{9,11},{10,... | collective-permute-start | bytes 1376264 | tf_op jit(solution)/shard_map/ppermute | solution.py:21
  241.1 5.3 %collective-permute-start.18 = (bf16[2,2,32,384]{3,2,1,0:T(8,128)(2,1)}, bf16[2,2,32,384]{3,2,1,0:T(8,128)(2,1)S(1)}, u32[]{:S(2)}, u32[]{:S(2)}) collective-permute-start(bf16[2,2,32,384]{3,2,1,0:T(8,128)(2,1)} %get-tuple-element.81), channel_id=1, source_target_pairs={{0,8},{4,12},{8,0},{12,4},{16,24},{20,28},{24,16},{28,20},{1,9},{5... | collective-permute-start | bytes 294920 | tf_op jit(solution)/shard_map/ppermute | solution.py:21
  241.2 8.7 %collective-permute-start.19 = (bf16[2,2,32,384]{3,2,1,0:T(8,128)(2,1)}, bf16[2,2,32,384]{3,2,1,0:T(8,128)(2,1)S(1)}, u32[]{:S(2)}, u32[]{:S(2)}) collective-permute-start(bf16[2,2,32,384]{3,2,1,0:T(8,128)(2,1)} %get-tuple-element.81), channel_id=1, source_target_pairs={{0,16},{4,20},{8,24},{12,28},{16,0},{20,4},{24,8},{28,12},{1,17},{... | collective-permute-start | bytes 294920 | tf_op jit(solution)/shard_map/ppermute | solution.py:21
  242.6 10.6 %collective-permute-start.15 = (bf16[4,2,32,768]{3,2,1,0:T(8,128)(2,1)S(1)}, bf16[4,2,32,768]{3,2,1,0:T(8,128)(2,1)S(1)}, u32[]{:S(2)}, u32[]{:S(2)}) collective-permute-start(bf16[4,2,32,768]{3,2,1,0:T(8,128)(2,1)S(1)} %get-tuple-element.65), channel_id=1, source_target_pairs={{0,4},{4,0},{8,12},{12,8},{16,20},{20,16},{24,28},{28,24},{1,5},{5... | collective-permute-start | bytes 1179656 | tf_op jit(solution)/shard_map/ppermute | solution.py:21
  246.4 6.6 %collective-permute-start.20 = (bf16[2,2,32,384]{3,2,1,0:T(8,128)(2,1)}, bf16[2,2,32,384]{3,2,1,0:T(8,128)(2,1)S(1)}, u32[]{:S(2)}, u32[]{:S(2)}) collective-permute-start(bf16[2,2,32,384]{3,2,1,0:T(8,128)(2,1)} %get-tuple-element.81), channel_id=1, source_target_pairs={{0,24},{4,28},{8,16},{12,20},{16,8},{20,12},{24,0},{28,4},{1,25},{... | collective-permute-start | bytes 294920 | tf_op jit(solution)/shard_map/ppermute | solution.py:21
  265.1 9.7 %all-to-all-start.7 = ((f32[8,1,64]{2,1,0:T(1,128)}), f32[8,1,64]{2,1,0:T(1,128)S(1)}, u32[]{:S(2)}, u32[]{:S(2)}) async-start(f32[8,1,64]{2,1,0:T(1,128)} %bitcast.66), calls=%async_computation.7 | async-start | bytes 8192 | tf_op jit(solution)/shard_map/all_to_all | solution.py:390
  (11 other events, 33.8 us)
Sparse Core Ops, SparseCore 0:
  10.4 65.6 all-gather.6
  109.8 59.0 all-gather.4

commit v12 on v11

--- a/solution.py
+++ b/solution.py
@@ -330,11 +330,14 @@
             VMEM((tokens, weights.shape[1] // 3), BF16),
             pltpu.SemaphoreType.DMA((4,)),
         ],
+        cost_estimate=pl.CostEstimate(
+            flops=32 * tokens * weights.size, bytes_accessed=2 * weights.size, transcendentals=0
+        ),
         compiler_params=pltpu.CompilerParams(vmem_limit_bytes=58 << 20),
     )(x, weights, pick, mine, gain)
 
 
-def greatest_kernel(full_hbm, own_hbm, other_hbm, best_ref, full, own, other, sems):
+def greatest_kernel(me_ref, full_hbm, own_hbm, other_hbm, best_ref, full, own, other, sems):
     loads = [
         pltpu.make_async_copy(there, here, sems.at[i])
         for i, (there, here) in enumerate(((full_hbm, full), (own_hbm, own), (other_hbm, other)))
@@ -352,20 +355,23 @@
             best = top if best is None else jnp.maximum(best, top)
     width = best_ref.shape[1]
     for k in range(best_ref.shape[0]):
-        best_ref[k : k + 1, :] = best[:, k * width : (k + 1) * width]
-
-
-def greatest_entries(blocks, full, own, other):
+        best_ref[pl.ds(me_ref[0] ^ k, 1), :] = best[:, k * width : (k + 1) * width]
+
+
+def greatest_entries(me, blocks, full, own, other):
     anywhere = pl.BlockSpec(memory_space=pl.ANY)
     return pl.pallas_call(
         greatest_kernel,
         out_shape=jax.ShapeDtypeStruct((blocks, full.shape[0] // blocks), F32),
-        in_specs=[anywhere] * 3,
+        in_specs=[pl.BlockSpec(memory_space=SMEM)] + [anywhere] * 3,
         out_specs=pl.BlockSpec(memory_space=VMEM),
         scratch_shapes=[VMEM(x.shape, BF16) for x in (full, own, other)]
         + [pltpu.SemaphoreType.DMA((3,))],
+        cost_estimate=pl.CostEstimate(
+            flops=8 * full.shape[0] * own.size, bytes_accessed=4 * own.size, transcendentals=0
+        ),
         compiler_params=pltpu.CompilerParams(vmem_limit_bytes=58 << 20),
-    )(full, own, other)
+    )(me, full, own, other)
 
 
 def exchange(block, dim, n, n_head):
@@ -426,7 +432,7 @@
 
     ids = ordered[:steps].T.reshape(n, tokens)
     table = embedding.shape[0]
-    room = tokens // 2
+    room = tokens * 3 // 8
     holder = lax.div(ids, jnp.int32(table))
     held = holder == r
     earlier = jnp.triu(jnp.ones((tokens, tokens), BF16), 1)
@@ -491,7 +497,6 @@
     for piece in pieces[1:]:
         piece = after(piece, after_mixer, *arrived, flops=50_000_000_000)
         arrived += [to_all(piece, "req")]
-    arrived_kv = to_all(after(kv, arrived[-1]).reshape(n, -1, width), "req")
 
     row = jnp.arange(n * rows, dtype=jnp.int32)
     by_owner, by_group, by_step = row // rows, (row % rows) // steps, row % steps
@@ -503,7 +508,7 @@
     pick = (wanted[None, :] == row[:, None]).astype(BF16)
     mine = (wanted[None, :] == (r * rows + row[:rows])[:, None]).astype(BF16)
     down, kept = feed_forward(everything, feed_weights, pick, mine, feed_gain[None])
-    down = after(down, arrived_kv, *arrived)
+    down = after(down, *arrived)
     hidden = kept.astype(F32) + jnp.sum(to_all(down.reshape(n, rows, D), "req").astype(F32), axis=0)
     mean_square = jnp.mean(hidden * hidden, axis=1, keepdims=True)
 
@@ -543,12 +548,12 @@
         ],
         axis=-1,
     ).reshape(n * 2 * rows, D)
+    arrived_kv = to_all(after(kv, full).reshape(n, -1, width), "req")
     new_states = update_states(
         slot_of, arrived_kv.reshape(requests, 2 * steps, width).astype(F32), arrived, steps
     )
-    best = greatest_entries(n, full, vocab_weight.T, vocab_other)
-    best = jnp.take(best, jnp.arange(n) ^ r, axis=0)
-    got = jnp.max(to_all(best, "req"), axis=0)
+    best = greatest_entries(r[None], n, full, vocab_weight.T, vocab_other)
+    got = jnp.max(to_all(after(best, arrived_kv), "req"), axis=0)
     got = lax.all_gather(got, "head", axis=0).reshape(n_head, 2, rows)
     crossed = jnp.stack([got[i ^ 2, 1] for i in range(n_head)])
     best = jnp.maximum(got[:, 0], crossed).reshape(requests, steps)

time: 290 us -> 278 us (0.959)
  waiting for transfers between devices: 130 us -> 119 us
    all_to_all x7, waiting for transfers between devices: 105 us -> 68.9 us  [to_all(): return lax.all_to_all(x, axis, split_axis=0, concat_axis=0, tiled=True)]
    all_gather x1, waiting for transfers between devices: 0.01 us -> 26.4 us  [on_device(): everything = lax.all_gather(after_mixer, 'req', axis=0, tiled=True)]
  transfers between devices with their start and end apart: 31 -> 31, of which waited for: 17 -> 17; matrix products, arithmetic and copies ran while one was open for 9% -> 10% of each run, Pallas kernels for 10% -> 13%
where the time goes in v12:
time: 278 us; the launch traced here: 277 us
  waiting for transfers between devices  119 us (43%)
  starting transfers between devices  52.7 us (19%)
  Pallas kernels  35.6 us (13%)
  local copies, waits for them, and re-layouts  18.4 us (7%)
  other arithmetic  17.4 us (6%)
  blocking collectives  17.3 us (6%)
  between operations  15.9 us (6%)
    all_to_all x7, waiting for transfers between devices, to_all(): return lax.all_to_all(x, axis, split_axis=0, concat_axis=0, tiled=True)  68.9 us
    all_to_all x7, starting transfers between devices, to_all(): return lax.all_to_all(x, axis, split_axis=0, concat_axis=0, tiled=True)  31.2 us
    all_gather x1, waiting for transfers between devices, on_device(): everything = lax.all_gather(after_mixer, 'req', axis=0, tiled=True)  26.4 us
    ppermute x22, waiting for transfers between devices, swap(): return lax.ppermute(x, axis, [(i, i ^ offset) for i in range(size)])  23.3 us
    ppermute x22, starting transfers between devices, swap(): return lax.ppermute(x, axis, [(i, i ^ offset) for i in range(size)])  21.4 us
    all_gather x1, blocking collectives, on_device(): lax.all_gather(jnp.concatenate([embed_part, gains_high, gains_low, extra]...  11.7 us
    pallas_call x1, Pallas kernels, greatest_entries(): pl.pallas_call(greatest_kernel, out_shape=jax.ShapeDtypeStruct((blocks, f...  8.22 us
    pallas_call x1, Pallas kernels, mixer(): pl.pallas_call(functools.partial(mixer_kernel, counts, owners, heads, cla...  8.03 us
  transfers between devices with their start and end apart: 31, of which 17 were waited for; matrix products, arithmetic and copies ran while one was open for 10% of the time, Pallas kernels for 13%

profile of v12, /device:TPU:0, one launch (start us, length us, event | category | flops | bytes accessed | tf_op | source)
XLA Modules:
  0.0 276.6 jit_solution(2704065439116475056)
XLA Ops:
  7.2 3.0 %pad_maximum_fusion = bf16[2112,512]{1,0:T(8,128)(2,1)} fusion(bf16[704,512]{1,0:T(8,128)(2,1)} %param.38, bf16[704,512]{1,0:T(8,128)(2,1)} %bitcast.129, bf16[704,512]{1,0:T(8,128)(2,1)} %bitcast.130), kind=kLoop, calls=%fused_computation.9 | loop fusion | flops 6488064 | bytes 4325376 | tf_op jit(solution)/shard_map/concatenate | solution.py:416
  11.6 7.3 %all-to-all-start.1 = ((s32[8,1,192]{2,1,0:T(1,128)}), s32[8,1,192]{2,1,0:T(1,128)S(1)}, u32[]{:S(2)}, u32[]{:S(2)}) async-start(s32[8,1,192]{2,1,0:T(1,128)} %reshape.485), calls=%async_computation.1 | async-start | bytes 16384 | tf_op jit(solution)/shard_map/all_to_all | solution.py:396
  19.5 5.9 %all-to-all-done.1 = s32[8,1,192]{2,1,0:T(1,128)S(1)} async-done(((s32[8,1,192]{2,1,0:T(1,128)}), s32[8,1,192]{2,1,0:T(1,128)S(1)}, u32[]{:S(2)}, u32[]{:S(2)}) %all-to-all-start.1) | async-done | bytes 6176 | tf_op jit(solution)/shard_map/all_to_all | solution.py:396
  28.1 5.3 %gather_fusion.1 = bf16[384,512]{1,0:T(8,128)(2,1)} fusion(bf16[4000,512]{1,0:T(8,128)(2,1)} %param.27, s32[1024]{0:T(1024)S(1)} %pad_clamp_fusion.2), kind=kCustom, calls=%fused_computation.1 | custom fusion | bytes 787968 | tf_op jit(solution)/shard_map/jit(_take)/gather | solution.py:443
  33.4 3.5 %all-to-all-start.2 = ((bf16[8,48,512]{2,1,0:T(8,128)(2,1)}), bf16[8,48,512]{2,1,0:T(8,128)(2,1)S(1)}, u32[]{:S(2)}, u32[]{:S(2)}) async-start(bf16[8,48,512]{2,1,0:T(8,128)(2,1)} %bitcast.10), calls=%async_computation.2 | async-start | bytes 786432 | tf_op jit(solution)/shard_map/all_to_all | solution.py:396
  39.9 4.6 %shard_map.219 = (bf16[8,2,4,128,128]{4,3,2,1,0:T(8,128)(2,1)}, bf16[8,2,4,128,128]{4,3,2,1,0:T(8,128)(2,1)}) custom-call(s32[32]{0:T(128)} %select_n.235.order_ref, bf16[32,4,128,128]{3,2,1,0:T(8,128)(2,1)} %old_ref.1), custom_call_target="tpu_custom_call" | custom-call | tf_op jit(solution)/shard_map/pallas_call | solution.py:65
  44.6 2.7 all-to-all-done.2
  47.6 3.7 %all-to-all-start.3 = ((bf16[8,2,4,128,128]{4,3,2,1,0:T(8,128)(2,1)}), bf16[8,2,4,128,128]{4,3,2,1,0:T(8,128)(2,1)S(1)}, u32[]{:S(2)}, u32[]{:S(2)}) async-start(bf16[8,2,4,128,128]{4,3,2,1,0:T(8,128)(2,1)} %get-tuple-element.42.rest_0_), calls=%async_computation.3 | async-start | bytes 4194304 | tf_op jit(solution)/shard_map/all_to_all | solution.py:396
  53.1 11.7 %all_gather.18.emb_ref = bf16[144,2048]{1,0:T(8,128)(2,1)} all-gather(bf16[144,512]{1,0:T(8,128)(2,1)S(1)} %maximum_maximum_fusion), channel_id=1, replica_groups=mesh['req'=8,'head'=4] {'head'}, dimensions={1}, use_global_device_ids=true | all-gather | bytes 737280 | tf_op jit(solution)/shard_map/all_gather | solution.py:472
  64.8 8.0 %shard_map.220 = (bf16[32,2048]{1,0:T(8,128)(2,1)}, bf16[256,512]{1,0:T(8,128)(2,1)}, bf16[32,2176]{1,0:T(8,128)(2,1)}, bf16[32,2176]{1,0:T(8,128)(2,1)}, bf16[3...) custom-call(s32[2]{0:T(128)} %pad_add_fusion.1.me_ref, bf16[144,2048]{1,0:T(8,128)(2,1)} %all_gather.18.emb_ref, ...), custom_call_target="tpu_custom_call" | custom-call | tf_op jit(solution)/shard_map/pallas_call | solution.py:215
  75.6 4.5 %collective-permute-done.1 = bf16[32,2176]{1,0:T(8,128)(2,1)S(1)} collective-permute-done((bf16[32,2176]{1,0:T(8,128)(2,1)}, bf16[32,2176]{1,0:T(8,128)(2,1)S(1)}, u32[]{:S(2)}, u32[]{:S(2)}) %collective-permute-start.1) | collective-permute-done | bytes 139296 | tf_op jit(solution)/shard_map/ppermute | solution.py:21
  82.6 1.7 fusion.2.refs_0_
  84.3 15.9 %all-to-all-done.3.refs_2_.refs_1_.rest_0_ = bf16[8,2,4,128,128]{4,3,2,1,0:T(8,128)(2,1)S(1)} async-done(((bf16[8,2,4,128,128]{4,3,2,1,0:T(8,128)(2,1)}), bf16[8,2,4,128,128]{4,3,2,1,0:T(8,128)(2,1)S(1)}, u32[]{:S(2)}, u32[]{:S(2)}) %all-to-all-start.3) | async-done | bytes 2097184 | tf_op jit(solution)/shard_map/all_to_all | solution.py:396
  101.5 3.8 %all-to-all-start.4 = ((bf16[8,2,4,128,128]{4,3,2,1,0:T(8,128)(2,1)}), bf16[8,2,4,128,128]{4,3,2,1,0:T(8,128)(2,1)S(1)}, u32[]{:S(2)}, u32[]{:S(2)}) async-start(bf16[8,2,4,128,128]{4,3,2,1,0:T(8,128)(2,1)} %shard_map.223), calls=%async_computation.4 | async-start | bytes 4194304 | tf_op jit(solution)/shard_map/all_to_all | solution.py:396
  106.7 26.4 %all-gather.5.cloned.1.call-done.x_hbm = bf16[256,2048]{1,0:T(8,128)(2,1)} async-done(((bf16[32,2048]{1,0:T(8,128)(2,1)}), bf16[256,2048]{1,0:T(8,128)(2,1)}) %all-gather.5.cloned.1.call-update) | async-done | bytes 1048592 | tf_op jit(solution)/shard_map/all_gather | solution.py:496
  133.1 8.0 %shard_map.222 = (bf16[256,2048]{1,0:T(8,128)(2,1)}, bf16[32,2048]{1,0:T(8,128)(2,1)}) custom-call(bf16[256,2048]{1,0:T(8,128)(2,1)} %all-gather.5.cloned.1.call-done.x_hbm, bf16[4,2112,512]{2,1,0:T(8,128)(2,1)} %bitcast.121, bf16[256,256]{1,0:T(8,128)(2,1)} %fusion.4.pick_ref, bf16[32,256]{1,0:T(8,128)(2,1)} %compare_convert_fusion.mine_ref, ...), custom_call_target="tpu_custom_call" | custom-call | flops 35433480192 | bytes 8650752 | tf_op jit(solution)/shard_map/pallas_call | solution.py:318
  141.1 21.0 %all-to-all-done.4.refs_2_.rest_1_ = bf16[8,2,4,128,128]{4,3,2,1,0:T(8,128)(2,1)S(1)} async-done(((bf16[8,2,4,128,128]{4,3,2,1,0:T(8,128)(2,1)}), bf16[8,2,4,128,128]{4,3,2,1,0:T(8,128)(2,1)S(1)}, u32[]{:S(2)}, u32[]{:S(2)}) %all-to-all-start.4) | async-done | bytes 2097184 | tf_op jit(solution)/shard_map/all_to_all | solution.py:396
  163.4 3.7 %all-to-all-start.5 = ((bf16[8,32,2048]{2,1,0:T(8,128)(2,1)}), bf16[8,32,2048]{2,1,0:T(8,128)(2,1)S(1)}, u32[]{:S(2)}, u32[]{:S(2)}) async-start(bf16[8,32,2048]{2,1,0:T(8,128)(2,1)} %bitcast.125), calls=%async_computation.5 | async-start | bytes 2097152 | tf_op jit(solution)/shard_map/all_to_all | solution.py:396
  169.5 23.5 %all-to-all-done.5 = bf16[8,32,2048]{2,1,0:T(8,128)(2,1)S(1)} async-done(((bf16[8,32,2048]{2,1,0:T(8,128)(2,1)}), bf16[8,32,2048]{2,1,0:T(8,128)(2,1)S(1)}, u32[]{:S(2)}, u32[]{:S(2)}) %all-to-all-start.5) | async-done | bytes 1048608 | tf_op jit(solution)/shard_map/all_to_all | solution.py:396
  193.5 2.1 collective-permute-start.7
  195.6 2.3 collective-permute-start.8
  200.0 2.0 collective-permute-done.16
  208.9 3.1 %collective-permute-done.9 = bf16[4,32,896]{2,1,0:T(8,128)(2,1)S(1)} collective-permute-done((bf16[4,32,896]{2,1,0:T(8,128)(2,1)S(1)}, bf16[4,32,896]{2,1,0:T(8,128)(2,1)S(1)}, u32[]{:S(2)}, u32[]{:S(2)}) %collective-permute-start.9) | collective-permute-done | bytes 229408 | tf_op jit(solution)/shard_map/ppermute | solution.py:21
  215.5 3.0 %collective-permute-done.14 = bf16[2,32,768]{2,1,0:T(8,128)(2,1)S(1)} collective-permute-done((bf16[2,32,768]{2,1,0:T(8,128)(2,1)S(1)}, bf16[2,32,768]{2,1,0:T(8,128)(2,1)S(1)}, u32[]{:S(2)}, u32[]{:S(2)}) %collective-permute-start.14) | collective-permute-done | bytes 98336 | tf_op jit(solution)/shard_map/ppermute | solution.py:21
  227.0 2.9 %collective-permute-done.19 = bf16[2,2,32,384]{3,2,1,0:T(8,128)(2,1)S(1)} collective-permute-done((bf16[2,2,32,384]{3,2,1,0:T(8,128)(2,1)}, bf16[2,2,32,384]{3,2,1,0:T(8,128)(2,1)S(1)}, u32[]{:S(2)}, u32[]{:S(2)}) %collective-permute-start.19) | collective-permute-done | bytes 98336 | tf_op jit(solution)/shard_map/ppermute | solution.py:21
  229.9 2.8 %collective-permute-done.20 = bf16[2,2,32,384]{3,2,1,0:T(8,128)(2,1)S(1)} collective-permute-done((bf16[2,2,32,384]{3,2,1,0:T(8,128)(2,1)}, bf16[2,2,32,384]{3,2,1,0:T(8,128)(2,1)S(1)}, u32[]{:S(2)}, u32[]{:S(2)}) %collective-permute-start.20) | collective-permute-done | bytes 98336 | tf_op jit(solution)/shard_map/ppermute | solution.py:21
  234.7 3.4 %all-to-all-start.6 = ((bf16[8,32,512]{2,1,0:T(8,128)(2,1)}), bf16[8,32,512]{2,1,0:T(8,128)(2,1)S(1)}, u32[]{:S(2)}, u32[]{:S(2)}) async-start(bf16[8,32,512]{2,1,0:T(8,128)(2,1)} %bitcast.128), calls=%async_computation.6 | async-start | bytes 524288 | tf_op jit(solution)/shard_map/all_to_all | solution.py:396
  238.1 8.2 %shard_map.227.refs_0_ = f32[8,64]{1,0:T(8,128)} custom-call(s32[1]{0:T(128)} %bitcast.2.me_ref, bf16[512,2048]{1,0:T(8,128)(2,1)} %bitcast.123, bf16[1000,2048]{1,0:T(8,128)(2,1)} %bitcast.168, bf16[1000,2048]{1,0:T(8,128)(2,1)} %collective-permute-done.21.other_hbm), custom_call_target="tpu_custom_call" | custom-call | flops 8388608000 | bytes 8192000 | tf_op jit(solution)/shard_map/pallas_call | solution.py:363
  247.1 5.9 %all-to-all-start.7 = ((f32[8,1,64]{2,1,0:T(1,128)}), f32[8,1,64]{2,1,0:T(1,128)S(1)}, u32[]{:S(2)}, u32[]{:S(2)}) async-start(f32[8,1,64]{2,1,0:T(1,128)} %bitcast.159), calls=%async_computation.7 | async-start | bytes 8192 | tf_op jit(solution)/shard_map/all_to_all | solution.py:396
  254.2 1.8 convert.2.kv_ref
  256.0 6.8 %shard_map.226 = bf16[32,4,128,128]{3,2,1,0:T(8,128)(2,1)} custom-call(s32[32]{0:T(128)} %select_reduce_fusion.2.slot_ref, f32[32,8,512]{2,1,0:T(8,128)} %convert.2.kv_ref, bf16[8,2,4,128,128]{4,3,2,1,0:T(8,128)(2,1)} %copy-done, bf16[8,2,4,128,128]{4,3,2,1,0:T(8,128)(2,1)} %copy-done.1), custom_call_target="tpu_custom_call" | custom-call | tf_op jit(solution)/shard_map/pallas_call | solution.py:266
  263.1 5.6 %all-reduce = f32[256]{0:T(256)S(1)} all-reduce(f32[256]{0:T(256)S(1)} %dynamic-update-slice), channel_id=3, replica_groups=mesh['req'=8,'head'=4] {'head'}, use_global_device_ids=true, to_apply=%add | all-reduce | flops 256 | bytes 2048
  (188 shorter events, 46.7 us)
Async XLA Ops:
  7.2 77.1 %all-gather.7.cloned.1.call-start = ((), (), s32[]{:S(2)}) async-start(), calls=%async_computation.9 | async-start | bytes 10813440 | tf_op jit(solution)/shard_map/all_gather | solution.py:417
  11.6 13.8 %all-to-all-start.1 = ((s32[8,1,192]{2,1,0:T(1,128)}), s32[8,1,192]{2,1,0:T(1,128)S(1)}, u32[]{:S(2)}, u32[]{:S(2)}) async-start(s32[8,1,192]{2,1,0:T(1,128)} %reshape.485), calls=%async_computation.1 | async-start | bytes 16384 | tf_op jit(solution)/shard_map/all_to_all | solution.py:396
  33.4 13.9 %all-to-all-start.2 = ((bf16[8,48,512]{2,1,0:T(8,128)(2,1)}), bf16[8,48,512]{2,1,0:T(8,128)(2,1)S(1)}, u32[]{:S(2)}, u32[]{:S(2)}) async-start(bf16[8,48,512]{2,1,0:T(8,128)(2,1)} %bitcast.10), calls=%async_computation.2 | async-start | bytes 786432 | tf_op jit(solution)/shard_map/all_to_all | solution.py:396
  47.6 52.6 %all-to-all-start.3 = ((bf16[8,2,4,128,128]{4,3,2,1,0:T(8,128)(2,1)}), bf16[8,2,4,128,128]{4,3,2,1,0:T(8,128)(2,1)S(1)}, u32[]{:S(2)}, u32[]{:S(2)}) async-start(bf16[8,2,4,128,128]{4,3,2,1,0:T(8,128)(2,1)} %get-tuple-element.42.rest_0_), calls=%async_computation.3 | async-start | bytes 4194304 | tf_op jit(solution)/shard_map/all_to_all | solution.py:396
  51.3 81.8 %all-gather.5.cloned.1.call-start = ((), (), s32[]{:S(2)}) async-start(), calls=%async_computation.8 | async-start | bytes 1179648 | tf_op jit(solution)/shard_map/all_gather | solution.py:496
  51.3 186.8 %collective-permute-start.21 = (bf16[1000,2048]{1,0:T(8,128)(2,1)}, bf16[1000,2048]{1,0:T(8,128)(2,1)}, u32[]{:S(2)}, u32[]{:S(2)}) collective-permute-start(bf16[1000,2048]{1,0:T(8,128)(2,1)} %bitcast.167), channel_id=1, source_target_pairs={{0,1},{1,0},{2,3},{3,2},{4,5},{5,4},{6,7},{7,6},{8,9},{9,8},{10,11... | collective-permute-start | bytes 12288008 | tf_op jit(solution)/shard_map/ppermute | solution.py:21
  72.8 2.7 collective-permute-start
  73.3 6.7 %collective-permute-start.1 = (bf16[32,2176]{1,0:T(8,128)(2,1)}, bf16[32,2176]{1,0:T(8,128)(2,1)S(1)}, u32[]{:S(2)}, u32[]{:S(2)}) collective-permute-start(bf16[32,2176]{1,0:T(8,128)(2,1)} %get-tuple-element.47), channel_id=1, source_target_pairs={{0,2},{1,3},{2,0},{3,1},{4,6},{5,7},{6,4},{7,5},{8,10},{9,11},{10,... | collective-permute-start | bytes 417800 | tf_op jit(solution)/shard_map/ppermute | solution.py:21
  74.9 6.6 %collective-permute-start.2 = (bf16[32,2176]{1,0:T(8,128)(2,1)}, bf16[32,2176]{1,0:T(8,128)(2,1)S(1)}, u32[]{:S(2)}, u32[]{:S(2)}) collective-permute-start(bf16[32,2176]{1,0:T(8,128)(2,1)} %get-tuple-element.48), channel_id=1, source_target_pairs={{0,3},{1,2},{2,1},{3,0},{4,7},{5,6},{6,5},{7,4},{8,11},{9,10},{10,... | collective-permute-start | bytes 417800 | tf_op jit(solution)/shard_map/ppermute | solution.py:21
  101.5 60.5 %all-to-all-start.4 = ((bf16[8,2,4,128,128]{4,3,2,1,0:T(8,128)(2,1)}), bf16[8,2,4,128,128]{4,3,2,1,0:T(8,128)(2,1)S(1)}, u32[]{:S(2)}, u32[]{:S(2)}) async-start(bf16[8,2,4,128,128]{4,3,2,1,0:T(8,128)(2,1)} %shard_map.223), calls=%async_computation.4 | async-start | bytes 4194304 | tf_op jit(solution)/shard_map/all_to_all | solution.py:396
  163.4 29.8 %copy-start.3 = (bf16[32,2048]{1,0:T(8,128)(2,1)S(1)}, bf16[32,2048]{1,0:T(8,128)(2,1)}, u32[]{:S(2)}) copy-start(bf16[32,2048]{1,0:T(8,128)(2,1)} %get-tuple-element.49) | copy-start | bytes 393220
  163.4 29.6 %all-to-all-start.5 = ((bf16[8,32,2048]{2,1,0:T(8,128)(2,1)}), bf16[8,32,2048]{2,1,0:T(8,128)(2,1)S(1)}, u32[]{:S(2)}, u32[]{:S(2)}) async-start(bf16[8,32,2048]{2,1,0:T(8,128)(2,1)} %bitcast.125), calls=%async_computation.5 | async-start | bytes 2097152 | tf_op jit(solution)/shard_map/all_to_all | solution.py:396
  193.5 10.1 %collective-permute-start.6 = (bf16[32,896]{1,0:T(8,128)(2,1)S(1)}, bf16[32,896]{1,0:T(8,128)(2,1)S(1)}, u32[]{:S(2)}, u32[]{:S(2)}) collective-permute-start(bf16[32,896]{1,0:T(8,128)(2,1)S(1)} %get-tuple-element.73), channel_id=1, source_target_pairs={{0,8},{4,12},{8,0},{12,4},{16,24},{20,28},{24,16},{28,20},{1,9},{5... | collective-permute-start | bytes 172040 | tf_op jit(solution)/shard_map/ppermute | solution.py:21
  193.5 10.1 %collective-permute-start.7 = (bf16[32,896]{1,0:T(8,128)(2,1)S(1)}, bf16[32,896]{1,0:T(8,128)(2,1)S(1)}, u32[]{:S(2)}, u32[]{:S(2)}) collective-permute-start(bf16[32,896]{1,0:T(8,128)(2,1)S(1)} %get-tuple-element.73), channel_id=1, source_target_pairs={{0,16},{4,20},{8,24},{12,28},{16,0},{20,4},{24,8},{28,12},{1,17},{... | collective-permute-start | bytes 172040 | tf_op jit(solution)/shard_map/ppermute | solution.py:21
  195.6 8.6 %collective-permute-start.8 = (bf16[32,896]{1,0:T(8,128)(2,1)S(1)}, bf16[32,896]{1,0:T(8,128)(2,1)S(1)}, u32[]{:S(2)}, u32[]{:S(2)}) collective-permute-start(bf16[32,896]{1,0:T(8,128)(2,1)S(1)} %get-tuple-element.73), channel_id=1, source_target_pairs={{0,24},{4,28},{8,16},{12,20},{16,8},{20,12},{24,0},{28,4},{1,25},{... | collective-permute-start | bytes 172040 | tf_op jit(solution)/shard_map/ppermute | solution.py:21
  198.1 3.9 %collective-permute-start.16 = (bf16[32,384]{1,0:T(8,128)(2,1)S(1)}, bf16[32,384]{1,0:T(8,128)(2,1)S(1)}, u32[]{:S(2)}, u32[]{:S(2)}) collective-permute-start(bf16[32,384]{1,0:T(8,128)(2,1)S(1)} %get-tuple-element.77), channel_id=1, source_target_pairs={{0,4},{4,0},{8,12},{12,8},{16,20},{20,16},{24,28},{28,24},{1,5},{5... | collective-permute-start | bytes 73736 | tf_op jit(solution)/shard_map/ppermute | solution.py:21
  202.0 4.1 %collective-permute-start.11 = (bf16[32,768]{1,0:T(8,128)(2,1)S(1)}, bf16[32,768]{1,0:T(8,128)(2,1)S(1)}, u32[]{:S(2)}, u32[]{:S(2)}) collective-permute-start(bf16[32,768]{1,0:T(8,128)(2,1)S(1)} %get-tuple-element.75), channel_id=1, source_target_pairs={{0,2},{1,3},{2,0},{3,1},{4,6},{5,7},{6,4},{7,5},{8,10},{9,11},{10,... | collective-permute-start | bytes 147464 | tf_op jit(solution)/shard_map/ppermute | solution.py:21
  203.6 16.6 %collective-permute-start.3 = (f32[32,640]{1,0:T(8,128)S(1)}, f32[32,640]{1,0:T(8,128)S(1)}, u32[]{:S(2)}, u32[]{:S(2)}) collective-permute-start(f32[32,640]{1,0:T(8,128)S(1)} %get-tuple-element.90), channel_id=1, source_target_pairs={{0,1},{1,0},{2,3},{3,2},{4,5},{5,4},{6,7},{7,6},{8,9},{9,8},{10,11... | collective-permute-start | bytes 245768 | tf_op jit(solution)/shard_map/ppermute | solution.py:21
  203.7 4.2 %collective-permute-start.17 = (bf16[2,32,384]{2,1,0:T(8,128)(2,1)S(1)}, bf16[2,32,384]{2,1,0:T(8,128)(2,1)S(1)}, u32[]{:S(2)}, u32[]{:S(2)}) collective-permute-start(bf16[2,32,384]{2,1,0:T(8,128)(2,1)S(1)} %get-tuple-element.88), channel_id=1, source_target_pairs={{0,2},{1,3},{2,0},{3,1},{4,6},{5,7},{6,4},{7,5},{8,10},{9,11},{10,... | collective-permute-start | bytes 147464 | tf_op jit(solution)/shard_map/ppermute | solution.py:21
  204.3 7.7 %collective-permute-start.9 = (bf16[4,32,896]{2,1,0:T(8,128)(2,1)S(1)}, bf16[4,32,896]{2,1,0:T(8,128)(2,1)S(1)}, u32[]{:S(2)}, u32[]{:S(2)}) collective-permute-start(bf16[4,32,896]{2,1,0:T(8,128)(2,1)S(1)} %get-tuple-element.71), channel_id=1, source_target_pairs={{0,4},{4,0},{8,12},{12,8},{16,20},{20,16},{24,28},{28,24},{1,5},{5... | collective-permute-start | bytes 688136 | tf_op jit(solution)/shard_map/ppermute | solution.py:21
  206.1 7.5 %collective-permute-start.12 = (bf16[2,32,768]{2,1,0:T(8,128)(2,1)S(1)}, bf16[2,32,768]{2,1,0:T(8,128)(2,1)S(1)}, u32[]{:S(2)}, u32[]{:S(2)}) collective-permute-start(bf16[2,32,768]{2,1,0:T(8,128)(2,1)S(1)} %get-tuple-element.79), channel_id=1, source_target_pairs={{0,8},{4,12},{8,0},{12,4},{16,24},{20,28},{24,16},{28,20},{1,9},{5... | collective-permute-start | bytes 294920 | tf_op jit(solution)/shard_map/ppermute | solution.py:21
  207.8 7.6 %collective-permute-start.13 = (bf16[2,32,768]{2,1,0:T(8,128)(2,1)S(1)}, bf16[2,32,768]{2,1,0:T(8,128)(2,1)S(1)}, u32[]{:S(2)}, u32[]{:S(2)}) collective-permute-start(bf16[2,32,768]{2,1,0:T(8,128)(2,1)S(1)} %get-tuple-element.79), channel_id=1, source_target_pairs={{0,16},{4,20},{8,24},{12,28},{16,0},{20,4},{24,8},{28,12},{1,17},{... | collective-permute-start | bytes 294920 | tf_op jit(solution)/shard_map/ppermute | solution.py:21
  212.0 6.5 %collective-permute-start.14 = (bf16[2,32,768]{2,1,0:T(8,128)(2,1)S(1)}, bf16[2,32,768]{2,1,0:T(8,128)(2,1)S(1)}, u32[]{:S(2)}, u32[]{:S(2)}) collective-permute-start(bf16[2,32,768]{2,1,0:T(8,128)(2,1)S(1)} %get-tuple-element.79), channel_id=1, source_target_pairs={{0,24},{4,28},{8,16},{12,20},{16,8},{20,12},{24,0},{28,4},{1,25},{... | collective-permute-start | bytes 294920 | tf_op jit(solution)/shard_map/ppermute | solution.py:21
  213.6 7.4 %collective-permute-start.4 = (f32[32,640]{1,0:T(8,128)S(1)}, f32[32,640]{1,0:T(8,128)S(1)}, u32[]{:S(2)}, u32[]{:S(2)}) collective-permute-start(f32[32,640]{1,0:T(8,128)S(1)} %get-tuple-element.91), channel_id=1, source_target_pairs={{0,2},{1,3},{2,0},{3,1},{4,6},{5,7},{6,4},{7,5},{8,10},{9,11},{10,... | collective-permute-start | bytes 245768 | tf_op jit(solution)/shard_map/ppermute | solution.py:21
  215.4 6.9 %collective-permute-start.5 = (f32[32,640]{1,0:T(8,128)S(1)}, f32[32,640]{1,0:T(8,128)S(1)}, u32[]{:S(2)}, u32[]{:S(2)}) collective-permute-start(f32[32,640]{1,0:T(8,128)S(1)} %get-tuple-element.92), channel_id=1, source_target_pairs={{0,3},{1,2},{2,1},{3,0},{4,7},{5,6},{6,5},{7,4},{8,11},{9,10},{10,... | collective-permute-start | bytes 245768 | tf_op jit(solution)/shard_map/ppermute | solution.py:21
  218.5 14.3 %collective-permute-start.10 = (bf16[2,4,32,896]{3,2,1,0:T(8,128)(2,1)S(1)}, bf16[2,4,32,896]{3,2,1,0:T(8,128)(2,1)S(1)}, u32[]{:S(2)}, u32[]{:S(2)}) collective-permute-start(bf16[2,4,32,896]{3,2,1,0:T(8,128)(2,1)S(1)} %get-tuple-element.63), channel_id=1, source_target_pairs={{0,2},{1,3},{2,0},{3,1},{4,6},{5,7},{6,4},{7,5},{8,10},{9,11},{10,... | collective-permute-start | bytes 1376264 | tf_op jit(solution)/shard_map/ppermute | solution.py:21
  220.1 5.9 %collective-permute-start.18 = (bf16[2,2,32,384]{3,2,1,0:T(8,128)(2,1)}, bf16[2,2,32,384]{3,2,1,0:T(8,128)(2,1)S(1)}, u32[]{:S(2)}, u32[]{:S(2)}) collective-permute-start(bf16[2,2,32,384]{3,2,1,0:T(8,128)(2,1)} %get-tuple-element.81), channel_id=1, source_target_pairs={{0,8},{4,12},{8,0},{12,4},{16,24},{20,28},{24,16},{28,20},{1,9},{5... | collective-permute-start | bytes 294920 | tf_op jit(solution)/shard_map/ppermute | solution.py:21
  221.0 8.9 %collective-permute-start.19 = (bf16[2,2,32,384]{3,2,1,0:T(8,128)(2,1)}, bf16[2,2,32,384]{3,2,1,0:T(8,128)(2,1)S(1)}, u32[]{:S(2)}, u32[]{:S(2)}) collective-permute-start(bf16[2,2,32,384]{3,2,1,0:T(8,128)(2,1)} %get-tuple-element.81), channel_id=1, source_target_pairs={{0,16},{4,20},{8,24},{12,28},{16,0},{20,4},{24,8},{28,12},{1,17},{... | collective-permute-start | bytes 294920 | tf_op jit(solution)/shard_map/ppermute | solution.py:21
  222.3 10.6 %collective-permute-start.15 = (bf16[4,2,32,768]{3,2,1,0:T(8,128)(2,1)S(1)}, bf16[4,2,32,768]{3,2,1,0:T(8,128)(2,1)S(1)}, u32[]{:S(2)}, u32[]{:S(2)}) collective-permute-start(bf16[4,2,32,768]{3,2,1,0:T(8,128)(2,1)S(1)} %get-tuple-element.65), channel_id=1, source_target_pairs={{0,4},{4,0},{8,12},{12,8},{16,20},{20,16},{24,28},{28,24},{1,5},{5... | collective-permute-start | bytes 1179656 | tf_op jit(solution)/shard_map/ppermute | solution.py:21
  226.1 6.6 %collective-permute-start.20 = (bf16[2,2,32,384]{3,2,1,0:T(8,128)(2,1)}, bf16[2,2,32,384]{3,2,1,0:T(8,128)(2,1)S(1)}, u32[]{:S(2)}, u32[]{:S(2)}) collective-permute-start(bf16[2,2,32,384]{3,2,1,0:T(8,128)(2,1)} %get-tuple-element.81), channel_id=1, source_target_pairs={{0,24},{4,28},{8,16},{12,20},{16,8},{20,12},{24,0},{28,4},{1,25},{... | collective-permute-start | bytes 294920 | tf_op jit(solution)/shard_map/ppermute | solution.py:21
  234.7 11.7 %all-to-all-start.6 = ((bf16[8,32,512]{2,1,0:T(8,128)(2,1)}), bf16[8,32,512]{2,1,0:T(8,128)(2,1)S(1)}, u32[]{:S(2)}, u32[]{:S(2)}) async-start(bf16[8,32,512]{2,1,0:T(8,128)(2,1)} %bitcast.128), calls=%async_computation.6 | async-start | bytes 524288 | tf_op jit(solution)/shard_map/all_to_all | solution.py:396
  247.1 15.8 %all-to-all-start.7 = ((f32[8,1,64]{2,1,0:T(1,128)}), f32[8,1,64]{2,1,0:T(1,128)S(1)}, u32[]{:S(2)}, u32[]{:S(2)}) async-start(f32[8,1,64]{2,1,0:T(1,128)} %bitcast.159), calls=%async_computation.7 | async-start | bytes 8192 | tf_op jit(solution)/shard_map/all_to_all | solution.py:396
  (10 other events, 26.9 us)
Sparse Core Ops, SparseCore 0:
  10.4 65.6 all-gather.6
  84.4 48.6 all-gather.4

commit v13 on v12

--- a/solution.py
+++ b/solution.py
@@ -197,8 +197,7 @@
     shape = (2 * tokens, 2 * tokens)
     target = lax.broadcasted_iota(jnp.int32, shape, 0)
     source = lax.broadcasted_iota(jnp.int32, shape, 1)
-    slot, within = target // (2 * steps), target % (2 * steps)
-    place = ((slot // sends) ^ here) * sends + slot % sends
+    place, within = target // (2 * steps), target % (2 * steps)
     request = (place % classes) * group + place // classes
     wanted = request * steps + within % steps + jnp.where(within >= steps, tokens, 0)
     pick = jnp.where(source == wanted, 1.0, 0.0).astype(BF16)
@@ -234,7 +233,7 @@
     )(me, emb, live, gain, floor, ggain, *weights, *states)
 
 
-def update_kernel(steps, slot_ref, kv_ref, *rest):
+def update_kernel(steps, me_ref, slot_ref, kv_ref, *rest):
     states, out_ref = rest[:-1], rest[-1]
     owners, _, heads = states[0].shape[:3]
     ranks = [(piece, i) for piece in states for i in range(piece.shape[1])]
@@ -249,7 +248,7 @@
             slot = slot_ref[place]
             for head in range(heads):
                 cols = slice(head * HEAD_DIM, (head + 1) * HEAD_DIM)
-                both = kv_ref[place, :, cols]
+                both = kv_ref[(k ^ me_ref[0]) * sends + rank, :, cols]
                 key = jnp.where(first, both, 0.0)
                 value = jnp.where(first, roll(both, steps), 0.0)
                 kept = 1.0 - jnp.sum(key, axis=0, keepdims=True)
@@ -261,15 +260,15 @@
                 out_ref[slot, head] = (old + fresh).astype(BF16)
 
 
-def update_states(slots, kv, states, steps):
+def update_states(me, slots, kv, states, steps):
     vmem = pl.BlockSpec(memory_space=VMEM)
     return pl.pallas_call(
         functools.partial(update_kernel, steps),
         out_shape=jax.ShapeDtypeStruct((slots.shape[0],) + states[0].shape[2:], BF16),
-        in_specs=[pl.BlockSpec(memory_space=SMEM)] + [vmem] * (1 + len(states)),
+        in_specs=[pl.BlockSpec(memory_space=SMEM)] * 2 + [vmem] * (1 + len(states)),
         out_specs=vmem,
         compiler_params=pltpu.CompilerParams(vmem_limit_bytes=56 << 20),
-    )(slots, kv, *states)
+    )(me, slots, kv, *states)
 
 
 def dot_rows(a, b):
@@ -539,6 +538,12 @@
     token_gain = jnp.repeat(tenant_rows * gains[0][None, :], steps, axis=0)
     final = (hidden * lax.rsqrt(mean_square + epsilon) * token_gain).astype(BF16)
 
+    kv = kv.reshape(n, -1, width)
+    kv = jnp.stack([kv[0]] + [swap(kv[k], "req", n, k) for k in range(1, n)])
+    new_states = update_states(
+        r[None], slot_of, kv.reshape(requests, 2 * steps, width).astype(F32), arrived, steps
+    )
+    final = after(final, new_states)
     c1, c2 = D * 7 // 16, D * 13 // 16
     full = jnp.concatenate(
         [
@@ -548,12 +553,8 @@
         ],
         axis=-1,
     ).reshape(n * 2 * rows, D)
-    arrived_kv = to_all(after(kv, full).reshape(n, -1, width), "req")
-    new_states = update_states(
-        slot_of, arrived_kv.reshape(requests, 2 * steps, width).astype(F32), arrived, steps
-    )
     best = greatest_entries(r[None], n, full, vocab_weight.T, vocab_other)
-    got = jnp.max(to_all(after(best, arrived_kv), "req"), axis=0)
+    got = jnp.max(to_all(best, "req"), axis=0)
     got = lax.all_gather(got, "head", axis=0).reshape(n_head, 2, rows)
     crossed = jnp.stack([got[i ^ 2, 1] for i in range(n_head)])
     best = jnp.maximum(got[:, 0], crossed).reshape(requests, steps)

time: 278 us -> 285 us (1.025)
  starting transfers between devices: 52.7 us -> 56.1 us
  local copies, waits for them, and re-layouts: 18.4 us -> 21.7 us
    all_to_all x7 -> x6, waiting for transfers between devices: 68.9 us -> 25.4 us  [to_all(): return lax.all_to_all(x, axis, split_axis=0, concat_axis=0, tiled=True)]
    all_gather x1, waiting for transfers between devices: 26.4 us -> 51.7 us  [on_device(): everything = lax.all_gather(after_mixer, 'req', axis=0, tiled=True)]
    ppermute x22 -> x29, waiting for transfers between devices: 23.3 us -> 41.7 us  [swap(): return lax.ppermute(x, axis, [(i, i ^ offset) for i in range(size)])]
    ppermute x22 -> x29, starting transfers between devices: 21.4 us -> 30.8 us  [swap(): return lax.ppermute(x, axis, [(i, i ^ offset) for i in range(size)])]
    all_to_all x7 -> x6, starting transfers between devices: 31.2 us -> 25.2 us  [to_all(): return lax.all_to_all(x, axis, split_axis=0, concat_axis=0, tiled=True)]
  transfers between devices with their start and end apart: 31 -> 37, of which waited for: 17 -> 19; matrix products, arithmetic and copies ran while one was open for 10% -> 11% of each run, Pallas kernels for 13% -> 10%
where the time goes in v13:
time: 285 us; the launch traced here: 283 us
  waiting for transfers between devices  119 us (42%)
  starting transfers between devices  56.1 us (20%)
  Pallas kernels  35.6 us (12%)
  local copies, waits for them, and re-layouts  21.7 us (8%)
  other arithmetic  17.2 us (6%)
  blocking collectives  17.2 us (6%)
  between operations  16 us (6%)
    all_gather x1, waiting for transfers between devices, on_device(): everything = lax.all_gather(after_mixer, 'req', axis=0, tiled=True)  51.7 us
    ppermute x29, waiting for transfers between devices, swap(): return lax.ppermute(x, axis, [(i, i ^ offset) for i in range(size)])  41.7 us
    ppermute x29, starting transfers between devices, swap(): return lax.ppermute(x, axis, [(i, i ^ offset) for i in range(size)])  30.8 us
    all_to_all x6, waiting for transfers between devices, to_all(): return lax.all_to_all(x, axis, split_axis=0, concat_axis=0, tiled=True)  25.4 us
    all_to_all x6, starting transfers between devices, to_all(): return lax.all_to_all(x, axis, split_axis=0, concat_axis=0, tiled=True)  25.2 us
    all_gather x1, blocking collectives, on_device(): lax.all_gather(jnp.concatenate([embed_part, gains_high, gains_low, extra]...  11.6 us
    pallas_call x1, Pallas kernels, greatest_entries(): pl.pallas_call(greatest_kernel, out_shape=jax.ShapeDtypeStruct((blocks, f...  8.22 us
    pallas_call x1, Pallas kernels, mixer(): pl.pallas_call(functools.partial(mixer_kernel, counts, owners, heads, cla...  8.05 us
  transfers between devices with their start and end apart: 37, of which 19 were waited for; matrix products, arithmetic and copies ran while one was open for 11% of the time, Pallas kernels for 10%

profile of v13, /device:TPU:0, one launch (start us, length us, event | category | flops | bytes accessed | tf_op | source)
XLA Modules:
  0.0 283.4 jit_solution(11276293447740576039)
XLA Ops:
  7.2 3.0 %pad_maximum_fusion = bf16[2112,512]{1,0:T(8,128)(2,1)} fusion(bf16[704,512]{1,0:T(8,128)(2,1)} %param.38, bf16[704,512]{1,0:T(8,128)(2,1)} %bitcast.141, bf16[704,512]{1,0:T(8,128)(2,1)} %bitcast.142), kind=kLoop, calls=%fused_computation.9 | loop fusion | flops 6488064 | bytes 4325376 | tf_op jit(solution)/shard_map/concatenate | solution.py:415
  11.6 7.3 %all-to-all-start.1 = ((s32[8,1,192]{2,1,0:T(1,128)}), s32[8,1,192]{2,1,0:T(1,128)S(1)}, u32[]{:S(2)}, u32[]{:S(2)}) async-start(s32[8,1,192]{2,1,0:T(1,128)} %reshape.497), calls=%async_computation.1 | async-start | bytes 16384 | tf_op jit(solution)/shard_map/all_to_all | solution.py:395
  20.3 5.2 %all-to-all-done.1 = s32[8,1,192]{2,1,0:T(1,128)S(1)} async-done(((s32[8,1,192]{2,1,0:T(1,128)}), s32[8,1,192]{2,1,0:T(1,128)S(1)}, u32[]{:S(2)}, u32[]{:S(2)}) %all-to-all-start.1) | async-done | bytes 6176 | tf_op jit(solution)/shard_map/all_to_all | solution.py:395
  28.1 5.3 %gather_fusion.1 = bf16[384,512]{1,0:T(8,128)(2,1)} fusion(bf16[4000,512]{1,0:T(8,128)(2,1)} %param.27, s32[1024]{0:T(1024)S(1)} %pad_clamp_fusion.2), kind=kCustom, calls=%fused_computation.1 | custom fusion | bytes 787968 | tf_op jit(solution)/shard_map/jit(_take)/gather | solution.py:442
  33.4 3.5 %all-to-all-start.2 = ((bf16[8,48,512]{2,1,0:T(8,128)(2,1)}), bf16[8,48,512]{2,1,0:T(8,128)(2,1)S(1)}, u32[]{:S(2)}, u32[]{:S(2)}) async-start(bf16[8,48,512]{2,1,0:T(8,128)(2,1)} %bitcast.10), calls=%async_computation.2 | async-start | bytes 786432 | tf_op jit(solution)/shard_map/all_to_all | solution.py:395
  39.9 4.6 %shard_map.219 = (bf16[8,2,4,128,128]{4,3,2,1,0:T(8,128)(2,1)}, bf16[8,2,4,128,128]{4,3,2,1,0:T(8,128)(2,1)}) custom-call(s32[32]{0:T(128)} %select_n.235.order_ref, bf16[32,4,128,128]{3,2,1,0:T(8,128)(2,1)} %old_ref.1), custom_call_target="tpu_custom_call" | custom-call | tf_op jit(solution)/shard_map/pallas_call | solution.py:65
  44.6 2.9 %all-to-all-done.2 = bf16[8,48,512]{2,1,0:T(8,128)(2,1)S(1)} async-done(((bf16[8,48,512]{2,1,0:T(8,128)(2,1)}), bf16[8,48,512]{2,1,0:T(8,128)(2,1)S(1)}, u32[]{:S(2)}, u32[]{:S(2)}) %all-to-all-start.2) | async-done | bytes 393248 | tf_op jit(solution)/shard_map/all_to_all | solution.py:395
  47.9 3.8 %all-to-all-start.3 = ((bf16[8,2,4,128,128]{4,3,2,1,0:T(8,128)(2,1)}), bf16[8,2,4,128,128]{4,3,2,1,0:T(8,128)(2,1)S(1)}, u32[]{:S(2)}, u32[]{:S(2)}) async-start(bf16[8,2,4,128,128]{4,3,2,1,0:T(8,128)(2,1)} %get-tuple-element.42.rest_0_), calls=%async_computation.3 | async-start | bytes 4194304 | tf_op jit(solution)/shard_map/all_to_all | solution.py:395
  56.1 11.6 %all_gather.18.emb_ref = bf16[144,2048]{1,0:T(8,128)(2,1)} all-gather(bf16[144,512]{1,0:T(8,128)(2,1)S(1)} %maximum_maximum_fusion), channel_id=1, replica_groups=mesh['req'=8,'head'=4] {'head'}, dimensions={1}, use_global_device_ids=true | all-gather | bytes 737280 | tf_op jit(solution)/shard_map/all_gather | solution.py:471
  67.7 8.1 %shard_map.220 = (bf16[32,2048]{1,0:T(8,128)(2,1)}, bf16[256,512]{1,0:T(8,128)(2,1)}, bf16[32,2176]{1,0:T(8,128)(2,1)}, bf16[32,2176]{1,0:T(8,128)(2,1)}, bf16[3...) custom-call(s32[2]{0:T(128)} %pad_add_fusion.1.me_ref, bf16[144,2048]{1,0:T(8,128)(2,1)} %all_gather.18.emb_ref, ...), custom_call_target="tpu_custom_call" | custom-call | tf_op jit(solution)/shard_map/pallas_call | solution.py:214
  79.5 2.0 collective-permute-start.6
  87.3 12.1 %all-to-all-done.3.refs_2_.refs_1_.rest_0_ = bf16[8,2,4,128,128]{4,3,2,1,0:T(8,128)(2,1)S(1)} async-done(((bf16[8,2,4,128,128]{4,3,2,1,0:T(8,128)(2,1)}), bf16[8,2,4,128,128]{4,3,2,1,0:T(8,128)(2,1)S(1)}, u32[]{:S(2)}, u32[]{:S(2)}) %all-to-all-start.3) | async-done | bytes 2097184 | tf_op jit(solution)/shard_map/all_to_all | solution.py:395
  100.7 3.8 %all-to-all-start.4 = ((bf16[8,2,4,128,128]{4,3,2,1,0:T(8,128)(2,1)}), bf16[8,2,4,128,128]{4,3,2,1,0:T(8,128)(2,1)S(1)}, u32[]{:S(2)}, u32[]{:S(2)}) async-start(bf16[8,2,4,128,128]{4,3,2,1,0:T(8,128)(2,1)} %shard_map.223), calls=%async_computation.4 | async-start | bytes 4194304 | tf_op jit(solution)/shard_map/all_to_all | solution.py:395
  104.6 51.7 %all-gather.5.cloned.1.call-done.x_hbm = bf16[256,2048]{1,0:T(8,128)(2,1)} async-done(((bf16[32,2048]{1,0:T(8,128)(2,1)}), bf16[256,2048]{1,0:T(8,128)(2,1)}) %all-gather.5.cloned.1.call-update) | async-done | bytes 1048592 | tf_op jit(solution)/shard_map/all_gather | solution.py:495
  156.3 8.0 %shard_map.222 = (bf16[256,2048]{1,0:T(8,128)(2,1)}, bf16[32,2048]{1,0:T(8,128)(2,1)}) custom-call(bf16[256,2048]{1,0:T(8,128)(2,1)} %all-gather.5.cloned.1.call-done.x_hbm, bf16[4,2112,512]{2,1,0:T(8,128)(2,1)} %bitcast.136, bf16[256,256]{1,0:T(8,128)(2,1)} %fusion.4.pick_ref, bf16[32,256]{1,0:T(8,128)(2,1)} %compare_convert_fusion.mine_ref, ...), custom_call_target="tpu_custom_call" | custom-call | flops 35433480192 | bytes 8650752 | tf_op jit(solution)/shard_map/pallas_call | solution.py:317
  165.6 3.6 %all-to-all-start.5 = ((bf16[8,32,2048]{2,1,0:T(8,128)(2,1)}), bf16[8,32,2048]{2,1,0:T(8,128)(2,1)S(1)}, u32[]{:S(2)}, u32[]{:S(2)}) async-start(bf16[8,32,2048]{2,1,0:T(8,128)(2,1)} %bitcast.138), calls=%async_computation.5 | async-start | bytes 2097152 | tf_op jit(solution)/shard_map/all_to_all | solution.py:395
  170.2 2.0 collective-permute-start.7
  173.6 2.4 collective-permute-start.9
  176.1 12.6 %collective-permute-done.7 = bf16[32,512]{1,0:T(8,128)(2,1)S(1)} collective-permute-done((bf16[32,512]{1,0:T(8,128)(2,1)S(1)}, bf16[32,512]{1,0:T(8,128)(2,1)S(1)}, u32[]{:S(2)}, u32[]{:S(2)}) %collective-permute-start.7) | collective-permute-done | bytes 32800 | tf_op jit(solution)/shard_map/ppermute | solution.py:21
  188.8 3.1 %collective-permute-start.11 = (bf16[32,512]{1,0:T(8,128)(2,1)S(1)}, bf16[32,512]{1,0:T(8,128)(2,1)S(1)}, u32[]{:S(2)}, u32[]{:S(2)}) collective-permute-start(bf16[32,512]{1,0:T(8,128)(2,1)S(1)} %get-tuple-element.67), channel_id=1, source_target_pairs={{0,24},{4,28},{8,16},{12,20},{16,8},{20,12},{24,0},{28,4},{1,25},{... | collective-permute-start | bytes 98312 | tf_op jit(solution)/shard_map/ppermute | solution.py:21
  193.5 6.3 %collective-permute-done.9 = bf16[32,512]{1,0:T(8,128)(2,1)S(1)} collective-permute-done((bf16[32,512]{1,0:T(8,128)(2,1)S(1)}, bf16[32,512]{1,0:T(8,128)(2,1)S(1)}, u32[]{:S(2)}, u32[]{:S(2)}) %collective-permute-start.9) | collective-permute-done | bytes 32800 | tf_op jit(solution)/shard_map/ppermute | solution.py:21
  202.0 6.8 %shard_map.225.refs_1_ = bf16[32,4,128,128]{3,2,1,0:T(8,128)(2,1)} custom-call(s32[1]{0:T(128)} %bitcast.2.me_ref, s32[32]{0:T(128)} %select_reduce_fusion.2.slot_ref, f32[32,8,512]{2,1,0:T(8,128)} %convert.2.kv_ref, bf16[8,2,4,128,128]{4,3,2,1,0:T(8,128)(2,1)} %copy-done, bf16[8,2,4,128,128]{4,3,2,1,0:T(8,128)(2,1)} %copy-done.1), custom_call_target="tpu_custom_call" | custom-call | tf_op jit(solution)/shard_map/pallas_call | solution.py:265
  212.3 3.0 %collective-permute-start.15 = (bf16[32,896]{1,0:T(8,128)(2,1)S(1)}, bf16[32,896]{1,0:T(8,128)(2,1)S(1)}, u32[]{:S(2)}, u32[]{:S(2)}) collective-permute-start(bf16[32,896]{1,0:T(8,128)(2,1)S(1)} %get-tuple-element.80), channel_id=1, source_target_pairs={{0,24},{4,28},{8,16},{12,20},{16,8},{20,12},{24,0},{28,4},{1,25},{... | collective-permute-start | bytes 172040 | tf_op jit(solution)/shard_map/ppermute | solution.py:21
  218.0 2.0 collective-permute-done.23
  226.7 3.2 %collective-permute-done.16 = bf16[4,32,896]{2,1,0:T(8,128)(2,1)S(1)} collective-permute-done((bf16[4,32,896]{2,1,0:T(8,128)(2,1)S(1)}, bf16[4,32,896]{2,1,0:T(8,128)(2,1)S(1)}, u32[]{:S(2)}, u32[]{:S(2)}) %collective-permute-start.16) | collective-permute-done | bytes 229408 | tf_op jit(solution)/shard_map/ppermute | solution.py:21
  233.3 3.2 %collective-permute-done.21 = bf16[2,32,768]{2,1,0:T(8,128)(2,1)S(1)} collective-permute-done((bf16[2,32,768]{2,1,0:T(8,128)(2,1)S(1)}, bf16[2,32,768]{2,1,0:T(8,128)(2,1)S(1)}, u32[]{:S(2)}, u32[]{:S(2)}) %collective-permute-start.21) | collective-permute-done | bytes 98336 | tf_op jit(solution)/shard_map/ppermute | solution.py:21
  244.2 2.5 collective-permute-done.26
  246.7 2.9 %collective-permute-done.27 = bf16[2,2,32,384]{3,2,1,0:T(8,128)(2,1)S(1)} collective-permute-done((bf16[2,2,32,384]{3,2,1,0:T(8,128)(2,1)}, bf16[2,2,32,384]{3,2,1,0:T(8,128)(2,1)S(1)}, u32[]{:S(2)}, u32[]{:S(2)}) %collective-permute-start.27) | collective-permute-done | bytes 98336 | tf_op jit(solution)/shard_map/ppermute | solution.py:21
  251.6 8.2 %shard_map.227 = f32[8,64]{1,0:T(8,128)} custom-call(s32[1]{0:T(128)} %bitcast.2.me_ref, bf16[512,2048]{1,0:T(8,128)(2,1)} %bitcast.139, bf16[1000,2048]{1,0:T(8,128)(2,1)} %bitcast.181, bf16[1000,2048]{1,0:T(8,128)(2,1)} %collective-permute-done.28.other_hbm), custom_call_target="tpu_custom_call" | custom-call | flops 8388608000 | bytes 8192000 | tf_op jit(solution)/shard_map/pallas_call | solution.py:362
  259.8 3.4 %all-to-all-start.6 = ((f32[8,1,64]{2,1,0:T(1,128)}), f32[8,1,64]{2,1,0:T(1,128)S(1)}, u32[]{:S(2)}, u32[]{:S(2)}) async-start(f32[8,1,64]{2,1,0:T(1,128)} %bitcast.173), calls=%async_computation.6 | async-start | bytes 8192 | tf_op jit(solution)/shard_map/all_to_all | solution.py:395
  264.4 5.2 %all-to-all-done.6 = f32[8,1,64]{2,1,0:T(1,128)S(1)} async-done(((f32[8,1,64]{2,1,0:T(1,128)}), f32[8,1,64]{2,1,0:T(1,128)S(1)}, u32[]{:S(2)}, u32[]{:S(2)}) %all-to-all-start.6) | async-done | bytes 2080 | tf_op jit(solution)/shard_map/all_to_all | solution.py:395
  269.9 5.6 %all-reduce = f32[256]{0:T(256)S(1)} all-reduce(f32[256]{0:T(256)S(1)} %dynamic-update-slice), channel_id=3, replica_groups=mesh['req'=8,'head'=4] {'head'}, use_global_device_ids=true, to_apply=%add | all-reduce | flops 256 | bytes 2048
  (205 shorter events, 58.6 us)
Async XLA Ops:
  7.2 80.1 %all-gather.7.cloned.1.call-start = ((), (), s32[]{:S(2)}) async-start(), calls=%async_computation.8 | async-start | bytes 10813440 | tf_op jit(solution)/shard_map/all_gather | solution.py:416
  11.6 13.8 %all-to-all-start.1 = ((s32[8,1,192]{2,1,0:T(1,128)}), s32[8,1,192]{2,1,0:T(1,128)S(1)}, u32[]{:S(2)}, u32[]{:S(2)}) async-start(s32[8,1,192]{2,1,0:T(1,128)} %reshape.497), calls=%async_computation.1 | async-start | bytes 16384 | tf_op jit(solution)/shard_map/all_to_all | solution.py:395
  18.9 232.7 %collective-permute-start.28 = (bf16[1000,2048]{1,0:T(8,128)(2,1)}, bf16[1000,2048]{1,0:T(8,128)(2,1)}, u32[]{:S(2)}, u32[]{:S(2)}) collective-permute-start(bf16[1000,2048]{1,0:T(8,128)(2,1)} %bitcast.180), channel_id=1, source_target_pairs={{0,1},{1,0},{2,3},{3,2},{4,5},{5,4},{6,7},{7,6},{8,9},{9,8},{10,11... | collective-permute-start | bytes 12288008 | tf_op jit(solution)/shard_map/ppermute | solution.py:21
  33.4 14.2 %all-to-all-start.2 = ((bf16[8,48,512]{2,1,0:T(8,128)(2,1)}), bf16[8,48,512]{2,1,0:T(8,128)(2,1)S(1)}, u32[]{:S(2)}, u32[]{:S(2)}) async-start(bf16[8,48,512]{2,1,0:T(8,128)(2,1)} %bitcast.10), calls=%async_computation.2 | async-start | bytes 786432 | tf_op jit(solution)/shard_map/all_to_all | solution.py:395
  47.9 51.5 %all-to-all-start.3 = ((bf16[8,2,4,128,128]{4,3,2,1,0:T(8,128)(2,1)}), bf16[8,2,4,128,128]{4,3,2,1,0:T(8,128)(2,1)S(1)}, u32[]{:S(2)}, u32[]{:S(2)}) async-start(bf16[8,2,4,128,128]{4,3,2,1,0:T(8,128)(2,1)} %get-tuple-element.42.rest_0_), calls=%async_computation.3 | async-start | bytes 4194304 | tf_op jit(solution)/shard_map/all_to_all | solution.py:395
  51.7 104.6 %all-gather.5.cloned.1.call-start = ((), (), s32[]{:S(2)}) async-start(), calls=%async_computation.7 | async-start | bytes 1179648 | tf_op jit(solution)/shard_map/all_gather | solution.py:495
  76.1 6.7 %collective-permute-start.1 = (bf16[32,2176]{1,0:T(8,128)(2,1)}, bf16[32,2176]{1,0:T(8,128)(2,1)S(1)}, u32[]{:S(2)}, u32[]{:S(2)}) collective-permute-start(bf16[32,2176]{1,0:T(8,128)(2,1)} %get-tuple-element.47), channel_id=1, source_target_pairs={{0,2},{1,3},{2,0},{3,1},{4,6},{5,7},{6,4},{7,5},{8,10},{9,11},{10,... | collective-permute-start | bytes 417800 | tf_op jit(solution)/shard_map/ppermute | solution.py:21
  77.4 7.1 %collective-permute-start.2 = (bf16[32,2176]{1,0:T(8,128)(2,1)}, bf16[32,2176]{1,0:T(8,128)(2,1)S(1)}, u32[]{:S(2)}, u32[]{:S(2)}) collective-permute-start(bf16[32,2176]{1,0:T(8,128)(2,1)} %get-tuple-element.48), channel_id=1, source_target_pairs={{0,3},{1,2},{2,1},{3,0},{4,7},{5,6},{6,5},{7,4},{8,11},{9,10},{10,... | collective-permute-start | bytes 417800 | tf_op jit(solution)/shard_map/ppermute | solution.py:21
  79.5 96.5 %collective-permute-start.6 = (bf16[32,512]{1,0:T(8,128)(2,1)S(1)}, bf16[32,512]{1,0:T(8,128)(2,1)S(1)}, u32[]{:S(2)}, u32[]{:S(2)}) collective-permute-start(bf16[32,512]{1,0:T(8,128)(2,1)S(1)} %get-tuple-element.72), channel_id=1, source_target_pairs={{0,4},{4,0},{8,12},{12,8},{16,20},{20,16},{24,28},{28,24},{1,5},{5... | collective-permute-start | bytes 98312 | tf_op jit(solution)/shard_map/ppermute | solution.py:21
  100.7 63.6 %all-to-all-start.4 = ((bf16[8,2,4,128,128]{4,3,2,1,0:T(8,128)(2,1)}), bf16[8,2,4,128,128]{4,3,2,1,0:T(8,128)(2,1)S(1)}, u32[]{:S(2)}, u32[]{:S(2)}) async-start(bf16[8,2,4,128,128]{4,3,2,1,0:T(8,128)(2,1)} %shard_map.223), calls=%async_computation.4 | async-start | bytes 4194304 | tf_op jit(solution)/shard_map/all_to_all | solution.py:395
  165.6 43.3 %all-to-all-start.5 = ((bf16[8,32,2048]{2,1,0:T(8,128)(2,1)}), bf16[8,32,2048]{2,1,0:T(8,128)(2,1)S(1)}, u32[]{:S(2)}, u32[]{:S(2)}) async-start(bf16[8,32,2048]{2,1,0:T(8,128)(2,1)} %bitcast.138), calls=%async_computation.5 | async-start | bytes 2097152 | tf_op jit(solution)/shard_map/all_to_all | solution.py:395
  170.2 18.6 %collective-permute-start.7 = (bf16[32,512]{1,0:T(8,128)(2,1)S(1)}, bf16[32,512]{1,0:T(8,128)(2,1)S(1)}, u32[]{:S(2)}, u32[]{:S(2)}) collective-permute-start(bf16[32,512]{1,0:T(8,128)(2,1)S(1)} %get-tuple-element.71), channel_id=1, source_target_pairs={{0,8},{4,12},{8,0},{12,4},{16,24},{20,28},{24,16},{28,20},{1,9},{5... | collective-permute-start | bytes 98312 | tf_op jit(solution)/shard_map/ppermute | solution.py:21
  172.2 19.7 %collective-permute-start.8 = (bf16[32,512]{1,0:T(8,128)(2,1)S(1)}, bf16[32,512]{1,0:T(8,128)(2,1)S(1)}, u32[]{:S(2)}, u32[]{:S(2)}) collective-permute-start(bf16[32,512]{1,0:T(8,128)(2,1)S(1)} %get-tuple-element.70), channel_id=1, source_target_pairs={{0,12},{4,8},{8,4},{12,0},{16,28},{20,24},{24,20},{28,16},{1,13},{... | collective-permute-start | bytes 98312 | tf_op jit(solution)/shard_map/ppermute | solution.py:21
  173.6 26.1 %collective-permute-start.9 = (bf16[32,512]{1,0:T(8,128)(2,1)S(1)}, bf16[32,512]{1,0:T(8,128)(2,1)S(1)}, u32[]{:S(2)}, u32[]{:S(2)}) collective-permute-start(bf16[32,512]{1,0:T(8,128)(2,1)S(1)} %get-tuple-element.69), channel_id=1, source_target_pairs={{0,16},{4,20},{8,24},{12,28},{16,0},{20,4},{24,8},{28,12},{1,17},{... | collective-permute-start | bytes 98312 | tf_op jit(solution)/shard_map/ppermute | solution.py:21
  176.0 25.1 %collective-permute-start.10 = (bf16[32,512]{1,0:T(8,128)(2,1)S(1)}, bf16[32,512]{1,0:T(8,128)(2,1)S(1)}, u32[]{:S(2)}, u32[]{:S(2)}) collective-permute-start(bf16[32,512]{1,0:T(8,128)(2,1)S(1)} %get-tuple-element.68), channel_id=1, source_target_pairs={{0,20},{4,16},{8,28},{12,24},{16,4},{20,0},{24,12},{28,8},{1,21},{... | collective-permute-start | bytes 98312 | tf_op jit(solution)/shard_map/ppermute | solution.py:21
  188.8 12.4 %collective-permute-start.11 = (bf16[32,512]{1,0:T(8,128)(2,1)S(1)}, bf16[32,512]{1,0:T(8,128)(2,1)S(1)}, u32[]{:S(2)}, u32[]{:S(2)}) collective-permute-start(bf16[32,512]{1,0:T(8,128)(2,1)S(1)} %get-tuple-element.67), channel_id=1, source_target_pairs={{0,24},{4,28},{8,16},{12,20},{16,8},{20,12},{24,0},{28,4},{1,25},{... | collective-permute-start | bytes 98312 | tf_op jit(solution)/shard_map/ppermute | solution.py:21
  191.9 9.2 %collective-permute-start.12 = (bf16[32,512]{1,0:T(8,128)(2,1)S(1)}, bf16[32,512]{1,0:T(8,128)(2,1)S(1)}, u32[]{:S(2)}, u32[]{:S(2)}) collective-permute-start(bf16[32,512]{1,0:T(8,128)(2,1)S(1)} %get-tuple-element.66), channel_id=1, source_target_pairs={{0,28},{4,24},{8,20},{12,16},{16,12},{20,8},{24,4},{28,0},{1,29},{... | collective-permute-start | bytes 98312 | tf_op jit(solution)/shard_map/ppermute | solution.py:21
  210.8 10.7 %collective-permute-start.13 = (bf16[32,896]{1,0:T(8,128)(2,1)S(1)}, bf16[32,896]{1,0:T(8,128)(2,1)S(1)}, u32[]{:S(2)}, u32[]{:S(2)}) collective-permute-start(bf16[32,896]{1,0:T(8,128)(2,1)S(1)} %get-tuple-element.80), channel_id=1, source_target_pairs={{0,8},{4,12},{8,0},{12,4},{16,24},{20,28},{24,16},{28,20},{1,9},{5... | collective-permute-start | bytes 172040 | tf_op jit(solution)/shard_map/ppermute | solution.py:21
  212.1 9.5 %collective-permute-start.14 = (bf16[32,896]{1,0:T(8,128)(2,1)S(1)}, bf16[32,896]{1,0:T(8,128)(2,1)S(1)}, u32[]{:S(2)}, u32[]{:S(2)}) collective-permute-start(bf16[32,896]{1,0:T(8,128)(2,1)S(1)} %get-tuple-element.80), channel_id=1, source_target_pairs={{0,16},{4,20},{8,24},{12,28},{16,0},{20,4},{24,8},{28,12},{1,17},{... | collective-permute-start | bytes 172040 | tf_op jit(solution)/shard_map/ppermute | solution.py:21
  212.3 9.9 %collective-permute-start.15 = (bf16[32,896]{1,0:T(8,128)(2,1)S(1)}, bf16[32,896]{1,0:T(8,128)(2,1)S(1)}, u32[]{:S(2)}, u32[]{:S(2)}) collective-permute-start(bf16[32,896]{1,0:T(8,128)(2,1)S(1)} %get-tuple-element.80), channel_id=1, source_target_pairs={{0,24},{4,28},{8,16},{12,20},{16,8},{20,12},{24,0},{28,4},{1,25},{... | collective-permute-start | bytes 172040 | tf_op jit(solution)/shard_map/ppermute | solution.py:21
  221.5 16.6 %collective-permute-start.3 = (f32[32,640]{1,0:T(8,128)S(1)}, f32[32,640]{1,0:T(8,128)S(1)}, u32[]{:S(2)}, u32[]{:S(2)}) collective-permute-start(f32[32,640]{1,0:T(8,128)S(1)} %get-tuple-element.97), channel_id=1, source_target_pairs={{0,1},{1,0},{2,3},{3,2},{4,5},{5,4},{6,7},{7,6},{8,9},{9,8},{10,11... | collective-permute-start | bytes 245768 | tf_op jit(solution)/shard_map/ppermute | solution.py:21
  222.3 7.7 %collective-permute-start.16 = (bf16[4,32,896]{2,1,0:T(8,128)(2,1)S(1)}, bf16[4,32,896]{2,1,0:T(8,128)(2,1)S(1)}, u32[]{:S(2)}, u32[]{:S(2)}) collective-permute-start(bf16[4,32,896]{2,1,0:T(8,128)(2,1)S(1)} %get-tuple-element.78), channel_id=1, source_target_pairs={{0,4},{4,0},{8,12},{12,8},{16,20},{20,16},{24,28},{28,24},{1,5},{5... | collective-permute-start | bytes 688136 | tf_op jit(solution)/shard_map/ppermute | solution.py:21
  224.1 6.8 %collective-permute-start.19 = (bf16[2,32,768]{2,1,0:T(8,128)(2,1)S(1)}, bf16[2,32,768]{2,1,0:T(8,128)(2,1)S(1)}, u32[]{:S(2)}, u32[]{:S(2)}) collective-permute-start(bf16[2,32,768]{2,1,0:T(8,128)(2,1)S(1)} %get-tuple-element.86), channel_id=1, source_target_pairs={{0,8},{4,12},{8,0},{12,4},{16,24},{20,28},{24,16},{28,20},{1,9},{5... | collective-permute-start | bytes 294920 | tf_op jit(solution)/shard_map/ppermute | solution.py:21
  225.7 7.6 %collective-permute-start.20 = (bf16[2,32,768]{2,1,0:T(8,128)(2,1)S(1)}, bf16[2,32,768]{2,1,0:T(8,128)(2,1)S(1)}, u32[]{:S(2)}, u32[]{:S(2)}) collective-permute-start(bf16[2,32,768]{2,1,0:T(8,128)(2,1)S(1)} %get-tuple-element.86), channel_id=1, source_target_pairs={{0,16},{4,20},{8,24},{12,28},{16,0},{20,4},{24,8},{28,12},{1,17},{... | collective-permute-start | bytes 294920 | tf_op jit(solution)/shard_map/ppermute | solution.py:21
  230.0 6.5 %collective-permute-start.21 = (bf16[2,32,768]{2,1,0:T(8,128)(2,1)S(1)}, bf16[2,32,768]{2,1,0:T(8,128)(2,1)S(1)}, u32[]{:S(2)}, u32[]{:S(2)}) collective-permute-start(bf16[2,32,768]{2,1,0:T(8,128)(2,1)S(1)} %get-tuple-element.86), channel_id=1, source_target_pairs={{0,24},{4,28},{8,16},{12,20},{16,8},{20,12},{24,0},{28,4},{1,25},{... | collective-permute-start | bytes 294920 | tf_op jit(solution)/shard_map/ppermute | solution.py:21
  230.9 7.9 %collective-permute-start.4 = (f32[32,640]{1,0:T(8,128)S(1)}, f32[32,640]{1,0:T(8,128)S(1)}, u32[]{:S(2)}, u32[]{:S(2)}) collective-permute-start(f32[32,640]{1,0:T(8,128)S(1)} %get-tuple-element.98), channel_id=1, source_target_pairs={{0,2},{1,3},{2,0},{3,1},{4,6},{5,7},{6,4},{7,5},{8,10},{9,11},{10,... | collective-permute-start | bytes 245768 | tf_op jit(solution)/shard_map/ppermute | solution.py:21
  233.3 6.2 %collective-permute-start.5 = (f32[32,640]{1,0:T(8,128)S(1)}, f32[32,640]{1,0:T(8,128)S(1)}, u32[]{:S(2)}, u32[]{:S(2)}) collective-permute-start(f32[32,640]{1,0:T(8,128)S(1)} %get-tuple-element.99), channel_id=1, source_target_pairs={{0,3},{1,2},{2,1},{3,0},{4,7},{5,6},{6,5},{7,4},{8,11},{9,10},{10,... | collective-permute-start | bytes 245768 | tf_op jit(solution)/shard_map/ppermute | solution.py:21
  236.5 13.1 %collective-permute-start.17 = (bf16[2,4,32,896]{3,2,1,0:T(8,128)(2,1)S(1)}, bf16[2,4,32,896]{3,2,1,0:T(8,128)(2,1)S(1)}, u32[]{:S(2)}, u32[]{:S(2)}) collective-permute-start(bf16[2,4,32,896]{3,2,1,0:T(8,128)(2,1)S(1)} %get-tuple-element.63), channel_id=1, source_target_pairs={{0,2},{1,3},{2,0},{3,1},{4,6},{5,7},{6,4},{7,5},{8,10},{9,11},{10,... | collective-permute-start | bytes 1376264 | tf_op jit(solution)/shard_map/ppermute | solution.py:21
  238.9 7.8 %collective-permute-start.26 = (bf16[2,2,32,384]{3,2,1,0:T(8,128)(2,1)}, bf16[2,2,32,384]{3,2,1,0:T(8,128)(2,1)S(1)}, u32[]{:S(2)}, u32[]{:S(2)}) collective-permute-start(bf16[2,2,32,384]{3,2,1,0:T(8,128)(2,1)} %get-tuple-element.88), channel_id=1, source_target_pairs={{0,16},{4,20},{8,24},{12,28},{16,0},{20,4},{24,8},{28,12},{1,17},{... | collective-permute-start | bytes 294920 | tf_op jit(solution)/shard_map/ppermute | solution.py:21
  239.6 10.2 %collective-permute-start.22 = (bf16[4,2,32,768]{3,2,1,0:T(8,128)(2,1)S(1)}, bf16[4,2,32,768]{3,2,1,0:T(8,128)(2,1)S(1)}, u32[]{:S(2)}, u32[]{:S(2)}) collective-permute-start(bf16[4,2,32,768]{3,2,1,0:T(8,128)(2,1)S(1)} %get-tuple-element.65), channel_id=1, source_target_pairs={{0,4},{4,0},{8,12},{12,8},{16,20},{20,16},{24,28},{28,24},{1,5},{5... | collective-permute-start | bytes 1179656 | tf_op jit(solution)/shard_map/ppermute | solution.py:21
  243.0 6.6 %collective-permute-start.27 = (bf16[2,2,32,384]{3,2,1,0:T(8,128)(2,1)}, bf16[2,2,32,384]{3,2,1,0:T(8,128)(2,1)S(1)}, u32[]{:S(2)}, u32[]{:S(2)}) collective-permute-start(bf16[2,2,32,384]{3,2,1,0:T(8,128)(2,1)} %get-tuple-element.88), channel_id=1, source_target_pairs={{0,24},{4,28},{8,16},{12,20},{16,8},{20,12},{24,0},{28,4},{1,25},{... | collective-permute-start | bytes 294920 | tf_op jit(solution)/shard_map/ppermute | solution.py:21
  259.8 9.8 %all-to-all-start.6 = ((f32[8,1,64]{2,1,0:T(1,128)}), f32[8,1,64]{2,1,0:T(1,128)S(1)}, u32[]{:S(2)}, u32[]{:S(2)}) async-start(f32[8,1,64]{2,1,0:T(1,128)} %bitcast.173), calls=%async_computation.6 | async-start | bytes 8192 | tf_op jit(solution)/shard_map/all_to_all | solution.py:395
  (15 other events, 59.4 us)
Sparse Core Ops, SparseCore 0:
  10.4 65.6 all-gather.6
  87.4 68.8 all-gather.4
